TPU v7x, 512 devices: a whole 4x8x8 slice. The times are simulated.
512 devices in a mesh: gx: 8 (over x, core), gy: 8 (over z), gz: 8 (over y).
Axes of the slice: x: 4, y: 8, z: 8, core: 2. Of those that a mesh axis runs over, the one named last changes fastest.
Arguments:
- fine_coef: bfloat16 [4096, 512], P(('gx', 'gy', 'gz')), may hold values from -6 to 6
- mid_leaf: bfloat16 [512, 512], P(('gx', 'gy', 'gz')), may hold values from -6 to 6
- mid_child: int32 [512, 8], P(('gx', 'gy', 'gz')), may hold values from 0 to 7, as said below
- mid_parent: int32 [512], P(('gx', 'gy', 'gz')), may hold values from 0 to 511, each once
- mid_refined: int32 [512], P(('gx', 'gy', 'gz')), may hold values 0 or 1
- fine_nbr: int32 [4096, 27], P(('gx', 'gy', 'gz')), may hold values from -1 to 4095, as said below
- mid_nbr: int32 [512, 27], P(('gx', 'gy', 'gz')), may hold values from -1 to 511, as said below
- coarse_nbr: int32 [64, 27], replicated, may hold values from -1 to 63, as said below
- op_factor: float32 [3, 32, 3, 8, 8], replicated, may hold values from -1 to 1
- term_weight: float32 [32], replicated, may hold values from 0.05 to 1
Outputs:
- fine_out: float32 [4096, 512], P(('gx', 'gy', 'gz'))
- mid_out: float32 [512, 512], P(('gx', 'gy', 'gz'))
Inputs may be any that keep to these rules, and one draw needn't show every extreme that they name: `fine_nbr`: column d names the fine box adjacent across displacement (d // 9 - 1, d // 3 % 3 - 1, d % 3 - 1), or -1. Column 13 is the row's own box. Box g lies on device g // 8; the named box's device differs from the row's device along each of gx, gy, gz by 0 or by that component of the displacement. `mid_nbr`: column d names the middle box adjacent across displacement (d // 9 - 1, d // 3 % 3 - 1, d % 3 - 1), or -1. Column 13 is the row's own box. Box g lies on device g; the named box's device differs from the row's device along each of gx, gy, gz by 0 or by that component of the displacement. `coarse_nbr`: column d names the coarse box adjacent across displacement (d // 9 - 1, d // 3 % 3 - 1, d % 3 - 1), or -1. Column 13 is the row's own box. `mid_child`: the 1 row of one device together name each of its 8 local fine slots exactly once. `mid_parent`: each value appears once.
All inputs are finite; a program needn't handle non-finite values. No bound on the sum of `mid_refined` on one device may be relied on, other than what follows from the above.
Results may differ from a plain program's by a relative error of at most 0.006.
Values may be sent and summed in bfloat16 or wider, within the bound.
No kernel may reach another device: no remote copies, remote signals or barrier semaphores. Data moves between devices by JAX's collectives and lax.ppermute only.
A program may use at most 64 MiB of HBM per device.

v0:
```python
import math

import jax
import jax.numpy as jnp
import numpy as np
from jax import lax
from jax.sharding import Mesh
from jax.sharding import PartitionSpec as P

GX = ("gx_0", "gx_1")
GX_GY_GZ = ("gx_0", "gx_1", "gy", "gz")


exact_mode = lax.Precision.HIGHEST


def padded_2(cells, sides, width):
    for axis, dim in sides:
        count = lax.axis_size(axis)
        ends = count - 1
        head = lax.slice_in_dim(cells, 0, width, axis=dim)
        tail = lax.slice_in_dim(cells, cells.shape[dim] - width, cells.shape[dim], axis=dim)
        cells = jnp.concatenate(
            [
                lax.ppermute(tail, axis, [(i, (i + 1) % count) for i in range(ends)]),
                cells,
                lax.ppermute(head, axis, [((i + 1) % count, i) for i in range(ends)]),
            ],
            axis=dim,
        )
    return cells


def in_blocks(x, dim, count):
    lengths = x.shape
    pieces = x.reshape(*lengths[:dim], count, lengths[dim] // count, *lengths[dim + 1 :])
    return jnp.moveaxis(pieces, dim, 0)


def sum_at_owner(x, axis, dim):
    pieces = in_blocks(x, dim, lax.axis_size(axis))
    arrived = lax.all_to_all(pieces, axis, split_axis=0, concat_axis=0, tiled=True)
    return arrived.sum(axis=0)


def sum_by_axis(x, axes, dim):
    far, near = axes
    pieces = in_blocks(x, dim, lax.axis_size(far))
    nearer = sum_at_owner(pieces, near, dim + 1)
    arrived = lax.all_to_all(nearer, far, split_axis=0, concat_axis=0, tiled=True)
    return arrived.sum(axis=0)


def filled_up(lines, count):
    spare = -len(lines) % count
    return jnp.pad(lines, [(0, spare)] + [(0, 0)] * (lines.ndim - 1))


def copy_for_each(x, axis):
    copies = jnp.broadcast_to(x, (lax.axis_size(axis), *x.shape))
    return lax.all_to_all(copies, axis, split_axis=0, concat_axis=0, tiled=True)


def joined_along(pieces, dim):
    pieces = jnp.moveaxis(pieces, 0, dim)
    lengths = pieces.shape
    return pieces.reshape(*lengths[:dim], lengths[dim] * lengths[dim + 1], *lengths[dim + 2 :])


def gathered_by_axis(x, axes, dim):
    far, near = axes
    initial = copy_for_each(x, far)
    pieces = jnp.swapaxes(copy_for_each(initial, near), 0, 1)
    return joined_along(pieces.reshape(-1, *x.shape), dim)


def nested_sum(x, axes):
    lines = x.reshape(-1)
    own = sum_by_axis(filled_up(lines, lax.axis_size(axes[0]) * lax.axis_size(axes[1])), axes, 0)
    whole = gathered_by_axis(own, axes, 0)
    return whole[: len(lines)].reshape(x.shape)


def poly_multiply(left, right):
    result = [0.0] * (len(left) + len(right) - 1)
    for first, left_coef in enumerate(left):
        for second, right_coef in enumerate(right):
            result[first + second] += left_coef * right_coef
    return result


def poly_compose(coeffs, factor, offset):
    result = [0.0]
    power_term = [1.0]
    for coef in coeffs:
        padded = result + [0.0] * (len(power_term) - len(result))
        result = [padded[place] + coef * power_term[place] for place in range(len(power_term))]
        power_term = poly_multiply(power_term, [offset, factor])
    return result


def legendre_table(basis_order):
    polys = [[1.0], [0.0, 1.0]]
    for degree in range(1, basis_order):
        upper = [0.0] + [(2 * degree + 1) * coef for coef in polys[degree]]
        lower = [degree * coef for coef in polys[degree - 1]] + [0.0] * (
            len(upper) - len(polys[degree - 1])
        )
        polys.append([(upper[place] - lower[place]) / (degree + 1) for place in range(len(upper))])
    return [
        [math.sqrt(2 * degree + 1) * coef for coef in poly_compose(polys[degree], 2.0, -1.0)]
        for degree in range(basis_order)
    ]


def two_scale(basis_order):
    shifted = legendre_table(basis_order)
    filters = np.zeros((2, basis_order, basis_order))
    for which_half in range(2):
        for row_at in range(basis_order):
            halved = poly_compose(shifted[row_at], 0.5, 0.5 * which_half)
            for col_at in range(basis_order):
                product = poly_multiply(halved, shifted[col_at])
                total = sum((coef / (place + 1) for place, coef in enumerate(product)))
                filters[which_half, row_at, col_at] = total / math.sqrt(2.0)
    return jnp.asarray(filters, jnp.float32)


def compress(children, filters):
    box_count = children.shape[0]
    basis_order = filters.shape[1]
    cube_form = children.reshape(box_count, 2, 2, 2, basis_order, basis_order, basis_order)
    section_one = jnp.einsum("bijlxyz,ipx->bjlpyz", cube_form, filters, precision=exact_mode)
    section_two = jnp.einsum("bjlpyz,jqy->blpqz", section_one, filters, precision=exact_mode)
    section_three = jnp.einsum("blpqz,lrz->bpqr", section_two, filters, precision=exact_mode)
    return section_three.reshape(box_count, basis_order**3)


def prolong(parents, filters):
    box_count = parents.shape[0]
    basis_order = filters.shape[1]
    cube_form = parents.reshape(box_count, basis_order, basis_order, basis_order)
    section_one = jnp.einsum("bpqr,ipx->bixqr", cube_form, filters, precision=exact_mode)
    section_two = jnp.einsum("bixqr,jqy->bijxyr", section_one, filters, precision=exact_mode)
    section_three = jnp.einsum("bijxyr,lrz->bijlxyz", section_two, filters, precision=exact_mode)
    return section_three.reshape(box_count, 8, basis_order**3)


def level_tables(factors, weights):
    basis_order = factors.shape[-1]
    term_count = factors.shape[0]
    plane_size = basis_order * basis_order
    row_total = term_count * plane_size
    row_id = jnp.arange(row_total, dtype=jnp.int32)
    term_of = row_id // plane_size
    first_of = row_id // basis_order % basis_order
    second_of = row_id % basis_order
    pair_id = jnp.arange(term_count * basis_order, dtype=jnp.int32)
    select_first = ((term_of * basis_order + first_of)[:, None] == pair_id[None, :]).astype(
        jnp.float32
    )
    select_second = ((term_of * basis_order + second_of)[:, None] == pair_id[None, :]).astype(
        jnp.float32
    )
    col_id = jnp.arange(plane_size, dtype=jnp.int32)
    order_id = jnp.arange(basis_order, dtype=jnp.int32)
    spread_outer = (order_id[:, None] == (col_id // basis_order)[None, :]).astype(jnp.float32)
    spread_inner = (order_id[:, None] == (col_id % basis_order)[None, :]).astype(jnp.float32)
    across = jnp.transpose(factors, (1, 0, 3, 2)).reshape(3, term_count * basis_order, basis_order)
    left_pick = jnp.einsum("rs,esb->erb", select_first, across, precision=exact_mode)
    left_full = jnp.einsum("erb,bq->erq", left_pick, spread_outer, precision=exact_mode)
    right_pick = jnp.einsum("rs,esc->erc", select_second, across, precision=exact_mode)
    right_full = jnp.einsum("erc,cq->erq", right_pick, spread_inner, precision=exact_mode)
    weight_rows = jnp.dot(select_first, jnp.repeat(weights, basis_order), precision=exact_mode)
    blocks = weight_rows[None, None, :, None] * left_full[:, None] * right_full[None, :]
    return (factors.astype(jnp.bfloat16), blocks.astype(jnp.bfloat16))


def apply_boxes(sources, factor_bf, blocks):
    box_count = sources.shape[0]
    basis_order = factor_bf.shape[-1]
    plane_size = basis_order * basis_order
    cube_form = sources.reshape(box_count, 3, 3, 3, basis_order, plane_size)
    running = jnp.zeros((box_count * basis_order, plane_size), jnp.float32)
    for along_y in range(3):
        for along_z in range(3):
            picked = cube_form[:, :, along_y, along_z]
            mixed_terms = jnp.einsum(
                "mdax,bdxq->bamq", factor_bf, picked, preferred_element_type=jnp.float32
            ).astype(jnp.bfloat16)
            flat_terms = mixed_terms.reshape(box_count * basis_order, -1)
            running = running + jnp.dot(
                flat_terms, blocks[along_y, along_z], preferred_element_type=jnp.float32
            )
    return running.reshape(box_count, basis_order**3)


def pick_sources(source_table, near_ids):
    return source_table[jnp.maximum(near_ids, 0)] * (near_ids >= 0)[:, :, None].astype(jnp.bfloat16)


def apply_picked(source_table, near_ids, factor_bf, blocks):
    total_rows = near_ids.shape[0]
    group_rows = math.gcd(total_rows, 16)
    grouped = near_ids.reshape(total_rows // group_rows, group_rows, 27)

    def one_group(some_rows):
        return apply_boxes(pick_sources(source_table, some_rows), factor_bf, blocks)

    return lax.map(one_group, grouped).reshape(total_rows, -1)


def local_rows(near_ids, per_device):
    size_y = lax.axis_size("gy")
    size_z = lax.axis_size("gz")
    mine_x = lax.axis_index(GX)
    mine_y = lax.axis_index("gy")
    mine_z = lax.axis_index("gz")
    device = near_ids // per_device
    slot_at = near_ids % per_device
    other_x = device // (size_y * size_z)
    other_y = device // size_z % size_y
    other_z = device % size_z
    cell_at = (other_x - mine_x + 1) * 9 + (other_y - mine_y + 1) * 3 + (other_z - mine_z + 1)
    return jnp.where(near_ids >= 0, cell_at * per_device + slot_at, -1)


def near_fine(detail):
    shaped = detail.reshape((1, 1, 1) + detail.shape)
    extended = padded_2(shaped, ((GX, 0), ("gy", 1), ("gz", 2)), 1)
    return extended.reshape(-1, detail.shape[1])


def near_mid(detail):
    shaped = detail.reshape((1, 1, 1) + detail.shape)
    extended = padded_2(shaped, ((GX, 0), ("gy", 1), ("gz", 2)), 1)
    return extended.reshape(-1, detail.shape[1])


def shards(
    fine_coef,
    mid_leaf,
    mid_child,
    mid_parent,
    mid_refined,
    fine_nbr,
    mid_nbr,
    coarse_nbr,
    op_factor,
    term_weight,
):
    basis_order = op_factor.shape[-1]
    filters = two_scale(basis_order)
    mid_local = mid_child.shape[0]
    slots_dev = fine_coef.shape[0]
    coarse_count = coarse_nbr.shape[0]
    child_hot = (
        mid_child[:, :, None] == jnp.arange(slots_dev, dtype=jnp.int32)[None, None, :]
    ).astype(jnp.float32)
    refined = mid_refined.astype(jnp.float32)
    live_mask = jnp.einsum("mos,m->s", child_hot, refined, precision=exact_mode)
    children = fine_coef[mid_child].astype(jnp.float32)
    compressed = compress(children, filters)
    mid_source = jnp.where(
        mid_refined[:, None] > 0, compressed, mid_leaf.astype(jnp.float32)
    ).astype(jnp.bfloat16)
    mid_float = mid_source.astype(jnp.float32)
    spread = prolong(mid_float, filters)
    fine_from = jnp.einsum("mos,mok->sk", child_hot, spread, precision=exact_mode)
    fine_detail = (live_mask[:, None] * (fine_coef.astype(jnp.float32) - fine_from)).astype(
        jnp.bfloat16
    )
    parent = mid_parent // 8
    octant = mid_parent % 8
    octant_hot = (octant[:, None] == jnp.arange(8, dtype=jnp.int32)[None, :]).astype(jnp.float32)
    parent_hot = (parent[:, None] == jnp.arange(coarse_count, dtype=jnp.int32)[None, :]).astype(
        jnp.float32
    )
    placed = octant_hot[:, :, None] * mid_float[:, None, :]
    contribution = compress(placed, filters)
    partial_sum = jnp.dot(parent_hot.T, contribution, precision=exact_mode)
    coarse_source = nested_sum(partial_sum, (("gx_0", "gx_1"), ("gy", "gz")))
    fine_table = near_fine(fine_detail)
    fine_factor, fine_blocks = level_tables(op_factor[0], term_weight)
    fine_direct = apply_picked(
        fine_table, local_rows(fine_nbr, slots_dev), fine_factor, fine_blocks
    )
    parent_source = jnp.dot(parent_hot, coarse_source, precision=exact_mode)
    from_coarse = jnp.einsum(
        "mo,mok->mk", octant_hot, prolong(parent_source, filters), precision=exact_mode
    )
    mid_detail = (mid_float - from_coarse).astype(jnp.bfloat16)
    mid_table = near_mid(mid_detail)
    mid_factor, mid_blocks = level_tables(op_factor[1], term_weight)
    mid_direct = apply_picked(mid_table, local_rows(mid_nbr, mid_local), mid_factor, mid_blocks)
    coarse_table = coarse_source.astype(jnp.bfloat16)
    coarse_factor, coarse_blocks = level_tables(op_factor[2], term_weight)
    parent_out = apply_picked(coarse_table, coarse_nbr[parent], coarse_factor, coarse_blocks)
    mid_out = mid_direct + jnp.einsum(
        "mo,mok->mk", octant_hot, prolong(parent_out, filters), precision=exact_mode
    )
    fine_back = jnp.einsum(
        "mos,mok->sk", child_hot, prolong(mid_out, filters), precision=exact_mode
    )
    fine_out = live_mask[:, None] * (fine_direct + fine_back)
    return (fine_out, mid_out)


def solution(mesh):
    finer = Mesh(
        mesh.devices.reshape(4, 2, mesh.shape["gy"], mesh.shape["gz"]), ("gx_0", "gx_1", "gy", "gz")
    )
    placed = (
        P(GX_GY_GZ, None),
        P(GX_GY_GZ, None),
        P(GX_GY_GZ, None),
        P(GX_GY_GZ),
        P(GX_GY_GZ),
        P(GX_GY_GZ, None),
        P(GX_GY_GZ, None),
        P(),
        P(),
        P(),
    )
    return jax.shard_map(
        shards,
        mesh=finer,
        in_specs=placed,
        out_specs=(P(GX_GY_GZ, None), P(GX_GY_GZ, None)),
        check_vma=False,
    )
```

profile of v0, /device:TPU:1, one launch (start us, length us, event | category | flops | bytes accessed | tf_op | source)
XLA Modules:
  0.0 209.6 jit_solution(7499969370694679295)
XLA Ops:
  9.9 2.6 %convolution_bitcast_fusion.18 = f32[1,2,2,2,8,8,8]{5,6,4,2,1,3,0:T(8,128)S(1)} fusion(f32[2,8,8,1,1,1]{2,1,5,4,3,0:T(8,128)} %constant.326, f32[2,2,8,8,8]{4,3,2,0,1:T(8,128)S(1)} %convolution_bitcast_fusion.42), kind=kOutput, calls=%fused_computation.49 | convolution fusion | flops 393216 | bytes 25088 | tf_op jit(solution)/shard_map/bijxyr,lrz->bijlxyz/dot_general | solution.py:145
  13.8 4.5 %collective-permute-start = (bf16[1,1,1,8,512]{4,3,2,1,0:T(8,128)(2,1)S(1)}, bf16[1,1,1,8,512]{4,3,2,1,0:T(8,128)(2,1)S(1)}, u32[]{:S(2)}, u32[]{:S(2)}) collective-permute-start(bf16[1,1,1,8,512]{4,3,2,1,0:T(8,128)(2,1)S(1)} %fusion.58), channel_id=1, source_target_pairs={{0,64},{64,128},{128,192},{192,256},{256,320},{320,384},{384,448},... | collective-permute-start | bytes 24584 | tf_op jit(solution)/shard_map/ppermute | solution.py:25
  18.3 5.6 %collective-permute-start.1 = (bf16[1,1,1,8,512]{4,3,2,1,0:T(8,128)(2,1)S(1)}, bf16[1,1,1,8,512]{4,3,2,1,0:T(8,128)(2,1)S(1)}, u32[]{:S(2)}, u32[]{:S(2)}) collective-permute-start(bf16[1,1,1,8,512]{4,3,2,1,0:T(8,128)(2,1)S(1)} %fusion.58), channel_id=1, source_target_pairs={{64,0},{128,64},{192,128},{256,192},{320,256},{384,320},{448,384},... | collective-permute-start | bytes 24584 | tf_op jit(solution)/shard_map/ppermute | solution.py:27
  26.8 13.1 %all-to-all-start = ((f32[64,1,512]{2,1,0:T(1,128)}), f32[64,1,512]{2,1,0:T(1,128)}, u32[]{:S(2)}, u32[]{:S(2)}) async-start(f32[64,1,512]{2,1,0:T(1,128)} %reshape.1085), calls=%async_computation | async-start | bytes 262144 | tf_op jit(solution)/shard_map/all_to_all | solution.py:42
  55.5 1.9 multiply_convert_fusion
  58.0 1.9 multiply_convert_fusion.2
  59.9 2.7 %collective-permute-start.2 = (bf16[3,1,1,8,512]{4,3,2,1,0:T(8,128)(2,1)S(1)}, bf16[3,1,1,8,512]{4,3,2,1,0:T(8,128)(2,1)S(1)}, u32[]{:S(2)}, u32[]{:S(2)}) collective-permute-start(bf16[3,1,1,8,512]{4,3,2,1,0:T(8,128)(2,1)S(1)} %pad_maximum_fusion.3), channel_id=1, source_target_pairs={{0,8},{8,16},{16,24},{24,32},{32,40},{40,48},{48,56},{1,9},{9,17},... | collective-permute-start | bytes 73736 | tf_op jit(solution)/shard_map/ppermute | solution.py:25
  64.7 2.5 %collective-permute-done.3 = bf16[3,1,1,8,512]{4,3,2,1,0:T(8,128)(2,1)S(1)} collective-permute-done((bf16[3,1,1,8,512]{4,3,2,1,0:T(8,128)(2,1)S(1)}, bf16[3,1,1,8,512]{4,3,2,1,0:T(8,128)(2,1)S(1)}, u32[]{:S(2)}, u32[]{:S(2)}) %collective-permute-start.3) | collective-permute-done | bytes 24608 | tf_op jit(solution)/shard_map/ppermute | solution.py:27
  67.2 3.1 %collective-permute-start.4 = (bf16[3,3,1,8,512]{4,3,2,1,0:T(8,128)(2,1)S(1)}, bf16[3,3,1,8,512]{4,3,2,1,0:T(8,128)(2,1)S(1)}, u32[]{:S(2)}, u32[]{:S(2)}) collective-permute-start(bf16[3,3,1,8,512]{4,3,2,1,0:T(8,128)(2,1)S(1)} %pad_maximum_fusion.1), channel_id=1, source_target_pairs={{0,1},{1,2},{2,3},{3,4},{4,5},{5,6},{6,7},{8,9},{9,10},{10,11},{11... | collective-permute-start | bytes 221192 | tf_op jit(solution)/shard_map/ppermute | solution.py:25
  71.9 3.5 %collective-permute-done.5 = bf16[3,3,1,8,512]{4,3,2,1,0:T(8,128)(2,1)S(1)} collective-permute-done((bf16[3,3,1,8,512]{4,3,2,1,0:T(8,128)(2,1)S(1)}, bf16[3,3,1,8,512]{4,3,2,1,0:T(8,128)(2,1)S(1)}, u32[]{:S(2)}, u32[]{:S(2)}) %collective-permute-start.5) | collective-permute-done | bytes 73760 | tf_op jit(solution)/shard_map/ppermute | solution.py:27
  85.4 2.2 %reshape.825 = bf16[64,2048]{1,0:T(8,128)(2,1)} reshape(bf16[8,8,32,64]{3,2,1,0:T(8,128)(2,1)} %fusion.18) | data formatting | bytes 524288 | tf_op jit(solution)/shard_map/while/body/eval_jaxpr/reshape | solution.py:191
  87.6 2.2 %reshape.828 = bf16[64,2048]{1,0:T(8,128)(2,1)} reshape(bf16[8,8,32,64]{3,2,1,0:T(8,128)(2,1)} %fusion.17) | data formatting | bytes 524288 | tf_op jit(solution)/shard_map/while/body/eval_jaxpr/reshape | solution.py:191
  89.8 2.2 %reshape.829 = bf16[64,2048]{1,0:T(8,128)(2,1)} reshape(bf16[8,8,32,64]{3,2,1,0:T(8,128)(2,1)} %fusion.16) | data formatting | bytes 524288 | tf_op jit(solution)/shard_map/while/body/eval_jaxpr/reshape | solution.py:191
  92.1 2.2 %reshape.830 = bf16[64,2048]{1,0:T(8,128)(2,1)} reshape(bf16[8,8,32,64]{3,2,1,0:T(8,128)(2,1)} %fusion.15) | data formatting | bytes 524288 | tf_op jit(solution)/shard_map/while/body/eval_jaxpr/reshape | solution.py:191
  94.3 2.2 %reshape.831 = bf16[64,2048]{1,0:T(8,128)(2,1)} reshape(bf16[8,8,32,64]{3,2,1,0:T(8,128)(2,1)} %fusion.14) | data formatting | bytes 524288 | tf_op jit(solution)/shard_map/while/body/eval_jaxpr/reshape | solution.py:191
  102.7 2.2 %reshape.832 = bf16[64,2048]{1,0:T(8,128)(2,1)} reshape(bf16[8,8,32,64]{3,2,1,0:T(8,128)(2,1)} %fusion.13) | data formatting | bytes 524288 | tf_op jit(solution)/shard_map/while/body/eval_jaxpr/reshape | solution.py:191
  106.6 1.8 reduce.15
  109.2 8.3 %all-to-all-start.1 = ((f32[8,1,64]{2,1,0:T(1,128)}), f32[8,1,64]{2,1,0:T(1,128)S(1)}, u32[]{:S(2)}, u32[]{:S(2)}) async-start(f32[8,1,64]{2,1,0:T(1,128)} %bitcast.141), calls=%async_computation.1 | async-start | bytes 8192 | tf_op jit(solution)/shard_map/all_to_all | solution.py:50
  120.3 1.8 all-to-all-done.1
  122.7 3.9 %all-to-all-start.2 = ((f32[8,1,64]{2,1,0:T(1,128)}), f32[8,1,64]{2,1,0:T(1,128)S(1)}, u32[]{:S(2)}, u32[]{:S(2)}) async-start(f32[8,1,64]{2,1,0:T(1,128)} %broadcast_in_dim.47), calls=%async_computation.2 | async-start | bytes 8192 | tf_op jit(solution)/shard_map/all_to_all | solution.py:61
  128.2 2.9 %all-to-all-done.2 = f32[8,1,64]{2,1,0:T(1,128)S(1)} async-done(((f32[8,1,64]{2,1,0:T(1,128)}), f32[8,1,64]{2,1,0:T(1,128)S(1)}, u32[]{:S(2)}, u32[]{:S(2)}) %all-to-all-start.2) | async-done | bytes 2080 | tf_op jit(solution)/shard_map/all_to_all | solution.py:61
  132.0 13.2 %all-to-all-start.3 = ((f32[64,1,512]{2,1,0:T(1,128)}), f32[64,1,512]{2,1,0:T(1,128)S(1)}, u32[]{:S(2)}, u32[]{:S(2)}) async-start(f32[64,1,512]{2,1,0:T(1,128)} %reshape.1087), calls=%async_computation.3 | async-start | bytes 262144 | tf_op jit(solution)/shard_map/all_to_all | solution.py:61
  149.1 7.3 %all-to-all-done.3 = f32[64,1,512]{2,1,0:T(1,128)S(1)} async-done(((f32[64,1,512]{2,1,0:T(1,128)}), f32[64,1,512]{2,1,0:T(1,128)S(1)}, u32[]{:S(2)}, u32[]{:S(2)}) %all-to-all-start.3) | async-done | bytes 131104 | tf_op jit(solution)/shard_map/all_to_all | solution.py:61
  161.8 1.8 fusion.168
  164.3 1.9 convolution_bitcast_fusion.17
  166.6 4.2 %collective-permute-start.6 = (bf16[1,1,1,1,512]{4,2,1,0,3:T(2,128)(2,1)S(1)}, bf16[1,1,1,1,512]{4,2,1,0,3:T(2,128)(2,1)S(1)}, u32[]{:S(2)}, u32[]{:S(2)}) collective-permute-start(bf16[1,1,1,1,512]{4,2,1,0,3:T(2,128)(2,1)S(1)} %fusion.60), channel_id=1, source_target_pairs={{0,64},{64,128},{128,192},{192,256},{256,320},{320,384},{384,448},... | collective-permute-start | bytes 3080 | tf_op jit(solution)/shard_map/ppermute | solution.py:25
  170.8 1.9 collective-permute-start.7
  186.5 2.2 %collective-permute-start.8 = (bf16[3,1,1,1,512]{4,2,1,0,3:T(2,128)(2,1)S(1)}, bf16[3,1,1,1,512]{4,2,1,0,3:T(2,128)(2,1)S(1)}, u32[]{:S(2)}, u32[]{:S(2)}) collective-permute-start(bf16[3,1,1,1,512]{4,2,1,0,3:T(2,128)(2,1)S(1)} %pad_maximum_fusion.5), channel_id=1, source_target_pairs={{0,8},{8,16},{16,24},{24,32},{32,40},{40,48},{48,56},{1,9},{9,17},... | collective-permute-start | bytes 9224 | tf_op jit(solution)/shard_map/ppermute | solution.py:25
  190.1 1.9 convolution_bitcast_fusion.16
  193.2 2.3 %collective-permute-start.10 = (bf16[3,3,1,1,512]{4,2,1,0,3:T(2,128)(2,1)S(1)}, bf16[3,3,1,1,512]{4,2,1,0,3:T(2,128)(2,1)S(1)}, u32[]{:S(2)}, u32[]{:S(2)}) collective-permute-start(bf16[3,3,1,1,512]{4,2,1,0,3:T(2,128)(2,1)S(1)} %pad_maximum_fusion.4), channel_id=1, source_target_pairs={{0,1},{1,2},{2,3},{3,4},{4,5},{5,6},{6,7},{8,9},{9,10},{10,11},{11... | collective-permute-start | bytes 27656 | tf_op jit(solution)/shard_map/ppermute | solution.py:25
  196.9 3.1 %collective-permute-done.11 = bf16[3,3,1,1,512]{4,2,1,0,3:T(2,128)(2,1)S(1)} collective-permute-done((bf16[3,3,1,1,512]{4,2,1,0,3:T(2,128)(2,1)S(1)}, bf16[3,3,1,1,512]{4,2,1,0,3:T(2,128)(2,1)S(1)}, u32[]{:S(2)}, u32[]{:S(2)}) %collective-permute-start.11) | collective-permute-done | bytes 9248 | tf_op jit(solution)/shard_map/ppermute | solution.py:27
  206.5 1.9 convolution_bitcast_fusion.15
  (239 shorter events, 91.4 us)
Async XLA Ops:
  0.6 48.3 %copy-start = (s32[64,27]{0,1:T(8,128)S(1)}, s32[64,27]{0,1:T(8,128)}, u32[]{:S(2)}) copy-start(s32[64,27]{0,1:T(8,128)} %param.18) | copy-start | bytes 20740
  0.6 24.0 %copy-start.6 = (f32[2,8,8,1,1,1]{2,1,0,5,4,3:T(8,128)S(1)}, f32[2,8,8,1,1,1]{2,1,0,5,4,3:T(8,128)}, u32[]{:S(2)}) copy-start(f32[2,8,8,1,1,1]{2,1,0,5,4,3:T(8,128)} %constant.330) | copy-start | bytes 1540
  0.7 24.4 %copy-start.5 = (f32[2,8,8,1,1]{2,1,0,4,3:T(8,128)S(1)}, f32[2,8,8,1,1]{2,1,0,4,3:T(8,128)}, u32[]{:S(2)}) copy-start(f32[2,8,8,1,1]{2,1,0,4,3:T(8,128)} %constant.329) | copy-start | bytes 1540
  0.7 24.6 %copy-start.2 = (f32[2,8,8,1]{2,1,3,0:T(8,128)S(1)}, f32[2,8,8,1]{2,1,3,0:T(8,128)}, u32[]{:S(2)}) copy-start(f32[2,8,8,1]{2,1,3,0:T(8,128)} %constant.328) | copy-start | bytes 1540
  3.3 36.6 %copy-start.1 = (f32[3,32,3,8,8]{1,4,3,2,0:T(8,128)S(1)}, f32[3,32,3,8,8]{1,4,3,2,0:T(8,128)}, u32[]{:S(2)}) copy-start(f32[3,32,3,8,8]{1,4,3,2,0:T(8,128)} %param.19) | copy-start | bytes 221188
  13.8 46.1 %collective-permute-start = (bf16[1,1,1,8,512]{4,3,2,1,0:T(8,128)(2,1)S(1)}, bf16[1,1,1,8,512]{4,3,2,1,0:T(8,128)(2,1)S(1)}, u32[]{:S(2)}, u32[]{:S(2)}) collective-permute-start(bf16[1,1,1,8,512]{4,3,2,1,0:T(8,128)(2,1)S(1)} %fusion.58), channel_id=1, source_target_pairs={{0,64},{64,128},{128,192},{192,256},{256,320},{320,384},{384,448},... | collective-permute-start | bytes 24584 | tf_op jit(solution)/shard_map/ppermute | solution.py:25
  18.3 41.6 %collective-permute-start.1 = (bf16[1,1,1,8,512]{4,3,2,1,0:T(8,128)(2,1)S(1)}, bf16[1,1,1,8,512]{4,3,2,1,0:T(8,128)(2,1)S(1)}, u32[]{:S(2)}, u32[]{:S(2)}) collective-permute-start(bf16[1,1,1,8,512]{4,3,2,1,0:T(8,128)(2,1)S(1)} %fusion.58), channel_id=1, source_target_pairs={{64,0},{128,64},{192,128},{256,192},{320,256},{384,320},{448,384},... | collective-permute-start | bytes 24584 | tf_op jit(solution)/shard_map/ppermute | solution.py:27
  26.8 79.3 %all-to-all-start = ((f32[64,1,512]{2,1,0:T(1,128)}), f32[64,1,512]{2,1,0:T(1,128)}, u32[]{:S(2)}, u32[]{:S(2)}) async-start(f32[64,1,512]{2,1,0:T(1,128)} %reshape.1085), calls=%async_computation | async-start | bytes 262144 | tf_op jit(solution)/shard_map/all_to_all | solution.py:42
  41.7 7.4 %copy-start.9 = (f32[32]{0:T(128)S(1)}, f32[32]{0:T(128)}, u32[]{:S(2)}) copy-start(f32[32]{0:T(128)} %param.20) | copy-start | bytes 388
  43.0 7.4 %copy-start.10 = (s32[1,27]{1,0:T(1,128)S(1)}, s32[1,27]{1,0:T(1,128)}, u32[]{:S(2)}) copy-start(s32[1,27]{1,0:T(1,128)} %param.17) | copy-start | bytes 328
  51.2 2.5 %copy-start.8 = (s32[8,27]{1,0:T(8,128)S(1)}, s32[8,27]{1,0:T(8,128)}, u32[]{:S(2)}) copy-start(s32[8,27]{1,0:T(8,128)} %param.16) | copy-start | bytes 2596
  59.9 4.8 %collective-permute-start.2 = (bf16[3,1,1,8,512]{4,3,2,1,0:T(8,128)(2,1)S(1)}, bf16[3,1,1,8,512]{4,3,2,1,0:T(8,128)(2,1)S(1)}, u32[]{:S(2)}, u32[]{:S(2)}) collective-permute-start(bf16[3,1,1,8,512]{4,3,2,1,0:T(8,128)(2,1)S(1)} %pad_maximum_fusion.3), channel_id=1, source_target_pairs={{0,8},{8,16},{16,24},{24,32},{32,40},{40,48},{48,56},{1,9},{9,17},... | collective-permute-start | bytes 73736 | tf_op jit(solution)/shard_map/ppermute | solution.py:25
  62.6 4.6 %collective-permute-start.3 = (bf16[3,1,1,8,512]{4,3,2,1,0:T(8,128)(2,1)S(1)}, bf16[3,1,1,8,512]{4,3,2,1,0:T(8,128)(2,1)S(1)}, u32[]{:S(2)}, u32[]{:S(2)}) collective-permute-start(bf16[3,1,1,8,512]{4,3,2,1,0:T(8,128)(2,1)S(1)} %pad_maximum_fusion.3), channel_id=1, source_target_pairs={{8,0},{16,8},{24,16},{32,24},{40,32},{48,40},{56,48},{9,1},{17,9},... | collective-permute-start | bytes 73736 | tf_op jit(solution)/shard_map/ppermute | solution.py:27
  67.2 4.7 %collective-permute-start.4 = (bf16[3,3,1,8,512]{4,3,2,1,0:T(8,128)(2,1)S(1)}, bf16[3,3,1,8,512]{4,3,2,1,0:T(8,128)(2,1)S(1)}, u32[]{:S(2)}, u32[]{:S(2)}) collective-permute-start(bf16[3,3,1,8,512]{4,3,2,1,0:T(8,128)(2,1)S(1)} %pad_maximum_fusion.1), channel_id=1, source_target_pairs={{0,1},{1,2},{2,3},{3,4},{4,5},{5,6},{6,7},{8,9},{9,10},{10,11},{11... | collective-permute-start | bytes 221192 | tf_op jit(solution)/shard_map/ppermute | solution.py:25
  70.3 5.1 %collective-permute-start.5 = (bf16[3,3,1,8,512]{4,3,2,1,0:T(8,128)(2,1)S(1)}, bf16[3,3,1,8,512]{4,3,2,1,0:T(8,128)(2,1)S(1)}, u32[]{:S(2)}, u32[]{:S(2)}) collective-permute-start(bf16[3,3,1,8,512]{4,3,2,1,0:T(8,128)(2,1)S(1)} %pad_maximum_fusion.1), channel_id=1, source_target_pairs={{1,0},{2,1},{3,2},{4,3},{5,4},{6,5},{7,6},{9,8},{10,9},{11,10},{12... | collective-permute-start | bytes 221192 | tf_op jit(solution)/shard_map/ppermute | solution.py:27
  109.2 12.8 %all-to-all-start.1 = ((f32[8,1,64]{2,1,0:T(1,128)}), f32[8,1,64]{2,1,0:T(1,128)S(1)}, u32[]{:S(2)}, u32[]{:S(2)}) async-start(f32[8,1,64]{2,1,0:T(1,128)} %bitcast.141), calls=%async_computation.1 | async-start | bytes 8192 | tf_op jit(solution)/shard_map/all_to_all | solution.py:50
  122.7 8.4 %all-to-all-start.2 = ((f32[8,1,64]{2,1,0:T(1,128)}), f32[8,1,64]{2,1,0:T(1,128)S(1)}, u32[]{:S(2)}, u32[]{:S(2)}) async-start(f32[8,1,64]{2,1,0:T(1,128)} %broadcast_in_dim.47), calls=%async_computation.2 | async-start | bytes 8192 | tf_op jit(solution)/shard_map/all_to_all | solution.py:61
  132.0 24.5 %all-to-all-start.3 = ((f32[64,1,512]{2,1,0:T(1,128)}), f32[64,1,512]{2,1,0:T(1,128)S(1)}, u32[]{:S(2)}, u32[]{:S(2)}) async-start(f32[64,1,512]{2,1,0:T(1,128)} %reshape.1087), calls=%async_computation.3 | async-start | bytes 262144 | tf_op jit(solution)/shard_map/all_to_all | solution.py:61
  147.8 16.1 %copy-start.4 = (f32[2,8,8,1,1]{2,1,4,3,0:T(8,128)S(1)}, f32[2,8,8,1,1]{2,1,4,3,0:T(8,128)}, u32[]{:S(2)}) copy-start(f32[2,8,8,1,1]{2,1,4,3,0:T(8,128)} %constant.327) | copy-start | bytes 1540
  147.9 16.4 %copy-start.3 = (f32[2,8,8,1,1,1]{2,1,5,4,3,0:T(8,128)S(1)}, f32[2,8,8,1,1,1]{2,1,5,4,3,0:T(8,128)}, u32[]{:S(2)}) copy-start(f32[2,8,8,1,1,1]{2,1,5,4,3,0:T(8,128)} %constant.326) | copy-start | bytes 1540
  166.6 19.9 %collective-permute-start.6 = (bf16[1,1,1,1,512]{4,2,1,0,3:T(2,128)(2,1)S(1)}, bf16[1,1,1,1,512]{4,2,1,0,3:T(2,128)(2,1)S(1)}, u32[]{:S(2)}, u32[]{:S(2)}) collective-permute-start(bf16[1,1,1,1,512]{4,2,1,0,3:T(2,128)(2,1)S(1)} %fusion.60), channel_id=1, source_target_pairs={{0,64},{64,128},{128,192},{192,256},{256,320},{320,384},{384,448},... | collective-permute-start | bytes 3080 | tf_op jit(solution)/shard_map/ppermute | solution.py:25
  170.8 15.7 %collective-permute-start.7 = (bf16[1,1,1,1,512]{4,2,1,0,3:T(2,128)(2,1)S(1)}, bf16[1,1,1,1,512]{4,2,1,0,3:T(2,128)(2,1)S(1)}, u32[]{:S(2)}, u32[]{:S(2)}) collective-permute-start(bf16[1,1,1,1,512]{4,2,1,0,3:T(2,128)(2,1)S(1)} %fusion.60), channel_id=1, source_target_pairs={{64,0},{128,64},{192,128},{256,192},{320,256},{384,320},{448,384},... | collective-permute-start | bytes 3080 | tf_op jit(solution)/shard_map/ppermute | solution.py:27
  186.5 5.7 %collective-permute-start.8 = (bf16[3,1,1,1,512]{4,2,1,0,3:T(2,128)(2,1)S(1)}, bf16[3,1,1,1,512]{4,2,1,0,3:T(2,128)(2,1)S(1)}, u32[]{:S(2)}, u32[]{:S(2)}) collective-permute-start(bf16[3,1,1,1,512]{4,2,1,0,3:T(2,128)(2,1)S(1)} %pad_maximum_fusion.5), channel_id=1, source_target_pairs={{0,8},{8,16},{16,24},{24,32},{32,40},{40,48},{48,56},{1,9},{9,17},... | collective-permute-start | bytes 9224 | tf_op jit(solution)/shard_map/ppermute | solution.py:25
  188.8 4.4 %collective-permute-start.9 = (bf16[3,1,1,1,512]{4,2,1,0,3:T(2,128)(2,1)S(1)}, bf16[3,1,1,1,512]{4,2,1,0,3:T(2,128)(2,1)S(1)}, u32[]{:S(2)}, u32[]{:S(2)}) collective-permute-start(bf16[3,1,1,1,512]{4,2,1,0,3:T(2,128)(2,1)S(1)} %pad_maximum_fusion.5), channel_id=1, source_target_pairs={{8,0},{16,8},{24,16},{32,24},{40,32},{48,40},{56,48},{9,1},{17,9},... | collective-permute-start | bytes 9224 | tf_op jit(solution)/shard_map/ppermute | solution.py:27
  193.2 3.8 %collective-permute-start.10 = (bf16[3,3,1,1,512]{4,2,1,0,3:T(2,128)(2,1)S(1)}, bf16[3,3,1,1,512]{4,2,1,0,3:T(2,128)(2,1)S(1)}, u32[]{:S(2)}, u32[]{:S(2)}) collective-permute-start(bf16[3,3,1,1,512]{4,2,1,0,3:T(2,128)(2,1)S(1)} %pad_maximum_fusion.4), channel_id=1, source_target_pairs={{0,1},{1,2},{2,3},{3,4},{4,5},{5,6},{6,7},{8,9},{9,10},{10,11},{11... | collective-permute-start | bytes 27656 | tf_op jit(solution)/shard_map/ppermute | solution.py:25
  195.5 4.5 %collective-permute-start.11 = (bf16[3,3,1,1,512]{4,2,1,0,3:T(2,128)(2,1)S(1)}, bf16[3,3,1,1,512]{4,2,1,0,3:T(2,128)(2,1)S(1)}, u32[]{:S(2)}, u32[]{:S(2)}) collective-permute-start(bf16[3,3,1,1,512]{4,2,1,0,3:T(2,128)(2,1)S(1)} %pad_maximum_fusion.4), channel_id=1, source_target_pairs={{1,0},{2,1},{3,2},{4,3},{5,4},{6,5},{7,6},{9,8},{10,9},{11,10},{12... | collective-permute-start | bytes 27656 | tf_op jit(solution)/shard_map/ppermute | solution.py:27
  203.5 5.2 %copy-start.11 = (s32[1,8]{1,0:T(1,128)S(1)}, s32[1,8]{1,0:T(1,128)}, u32[]{:S(2)}) copy-start(s32[1,8]{1,0:T(1,128)} %param.13) | copy-start | bytes 100
  205.8 3.7 %copy-start.7 = (f32[512]{0:T(512)}, f32[512]{0:T(512)S(1)}, u32[]{:S(2)}) copy-start(f32[512]{0:T(512)S(1)} %add.351) | copy-start | bytes 6148
where the time goes:
time: 214 us; the launch traced here: 210 us
  starting transfers between devices  70.5 us (33%)
  matrix products  70.3 us (33%)
  local copies, waits for them, and re-layouts  32.8 us (15%)
  waiting for transfers between devices  22 us (10%)
  other arithmetic  10.9 us (5%)
  between operations  2.94 us (1%)
    dot_general x27, matrix products, apply_boxes(): jnp.dot(flat_terms, blocks[along_y, along_z], preferred_element_type=jnp....  22.8 us
    reshape x27, local copies, waits for them, and re-layouts, apply_boxes(): flat_terms = mixed_terms.reshape(box_count * basis_order, -1)  20.7 us
    ppermute x6, starting transfers between devices, padded_2(): lax.ppermute(tail, axis, [(i, (i + 1) % count) for i in range(ends)])  19.1 us
    all_to_all x2, starting transfers between devices, copy_for_each(): return lax.all_to_all(copies, axis, split_axis=0, concat_axis=0, tiled=True)  17.1 us
    dot_general x27, matrix products, apply_boxes(): jnp.einsum('mdax,bdxq->bamq', factor_bf, picked, preferred_element_type=j...  14.6 us
    all_to_all x1, starting transfers between devices, sum_at_owner(): lax.all_to_all(pieces, axis, split_axis=0, concat_axis=0, tiled=True)  13.1 us
    ppermute x6, starting transfers between devices, padded_2(): lax.ppermute(head, axis, [((i + 1) % count, i) for i in range(ends)])  12.9 us
    all_to_all x2, waiting for transfers between devices, copy_for_each(): return lax.all_to_all(copies, axis, split_axis=0, concat_axis=0, tiled=True)  10.2 us
  transfers between devices with their start and end apart: 16, of which 8 were waited for; matrix products, arithmetic and copies ran while one was open for 37% of the time, Pallas kernels for 0%

commit v1 on v0

v1 whole, which is shorter than its diff:
```python
import functools
import math

import jax
import jax.numpy as jnp
import ml_dtypes
import numpy as np
from jax import lax
from jax.experimental import pallas as pl
from jax.experimental.pallas import tpu as pltpu
from jax.sharding import PartitionSpec as P

K = 8
PLANE = 64
TERMS = 32
QUADS = 8
ROWS_W = 640
GONE = 27 * 8
BF16 = jnp.bfloat16
F32 = jnp.float32
VMEM_LIMIT = 40 * 1024 * 1024


def poly_multiply(left, right):
    result = [0.0] * (len(left) + len(right) - 1)
    for first, left_coef in enumerate(left):
        for second, right_coef in enumerate(right):
            result[first + second] += left_coef * right_coef
    return result


def poly_compose(coeffs, factor, offset):
    result = [0.0]
    power_term = [1.0]
    for coef in coeffs:
        padded = result + [0.0] * (len(power_term) - len(result))
        result = [padded[place] + coef * power_term[place] for place in range(len(power_term))]
        power_term = poly_multiply(power_term, [offset, factor])
    return result


def legendre_table(basis_order):
    polys = [[1.0], [0.0, 1.0]]
    for degree in range(1, basis_order):
        upper = [0.0] + [(2 * degree + 1) * coef for coef in polys[degree]]
        lower = [degree * coef for coef in polys[degree - 1]] + [0.0] * (
            len(upper) - len(polys[degree - 1])
        )
        polys.append([(upper[place] - lower[place]) / (degree + 1) for place in range(len(upper))])
    return [
        [math.sqrt(2 * degree + 1) * coef for coef in poly_compose(polys[degree], 2.0, -1.0)]
        for degree in range(basis_order)
    ]


@functools.cache
def two_scale(basis_order):
    shifted = legendre_table(basis_order)
    filters = np.zeros((2, basis_order, basis_order))
    for which_half in range(2):
        for row_at in range(basis_order):
            halved = poly_compose(shifted[row_at], 0.5, 0.5 * which_half)
            for col_at in range(basis_order):
                product = poly_multiply(halved, shifted[col_at])
                total = sum((coef / (place + 1) for place, coef in enumerate(product)))
                filters[which_half, row_at, col_at] = total / math.sqrt(2.0)
    return filters.astype(np.float32).astype(np.float64)


def two_parts(matrix):
    high = matrix.astype(ml_dtypes.bfloat16)
    low = (matrix - high.astype(np.float64)).astype(ml_dtypes.bfloat16)
    return high, low


@functools.cache
def filter_tables():
    h = two_scale(K)
    pair = np.einsum("jqy,lrz->jlqryz", h, h).reshape(4, PLANE, PLANE)
    to_coarse = pair.transpose(0, 2, 1).reshape(4 * PLANE, PLANE)
    comp = np.concatenate(two_parts(to_coarse), axis=1)
    to_fine = pair.transpose(1, 0, 2).reshape(PLANE, 4 * PLANE)
    prol = np.concatenate(two_parts(to_fine), axis=1)
    contrib = np.stack([np.concatenate(two_parts(pair[k].T), axis=1) for k in range(4)])
    single = np.stack([np.concatenate(two_parts(pair[k]), axis=1) for k in range(4)])
    mid = np.zeros((2, PLANE, 4, 2, PLANE))
    for half in range(2):
        mid[half, :, :, half, :] = pair.transpose(1, 0, 2)
    mids = np.concatenate(two_parts(mid.reshape(128, 512)), axis=1)
    rows_c = np.broadcast_to(h.transpose(0, 2, 1).reshape(16, 8)[:, :, None], (16, 8, 128))
    rows_p = np.broadcast_to(h.reshape(16, 8)[:, :, None], (16, 8, 128))
    return dict(
        comp=comp,
        prol=prol,
        contrib=contrib,
        single=single,
        mids=mids,
        rows_c=np.ascontiguousarray(rows_c).astype(np.float32),
        rows_p=np.ascontiguousarray(rows_p).astype(np.float32),
    )


@functools.cache
def select_tables():
    n4 = np.arange(4)
    a = np.arange(8)
    eye4 = (n4[:, None] == n4[None, :]).astype(np.float64)
    eye8 = (a[:, None] == a[None, :]).astype(np.float64)
    one = np.ones(8)
    left = np.einsum("nm,ab,c->nambc", eye4, eye8, one).reshape(32, 256)
    right = np.einsum("nm,ac,b->nambc", eye4, eye8, one).reshape(32, 256)
    return np.concatenate([left, right], axis=1).astype(ml_dtypes.bfloat16)


def split(value):
    high = value.astype(BF16)
    return high, (value - high.astype(F32)).astype(BF16)


def dot(left, right):
    return jnp.dot(left, right, preferred_element_type=F32)


def fine_dot(value, table):
    rows = value.shape[0]
    width = table.shape[1] // 2
    if rows % 16 == 0:
        result = dot(jnp.concatenate(split(value), axis=0), table)
    else:
        high = value.astype(BF16).astype(F32)
        result = dot(jnp.concatenate([high, value - high], axis=0).astype(BF16), table)
    return result[:rows, :width] + result[rows:, :width] + result[:rows, width:]


def low_lanes(shape):
    return lax.broadcasted_iota(jnp.int32, shape, len(shape) - 1) < PLANE


def turned(value):
    return pltpu.roll(value, PLANE, value.ndim - 1)


def row_mix(tables, tile):
    total = None
    for p in range(8):
        term = tables[p] * tile[p : p + 1, :]
        total = term if total is None else total + term
    return total


def two_row_mixes(rows_ref, tile, width):
    return [
        row_mix([rows_ref[i * 8 + p, :, :width] for p in range(8)], tile) for i in range(2)
    ]


def local_cell(near, own, per_device):
    device = near // per_device if per_device == 1 else near >> 3
    step_x = (device >> 6) - (own >> 6) + 1
    step_y = ((device >> 3) & 7) - ((own >> 3) & 7) + 1
    step_z = (device & 7) - (own & 7) + 1
    return step_x * 9 + step_y * 3 + step_z


def build_tables(factors, weighted, select, ab_ref, w_ref):
    left = dot(jnp.concatenate(split(weighted), axis=0), select[:, :256])
    right = dot(jnp.concatenate(split(factors), axis=0), select[:, 256:])
    ab_ref[:, :, :256] = (left[:192] + left[192:]).reshape(8, 24, 256)
    ab_ref[:, :, 256:] = (right[:192] + right[192:]).reshape(8, 24, 256)

    def one_quad(quad, carry):
        inner = [ab_ref[quad, ez * 8 : ez * 8 + 8, 256:512] for ez in range(3)]
        for ey in range(3):
            for pair in range(4):
                at = ey * 8 + 2 * pair
                first = ab_ref[quad, at : at + 1, 0:256]
                second = ab_ref[quad, at + 1 : at + 2, 0:256]
                for ez in range(3):
                    tile = jnp.concatenate([first * inner[ez], second * inner[ez]], axis=0)
                    row = (ey * 3 + ez) * PLANE + pair * 16
                    w_ref[quad, row : row + 16, :] = tile.astype(BF16)
        w_ref[quad, 576:640, :] = jnp.zeros((64, 256), BF16)
        return carry

    lax.fori_loop(0, QUADS, one_quad, 0)


def diagonal_sum(result, rows):
    total = None
    for term in range(4):
        piece = result[term * rows : (term + 1) * rows, term * PLANE : (term + 1) * PLANE]
        total = piece if total is None else total + piece
    return total


def apply_one(sources, x_table, w_ref):
    mixed = dot(x_table, sources).astype(BF16)
    result = None
    for quad in range(QUADS):
        part = dot(mixed[quad * 32 : quad * 32 + 32, :], w_ref[quad])
        result = part if result is None else result + part
    return diagonal_sum(result, 8)


def first_kernel(
    child, parent, refined, fine_nbr, mid_nbr, coarse_nbr, coef, leaf,
    comp, prol, contrib, rows_c, rows_p,
    halo, payload, fine_at, mid_at, coarse_at, source, detail,
):
    near = fine_nbr[...]
    own = near[:, 13:14] >> 3
    cell = local_cell(near, own, 8) * 8 + (near & 7)
    fine_at[:, 0:27] = jnp.where(near >= 0, cell, GONE)
    near_mid = mid_nbr[...]
    own_mid = near_mid[:, 13:14]
    mid_at[:, 0:27] = jnp.where(near_mid >= 0, local_cell(near_mid, own_mid, 1), 27)
    mid_at[:, 27:32] = jnp.full((1, 5), 27, jnp.int32)
    slot = parent[0] >> 3
    octant = parent[0] & 7
    near_coarse = coarse_nbr[pl.ds(slot, 1), :]
    coarse_at[:, 0:27] = jnp.where(near_coarse >= 0, near_coarse, 64)
    coarse_at[:, 27:32] = jnp.full((1, 5), 64, jnp.int32)

    values = coef[...].astype(F32)
    for a in range(8):
        source[:, a, :] = values[:, a * PLANE : (a + 1) * PLANE]
    tiles = [source[child[0, o]] for o in range(8)]
    lhs = jnp.concatenate(
        [jnp.concatenate(tiles[0:4], axis=1), jnp.concatenate(tiles[4:8], axis=1)], axis=0
    ).astype(BF16)
    both = dot(lhs, comp[...])
    partial = both[:, :PLANE] + both[:, PLANE:]
    compressed = None
    for k in range(16):
        term = rows_c[k, :, :PLANE] * partial[k : k + 1, :]
        compressed = term if compressed is None else compressed + term
    leaf_row = leaf[...].astype(F32)
    leaf_tile = jnp.concatenate(
        [leaf_row[:, a * PLANE : (a + 1) * PLANE] for a in range(8)], axis=0
    )
    middle = jnp.where(refined[0] > 0, compressed, leaf_tile).astype(BF16).astype(F32)

    row_at = (octant >> 2) * 8
    inner = row_mix([rows_c[row_at + x, :, :PLANE] for x in range(8)], middle)
    added = fine_dot(inner, contrib[octant & 3])
    low8 = low_lanes((8, 128))
    tag = jnp.full((8, 128), slot, jnp.int32).astype(F32)
    tile = jnp.where(low8, jnp.concatenate([added, added], axis=1), tag).astype(BF16)
    payload[...] = jnp.broadcast_to(tile[None], payload.shape)

    live = jnp.full((8, PLANE), refined[0], jnp.int32).astype(F32)
    upper = jnp.concatenate(two_row_mixes(rows_p, middle, PLANE), axis=0)
    spread = fine_dot(upper, prol[...])
    for o in range(8):
        i, jl = o // 4, o % 4
        part = spread[i * 8 : i * 8 + 8, jl * PLANE : (jl + 1) * PLANE]
        detail[child[0, o]] = live * (tiles[o] - part)
    for group in range(2):
        base = group * 4
        halo[group * 16 : group * 16 + 16, :] = jnp.concatenate(
            [
                jnp.concatenate([detail[base], detail[base + 1]], axis=1),
                jnp.concatenate([detail[base + 2], detail[base + 3]], axis=1),
            ],
            axis=0,
        ).astype(BF16)
    meta = jnp.where(low8, tag, jnp.full((8, 128), octant, jnp.int32).astype(F32))
    halo[32:48, :] = jnp.concatenate(
        [jnp.concatenate([middle, middle], axis=1), meta], axis=0
    ).astype(BF16)


def plane_kernel(arrived, copies):
    rows = arrived[...].astype(F32).reshape(512, 128)
    other = turned(rows)
    low = low_lanes((512, 128))
    value = jnp.where(low, rows, other)
    tag = jnp.where(low, other, rows)
    half = jnp.where(low, 0, 1)
    rhs = jnp.where((tag.astype(jnp.int32) & 1) == half, value, 0.0).astype(BF16)
    pick = jnp.where(lax.broadcasted_iota(jnp.int32, (8, 128), 1) == 0, 1.0, 0.0).astype(BF16)
    along = lax.dot_general(
        pick, tag.astype(BF16), (((1,), (1,)), ((), ())), preferred_element_type=F32
    ).astype(jnp.int32)
    p_of = lax.broadcasted_iota(jnp.int32, (8, 512), 1) & 7
    key = jnp.where(p_of == lax.broadcasted_iota(jnp.int32, (8, 512), 0), along >> 1, -1)
    hot = jnp.concatenate(
        [jnp.where(key == c2, 1.0, 0.0) for c2 in range(32)], axis=0
    ).astype(BF16)
    partial = dot(hot, rhs).astype(BF16)
    copies[...] = jnp.broadcast_to(partial[None], copies.shape)


def fine_kernel(
    fine_at, left, centre, right, factors, weighted, x_table, select,
    direct, mid_tiles, parents, table, mixed, w_ref, ab_ref,
):
    low8 = low_lanes((8, 128))
    lanes = lax.broadcasted_iota(jnp.int32, (1, 128), 1)
    table[GONE] = jnp.zeros((8, 128), F32)
    mid_tiles[27] = jnp.zeros((8, 128), F32)
    names = jnp.full((1, 128), 512, jnp.int32)
    for step_x, ref in enumerate((left, centre, right)):
        for cell in range(9):
            at = (step_x * 9 + cell) * 8
            base = cell * 48
            for group in range(2):
                both = ref[base + group * 16 : base + group * 16 + 16, :].astype(F32)
                for sub in range(2):
                    tile = both[sub * 8 : sub * 8 + 8, :]
                    other = turned(tile)
                    table[at + group * 4 + sub * 2] = jnp.where(low8, tile, other)
                    table[at + group * 4 + sub * 2 + 1] = jnp.where(low8, other, tile)
            last = ref[base + 32 : base + 48, :].astype(F32)
            mid_tiles[step_x * 9 + cell] = last[0:8, :]
            meta = last[8:9, :]
            name = meta * 8.0 + turned(meta)
            name = jnp.where(low8[0:1], name, turned(name)).astype(jnp.int32)
            names = jnp.where(lanes == step_x * 9 + cell, name, names)
    parents[...] = names

    build_tables(factors[...], weighted[...], select[...], ab_ref, w_ref)

    def source(t, ex, e):
        if e > 8:
            return table[GONE]
        return table[fine_at[t, ex * 9 + e]]

    for pair in range(4):
        pieces = []
        for t in (2 * pair, 2 * pair + 1):
            for ep in range(5):
                pieces.append(
                    jnp.concatenate(
                        [
                            jnp.where(low8, source(t, ex, 2 * ep), source(t, ex, 2 * ep + 1))
                            for ex in range(3)
                        ],
                        axis=0,
                    ).astype(BF16)
                )
        product = dot(x_table[...], jnp.concatenate(pieces, axis=1))
        for n in range(TERMS):
            quad, term = n // 4, n % 4
            tile = jnp.concatenate(
                [product[n * 8 : n * 8 + 8, :640], product[n * 8 : n * 8 + 8, 640:]], axis=0
            )
            row = term * PLANE + pair * 16
            mixed[quad, row : row + 16, :] = tile.astype(BF16)
    result = None
    for quad in range(QUADS):
        part = dot(mixed[quad], w_ref[quad])
        result = part if result is None else result + part
    direct[...] = diagonal_sum(result, PLANE).reshape(8, 8, PLANE)


def last_kernel(
    child, parent, refined, mid_at, coarse_at, parents,
    planes, mid_tiles, direct, factors, weighted, x_tables, select, rows_p, prol, single, mids,
    fine_out, mid_out, coarse, back, w_mid, w_coarse, ab_ref,
):
    build_tables(factors[0], weighted[0], select[...], ab_ref, w_mid)
    build_tables(factors[1], weighted[1], select[...], ab_ref, w_coarse)
    low8 = low_lanes((8, 128))
    total = None
    for plane in range(8):
        term = planes[plane].astype(F32)
        total = term if total is None else total + term
    for c2 in range(32):
        tile = total[c2 * 8 : c2 * 8 + 8, :]
        other = turned(tile)
        coarse[2 * c2] = jnp.where(low8, tile, other)
        coarse[2 * c2 + 1] = jnp.where(low8, other, tile)
    coarse[64] = jnp.zeros((8, 128), F32)
    octant = parent[0] & 7

    def coarse_source(ex, e):
        return coarse[coarse_at[0, ex * 9 + e if e < 9 else 27]]

    sources = jnp.concatenate(
        [
            jnp.concatenate(
                [
                    jnp.where(low8, coarse_source(ex, 2 * ep), coarse_source(ex, 2 * ep + 1))
                    for ex in range(3)
                ],
                axis=0,
            ).astype(BF16)
            for ep in range(5)
        ],
        axis=1,
    )
    coarse_result = apply_one(sources, x_tables[1], w_coarse)

    uppers, octants, owns = [], [], []
    for ep in range(5):
        for ex in range(3):
            first = mid_at[0, ex * 9 + 2 * ep]
            second = mid_at[0, ex * 9 + 2 * ep + 1 if ep < 4 else 27]
            name_1, name_2 = parents[0, first], parents[0, second]
            owns.append(jnp.where(low8, mid_tiles[first], mid_tiles[second]))
            both = jnp.where(low8, coarse[name_1 >> 3], coarse[name_2 >> 3])
            named = jnp.where(low8, name_1 & 7, name_2 & 7)
            octants.append(named)
            mix_0, mix_1 = two_row_mixes(rows_p, both, 128)
            uppers.append(jnp.where(named >= 4, mix_1, mix_0))
    stacked = jnp.concatenate(uppers, axis=0)
    high = stacked.astype(BF16).astype(F32)
    spread = dot(jnp.concatenate([high, stacked - high], axis=0).astype(BF16), mids[...])
    spread = spread[:120, :512] + spread[120:, :512] + spread[:120, 512:]
    pieces = []
    for ep in range(5):
        tiles = []
        for ex in range(3):
            at = ep * 3 + ex
            which = octants[at] & 3
            chosen = spread[at * 8 : at * 8 + 8, 0:128]
            for jl in range(1, 4):
                chosen = jnp.where(
                    which == jl, spread[at * 8 : at * 8 + 8, jl * 128 : jl * 128 + 128], chosen
                )
            tiles.append(owns[at] - chosen)
        pieces.append(jnp.concatenate(tiles, axis=0).astype(BF16))
    mid_result = apply_one(jnp.concatenate(pieces, axis=1), x_tables[0], w_mid)

    row_at = (octant >> 2) * 8
    upper = row_mix([rows_p[row_at + p, :, :PLANE] for p in range(8)], coarse_result)
    middle = mid_result + fine_dot(upper, single[octant & 3])
    for a in range(8):
        mid_out[:, a * PLANE : (a + 1) * PLANE] = middle[a : a + 1, :]
    live = jnp.full((8, PLANE), refined[0], jnp.int32).astype(F32)
    upper = jnp.concatenate(two_row_mixes(rows_p, middle, PLANE), axis=0)
    spread = fine_dot(upper, prol[...])
    for o in range(8):
        i, jl = o // 4, o % 4
        slot = child[0, o]
        part = spread[i * 8 : i * 8 + 8, jl * PLANE : (jl + 1) * PLANE]
        back[slot] = live * (direct[slot] + part)
    for a in range(8):
        fine_out[:, a * PLANE : (a + 1) * PLANE] = back[:, a, :]


def call(kernel, kinds, outs, scratch, flops, *args):
    vmem = pl.BlockSpec(memory_space=pltpu.VMEM)
    smem = pl.BlockSpec(memory_space=pltpu.SMEM)
    moved = sum(math.prod(x.shape) * x.dtype.itemsize for x in (*args, *outs))
    return pl.pallas_call(
        kernel,
        out_shape=outs,
        in_specs=[smem if kind == "s" else vmem for kind in kinds],
        out_specs=[vmem] * len(outs),
        scratch_shapes=scratch,
        compiler_params=pltpu.CompilerParams(vmem_limit_bytes=VMEM_LIMIT),
        cost_estimate=pl.CostEstimate(flops=flops, bytes_accessed=moved, transcendentals=0),
        name=kernel.__name__,
    )(*args)


def both_ways(x, axis):
    count = lax.axis_size(axis)
    ends = count - 1
    before = lax.ppermute(x, axis, [(i, i + 1) for i in range(ends)])
    after = lax.ppermute(x, axis, [(i + 1, i) for i in range(ends)])
    return before, after


def shards(
    fine_coef, mid_leaf, mid_child, mid_parent, mid_refined,
    fine_nbr, mid_nbr, coarse_nbr, op_factor, term_weight,
):
    tables = filter_tables()
    select = jnp.asarray(select_tables())
    comp, prol, contrib, single, mids, rows_c, rows_p = (
        jnp.asarray(tables[name])
        for name in ("comp", "prol", "contrib", "single", "mids", "rows_c", "rows_p")
    )
    six = op_factor.reshape(3, QUADS, 4, 3, 8, 8)
    factors = six.transpose(0, 1, 3, 5, 2, 4).reshape(3, QUADS * 24, 32)
    weights = jnp.broadcast_to(
        jnp.repeat(term_weight.reshape(QUADS, 1, 4), 8, axis=2), (QUADS, 24, 32)
    ).reshape(QUADS * 24, 32)
    weighted = factors * weights[None]
    x_tables = op_factor.transpose(0, 1, 3, 2, 4).reshape(3, TERMS * 8, 24).astype(BF16)

    sds = jax.ShapeDtypeStruct
    halo, payload, fine_at, mid_at, coarse_at = call(
        first_kernel,
        "sssvvvvvvvvvv",
        [
            sds((48, 128), BF16),
            sds((64, 8, 128), BF16),
            sds((8, 27), jnp.int32),
            sds((1, 32), jnp.int32),
            sds((1, 32), jnp.int32),
        ],
        [pltpu.VMEM((8, 8, PLANE), F32), pltpu.VMEM((8, 8, PLANE), F32)],
        2_000_000,
        mid_child, mid_parent, mid_refined, fine_nbr, mid_nbr, coarse_nbr, fine_coef, mid_leaf,
        comp, prol, contrib, rows_c, rows_p,
    )
    arrived = lax.all_to_all(payload, ("gy", "gz"), 0, 0, tiled=True)
    before, after = both_ways(halo, "gz")
    line = jnp.concatenate([before, halo, after], axis=0)
    before, after = both_ways(line, "gy")
    sheet = jnp.concatenate([before, line, after], axis=0)
    before, after = both_ways(sheet, "gx")

    (copies,) = call(
        plane_kernel, "v", [sds((8, 256, 128), BF16)], [], 33_000_000, arrived
    )
    planes = lax.all_to_all(copies, "gx", 0, 0, tiled=True)

    direct, mid_tiles, parents = call(
        fine_kernel,
        "svvvvvvv",
        [
            sds((8, 8, PLANE), F32),
            sds((28, 8, 128), F32),
            sds((1, 128), jnp.int32),
        ],
        [
            pltpu.VMEM((GONE + 1, 8, 128), F32),
            pltpu.VMEM((QUADS, 256, ROWS_W), BF16),
            pltpu.VMEM((QUADS, ROWS_W, 256), BF16),
            pltpu.VMEM((QUADS, 24, 512), F32),
        ],
        700_000_000,
        fine_at, before, sheet, after, factors[0], weighted[0], x_tables[0], select,
    )
    fine_out, mid_out = call(
        last_kernel,
        "ssssssvvvvvvvvvvv",
        [sds((8, 512), F32), sds((1, 512), F32)],
        [
            pltpu.VMEM((65, 8, 128), F32),
            pltpu.VMEM((8, 8, PLANE), F32),
            pltpu.VMEM((QUADS, ROWS_W, 256), BF16),
            pltpu.VMEM((QUADS, ROWS_W, 256), BF16),
            pltpu.VMEM((QUADS, 24, 512), F32),
        ],
        200_000_000,
        mid_child, mid_parent, mid_refined, mid_at, coarse_at, parents,
        planes, mid_tiles, direct, factors[1:], weighted[1:], x_tables[1:], select,
        rows_p, prol, single, mids,
    )
    return fine_out, mid_out


def solution(mesh):
    cells = ("gx", "gy", "gz")
    rows = P(cells, None)
    return jax.shard_map(
        shards,
        mesh=mesh,
        in_specs=(rows, rows, rows, P(cells), P(cells), rows, rows, P(), P(), P()),
        out_specs=(rows, rows),
        check_vma=False,
    )
```

time: 214 us -> 75.6 us (0.35); the launches traced: 210 us -> 74.7 us
  matrix products: 70.3 us -> 0 us
  starting transfers between devices: 70.5 us -> 40.4 us
  waiting for transfers between devices: 22 us -> 3.56 us
  local copies, waits for them, and re-layouts: 32.8 us -> 15.9 us
  Pallas kernels: 0 us -> 11.8 us
  other arithmetic: 10.9 us -> 0.7 us
    dot_general x84 -> x0, matrix products: 62.7 us -> none  [the longest x27 22.8 us: apply_boxes(): jnp.dot(flat_terms, blocks[along_y, along_z], preferred_element_type=jnp....]
    reshape x35 -> x2, local copies, waits for them, and re-layouts: 21.8 us -> 0.59 us  [the longest x1 0.52 us: shards(): factors = six.transpose(0, 1, 3, 5, 2, 4).reshape(3, QUADS * 24, 32)]
    ppermute x12 -> x6, starting transfers between devices: 32 us -> 15 us  [the longest x3 10.5 us: both_ways(): before = lax.ppermute(x, axis, [(i, i + 1) for i in range(ends)])]
    all_to_all x4 -> x2, starting transfers between devices: 38.5 us -> 25.4 us  [the longest x1 18.3 us: shards(): arrived = lax.all_to_all(payload, ('gy', 'gz'), 0, 0, tiled=True)]
    pallas_call x0 -> x4, Pallas kernels: none -> 11.8 us  [call(): pl.pallas_call(kernel, out_shape=outs, in_specs=[smem if kind == 's' else...]
    ppermute x12 -> x6, waiting for transfers between devices: 10 us -> 0.02 us  [the longest x3 0.01 us: both_ways(): before = lax.ppermute(x, axis, [(i, i + 1) for i in range(ends)])]
    all_to_all x4 -> x2, waiting for transfers between devices: 12 us -> 3.55 us  [the longest x1 3.54 us: shards(): arrived = lax.all_to_all(payload, ('gy', 'gz'), 0, 0, tiled=True)]
    unnamed x29 -> x44, local copies, waits for them, and re-layouts: 2.03 us -> 9.97 us
  transfers between devices with their start and end apart: 16 -> 8, of which waited for: 8 -> 1; matrix products, arithmetic and copies ran while one was open for 37% -> 11% of each run, Pallas kernels for 0% -> 7%
where the time goes in v1:
time: 75.6 us; the launch traced here: 74.7 us
  starting transfers between devices  40.4 us (53%)
  local copies, waits for them, and re-layouts  15.9 us (21%)
  Pallas kernels  11.8 us (16%)
  waiting for transfers between devices  3.56 us (5%)
  between operations  2.32 us (3%)
    all_to_all x1, starting transfers between devices, shards(): arrived = lax.all_to_all(payload, ('gy', 'gz'), 0, 0, tiled=True)  18.3 us
    pallas_call x4, Pallas kernels, call(): pl.pallas_call(kernel, out_shape=outs, in_specs=[smem if kind == 's' else...  11.8 us
    ppermute x3, starting transfers between devices, both_ways(): before = lax.ppermute(x, axis, [(i, i + 1) for i in range(ends)])  10.5 us
    unnamed x44, local copies, waits for them, and re-layouts  9.97 us
    all_to_all x1, starting transfers between devices, shards(): planes = lax.all_to_all(copies, 'gx', 0, 0, tiled=True)  7.12 us
    ppermute x3, starting transfers between devices, both_ways(): after = lax.ppermute(x, axis, [(i + 1, i) for i in range(ends)])  4.49 us
    all_to_all x1, waiting for transfers between devices, shards(): arrived = lax.all_to_all(payload, ('gy', 'gz'), 0, 0, tiled=True)  3.54 us
    slice x2, local copies, waits for them, and re-layouts, shards(): factors[0]  1.98 us
  transfers between devices with their start and end apart: 8, of which 1 were waited for; matrix products, arithmetic and copies ran while one was open for 11% of the time, Pallas kernels for 7%

profile of v1, /device:TPU:1, one launch (start us, length us, event | category | flops | bytes accessed | tf_op | source)
XLA Modules:
  0.0 74.7 jit_solution(18060148266291346245)
XLA Ops:
  1.9 0.8 %copy.24.coarse_nbr = s32[64,27]{1,0:T(8,128)S(1)} copy(s32[64,27]{0,1:T(8,128)} %param.25) | data formatting | bytes 13824 | tf_op args[7]
  2.7 0.8 %copy-done = bf16[64,512]{1,0:T(8,128)(2,1)S(1)} copy-done((bf16[64,512]{1,0:T(8,128)(2,1)S(1)}, bf16[64,512]{1,0:T(8,128)(2,1)}, u32[]{:S(2)}) %copy-start) | copy-done | bytes 65560
  3.6 0.8 %copy-done.2 = f32[16,8,128]{2,1,0:T(8,128)S(1)} copy-done((f32[16,8,128]{2,1,0:T(8,128)S(1)}, f32[16,8,128]{2,1,0:T(8,128)}, u32[]{:S(2)}) %copy-start.2) | copy-done | bytes 65560
  4.4 0.8 %copy-done.6 = bf16[256,128]{1,0:T(8,128)(2,1)S(1)} copy-done((bf16[256,128]{1,0:T(8,128)(2,1)S(1)}, bf16[256,128]{1,0:T(8,128)(2,1)}, u32[]{:S(2)}) %copy-start.6) | copy-done | bytes 65560
  5.2 0.8 %copy-done.7 = bf16[4,64,128]{2,1,0:T(8,128)(2,1)S(1)} copy-done((bf16[4,64,128]{2,1,0:T(8,128)(2,1)S(1)}, bf16[4,64,128]{2,1,0:T(8,128)(2,1)}, u32[]{:S(2)}) %copy-start.7) | copy-done | bytes 65560
  6.1 0.8 %copy-done.8 = f32[16,8,128]{2,1,0:T(8,128)S(1)} copy-done((f32[16,8,128]{2,1,0:T(8,128)S(1)}, f32[16,8,128]{2,1,0:T(8,128)}, u32[]{:S(2)}) %copy-start.8) | copy-done | bytes 65560
  6.9 0.7 copy-done.10
  7.6 0.7 copy-done.11
  8.3 0.7 copy-done.12
  9.0 0.7 copy-done.13
  9.6 0.7 copy-done.15
  10.3 1.9 %first_kernel.1 = (bf16[48,128]{1,0:T(8,128)(2,1)S(1)}, bf16[64,8,128]{2,1,0:T(8,128)(2,1)}, s32[8,27]{1,0:T(8,128)S(1)}, s32[1,32]{1,0:T(1,128)S(1)}, s32[1,32]{1,0:T(1,128)S(1)}) custom-call(s32[1,8]{1,0:T(1,128)S(1)} %copy-done.13, s32[1]{0:T(128)S(6)} %copy.39.parent, s32[1]{0:T(128)S(6)} %copy.40.refined, s32[8,27]{1,0:T(8,128)S(1)} %copy-done.11, ...), custom_call_target="tpu_custom_call" | custom-call | flops 2000000 | bytes 489300 | tf_op jit(solution)/shard_map/first_kernel/pallas_call | solution.py:447
  12.2 4.0 %collective-permute-start = (bf16[48,128]{1,0:T(8,128)(2,1)S(1)}, bf16[48,128]{1,0:T(8,128)(2,1)S(1)}, u32[]{:S(2)}, u32[]{:S(2)}) collective-permute-start(bf16[48,128]{1,0:T(8,128)(2,1)S(1)} %get-tuple-element.13), channel_id=1, source_target_pairs={{0,1},{1,2},{2,3},{3,4},{4,5},{5,6},{6,7},{8,9},{9,10},{10,11},{11... | collective-permute-start | bytes 36872 | tf_op jit(solution)/shard_map/ppermute | solution.py:462
  16.2 1.3 %collective-permute-start.1 = (bf16[48,128]{1,0:T(8,128)(2,1)S(1)}, bf16[48,128]{1,0:T(8,128)(2,1)S(1)}, u32[]{:S(2)}, u32[]{:S(2)}) collective-permute-start(bf16[48,128]{1,0:T(8,128)(2,1)S(1)} %get-tuple-element.13), channel_id=1, source_target_pairs={{1,0},{2,1},{3,2},{4,3},{5,4},{6,5},{7,6},{9,8},{10,9},{11,10},{12... | collective-permute-start | bytes 36872 | tf_op jit(solution)/shard_map/ppermute | solution.py:463
  17.5 18.3 %all-to-all-start = ((bf16[64,8,128]{2,1,0:T(8,128)(2,1)}), bf16[64,8,128]{2,1,0:T(8,128)(2,1)S(1)}, u32[]{:S(2)}, u32[]{:S(2)}) async-start(bf16[64,8,128]{2,1,0:T(8,128)(2,1)} %get-tuple-element.15), calls=%async_computation | async-start | bytes 262144 | tf_op jit(solution)/shard_map/all_to_all | solution.py:501
  35.8 1.4 %copy.25 = f32[3,32,3,8,8]{4,3,2,1,0:T(8,128)S(1)} copy(f32[3,32,3,8,8]{1,4,3,2,0:T(8,128)} %param.26) | data formatting | bytes 147456 | tf_op args[8]
  37.2 0.6 copy.27
  37.9 0.5 reshape.29
  38.9 2.9 %collective-permute-start.2 = (bf16[144,128]{1,0:T(8,128)(2,1)S(1)}, bf16[144,128]{1,0:T(8,128)(2,1)S(1)}, u32[]{:S(2)}, u32[]{:S(2)}) collective-permute-start(bf16[144,128]{1,0:T(8,128)(2,1)S(1)} %constant_dynamic-update-slice_fusion), channel_id=1, source_target_pairs={{0,8},{8,16},{16,24},{24,32},{32,40},{40,48},{48,56},{1,9},{9,17},... | collective-permute-start | bytes 110600 | tf_op jit(solution)/shard_map/ppermute | solution.py:462
  41.8 0.7 convert_bitcast_fusion
  42.5 1.3 %collective-permute-start.3 = (bf16[144,128]{1,0:T(8,128)(2,1)S(1)}, bf16[144,128]{1,0:T(8,128)(2,1)S(1)}, u32[]{:S(2)}, u32[]{:S(2)}) collective-permute-start(bf16[144,128]{1,0:T(8,128)(2,1)S(1)} %constant_dynamic-update-slice_fusion), channel_id=1, source_target_pairs={{8,0},{16,8},{24,16},{32,24},{40,32},{48,40},{56,48},{9,1},{17,9},... | collective-permute-start | bytes 110600 | tf_op jit(solution)/shard_map/ppermute | solution.py:463
  43.8 3.5 %all-to-all-done.arrived = bf16[64,8,128]{2,1,0:T(8,128)(2,1)S(1)} async-done(((bf16[64,8,128]{2,1,0:T(8,128)(2,1)}), bf16[64,8,128]{2,1,0:T(8,128)(2,1)S(1)}, u32[]{:S(2)}, u32[]{:S(2)}) %all-to-all-start) | async-done | bytes 131104 | tf_op jit(solution)/shard_map/all_to_all | solution.py:501
  47.4 1.2 %plane_kernel.1 = bf16[8,256,128]{2,1,0:T(8,128)(2,1)} custom-call(bf16[64,8,128]{2,1,0:T(8,128)(2,1)S(1)} %all-to-all-done.arrived), custom_call_target="tpu_custom_call" | custom-call | flops 33000000 | bytes 655360 | tf_op jit(solution)/shard_map/plane_kernel/pallas_call | solution.py:447
  48.6 7.1 %all-to-all-start.1 = ((bf16[8,256,128]{2,1,0:T(8,128)(2,1)}), bf16[8,256,128]{2,1,0:T(8,128)(2,1)S(1)}, u32[]{:S(2)}, u32[]{:S(2)}) async-start(bf16[8,256,128]{2,1,0:T(8,128)(2,1)} %plane_kernel.1), calls=%async_computation.1 | async-start | bytes 1048576 | tf_op jit(solution)/shard_map/all_to_all | solution.py:511
  55.8 3.5 %collective-permute-start.4 = (bf16[432,128]{1,0:T(8,128)(2,1)S(1)}, bf16[432,128]{1,0:T(8,128)(2,1)S(1)}, u32[]{:S(2)}, u32[]{:S(2)}) collective-permute-start(bf16[432,128]{1,0:T(8,128)(2,1)S(1)} %constant_dynamic-update-slice_fusion.3.centre), channel_id=1, source_target_pairs={{0,64},{64,128},{128,192},{192,256},{256,320},{320,384},{384,448},... | collective-permute-start | bytes 331784 | tf_op jit(solution)/shard_map/ppermute | solution.py:462
  59.3 1.9 %collective-permute-start.5 = (bf16[432,128]{1,0:T(8,128)(2,1)S(1)}, bf16[432,128]{1,0:T(8,128)(2,1)S(1)}, u32[]{:S(2)}, u32[]{:S(2)}) collective-permute-start(bf16[432,128]{1,0:T(8,128)(2,1)S(1)} %constant_dynamic-update-slice_fusion.3.centre), channel_id=1, source_target_pairs={{64,0},{128,64},{192,128},{256,192},{320,256},{384,320},{448,384},... | collective-permute-start | bytes 331784 | tf_op jit(solution)/shard_map/ppermute | solution.py:463
  61.2 0.8 %slice.34 = f32[1,8,3,8,4,8]{3,5,2,4,1,0:T(8,128)} slice(f32[3,8,3,8,4,8]{3,5,2,4,1,0:T(8,128)S(1)} %bitcast.17), slice={[0:1], [0:8], [0:3], [0:8], [0:4], [0:8]} | slice | bytes 49152 | tf_op jit(solution)/shard_map/slice | solution.py:528
  62.1 1.2 %copy.26 = f32[1,8,3,8,4,8]{5,4,3,2,1,0:T(4,128)S(1)} copy(f32[1,8,3,8,4,8]{3,5,2,4,1,0:T(8,128)} %slice.34) | data formatting | bytes 49152 | tf_op jit(solution)/shard_map/slice | solution.py:528
  64.4 0.4 slice.30.factors
  65.2 0.5 slice.33
  66.0 4.3 %fine_kernel.1 = (f32[8,8,64]{2,1,0:T(8,128)S(1)}, f32[28,8,128]{2,1,0:T(8,128)S(1)}, s32[1,128]{1,0:T(1,128)S(1)}) custom-call(s32[8,27]{1,0:T(8,128)S(1)} %get-tuple-element.12.fine_at, bf16[432,128]{1,0:T(8,128)(2,1)S(1)} %collective-permute-done.4.left, bf16[432,128]{1,0:T(8,128)(2,1)S(1)} %constant_dynamic-update-slice_fusion.3.centre, ...), custom_call_target="tpu_custom_call" | custom-call | flops 700000000 | bytes 558432 | tf_op jit(solution)/shard_map/fine_kernel/pallas_call | solution.py:447
  70.4 4.3 %last_kernel.1 = (f32[8,512]{1,0:T(8,128)}, f32[1,512]{1,0:T(1,128)}) custom-call(s32[1,8]{1,0:T(1,128)S(1)} %copy-done.14, s32[1]{0:T(128)S(6)} %copy.39.parent, s32[1]{0:T(128)S(6)} %copy.40.refined, s32[1,32]{1,0:T(1,128)S(1)} %get-tuple-element.10.mid_at, s32[1,32]{1,0:T(1,128)S(1)} %get-tuple-element.11.coarse_at, ...), custom_call_target="tpu_custom_call" | custom-call | flops 200000000 | bytes 1289000 | tf_op jit(solution)/shard_map/last_kernel/pallas_call | solution.py:447
  (60 shorter events, 2.2 us)
Async XLA Ops:
  2.7 0.8 %copy-start = (bf16[64,512]{1,0:T(8,128)(2,1)S(1)}, bf16[64,512]{1,0:T(8,128)(2,1)}, u32[]{:S(2)}) copy-start(bf16[64,512]{1,0:T(8,128)(2,1)} %constant.18.clone.prol) | copy-start | bytes 196612
  3.6 0.8 %copy-start.2 = (f32[16,8,128]{2,1,0:T(8,128)S(1)}, f32[16,8,128]{2,1,0:T(8,128)}, u32[]{:S(2)}) copy-start(f32[16,8,128]{2,1,0:T(8,128)} %constant.23.clone.rows_p) | copy-start | bytes 196612
  4.4 0.8 %copy-start.6 = (bf16[256,128]{1,0:T(8,128)(2,1)S(1)}, bf16[256,128]{1,0:T(8,128)(2,1)}, u32[]{:S(2)}) copy-start(bf16[256,128]{1,0:T(8,128)(2,1)} %constant.17.clone.comp) | copy-start | bytes 196612
  5.2 0.8 %copy-start.7 = (bf16[4,64,128]{2,1,0:T(8,128)(2,1)S(1)}, bf16[4,64,128]{2,1,0:T(8,128)(2,1)}, u32[]{:S(2)}) copy-start(bf16[4,64,128]{2,1,0:T(8,128)(2,1)} %constant.19.clone.contrib) | copy-start | bytes 196612
  6.1 0.8 %copy-start.8 = (f32[16,8,128]{2,1,0:T(8,128)S(1)}, f32[16,8,128]{2,1,0:T(8,128)}, u32[]{:S(2)}) copy-start(f32[16,8,128]{2,1,0:T(8,128)} %constant.22.clone.rows_c) | copy-start | bytes 196612
  6.9 0.7 copy-start.10
  7.6 0.7 copy-start.11
  8.3 0.7 copy-start.12
  9.0 0.7 copy-start.13
  9.6 0.7 copy-start.15
  12.2 26.6 %collective-permute-start = (bf16[48,128]{1,0:T(8,128)(2,1)S(1)}, bf16[48,128]{1,0:T(8,128)(2,1)S(1)}, u32[]{:S(2)}, u32[]{:S(2)}) collective-permute-start(bf16[48,128]{1,0:T(8,128)(2,1)S(1)} %get-tuple-element.13), channel_id=1, source_target_pairs={{0,1},{1,2},{2,3},{3,4},{4,5},{5,6},{6,7},{8,9},{9,10},{10,11},{11... | collective-permute-start | bytes 36872 | tf_op jit(solution)/shard_map/ppermute | solution.py:462
  16.2 22.7 %collective-permute-start.1 = (bf16[48,128]{1,0:T(8,128)(2,1)S(1)}, bf16[48,128]{1,0:T(8,128)(2,1)S(1)}, u32[]{:S(2)}, u32[]{:S(2)}) collective-permute-start(bf16[48,128]{1,0:T(8,128)(2,1)S(1)} %get-tuple-element.13), channel_id=1, source_target_pairs={{1,0},{2,1},{3,2},{4,3},{5,4},{6,5},{7,6},{9,8},{10,9},{11,10},{12... | collective-permute-start | bytes 36872 | tf_op jit(solution)/shard_map/ppermute | solution.py:463
  17.5 29.9 %all-to-all-start = ((bf16[64,8,128]{2,1,0:T(8,128)(2,1)}), bf16[64,8,128]{2,1,0:T(8,128)(2,1)S(1)}, u32[]{:S(2)}, u32[]{:S(2)}) async-start(bf16[64,8,128]{2,1,0:T(8,128)(2,1)} %get-tuple-element.15), calls=%async_computation | async-start | bytes 262144 | tf_op jit(solution)/shard_map/all_to_all | solution.py:501
  37.9 0.7 copy-start.17
  37.9 3.9 %copy-start.16 = (f32[3,32,3,8,8]{1,4,3,2,0:T(8,128)S(1)}, f32[3,32,3,8,8]{1,4,3,2,0:T(8,128)}, u32[]{:S(2)}) copy-start(f32[3,32,3,8,8]{1,4,3,2,0:T(8,128)} %param.26) | copy-start | bytes 221188
  38.9 4.9 %collective-permute-start.2 = (bf16[144,128]{1,0:T(8,128)(2,1)S(1)}, bf16[144,128]{1,0:T(8,128)(2,1)S(1)}, u32[]{:S(2)}, u32[]{:S(2)}) collective-permute-start(bf16[144,128]{1,0:T(8,128)(2,1)S(1)} %constant_dynamic-update-slice_fusion), channel_id=1, source_target_pairs={{0,8},{8,16},{16,24},{24,32},{32,40},{40,48},{48,56},{1,9},{9,17},... | collective-permute-start | bytes 110600 | tf_op jit(solution)/shard_map/ppermute | solution.py:462
  42.5 13.2 %collective-permute-start.3 = (bf16[144,128]{1,0:T(8,128)(2,1)S(1)}, bf16[144,128]{1,0:T(8,128)(2,1)S(1)}, u32[]{:S(2)}, u32[]{:S(2)}) collective-permute-start(bf16[144,128]{1,0:T(8,128)(2,1)S(1)} %constant_dynamic-update-slice_fusion), channel_id=1, source_target_pairs={{8,0},{16,8},{24,16},{32,24},{40,32},{48,40},{56,48},{9,1},{17,9},... | collective-permute-start | bytes 110600 | tf_op jit(solution)/shard_map/ppermute | solution.py:463
  48.6 21.7 %all-to-all-start.1 = ((bf16[8,256,128]{2,1,0:T(8,128)(2,1)}), bf16[8,256,128]{2,1,0:T(8,128)(2,1)S(1)}, u32[]{:S(2)}, u32[]{:S(2)}) async-start(bf16[8,256,128]{2,1,0:T(8,128)(2,1)} %plane_kernel.1), calls=%async_computation.1 | async-start | bytes 1048576 | tf_op jit(solution)/shard_map/all_to_all | solution.py:511
  55.8 10.1 %collective-permute-start.4 = (bf16[432,128]{1,0:T(8,128)(2,1)S(1)}, bf16[432,128]{1,0:T(8,128)(2,1)S(1)}, u32[]{:S(2)}, u32[]{:S(2)}) collective-permute-start(bf16[432,128]{1,0:T(8,128)(2,1)S(1)} %constant_dynamic-update-slice_fusion.3.centre), channel_id=1, source_target_pairs={{0,64},{64,128},{128,192},{192,256},{256,320},{320,384},{384,448},... | collective-permute-start | bytes 331784 | tf_op jit(solution)/shard_map/ppermute | solution.py:462
  59.3 6.6 %collective-permute-start.5 = (bf16[432,128]{1,0:T(8,128)(2,1)S(1)}, bf16[432,128]{1,0:T(8,128)(2,1)S(1)}, u32[]{:S(2)}, u32[]{:S(2)}) collective-permute-start(bf16[432,128]{1,0:T(8,128)(2,1)S(1)} %constant_dynamic-update-slice_fusion.3.centre), channel_id=1, source_target_pairs={{64,0},{128,64},{192,128},{256,192},{320,256},{384,320},{448,384},... | collective-permute-start | bytes 331784 | tf_op jit(solution)/shard_map/ppermute | solution.py:463
  62.1 1.4 %slice-start = ((bf16[3,32,8,3,8]{1,4,2,3,0:T(8,128)(2,1)}), bf16[1,32,8,3,8]{1,4,2,3,0:T(8,128)(2,1)S(1)}, s32[]{:S(2)}) async-start(bf16[3,32,8,3,8]{1,4,2,3,0:T(8,128)(2,1)} %convert_bitcast_fusion), calls=%async_computation.2 | async-start | bytes 98304 | tf_op jit(solution)/shard_map/slice | solution.py:528
  64.1 0.9 %slice-start.1 = ((bf16[3,32,8,3,8]{1,4,2,3,0:T(8,128)(2,1)}), bf16[2,32,8,3,8]{1,4,2,3,0:T(8,128)(2,1)S(1)}, s32[]{:S(2)}) async-start(bf16[3,32,8,3,8]{1,4,2,3,0:T(8,128)(2,1)} %convert_bitcast_fusion), calls=%async_computation.3 | async-start | bytes 196608 | tf_op jit(solution)/shard_map/slice | solution.py:543
  64.4 1.5 %copy-start.9 = (bf16[32,512]{1,0:T(8,128)(2,1)S(1)}, bf16[32,512]{1,0:T(8,128)(2,1)}, u32[]{:S(2)}) copy-start(bf16[32,512]{1,0:T(8,128)(2,1)} %constant.16.clone.select) | copy-start | bytes 98308
  65.9 4.4 %copy-start.1 = (bf16[64,512]{1,0:T(8,128)(2,1)S(1)}, bf16[64,512]{1,0:T(8,128)(2,1)}, u32[]{:S(2)}) copy-start(bf16[64,512]{1,0:T(8,128)(2,1)} %constant.18.clone.prol) | copy-start | bytes 196612
  65.9 4.4 %copy-start.3 = (f32[16,8,128]{2,1,0:T(8,128)S(1)}, f32[16,8,128]{2,1,0:T(8,128)}, u32[]{:S(2)}) copy-start(f32[16,8,128]{2,1,0:T(8,128)} %constant.23.clone.rows_p) | copy-start | bytes 196612
  65.9 4.4 %copy-start.4 = (bf16[128,1024]{1,0:T(8,128)(2,1)S(1)}, bf16[128,1024]{1,0:T(8,128)(2,1)}, u32[]{:S(2)}) copy-start(bf16[128,1024]{1,0:T(8,128)(2,1)} %constant.21.clone.mids) | copy-start | bytes 786436
  65.9 4.4 %copy-start.5 = (bf16[4,64,128]{2,1,0:T(8,128)(2,1)S(1)}, bf16[4,64,128]{2,1,0:T(8,128)(2,1)}, u32[]{:S(2)}) copy-start(bf16[4,64,128]{2,1,0:T(8,128)(2,1)} %constant.20.clone.single) | copy-start | bytes 196612
  66.0 4.4 %copy-start.14 = (s32[1,8]{1,0:T(1,128)S(1)}, s32[1,8]{1,0:T(1,128)}, u32[]{:S(2)}) copy-start(s32[1,8]{1,0:T(1,128)} %child.3) | copy-start | bytes 100

commit v2 on v1

--- a/solution.py
+++ b/solution.py
@@ -15,7 +15,7 @@
 TERMS = 32
 QUADS = 8
 ROWS_W = 640
-GONE = 27 * 8
+GONE = 27 * 10
 BF16 = jnp.bfloat16
 F32 = jnp.float32
 VMEM_LIMIT = 40 * 1024 * 1024
@@ -102,14 +102,14 @@
 
 @functools.cache
 def select_tables():
-    n4 = np.arange(4)
-    a = np.arange(8)
-    eye4 = (n4[:, None] == n4[None, :]).astype(np.float64)
-    eye8 = (a[:, None] == a[None, :]).astype(np.float64)
-    one = np.ones(8)
-    left = np.einsum("nm,ab,c->nambc", eye4, eye8, one).reshape(32, 256)
-    right = np.einsum("nm,ac,b->nambc", eye4, eye8, one).reshape(32, 256)
-    return np.concatenate([left, right], axis=1).astype(ml_dtypes.bfloat16)
+    out = np.arange(256) // TERMS
+    term = np.arange(256) % TERMS
+    col = np.arange(256)
+    group = term[:, None] % 4 == (col // PLANE)[None, :]
+    left = group & (out[:, None] == (col // 8 % 8)[None, :])
+    right = group & (out[:, None] == (col % 8)[None, :])
+    turn = (term[None, :] == (col // 8)[:, None]) & (out[None, :] == (col % 8)[:, None])
+    return np.concatenate([left, right, turn], axis=1).astype(ml_dtypes.bfloat16)
 
 
 def split(value):
@@ -154,35 +154,77 @@
     ]
 
 
-def local_cell(near, own, per_device):
-    device = near // per_device if per_device == 1 else near >> 3
+def local_cell(device, own):
     step_x = (device >> 6) - (own >> 6) + 1
     step_y = ((device >> 3) & 7) - ((own >> 3) & 7) + 1
     step_z = (device & 7) - (own & 7) + 1
     return step_x * 9 + step_y * 3 + step_z
 
 
-def build_tables(factors, weighted, select, ab_ref, w_ref):
-    left = dot(jnp.concatenate(split(weighted), axis=0), select[:, :256])
-    right = dot(jnp.concatenate(split(factors), axis=0), select[:, 256:])
-    ab_ref[:, :, :256] = (left[:192] + left[192:]).reshape(8, 24, 256)
-    ab_ref[:, :, 256:] = (right[:192] + right[192:]).reshape(8, 24, 256)
-
-    def one_quad(quad, carry):
-        inner = [ab_ref[quad, ez * 8 : ez * 8 + 8, 256:512] for ez in range(3)]
+def tables_kernel(factors, weights, select, sheet, w_ref, x_ref, tiles, ab_ref):
+    lane = lax.broadcasted_iota(jnp.int32, (24, 256), 1)
+    quad_of = (lane & 31) >> 2
+    weight = jnp.concatenate([weights[...]] * 8, axis=1)
+    weighted, plain = [], []
+    for level in range(3):
+        rows = []
+        for e in range(3):
+            rows.append(
+                jnp.concatenate(
+                    [factors[level, e * 64 + b * 8 : e * 64 + b * 8 + 8, :] for b in range(8)],
+                    axis=1,
+                )
+            )
+        values = jnp.concatenate(rows, axis=0)
+        scaled = values * weight
+        for quad in range(QUADS):
+            weighted.append(jnp.where(quad_of == quad, scaled, 0.0))
+            plain.append(jnp.where(quad_of == quad, values, 0.0))
+        x_ref[level] = lax.dot_general(
+            select[:, 512:768],
+            values.astype(BF16),
+            (((1,), (1,)), ((), ())),
+            preferred_element_type=F32,
+        ).astype(BF16)
+    for which, parts in enumerate((weighted, plain)):
+        both = dot(
+            jnp.concatenate(split(jnp.concatenate(parts, axis=0)), axis=0),
+            select[:, which * 256 : which * 256 + 256],
+        )
+        ab_ref[which] = (both[:576] + both[576:]).reshape(24, 24, 256)
+
+    def one_quad(at, carry):
+        inner = [ab_ref[1, at, ez * 8 : ez * 8 + 8, :] for ez in range(3)]
         for ey in range(3):
             for pair in range(4):
-                at = ey * 8 + 2 * pair
-                first = ab_ref[quad, at : at + 1, 0:256]
-                second = ab_ref[quad, at + 1 : at + 2, 0:256]
+                row = ey * 8 + 2 * pair
+                first = ab_ref[0, at, row : row + 1, :]
+                second = ab_ref[0, at, row + 1 : row + 2, :]
                 for ez in range(3):
                     tile = jnp.concatenate([first * inner[ez], second * inner[ez]], axis=0)
-                    row = (ey * 3 + ez) * PLANE + pair * 16
-                    w_ref[quad, row : row + 16, :] = tile.astype(BF16)
-        w_ref[quad, 576:640, :] = jnp.zeros((64, 256), BF16)
+                    to = (ey * 3 + ez) * PLANE + pair * 16
+                    w_ref[at, to : to + 16, :] = tile.astype(BF16)
+        w_ref[at, 576:640, :] = jnp.zeros((64, 256), BF16)
         return carry
 
-    lax.fori_loop(0, QUADS, one_quad, 0)
+    lax.fori_loop(0, 3 * QUADS, one_quad, 0)
+    for cell in range(9):
+        spread_cell(sheet, cell, tiles, cell)
+
+
+def spread_cell(sheet, cell, tiles, to):
+    low = low_lanes((8, 128))
+    base = cell * 48
+    for group in range(2):
+        both = sheet[base + group * 16 : base + group * 16 + 16, :].astype(F32)
+        for sub in range(2):
+            tile = both[sub * 8 : sub * 8 + 8, :]
+            other = turned(tile)
+            tiles[to * 10 + group * 4 + sub * 2] = jnp.where(low, tile, other)
+            tiles[to * 10 + group * 4 + sub * 2 + 1] = jnp.where(low, other, tile)
+    last = sheet[base + 32 : base + 48, :].astype(F32)
+    tiles[to * 10 + 8] = last[0:8, :]
+    tiles[to * 10 + 9] = last[8:16, :]
 
 
 def diagonal_sum(result, rows):
@@ -193,33 +235,67 @@
     return total
 
 
-def apply_one(sources, x_table, w_ref):
+def apply_one(sources, x_table, w_ref, base):
     mixed = dot(x_table, sources).astype(BF16)
     result = None
     for quad in range(QUADS):
-        part = dot(mixed[quad * 32 : quad * 32 + 32, :], w_ref[quad])
+        part = dot(mixed[quad * 32 : quad * 32 + 32, :], w_ref[base + quad])
         result = part if result is None else result + part
     return diagonal_sum(result, 8)
 
 
 def first_kernel(
-    child, parent, refined, fine_nbr, mid_nbr, coarse_nbr, coef, leaf,
-    comp, prol, contrib, rows_c, rows_p,
-    halo, payload, fine_at, mid_at, coarse_at, source, detail,
+    child_h, parent_h, refined_h, fine_h, mid_h, coarse_h, coef_h, leaf_h, filters_h, rows_h,
+    halo, payload, numbers,
+    child, parent, refined, child_v, fine_nbr, mid_nbr, coarse_nbr, coef, leaf, filters, rows,
+    source, detail, sems,
 ):
+    copies = [
+        pltpu.make_async_copy(there, here, sems.at[at])
+        for at, (there, here) in enumerate(
+            (
+                (coef_h, coef),
+                (filters_h, filters),
+                (rows_h, rows),
+                (child_h, child),
+                (parent_h, parent),
+                (refined_h, refined),
+                (leaf_h, leaf),
+                (child_h, child_v),
+                (fine_h, fine_nbr),
+                (mid_h, mid_nbr),
+                (coarse_h, coarse_nbr),
+            )
+        )
+    ]
+    for copy in copies:
+        copy.start()
+    for copy in copies:
+        copy.wait()
+    comp = filters[0:256, :]
+    prol = jnp.concatenate([filters[256 + 64 * k : 320 + 64 * k, :] for k in range(4)], axis=1)
+    slot = parent[0] >> 3
+    octant = parent[0] & 7
     near = fine_nbr[...]
     own = near[:, 13:14] >> 3
-    cell = local_cell(near, own, 8) * 8 + (near & 7)
-    fine_at[:, 0:27] = jnp.where(near >= 0, cell, GONE)
+    cell = local_cell(near >> 3, own) * 10 + (near & 7)
+    numbers[0:8, 0:27] = jnp.where(near >= 0, cell, GONE)
     near_mid = mid_nbr[...]
     own_mid = near_mid[:, 13:14]
-    mid_at[:, 0:27] = jnp.where(near_mid >= 0, local_cell(near_mid, own_mid, 1), 27)
-    mid_at[:, 27:32] = jnp.full((1, 5), 27, jnp.int32)
-    slot = parent[0] >> 3
-    octant = parent[0] & 7
-    near_coarse = coarse_nbr[pl.ds(slot, 1), :]
-    coarse_at[:, 0:27] = jnp.where(near_coarse >= 0, near_coarse, 64)
-    coarse_at[:, 27:32] = jnp.full((1, 5), 64, jnp.int32)
+    numbers[8:9, 0:27] = jnp.where(near_mid >= 0, local_cell(near_mid, own_mid), 27)
+    numbers[8:9, 27:28] = jnp.full((1, 1), 27, jnp.int32)
+    hot = jnp.where(lax.broadcasted_iota(jnp.int32, (8, 64), 1) == slot, 1.0, 0.0).astype(BF16)
+    near_coarse = lax.dot_general(
+        hot,
+        coarse_nbr[...].astype(F32).astype(BF16),
+        (((1,), (1,)), ((), ())),
+        preferred_element_type=F32,
+    )[0:1].astype(jnp.int32)
+    numbers[9:10, 0:27] = jnp.where(near_coarse >= 0, near_coarse, 64)
+    numbers[9:10, 27:28] = jnp.full((1, 1), 64, jnp.int32)
+    numbers[10:11, 0:8] = child_v[...]
+    numbers[10:11, 8:9] = jnp.full((1, 1), parent[0], jnp.int32)
+    numbers[10:11, 9:10] = jnp.full((1, 1), refined[0], jnp.int32)
 
     values = coef[...].astype(F32)
     for a in range(8):
@@ -228,11 +304,11 @@
     lhs = jnp.concatenate(
         [jnp.concatenate(tiles[0:4], axis=1), jnp.concatenate(tiles[4:8], axis=1)], axis=0
     ).astype(BF16)
-    both = dot(lhs, comp[...])
+    both = dot(lhs, comp)
     partial = both[:, :PLANE] + both[:, PLANE:]
     compressed = None
     for k in range(16):
-        term = rows_c[k, :, :PLANE] * partial[k : k + 1, :]
+        term = rows[k, :, :PLANE] * partial[k : k + 1, :]
         compressed = term if compressed is None else compressed + term
     leaf_row = leaf[...].astype(F32)
     leaf_tile = jnp.concatenate(
@@ -241,16 +317,17 @@
     middle = jnp.where(refined[0] > 0, compressed, leaf_tile).astype(BF16).astype(F32)
 
     row_at = (octant >> 2) * 8
-    inner = row_mix([rows_c[row_at + x, :, :PLANE] for x in range(8)], middle)
-    added = fine_dot(inner, contrib[octant & 3])
+    inner = row_mix([rows[row_at + x, :, :PLANE] for x in range(8)], middle)
+    table = filters[pl.ds(pl.multiple_of(512 + (octant & 3) * 64, 64), 64), :]
+    added = fine_dot(inner, table)
     low8 = low_lanes((8, 128))
     tag = jnp.full((8, 128), slot, jnp.int32).astype(F32)
     tile = jnp.where(low8, jnp.concatenate([added, added], axis=1), tag).astype(BF16)
     payload[...] = jnp.broadcast_to(tile[None], payload.shape)
 
     live = jnp.full((8, PLANE), refined[0], jnp.int32).astype(F32)
-    upper = jnp.concatenate(two_row_mixes(rows_p, middle, PLANE), axis=0)
-    spread = fine_dot(upper, prol[...])
+    upper = jnp.concatenate(two_row_mixes(rows.at[16:32], middle, PLANE), axis=0)
+    spread = fine_dot(upper, prol)
     for o in range(8):
         i, jl = o // 4, o % 4
         part = spread[i * 8 : i * 8 + 8, jl * PLANE : (jl + 1) * PLANE]
@@ -291,40 +368,38 @@
     copies[...] = jnp.broadcast_to(partial[None], copies.shape)
 
 
-def fine_kernel(
-    fine_at, left, centre, right, factors, weighted, x_table, select,
-    direct, mid_tiles, parents, table, mixed, w_ref, ab_ref,
+def pair_of(first, second):
+    return jnp.where(low_lanes((8, 128)), first, second)
+
+
+def last_kernel(
+    numbers, left, centre, right, planes, w_ref, x_ref, rows_p, filters, mids,
+    fine_out, mid_out,
+    table, mixed, coarse, back, names_v, names_s, sem,
 ):
+    lanes = lax.broadcasted_iota(jnp.int32, (1, 128), 1)
     low8 = low_lanes((8, 128))
-    lanes = lax.broadcasted_iota(jnp.int32, (1, 128), 1)
     table[GONE] = jnp.zeros((8, 128), F32)
-    mid_tiles[27] = jnp.zeros((8, 128), F32)
+    table[GONE + 8] = jnp.zeros((8, 128), F32)
+    for cell in range(9):
+        spread_cell(left, cell, table, cell)
+        spread_cell(right, cell, table, 18 + cell)
+    for at in range(90):
+        table[90 + at] = centre[at]
     names = jnp.full((1, 128), 512, jnp.int32)
-    for step_x, ref in enumerate((left, centre, right)):
-        for cell in range(9):
-            at = (step_x * 9 + cell) * 8
-            base = cell * 48
-            for group in range(2):
-                both = ref[base + group * 16 : base + group * 16 + 16, :].astype(F32)
-                for sub in range(2):
-                    tile = both[sub * 8 : sub * 8 + 8, :]
-                    other = turned(tile)
-                    table[at + group * 4 + sub * 2] = jnp.where(low8, tile, other)
-                    table[at + group * 4 + sub * 2 + 1] = jnp.where(low8, other, tile)
-            last = ref[base + 32 : base + 48, :].astype(F32)
-            mid_tiles[step_x * 9 + cell] = last[0:8, :]
-            meta = last[8:9, :]
-            name = meta * 8.0 + turned(meta)
-            name = jnp.where(low8[0:1], name, turned(name)).astype(jnp.int32)
-            names = jnp.where(lanes == step_x * 9 + cell, name, names)
-    parents[...] = names
-
-    build_tables(factors[...], weighted[...], select[...], ab_ref, w_ref)
+    for cell in range(27):
+        meta = table[cell * 10 + 9, 0:1, :]
+        other = turned(meta)
+        name = jnp.where(low8[0:1], meta * 8.0 + other, other * 8.0 + meta).astype(jnp.int32)
+        names = jnp.where(lanes == cell, name, names)
+    names_v[...] = names
+    fetch = pltpu.make_async_copy(names_v, names_s, sem)
+    fetch.start()
 
     def source(t, ex, e):
         if e > 8:
             return table[GONE]
-        return table[fine_at[t, ex * 9 + e]]
+        return table[numbers[t, ex * 9 + e]]
 
     for pair in range(4):
         pieces = []
@@ -333,13 +408,13 @@
                 pieces.append(
                     jnp.concatenate(
                         [
-                            jnp.where(low8, source(t, ex, 2 * ep), source(t, ex, 2 * ep + 1))
+                            pair_of(source(t, ex, 2 * ep), source(t, ex, 2 * ep + 1))
                             for ex in range(3)
                         ],
                         axis=0,
                     ).astype(BF16)
                 )
-        product = dot(x_table[...], jnp.concatenate(pieces, axis=1))
+        product = dot(x_ref[0], jnp.concatenate(pieces, axis=1))
         for n in range(TERMS):
             quad, term = n // 4, n % 4
             tile = jnp.concatenate(
@@ -351,17 +426,8 @@
     for quad in range(QUADS):
         part = dot(mixed[quad], w_ref[quad])
         result = part if result is None else result + part
-    direct[...] = diagonal_sum(result, PLANE).reshape(8, 8, PLANE)
-
-
-def last_kernel(
-    child, parent, refined, mid_at, coarse_at, parents,
-    planes, mid_tiles, direct, factors, weighted, x_tables, select, rows_p, prol, single, mids,
-    fine_out, mid_out, coarse, back, w_mid, w_coarse, ab_ref,
-):
-    build_tables(factors[0], weighted[0], select[...], ab_ref, w_mid)
-    build_tables(factors[1], weighted[1], select[...], ab_ref, w_coarse)
-    low8 = low_lanes((8, 128))
+    direct = diagonal_sum(result, PLANE)
+
     total = None
     for plane in range(8):
         term = planes[plane].astype(F32)
@@ -372,16 +438,16 @@
         coarse[2 * c2] = jnp.where(low8, tile, other)
         coarse[2 * c2 + 1] = jnp.where(low8, other, tile)
     coarse[64] = jnp.zeros((8, 128), F32)
-    octant = parent[0] & 7
+    octant = numbers[10, 8] & 7
 
     def coarse_source(ex, e):
-        return coarse[coarse_at[0, ex * 9 + e if e < 9 else 27]]
+        return coarse[numbers[9, ex * 9 + e if e < 9 else 27]]
 
     sources = jnp.concatenate(
         [
             jnp.concatenate(
                 [
-                    jnp.where(low8, coarse_source(ex, 2 * ep), coarse_source(ex, 2 * ep + 1))
+                    pair_of(coarse_source(ex, 2 * ep), coarse_source(ex, 2 * ep + 1))
                     for ex in range(3)
                 ],
                 axis=0,
@@ -390,16 +456,17 @@
         ],
         axis=1,
     )
-    coarse_result = apply_one(sources, x_tables[1], w_coarse)
-
+    coarse_result = apply_one(sources, x_ref[2], w_ref, 16)
+
+    fetch.wait()
     uppers, octants, owns = [], [], []
     for ep in range(5):
         for ex in range(3):
-            first = mid_at[0, ex * 9 + 2 * ep]
-            second = mid_at[0, ex * 9 + 2 * ep + 1 if ep < 4 else 27]
-            name_1, name_2 = parents[0, first], parents[0, second]
-            owns.append(jnp.where(low8, mid_tiles[first], mid_tiles[second]))
-            both = jnp.where(low8, coarse[name_1 >> 3], coarse[name_2 >> 3])
+            first = numbers[8, ex * 9 + 2 * ep]
+            second = numbers[8, ex * 9 + 2 * ep + 1 if ep < 4 else 27]
+            name_1, name_2 = names_s[0, first], names_s[0, second]
+            owns.append(pair_of(table[first * 10 + 8], table[second * 10 + 8]))
+            both = pair_of(coarse[name_1 >> 3], coarse[name_2 >> 3])
             named = jnp.where(low8, name_1 & 7, name_2 & 7)
             octants.append(named)
             mix_0, mix_1 = two_row_mixes(rows_p, both, 128)
@@ -421,34 +488,41 @@
                 )
             tiles.append(owns[at] - chosen)
         pieces.append(jnp.concatenate(tiles, axis=0).astype(BF16))
-    mid_result = apply_one(jnp.concatenate(pieces, axis=1), x_tables[0], w_mid)
+    mid_result = apply_one(jnp.concatenate(pieces, axis=1), x_ref[1], w_ref, 8)
 
     row_at = (octant >> 2) * 8
     upper = row_mix([rows_p[row_at + p, :, :PLANE] for p in range(8)], coarse_result)
-    middle = mid_result + fine_dot(upper, single[octant & 3])
+    single = filters[pl.ds(pl.multiple_of(256 + (octant & 3) * 64, 64), 64), :]
+    middle = mid_result + fine_dot(upper, single)
     for a in range(8):
         mid_out[:, a * PLANE : (a + 1) * PLANE] = middle[a : a + 1, :]
-    live = jnp.full((8, PLANE), refined[0], jnp.int32).astype(F32)
+    live = jnp.full((8, PLANE), numbers[10, 9], jnp.int32).astype(F32)
     upper = jnp.concatenate(two_row_mixes(rows_p, middle, PLANE), axis=0)
-    spread = fine_dot(upper, prol[...])
+    prol = jnp.concatenate([filters[64 * k : 64 * k + 64, :] for k in range(4)], axis=1)
+    spread = fine_dot(upper, prol)
+    for t in range(8):
+        back[t] = direct[t * 8 : t * 8 + 8, :]
     for o in range(8):
         i, jl = o // 4, o % 4
-        slot = child[0, o]
+        slot = numbers[10, o]
         part = spread[i * 8 : i * 8 + 8, jl * PLANE : (jl + 1) * PLANE]
-        back[slot] = live * (direct[slot] + part)
+        back[slot] = live * (back[slot] + part)
     for a in range(8):
         fine_out[:, a * PLANE : (a + 1) * PLANE] = back[:, a, :]
 
 
 def call(kernel, kinds, outs, scratch, flops, *args):
-    vmem = pl.BlockSpec(memory_space=pltpu.VMEM)
-    smem = pl.BlockSpec(memory_space=pltpu.SMEM)
+    spaces = {
+        "s": pltpu.SMEM,
+        "v": pltpu.VMEM,
+        "h": pltpu.HBM,
+    }
     moved = sum(math.prod(x.shape) * x.dtype.itemsize for x in (*args, *outs))
     return pl.pallas_call(
         kernel,
         out_shape=outs,
-        in_specs=[smem if kind == "s" else vmem for kind in kinds],
-        out_specs=[vmem] * len(outs),
+        in_specs=[pl.BlockSpec(memory_space=spaces[kind]) for kind in kinds],
+        out_specs=[pl.BlockSpec(memory_space=pltpu.VMEM)] * len(outs),
         scratch_shapes=scratch,
         compiler_params=pltpu.CompilerParams(vmem_limit_bytes=VMEM_LIMIT),
         cost_estimate=pl.CostEstimate(flops=flops, bytes_accessed=moved, transcendentals=0),
@@ -470,33 +544,43 @@
 ):
     tables = filter_tables()
     select = jnp.asarray(select_tables())
-    comp, prol, contrib, single, mids, rows_c, rows_p = (
-        jnp.asarray(tables[name])
-        for name in ("comp", "prol", "contrib", "single", "mids", "rows_c", "rows_p")
-    )
-    six = op_factor.reshape(3, QUADS, 4, 3, 8, 8)
-    factors = six.transpose(0, 1, 3, 5, 2, 4).reshape(3, QUADS * 24, 32)
-    weights = jnp.broadcast_to(
-        jnp.repeat(term_weight.reshape(QUADS, 1, 4), 8, axis=2), (QUADS, 24, 32)
-    ).reshape(QUADS * 24, 32)
-    weighted = factors * weights[None]
-    x_tables = op_factor.transpose(0, 1, 3, 2, 4).reshape(3, TERMS * 8, 24).astype(BF16)
+    prol_rows = np.concatenate(np.split(tables["prol"], 4, axis=1), axis=0)
+    single_rows = tables["single"].reshape(256, 128)
+    first_filters = jnp.asarray(
+        np.concatenate([tables["comp"], prol_rows, tables["contrib"].reshape(256, 128)])
+    )
+    last_filters = jnp.asarray(np.concatenate([prol_rows, single_rows]))
+    rows_both = jnp.asarray(np.concatenate([tables["rows_c"], tables["rows_p"]]))
+    rows_p = jnp.asarray(tables["rows_p"])
+    mids = jnp.asarray(tables["mids"])
+    factors = op_factor.transpose(0, 2, 3, 4, 1).reshape(3, 192, TERMS)
 
     sds = jax.ShapeDtypeStruct
-    halo, payload, fine_at, mid_at, coarse_at = call(
+    vmem, smem = pltpu.VMEM, pltpu.SMEM
+    i32 = jnp.int32
+    halo, payload, numbers = call(
         first_kernel,
-        "sssvvvvvvvvvv",
+        "hhhhhhhhhh",
+        [sds((48, 128), BF16), sds((64, 8, 128), BF16), sds((16, 128), i32)],
         [
-            sds((48, 128), BF16),
-            sds((64, 8, 128), BF16),
-            sds((8, 27), jnp.int32),
-            sds((1, 32), jnp.int32),
-            sds((1, 32), jnp.int32),
+            smem((1, 8), i32),
+            smem((1,), i32),
+            smem((1,), i32),
+            vmem((1, 8), i32),
+            vmem((8, 27), i32),
+            vmem((1, 27), i32),
+            vmem((27, 64), i32),
+            vmem((8, 512), BF16),
+            vmem((1, 512), BF16),
+            vmem((768, 128), BF16),
+            vmem((32, 8, 128), F32),
+            vmem((8, 8, PLANE), F32),
+            vmem((8, 8, PLANE), F32),
+            pltpu.SemaphoreType.DMA((11,)),
         ],
-        [pltpu.VMEM((8, 8, PLANE), F32), pltpu.VMEM((8, 8, PLANE), F32)],
         2_000_000,
-        mid_child, mid_parent, mid_refined, fine_nbr, mid_nbr, coarse_nbr, fine_coef, mid_leaf,
-        comp, prol, contrib, rows_c, rows_p,
+        mid_child, mid_parent, mid_refined, fine_nbr, mid_nbr, coarse_nbr.T, fine_coef, mid_leaf,
+        first_filters, rows_both,
     )
     arrived = lax.all_to_all(payload, ("gy", "gz"), 0, 0, tiled=True)
     before, after = both_ways(halo, "gz")
@@ -510,38 +594,33 @@
     )
     planes = lax.all_to_all(copies, "gx", 0, 0, tiled=True)
 
-    direct, mid_tiles, parents = call(
-        fine_kernel,
-        "svvvvvvv",
+    w_tables, x_tables, centre = call(
+        tables_kernel,
+        "vvvv",
         [
-            sds((8, 8, PLANE), F32),
-            sds((28, 8, 128), F32),
-            sds((1, 128), jnp.int32),
+            pltpu.VMEM((3 * QUADS, ROWS_W, 256), BF16),
+            pltpu.VMEM((3, 256, 24), BF16),
+            pltpu.VMEM((90, 8, 128), F32),
         ],
-        [
-            pltpu.VMEM((GONE + 1, 8, 128), F32),
-            pltpu.VMEM((QUADS, 256, ROWS_W), BF16),
-            pltpu.VMEM((QUADS, ROWS_W, 256), BF16),
-            pltpu.VMEM((QUADS, 24, 512), F32),
-        ],
-        700_000_000,
-        fine_at, before, sheet, after, factors[0], weighted[0], x_tables[0], select,
+        [vmem((2, 24, 24, 256), F32)],
+        600_000_000,
+        factors, term_weight.reshape(1, TERMS), select, sheet,
     )
     fine_out, mid_out = call(
         last_kernel,
-        "ssssssvvvvvvvvvvv",
+        "svvvvvvvvv",
         [sds((8, 512), F32), sds((1, 512), F32)],
         [
-            pltpu.VMEM((65, 8, 128), F32),
-            pltpu.VMEM((8, 8, PLANE), F32),
-            pltpu.VMEM((QUADS, ROWS_W, 256), BF16),
-            pltpu.VMEM((QUADS, ROWS_W, 256), BF16),
-            pltpu.VMEM((QUADS, 24, 512), F32),
+            vmem((GONE + 9, 8, 128), F32),
+            vmem((QUADS, 256, ROWS_W), BF16),
+            vmem((65, 8, 128), F32),
+            vmem((8, 8, PLANE), F32),
+            vmem((1, 128), i32),
+            smem((1, 128), i32),
+            pltpu.SemaphoreType.DMA,
         ],
-        200_000_000,
-        mid_child, mid_parent, mid_refined, mid_at, coarse_at, parents,
-        planes, mid_tiles, direct, factors[1:], weighted[1:], x_tables[1:], select,
-        rows_p, prol, single, mids,
+        900_000_000,
+        numbers, before, centre, after, planes, w_tables, x_tables, rows_p, last_filters, mids,
     )
     return fine_out, mid_out
 

time: 75.6 us -> 79.9 us (1.057)
  waiting for transfers between devices: 3.56 us -> 7.25 us
  local copies, waits for them, and re-layouts: 15.9 us -> 17.6 us
    unnamed x44 -> x38, local copies, waits for them, and re-layouts: 9.97 us -> 17.5 us
    slice x14 -> x0, local copies, waits for them, and re-layouts: 3.96 us -> none  [the longest x2 1.98 us: shards(): factors[0]]
    all_to_all x1, waiting for transfers between devices: 3.54 us -> 7.23 us  [shards(): arrived = lax.all_to_all(payload, ('gy', 'gz'), 0, 0, tiled=True)]
  transfers between devices with their start and end apart: 8 -> 8, of which waited for: 1 -> 1; matrix products, arithmetic and copies ran while one was open for 11% -> 0% of each run, Pallas kernels for 7% -> 4%
where the time goes in v2:
time: 79.9 us; the launch traced here: 79.1 us
  starting transfers between devices  40.4 us (51%)
  local copies, waits for them, and re-layouts  17.6 us (22%)
  Pallas kernels  11.7 us (15%)
  waiting for transfers between devices  7.25 us (9%)
  between operations  2.1 us (3%)
    all_to_all x1, starting transfers between devices, shards(): arrived = lax.all_to_all(payload, ('gy', 'gz'), 0, 0, tiled=True)  18.3 us
    unnamed x38, local copies, waits for them, and re-layouts  17.5 us
    pallas_call x4, Pallas kernels, call(): pl.pallas_call(kernel, out_shape=outs, in_specs=[pl.BlockSpec(memory_spac...  11.7 us
    ppermute x3, starting transfers between devices, both_ways(): before = lax.ppermute(x, axis, [(i, i + 1) for i in range(ends)])  10.6 us
    all_to_all x1, waiting for transfers between devices, shards(): arrived = lax.all_to_all(payload, ('gy', 'gz'), 0, 0, tiled=True)  7.23 us
    all_to_all x1, starting transfers between devices, shards(): planes = lax.all_to_all(copies, 'gx', 0, 0, tiled=True)  7.03 us
    ppermute x3, starting transfers between devices, both_ways(): after = lax.ppermute(x, axis, [(i + 1, i) for i in range(ends)])  4.51 us
  transfers between devices with their start and end apart: 8, of which 1 were waited for; matrix products, arithmetic and copies ran while one was open for 0% of the time, Pallas kernels for 4%

profile of v2, /device:TPU:1, one launch (start us, length us, event | category | flops | bytes accessed | tf_op | source)
XLA Modules:
  0.0 79.1 jit_solution(6360080023802996912)
XLA Ops:
  1.9 0.0 copy-start.3
  1.9 0.9 %copy-done.3 = bf16[768,128]{1,0:T(8,128)(2,1)S(1)} copy-done((bf16[768,128]{1,0:T(8,128)(2,1)S(1)}, bf16[768,128]{1,0:T(8,128)(2,1)}, u32[]{:S(2)}) %copy-start.3) | copy-done | bytes 196632
  2.9 0.9 %copy-done.5 = f32[32,8,128]{2,1,0:T(8,128)S(1)} copy-done((f32[32,8,128]{2,1,0:T(8,128)S(1)}, f32[32,8,128]{2,1,0:T(8,128)}, u32[]{:S(2)}) %copy-start.5) | copy-done | bytes 131096
  3.8 0.7 copy-done.7
  4.5 0.7 copy-done.8
  5.2 0.7 copy-done.9
  5.9 0.7 copy-done.10
  6.5 0.7 copy-done.11
  7.2 0.7 copy-done.12
  7.9 2.4 %first_kernel.1 = (bf16[48,128]{1,0:T(8,128)(2,1)S(1)}, bf16[64,8,128]{2,1,0:T(8,128)(2,1)}, s32[16,128]{1,0:T(8,128)S(1)}) custom-call(s32[1,8]{1,0:T(1,128)S(1)} %copy-done.11, s32[1]{0:T(128)S(6)} %copy.24.parent_h, s32[1]{0:T(128)S(6)} %copy.25.refined_h, s32[8,27]{1,0:T(8,128)S(1)} %copy-done.9, s32[1,27]{1,0:T(1,128)S(1)} %copy-done.12, ...), custom_call_target="tpu_custom_call" | custom-call | flops 2000000 | bytes 496372 | tf_op jit(solution)/shard_map/first_kernel/pallas_call | solution.py:521
  10.3 4.0 %collective-permute-start = (bf16[48,128]{1,0:T(8,128)(2,1)S(1)}, bf16[48,128]{1,0:T(8,128)(2,1)S(1)}, u32[]{:S(2)}, u32[]{:S(2)}) collective-permute-start(bf16[48,128]{1,0:T(8,128)(2,1)S(1)} %get-tuple-element.9), channel_id=1, source_target_pairs={{0,1},{1,2},{2,3},{3,4},{4,5},{5,6},{6,7},{8,9},{9,10},{10,11},{11... | collective-permute-start | bytes 36872 | tf_op jit(solution)/shard_map/ppermute | solution.py:536
  14.3 1.3 %collective-permute-start.1 = (bf16[48,128]{1,0:T(8,128)(2,1)S(1)}, bf16[48,128]{1,0:T(8,128)(2,1)S(1)}, u32[]{:S(2)}, u32[]{:S(2)}) collective-permute-start(bf16[48,128]{1,0:T(8,128)(2,1)S(1)} %get-tuple-element.9), channel_id=1, source_target_pairs={{1,0},{2,1},{3,2},{4,3},{5,4},{6,5},{7,6},{9,8},{10,9},{11,10},{12... | collective-permute-start | bytes 36872 | tf_op jit(solution)/shard_map/ppermute | solution.py:537
  15.6 18.3 %all-to-all-start = ((bf16[64,8,128]{2,1,0:T(8,128)(2,1)}), bf16[64,8,128]{2,1,0:T(8,128)(2,1)S(1)}, u32[]{:S(2)}, u32[]{:S(2)}) async-start(bf16[64,8,128]{2,1,0:T(8,128)(2,1)} %get-tuple-element.11), calls=%async_computation | async-start | bytes 262144 | tf_op jit(solution)/shard_map/all_to_all | solution.py:585
  33.9 0.0 collective-permute-done
  34.0 2.9 %collective-permute-start.2 = (bf16[144,128]{1,0:T(8,128)(2,1)S(1)}, bf16[144,128]{1,0:T(8,128)(2,1)S(1)}, u32[]{:S(2)}, u32[]{:S(2)}) collective-permute-start(bf16[144,128]{1,0:T(8,128)(2,1)S(1)} %constant_dynamic-update-slice_fusion), channel_id=1, source_target_pairs={{0,8},{8,16},{16,24},{24,32},{32,40},{40,48},{48,56},{1,9},{9,17},... | collective-permute-start | bytes 110600 | tf_op jit(solution)/shard_map/ppermute | solution.py:536
  36.9 1.3 %collective-permute-start.3 = (bf16[144,128]{1,0:T(8,128)(2,1)S(1)}, bf16[144,128]{1,0:T(8,128)(2,1)S(1)}, u32[]{:S(2)}, u32[]{:S(2)}) collective-permute-start(bf16[144,128]{1,0:T(8,128)(2,1)S(1)} %constant_dynamic-update-slice_fusion), channel_id=1, source_target_pairs={{8,0},{16,8},{24,16},{32,24},{40,32},{48,40},{56,48},{9,1},{17,9},... | collective-permute-start | bytes 110600 | tf_op jit(solution)/shard_map/ppermute | solution.py:537
  38.2 7.2 %all-to-all-done.arrived = bf16[64,8,128]{2,1,0:T(8,128)(2,1)S(1)} async-done(((bf16[64,8,128]{2,1,0:T(8,128)(2,1)}), bf16[64,8,128]{2,1,0:T(8,128)(2,1)S(1)}, u32[]{:S(2)}, u32[]{:S(2)}) %all-to-all-start) | async-done | bytes 131104 | tf_op jit(solution)/shard_map/all_to_all | solution.py:585
  45.5 1.3 %plane_kernel.1 = bf16[8,256,128]{2,1,0:T(8,128)(2,1)} custom-call(bf16[64,8,128]{2,1,0:T(8,128)(2,1)S(1)} %all-to-all-done.arrived), custom_call_target="tpu_custom_call" | custom-call | flops 33000000 | bytes 655360 | tf_op jit(solution)/shard_map/plane_kernel/pallas_call | solution.py:521
  46.8 7.0 %all-to-all-start.1 = ((bf16[8,256,128]{2,1,0:T(8,128)(2,1)}), bf16[8,256,128]{2,1,0:T(8,128)(2,1)S(1)}, u32[]{:S(2)}, u32[]{:S(2)}) async-start(bf16[8,256,128]{2,1,0:T(8,128)(2,1)} %plane_kernel.1), calls=%async_computation.1 | async-start | bytes 1048576 | tf_op jit(solution)/shard_map/all_to_all | solution.py:595
  53.8 1.9 %collective-permute-start.5 = (bf16[432,128]{1,0:T(8,128)(2,1)S(1)}, bf16[432,128]{1,0:T(8,128)(2,1)S(1)}, u32[]{:S(2)}, u32[]{:S(2)}) collective-permute-start(bf16[432,128]{1,0:T(8,128)(2,1)S(1)} %constant_dynamic-update-slice_fusion.3.sheet), channel_id=1, source_target_pairs={{64,0},{128,64},{192,128},{256,192},{320,256},{384,320},{448,384},... | collective-permute-start | bytes 331784 | tf_op jit(solution)/shard_map/ppermute | solution.py:537
  55.8 3.6 %collective-permute-start.4 = (bf16[432,128]{1,0:T(8,128)(2,1)S(1)}, bf16[432,128]{1,0:T(8,128)(2,1)S(1)}, u32[]{:S(2)}, u32[]{:S(2)}) collective-permute-start(bf16[432,128]{1,0:T(8,128)(2,1)S(1)} %constant_dynamic-update-slice_fusion.3.sheet), channel_id=1, source_target_pairs={{0,64},{64,128},{128,192},{192,256},{256,320},{320,384},{384,448},... | collective-permute-start | bytes 331784 | tf_op jit(solution)/shard_map/ppermute | solution.py:536
  59.4 0.0 copy-start.13
  59.4 1.0 %copy-done.13 = f32[3,32,3,8,8]{1,4,3,2,0:T(8,128)S(1)} copy-done((f32[3,32,3,8,8]{1,4,3,2,0:T(8,128)S(1)}, f32[3,32,3,8,8]{1,4,3,2,0:T(8,128)}, u32[]{:S(2)}) %copy-start.13) | copy-done | bytes 73752
  60.4 0.7 copy-done.14
  61.0 1.0 %copy-done.15 = bf16[256,768]{1,0:T(8,128)(2,1)S(1)} copy-done((bf16[256,768]{1,0:T(8,128)(2,1)S(1)}, bf16[256,768]{1,0:T(8,128)(2,1)}, u32[]{:S(2)}) %copy-start.15) | copy-done | bytes 393240
  62.0 1.6 %tables_kernel.1 = (bf16[24,640,256]{2,1,0:T(8,128)(2,1)S(1)}, bf16[3,256,24]{2,1,0:T(8,128)(2,1)S(1)}, f32[90,8,128]{2,1,0:T(8,128)S(1)}) custom-call(f32[3,192,32]{2,1,0:T(8,128)S(1)} %bitcast.6, f32[1,32]{1,0:T(1,128)S(1)} %bitcast.7, bf16[256,768]{1,0:T(8,128)(2,1)S(1)} %copy-done.15, bf16[432,128]{1,0:T(8,128)(2,1)S(1)} %constant_dynamic-update-slice_fusion.3.sheet), custom_call_target="tpu_custom_call" | custom-call | flops 600000000 | bytes 8847488 | tf_op jit(solution)/shard_map/tables_kernel/pallas_call | solution.py:521
  63.7 3.1 %copy-done = bf16[24,640,256]{2,1,0:T(8,128)(2,1)} copy-done((bf16[24,640,256]{2,1,0:T(8,128)(2,1)}, bf16[24,640,256]{2,1,0:T(8,128)(2,1)S(1)}, u32[]{:S(2)}) %copy-start) | copy-done | bytes 7864344
  66.7 3.2 %copy-done.1 = bf16[24,640,256]{2,1,0:T(8,128)(2,1)S(1)} copy-done((bf16[24,640,256]{2,1,0:T(8,128)(2,1)S(1)}, bf16[24,640,256]{2,1,0:T(8,128)(2,1)}, u32[]{:S(2)}) %copy-start.1) | copy-done | bytes 7864344
  70.0 0.9 %copy-done.2 = bf16[128,1024]{1,0:T(8,128)(2,1)S(1)} copy-done((bf16[128,1024]{1,0:T(8,128)(2,1)S(1)}, bf16[128,1024]{1,0:T(8,128)(2,1)}, u32[]{:S(2)}) %copy-start.2) | copy-done | bytes 262168
  70.9 0.9 %copy-done.4 = bf16[512,128]{1,0:T(8,128)(2,1)S(1)} copy-done((bf16[512,128]{1,0:T(8,128)(2,1)S(1)}, bf16[512,128]{1,0:T(8,128)(2,1)}, u32[]{:S(2)}) %copy-start.4) | copy-done | bytes 131096
  71.8 0.8 %copy-done.6 = f32[16,8,128]{2,1,0:T(8,128)S(1)} copy-done((f32[16,8,128]{2,1,0:T(8,128)S(1)}, f32[16,8,128]{2,1,0:T(8,128)}, u32[]{:S(2)}) %copy-start.6) | copy-done | bytes 65560
  72.7 6.4 %last_kernel.1 = (f32[8,512]{1,0:T(8,128)}, f32[1,512]{1,0:T(1,128)}) custom-call(s32[16,128]{1,0:T(8,128)S(1)} %get-tuple-element.8.numbers, bf16[432,128]{1,0:T(8,128)(2,1)S(1)} %collective-permute-done.4.left, f32[90,8,128]{2,1,0:T(8,128)S(1)} %get-tuple-element.10.centre, bf16[432,128]{1,0:T(8,128)(2,1)S(1)} %collective-permute-done.5.right, ...), custom_call_target="tpu_custom_call" | custom-call | flops 900000000 | bytes 9500672 | tf_op jit(solution)/shard_map/last_kernel/pallas_call | solution.py:521
  (28 shorter events, 0.1 us)
Async XLA Ops:
  1.9 0.9 %copy-start.3 = (bf16[768,128]{1,0:T(8,128)(2,1)S(1)}, bf16[768,128]{1,0:T(8,128)(2,1)}, u32[]{:S(2)}) copy-start(bf16[768,128]{1,0:T(8,128)(2,1)} %constant.13.clone.filters_h) | copy-start | bytes 589828
  2.9 0.9 %copy-start.5 = (f32[32,8,128]{2,1,0:T(8,128)S(1)}, f32[32,8,128]{2,1,0:T(8,128)}, u32[]{:S(2)}) copy-start(f32[32,8,128]{2,1,0:T(8,128)} %constant.15.clone.rows_h) | copy-start | bytes 393220
  3.8 0.7 copy-start.7
  4.5 0.7 copy-start.8
  5.2 0.7 copy-start.9
  5.9 0.7 copy-start.10
  6.5 0.7 copy-start.11
  7.2 0.7 copy-start.12
  10.3 23.7 %collective-permute-start = (bf16[48,128]{1,0:T(8,128)(2,1)S(1)}, bf16[48,128]{1,0:T(8,128)(2,1)S(1)}, u32[]{:S(2)}, u32[]{:S(2)}) collective-permute-start(bf16[48,128]{1,0:T(8,128)(2,1)S(1)} %get-tuple-element.9), channel_id=1, source_target_pairs={{0,1},{1,2},{2,3},{3,4},{4,5},{5,6},{6,7},{8,9},{9,10},{10,11},{11... | collective-permute-start | bytes 36872 | tf_op jit(solution)/shard_map/ppermute | solution.py:536
  14.3 19.7 %collective-permute-start.1 = (bf16[48,128]{1,0:T(8,128)(2,1)S(1)}, bf16[48,128]{1,0:T(8,128)(2,1)S(1)}, u32[]{:S(2)}, u32[]{:S(2)}) collective-permute-start(bf16[48,128]{1,0:T(8,128)(2,1)S(1)} %get-tuple-element.9), channel_id=1, source_target_pairs={{1,0},{2,1},{3,2},{4,3},{5,4},{6,5},{7,6},{9,8},{10,9},{11,10},{12... | collective-permute-start | bytes 36872 | tf_op jit(solution)/shard_map/ppermute | solution.py:537
  15.6 29.9 %all-to-all-start = ((bf16[64,8,128]{2,1,0:T(8,128)(2,1)}), bf16[64,8,128]{2,1,0:T(8,128)(2,1)S(1)}, u32[]{:S(2)}, u32[]{:S(2)}) async-start(bf16[64,8,128]{2,1,0:T(8,128)(2,1)} %get-tuple-element.11), calls=%async_computation | async-start | bytes 262144 | tf_op jit(solution)/shard_map/all_to_all | solution.py:585
  34.0 4.2 %collective-permute-start.2 = (bf16[144,128]{1,0:T(8,128)(2,1)S(1)}, bf16[144,128]{1,0:T(8,128)(2,1)S(1)}, u32[]{:S(2)}, u32[]{:S(2)}) collective-permute-start(bf16[144,128]{1,0:T(8,128)(2,1)S(1)} %constant_dynamic-update-slice_fusion), channel_id=1, source_target_pairs={{0,8},{8,16},{16,24},{24,32},{32,40},{40,48},{48,56},{1,9},{9,17},... | collective-permute-start | bytes 110600 | tf_op jit(solution)/shard_map/ppermute | solution.py:536
  36.9 16.9 %collective-permute-start.3 = (bf16[144,128]{1,0:T(8,128)(2,1)S(1)}, bf16[144,128]{1,0:T(8,128)(2,1)S(1)}, u32[]{:S(2)}, u32[]{:S(2)}) collective-permute-start(bf16[144,128]{1,0:T(8,128)(2,1)S(1)} %constant_dynamic-update-slice_fusion), channel_id=1, source_target_pairs={{8,0},{16,8},{24,16},{32,24},{40,32},{48,40},{56,48},{9,1},{17,9},... | collective-permute-start | bytes 110600 | tf_op jit(solution)/shard_map/ppermute | solution.py:537
  46.8 20.0 %all-to-all-start.1 = ((bf16[8,256,128]{2,1,0:T(8,128)(2,1)}), bf16[8,256,128]{2,1,0:T(8,128)(2,1)S(1)}, u32[]{:S(2)}, u32[]{:S(2)}) async-start(bf16[8,256,128]{2,1,0:T(8,128)(2,1)} %plane_kernel.1), calls=%async_computation.1 | async-start | bytes 1048576 | tf_op jit(solution)/shard_map/all_to_all | solution.py:595
  53.8 12.9 %collective-permute-start.5 = (bf16[432,128]{1,0:T(8,128)(2,1)S(1)}, bf16[432,128]{1,0:T(8,128)(2,1)S(1)}, u32[]{:S(2)}, u32[]{:S(2)}) collective-permute-start(bf16[432,128]{1,0:T(8,128)(2,1)S(1)} %constant_dynamic-update-slice_fusion.3.sheet), channel_id=1, source_target_pairs={{64,0},{128,64},{192,128},{256,192},{320,256},{384,320},{448,384},... | collective-permute-start | bytes 331784 | tf_op jit(solution)/shard_map/ppermute | solution.py:537
  55.8 11.0 %collective-permute-start.4 = (bf16[432,128]{1,0:T(8,128)(2,1)S(1)}, bf16[432,128]{1,0:T(8,128)(2,1)S(1)}, u32[]{:S(2)}, u32[]{:S(2)}) collective-permute-start(bf16[432,128]{1,0:T(8,128)(2,1)S(1)} %constant_dynamic-update-slice_fusion.3.sheet), channel_id=1, source_target_pairs={{0,64},{64,128},{128,192},{192,256},{256,320},{320,384},{384,448},... | collective-permute-start | bytes 331784 | tf_op jit(solution)/shard_map/ppermute | solution.py:536
  59.4 1.0 %copy-start.13 = (f32[3,32,3,8,8]{1,4,3,2,0:T(8,128)S(1)}, f32[3,32,3,8,8]{1,4,3,2,0:T(8,128)}, u32[]{:S(2)}) copy-start(f32[3,32,3,8,8]{1,4,3,2,0:T(8,128)} %param.24) | copy-start | bytes 221188
  60.4 0.7 copy-start.14
  61.0 1.0 %copy-start.15 = (bf16[256,768]{1,0:T(8,128)(2,1)S(1)}, bf16[256,768]{1,0:T(8,128)(2,1)}, u32[]{:S(2)}) copy-start(bf16[256,768]{1,0:T(8,128)(2,1)} %constant.12.clone.select) | copy-start | bytes 1179652
  63.7 3.1 %copy-start = (bf16[24,640,256]{2,1,0:T(8,128)(2,1)}, bf16[24,640,256]{2,1,0:T(8,128)(2,1)S(1)}, u32[]{:S(2)}) copy-start(bf16[24,640,256]{2,1,0:T(8,128)(2,1)S(1)} %get-tuple-element.12.w_ref) | copy-start | bytes 23592964
  66.7 3.2 %copy-start.1 = (bf16[24,640,256]{2,1,0:T(8,128)(2,1)S(1)}, bf16[24,640,256]{2,1,0:T(8,128)(2,1)}, u32[]{:S(2)}) copy-start(bf16[24,640,256]{2,1,0:T(8,128)(2,1)} %copy-done) | copy-start | bytes 23592964
  70.0 0.9 %copy-start.2 = (bf16[128,1024]{1,0:T(8,128)(2,1)S(1)}, bf16[128,1024]{1,0:T(8,128)(2,1)}, u32[]{:S(2)}) copy-start(bf16[128,1024]{1,0:T(8,128)(2,1)} %constant.17.clone.mids) | copy-start | bytes 786436
  70.9 0.9 %copy-start.4 = (bf16[512,128]{1,0:T(8,128)(2,1)S(1)}, bf16[512,128]{1,0:T(8,128)(2,1)}, u32[]{:S(2)}) copy-start(bf16[512,128]{1,0:T(8,128)(2,1)} %constant.14.clone.filters) | copy-start | bytes 393220
  71.8 0.8 %copy-start.6 = (f32[16,8,128]{2,1,0:T(8,128)S(1)}, f32[16,8,128]{2,1,0:T(8,128)}, u32[]{:S(2)}) copy-start(f32[16,8,128]{2,1,0:T(8,128)} %constant.16.clone.rows_p) | copy-start | bytes 196612

commit v3 on v2

--- a/solution.py
+++ b/solution.py
@@ -18,7 +18,7 @@
 GONE = 27 * 10
 BF16 = jnp.bfloat16
 F32 = jnp.float32
-VMEM_LIMIT = 40 * 1024 * 1024
+VMEM_LIMIT = 32 * 1024 * 1024
 
 
 def poly_multiply(left, right):
@@ -154,6 +154,15 @@
     ]
 
 
+def fetches(sems, *pairs):
+    copies = [
+        pltpu.make_async_copy(there, here, sems.at[at]) for at, (there, here) in enumerate(pairs)
+    ]
+    for copy in copies:
+        copy.start()
+    return copies
+
+
 def local_cell(device, own):
     step_x = (device >> 6) - (own >> 6) + 1
     step_y = ((device >> 3) & 7) - ((own >> 3) & 7) + 1
@@ -161,7 +170,16 @@
     return step_x * 9 + step_y * 3 + step_z
 
 
-def tables_kernel(factors, weights, select, sheet, w_ref, x_ref, tiles, ab_ref):
+def tables_kernel(
+    factors_h, weights_h, select_h, sheet,
+    w_hbm, x_ref, tiles,
+    ab_ref, factors, weights, select, sems, w_ref, w_sems,
+):
+    copies = fetches(sems, (factors_h, factors), (weights_h, weights), (select_h, select))
+    for cell in range(9):
+        spread_cell(sheet, cell, tiles, cell)
+    for copy in copies:
+        copy.wait()
     lane = lax.broadcasted_iota(jnp.int32, (24, 256), 1)
     quad_of = (lane & 31) >> 2
     weight = jnp.concatenate([weights[...]] * 8, axis=1)
@@ -204,12 +222,16 @@
                     tile = jnp.concatenate([first * inner[ez], second * inner[ez]], axis=0)
                     to = (ey * 3 + ez) * PLANE + pair * 16
                     w_ref[at, to : to + 16, :] = tile.astype(BF16)
-        w_ref[at, 576:640, :] = jnp.zeros((64, 256), BF16)
         return carry
 
-    lax.fori_loop(0, 3 * QUADS, one_quad, 0)
-    for cell in range(9):
-        spread_cell(sheet, cell, tiles, cell)
+    copies = []
+    for level in range(3):
+        lax.fori_loop(level * QUADS, (level + 1) * QUADS, one_quad, 0)
+        some = pl.ds(level * QUADS, QUADS)
+        copies.append(pltpu.make_async_copy(w_ref.at[some], w_hbm.at[some], w_sems.at[level]))
+        copies[-1].start()
+    for copy in copies:
+        copy.wait()
 
 
 def spread_cell(sheet, cell, tiles, to):
@@ -235,47 +257,39 @@
     return total
 
 
-def apply_one(sources, x_table, w_ref, base):
+def apply_one(sources, x_table, w_ref):
     mixed = dot(x_table, sources).astype(BF16)
     result = None
     for quad in range(QUADS):
-        part = dot(mixed[quad * 32 : quad * 32 + 32, :], w_ref[base + quad])
+        part = dot(mixed[quad * 32 : quad * 32 + 32, :576], w_ref[quad])
         result = part if result is None else result + part
     return diagonal_sum(result, 8)
 
 
 def first_kernel(
-    child_h, parent_h, refined_h, fine_h, mid_h, coarse_h, coef_h, leaf_h, filters_h, rows_h,
+    small_h, fine_h, mid_h, coarse_h, coef_h, leaf_h, filters_h, rows_h,
     halo, payload, numbers,
-    child, parent, refined, child_v, fine_nbr, mid_nbr, coarse_nbr, coef, leaf, filters, rows,
+    small, small_v, fine_nbr, mid_nbr, coarse_nbr, coef, leaf, filters, rows,
     source, detail, sems,
 ):
-    copies = [
-        pltpu.make_async_copy(there, here, sems.at[at])
-        for at, (there, here) in enumerate(
-            (
-                (coef_h, coef),
-                (filters_h, filters),
-                (rows_h, rows),
-                (child_h, child),
-                (parent_h, parent),
-                (refined_h, refined),
-                (leaf_h, leaf),
-                (child_h, child_v),
-                (fine_h, fine_nbr),
-                (mid_h, mid_nbr),
-                (coarse_h, coarse_nbr),
-            )
-        )
-    ]
-    for copy in copies:
-        copy.start()
+    copies = fetches(
+        sems,
+        (coef_h, coef),
+        (filters_h, filters),
+        (rows_h, rows),
+        (small_h, small),
+        (leaf_h, leaf),
+        (small_h, small_v),
+        (fine_h, fine_nbr),
+        (mid_h, mid_nbr),
+        (coarse_h, coarse_nbr),
+    )
     for copy in copies:
         copy.wait()
     comp = filters[0:256, :]
     prol = jnp.concatenate([filters[256 + 64 * k : 320 + 64 * k, :] for k in range(4)], axis=1)
-    slot = parent[0] >> 3
-    octant = parent[0] & 7
+    slot = small[0, 8] >> 3
+    octant = small[0, 8] & 7
     near = fine_nbr[...]
     own = near[:, 13:14] >> 3
     cell = local_cell(near >> 3, own) * 10 + (near & 7)
@@ -293,14 +307,12 @@
     )[0:1].astype(jnp.int32)
     numbers[9:10, 0:27] = jnp.where(near_coarse >= 0, near_coarse, 64)
     numbers[9:10, 27:28] = jnp.full((1, 1), 64, jnp.int32)
-    numbers[10:11, 0:8] = child_v[...]
-    numbers[10:11, 8:9] = jnp.full((1, 1), parent[0], jnp.int32)
-    numbers[10:11, 9:10] = jnp.full((1, 1), refined[0], jnp.int32)
+    numbers[10:11, 0:10] = small_v[...]
 
     values = coef[...].astype(F32)
     for a in range(8):
         source[:, a, :] = values[:, a * PLANE : (a + 1) * PLANE]
-    tiles = [source[child[0, o]] for o in range(8)]
+    tiles = [source[small[0, o]] for o in range(8)]
     lhs = jnp.concatenate(
         [jnp.concatenate(tiles[0:4], axis=1), jnp.concatenate(tiles[4:8], axis=1)], axis=0
     ).astype(BF16)
@@ -314,7 +326,7 @@
     leaf_tile = jnp.concatenate(
         [leaf_row[:, a * PLANE : (a + 1) * PLANE] for a in range(8)], axis=0
     )
-    middle = jnp.where(refined[0] > 0, compressed, leaf_tile).astype(BF16).astype(F32)
+    middle = jnp.where(small[0, 9] > 0, compressed, leaf_tile).astype(BF16).astype(F32)
 
     row_at = (octant >> 2) * 8
     inner = row_mix([rows[row_at + x, :, :PLANE] for x in range(8)], middle)
@@ -325,13 +337,13 @@
     tile = jnp.where(low8, jnp.concatenate([added, added], axis=1), tag).astype(BF16)
     payload[...] = jnp.broadcast_to(tile[None], payload.shape)
 
-    live = jnp.full((8, PLANE), refined[0], jnp.int32).astype(F32)
+    live = jnp.full((8, PLANE), small[0, 9], jnp.int32).astype(F32)
     upper = jnp.concatenate(two_row_mixes(rows.at[16:32], middle, PLANE), axis=0)
     spread = fine_dot(upper, prol)
     for o in range(8):
         i, jl = o // 4, o % 4
         part = spread[i * 8 : i * 8 + 8, jl * PLANE : (jl + 1) * PLANE]
-        detail[child[0, o]] = live * (tiles[o] - part)
+        detail[small[0, o]] = live * (tiles[o] - part)
     for group in range(2):
         base = group * 4
         halo[group * 16 : group * 16 + 16, :] = jnp.concatenate(
@@ -373,10 +385,14 @@
 
 
 def last_kernel(
-    numbers, left, centre, right, planes, w_ref, x_ref, rows_p, filters, mids,
+    numbers, left, centre, right, planes, w_hbm, x_ref, rows_h, filters_h, mids_h,
     fine_out, mid_out,
-    table, mixed, coarse, back, names_v, names_s, sem,
+    table, mixed, coarse, back, names_v, names_s, sem, rows_p, filters, mids, sems,
+    w_ref, w_sems,
 ):
+    levels = [pl.ds(level * QUADS, QUADS) for level in range(3)]
+    w_copies = fetches(w_sems, *((w_hbm.at[some], w_ref.at[some]) for some in levels))
+    copies = fetches(sems, (rows_h, rows_p), (filters_h, filters), (mids_h, mids))
     lanes = lax.broadcasted_iota(jnp.int32, (1, 128), 1)
     low8 = low_lanes((8, 128))
     table[GONE] = jnp.zeros((8, 128), F32)
@@ -422,9 +438,10 @@
             )
             row = term * PLANE + pair * 16
             mixed[quad, row : row + 16, :] = tile.astype(BF16)
+    w_copies[0].wait()
     result = None
     for quad in range(QUADS):
-        part = dot(mixed[quad], w_ref[quad])
+        part = dot(mixed[quad, :, :576], w_ref[quad])
         result = part if result is None else result + part
     direct = diagonal_sum(result, PLANE)
 
@@ -456,9 +473,12 @@
         ],
         axis=1,
     )
-    coarse_result = apply_one(sources, x_ref[2], w_ref, 16)
+    w_copies[2].wait()
+    coarse_result = apply_one(sources, x_ref[2], w_ref.at[16:24])
 
     fetch.wait()
+    for copy in copies:
+        copy.wait()
     uppers, octants, owns = [], [], []
     for ep in range(5):
         for ex in range(3):
@@ -488,7 +508,8 @@
                 )
             tiles.append(owns[at] - chosen)
         pieces.append(jnp.concatenate(tiles, axis=0).astype(BF16))
-    mid_result = apply_one(jnp.concatenate(pieces, axis=1), x_ref[1], w_ref, 8)
+    w_copies[1].wait()
+    mid_result = apply_one(jnp.concatenate(pieces, axis=1), x_ref[1], w_ref.at[8:16])
 
     row_at = (octant >> 2) * 8
     upper = row_mix([rows_p[row_at + p, :, :PLANE] for p in range(8)], coarse_result)
@@ -512,17 +533,20 @@
 
 
 def call(kernel, kinds, outs, scratch, flops, *args):
-    spaces = {
-        "s": pltpu.SMEM,
-        "v": pltpu.VMEM,
-        "h": pltpu.HBM,
-    }
+    any_space = pl.BlockSpec(memory_space=pl.ANY)
+    vmem = pl.BlockSpec(memory_space=pltpu.VMEM)
+    specs = dict(s=pl.BlockSpec(memory_space=pltpu.SMEM), v=vmem, w=vmem, h=any_space)
     moved = sum(math.prod(x.shape) * x.dtype.itemsize for x in (*args, *outs))
+    spaces = dict(w=pltpu.VMEM, h=pltpu.HBM)
+    args = [
+        pltpu.with_memory_space_constraint(x, spaces[kind]) if kind in spaces else x
+        for kind, x in zip(kinds, args, strict=True)
+    ]
     return pl.pallas_call(
         kernel,
         out_shape=outs,
-        in_specs=[pl.BlockSpec(memory_space=spaces[kind]) for kind in kinds],
-        out_specs=[pl.BlockSpec(memory_space=pltpu.VMEM)] * len(outs),
+        in_specs=[specs[kind] for kind in kinds],
+        out_specs=[any_space if getattr(x, "memory_space", None) == pltpu.HBM else vmem for x in outs],
         scratch_shapes=scratch,
         compiler_params=pltpu.CompilerParams(vmem_limit_bytes=VMEM_LIMIT),
         cost_estimate=pl.CostEstimate(flops=flops, bytes_accessed=moved, transcendentals=0),
@@ -558,15 +582,16 @@
     sds = jax.ShapeDtypeStruct
     vmem, smem = pltpu.VMEM, pltpu.SMEM
     i32 = jnp.int32
+    at = lax.broadcasted_iota(jnp.int32, (1, 10), 1)
+    named = jnp.where(at == 8, jnp.broadcast_to(mid_parent, (1, 10)), jnp.broadcast_to(mid_refined, (1, 10)))
+    small = jnp.where(at < 8, jnp.pad(mid_child, ((0, 0), (0, 2))), named)
     halo, payload, numbers = call(
         first_kernel,
-        "hhhhhhhhhh",
+        "hhhhhhhh",
         [sds((48, 128), BF16), sds((64, 8, 128), BF16), sds((16, 128), i32)],
         [
-            smem((1, 8), i32),
-            smem((1,), i32),
-            smem((1,), i32),
-            vmem((1, 8), i32),
+            smem((1, 10), i32),
+            vmem((1, 10), i32),
             vmem((8, 27), i32),
             vmem((1, 27), i32),
             vmem((27, 64), i32),
@@ -576,10 +601,10 @@
             vmem((32, 8, 128), F32),
             vmem((8, 8, PLANE), F32),
             vmem((8, 8, PLANE), F32),
-            pltpu.SemaphoreType.DMA((11,)),
+            pltpu.SemaphoreType.DMA((9,)),
         ],
         2_000_000,
-        mid_child, mid_parent, mid_refined, fine_nbr, mid_nbr, coarse_nbr.T, fine_coef, mid_leaf,
+        small, fine_nbr, mid_nbr, coarse_nbr.T, fine_coef, mid_leaf,
         first_filters, rows_both,
     )
     arrived = lax.all_to_all(payload, ("gy", "gz"), 0, 0, tiled=True)
@@ -596,19 +621,27 @@
 
     w_tables, x_tables, centre = call(
         tables_kernel,
-        "vvvv",
+        "hhhv",
         [
-            pltpu.VMEM((3 * QUADS, ROWS_W, 256), BF16),
+            pltpu.HBM((3 * QUADS, 576, 256), BF16),
             pltpu.VMEM((3, 256, 24), BF16),
             pltpu.VMEM((90, 8, 128), F32),
         ],
-        [vmem((2, 24, 24, 256), F32)],
+        [
+            vmem((2, 24, 24, 256), F32),
+            vmem((3, 192, TERMS), F32),
+            vmem((1, TERMS), F32),
+            vmem((256, 768), BF16),
+            pltpu.SemaphoreType.DMA((3,)),
+            vmem((3 * QUADS, 576, 256), BF16),
+            pltpu.SemaphoreType.DMA((3,)),
+        ],
         600_000_000,
         factors, term_weight.reshape(1, TERMS), select, sheet,
     )
     fine_out, mid_out = call(
         last_kernel,
-        "svvvvvvvvv",
+        "svwvvhwhhh",
         [sds((8, 512), F32), sds((1, 512), F32)],
         [
             vmem((GONE + 9, 8, 128), F32),
@@ -618,6 +651,12 @@
             vmem((1, 128), i32),
             smem((1, 128), i32),
             pltpu.SemaphoreType.DMA,
+            vmem((16, 8, 128), F32),
+            vmem((512, 128), BF16),
+            vmem((128, 1024), BF16),
+            pltpu.SemaphoreType.DMA((3,)),
+            vmem((3 * QUADS, 576, 256), BF16),
+            pltpu.SemaphoreType.DMA((3,)),
         ],
         900_000_000,
         numbers, before, centre, after, planes, w_tables, x_tables, rows_p, last_filters, mids,

time: 79.9 us -> 68.5 us (0.86)
  local copies, waits for them, and re-layouts: 17.6 us -> 0.06 us
  Pallas kernels: 11.7 us -> 17 us
  other arithmetic: 0 us -> 1.25 us
    unnamed x38 -> x6, local copies, waits for them, and re-layouts: 17.5 us -> 0.04 us
    pallas_call x4, Pallas kernels: 11.7 us -> 17 us  [call(): pl.pallas_call(kernel, out_shape=outs, in_specs=[specs[kind] for kind in...]
    select_n x0 -> x1, other arithmetic: none -> 1.25 us  [shards(): small = jnp.where(at < 8, jnp.pad(mid_child, ((0, 0), (0, 2))), named)]
  transfers between devices with their start and end apart: 8 -> 8, of which waited for: 1 -> 1; matrix products, arithmetic and copies ran while one was open for 0% -> 0% of each run, Pallas kernels for 4% -> 9%
where the time goes in v3:
time: 68.5 us; the launch traced here: 68.1 us
  starting transfers between devices  40.4 us (59%)
  Pallas kernels  17 us (25%)
  waiting for transfers between devices  7.25 us (11%)
  between operations  2.08 us (3%)
  other arithmetic  1.25 us (2%)
    all_to_all x1, starting transfers between devices, shards(): arrived = lax.all_to_all(payload, ('gy', 'gz'), 0, 0, tiled=True)  18.3 us
    pallas_call x4, Pallas kernels, call(): pl.pallas_call(kernel, out_shape=outs, in_specs=[specs[kind] for kind in...  17 us
    ppermute x3, starting transfers between devices, both_ways(): before = lax.ppermute(x, axis, [(i, i + 1) for i in range(ends)])  10.6 us
    all_to_all x1, waiting for transfers between devices, shards(): arrived = lax.all_to_all(payload, ('gy', 'gz'), 0, 0, tiled=True)  7.23 us
    all_to_all x1, starting transfers between devices, shards(): planes = lax.all_to_all(copies, 'gx', 0, 0, tiled=True)  7.02 us
    ppermute x3, starting transfers between devices, both_ways(): after = lax.ppermute(x, axis, [(i + 1, i) for i in range(ends)])  4.51 us
  transfers between devices with their start and end apart: 8, of which 1 were waited for; matrix products, arithmetic and copies ran while one was open for 0% of the time, Pallas kernels for 9%

profile of v3, /device:TPU:1, one launch (start us, length us, event | category | flops | bytes accessed | tf_op | source)
XLA Modules:
  0.0 68.1 jit_solution(8847475279511572081)
XLA Ops:
  1.9 1.2 %compare_select_fusion.1.small_h = s32[1,10]{1,0:T(1,128)} fusion(s32[1,8]{1,0:T(1,128)} %param.18, s32[]{:T(128)} %bitcast.8, s32[]{:T(128)} %bitcast.7), kind=kLoop, calls=%fused_computation.9 | loop fusion | flops 40 | bytes 80 | tf_op jit(solution)/shard_map/jit(_where)/select_n | solution.py:587
  3.2 2.4 %first_kernel.1 = (bf16[48,128]{1,0:T(8,128)(2,1)S(1)}, bf16[64,8,128]{2,1,0:T(8,128)(2,1)}, s32[16,128]{1,0:T(8,128)S(1)}) custom-call(s32[1,10]{1,0:T(1,128)} %compare_select_fusion.1.small_h, s32[8,27]{1,0:T(8,128)} %fine_h.1, s32[1,27]{1,0:T(1,128)} %mid_h.1, s32[27,64]{1,0:T(8,128)} %bitcast.9, bf16[8,512]{1,0:T(8,128)(2,1)} %coef_h.1, ...), custom_call_target="tpu_custom_call" | custom-call | flops 2000000 | bytes 496372 | tf_op jit(solution)/shard_map/first_kernel/pallas_call | solution.py:545
  5.6 4.0 %collective-permute-start = (bf16[48,128]{1,0:T(8,128)(2,1)S(1)}, bf16[48,128]{1,0:T(8,128)(2,1)S(1)}, u32[]{:S(2)}, u32[]{:S(2)}) collective-permute-start(bf16[48,128]{1,0:T(8,128)(2,1)S(1)} %get-tuple-element.9), channel_id=1, source_target_pairs={{0,1},{1,2},{2,3},{3,4},{4,5},{5,6},{6,7},{8,9},{9,10},{10,11},{11... | collective-permute-start | bytes 36872 | tf_op jit(solution)/shard_map/ppermute | solution.py:560
  9.7 1.3 %collective-permute-start.1 = (bf16[48,128]{1,0:T(8,128)(2,1)S(1)}, bf16[48,128]{1,0:T(8,128)(2,1)S(1)}, u32[]{:S(2)}, u32[]{:S(2)}) collective-permute-start(bf16[48,128]{1,0:T(8,128)(2,1)S(1)} %get-tuple-element.9), channel_id=1, source_target_pairs={{1,0},{2,1},{3,2},{4,3},{5,4},{6,5},{7,6},{9,8},{10,9},{11,10},{12... | collective-permute-start | bytes 36872 | tf_op jit(solution)/shard_map/ppermute | solution.py:561
  11.0 18.3 %all-to-all-start = ((bf16[64,8,128]{2,1,0:T(8,128)(2,1)}), bf16[64,8,128]{2,1,0:T(8,128)(2,1)S(1)}, u32[]{:S(2)}, u32[]{:S(2)}) async-start(bf16[64,8,128]{2,1,0:T(8,128)(2,1)} %get-tuple-element.11), calls=%async_computation | async-start | bytes 262144 | tf_op jit(solution)/shard_map/all_to_all | solution.py:610
  29.3 0.0 collective-permute-done
  29.3 0.0 collective-permute-done.1
  29.3 2.9 %collective-permute-start.2 = (bf16[144,128]{1,0:T(8,128)(2,1)S(1)}, bf16[144,128]{1,0:T(8,128)(2,1)S(1)}, u32[]{:S(2)}, u32[]{:S(2)}) collective-permute-start(bf16[144,128]{1,0:T(8,128)(2,1)S(1)} %constant_dynamic-update-slice_fusion), channel_id=1, source_target_pairs={{0,8},{8,16},{16,24},{24,32},{32,40},{40,48},{48,56},{1,9},{9,17},... | collective-permute-start | bytes 110600 | tf_op jit(solution)/shard_map/ppermute | solution.py:560
  32.3 1.3 %collective-permute-start.3 = (bf16[144,128]{1,0:T(8,128)(2,1)S(1)}, bf16[144,128]{1,0:T(8,128)(2,1)S(1)}, u32[]{:S(2)}, u32[]{:S(2)}) collective-permute-start(bf16[144,128]{1,0:T(8,128)(2,1)S(1)} %constant_dynamic-update-slice_fusion), channel_id=1, source_target_pairs={{8,0},{16,8},{24,16},{32,24},{40,32},{48,40},{56,48},{9,1},{17,9},... | collective-permute-start | bytes 110600 | tf_op jit(solution)/shard_map/ppermute | solution.py:561
  33.6 0.0 collective-permute-done.2
  33.6 7.2 %all-to-all-done.arrived = bf16[64,8,128]{2,1,0:T(8,128)(2,1)S(1)} async-done(((bf16[64,8,128]{2,1,0:T(8,128)(2,1)}), bf16[64,8,128]{2,1,0:T(8,128)(2,1)S(1)}, u32[]{:S(2)}, u32[]{:S(2)}) %all-to-all-start) | async-done | bytes 131104 | tf_op jit(solution)/shard_map/all_to_all | solution.py:610
  40.8 1.2 %plane_kernel.1 = bf16[8,256,128]{2,1,0:T(8,128)(2,1)} custom-call(bf16[64,8,128]{2,1,0:T(8,128)(2,1)S(1)} %all-to-all-done.arrived), custom_call_target="tpu_custom_call" | custom-call | flops 33000000 | bytes 655360 | tf_op jit(solution)/shard_map/plane_kernel/pallas_call | solution.py:545
  42.1 7.0 %all-to-all-start.1 = ((bf16[8,256,128]{2,1,0:T(8,128)(2,1)}), bf16[8,256,128]{2,1,0:T(8,128)(2,1)S(1)}, u32[]{:S(2)}, u32[]{:S(2)}) async-start(bf16[8,256,128]{2,1,0:T(8,128)(2,1)} %plane_kernel.1), calls=%async_computation.1 | async-start | bytes 1048576 | tf_op jit(solution)/shard_map/all_to_all | solution.py:620
  49.1 0.0 collective-permute-done.3
  49.1 1.9 %collective-permute-start.5 = (bf16[432,128]{1,0:T(8,128)(2,1)S(1)}, bf16[432,128]{1,0:T(8,128)(2,1)S(1)}, u32[]{:S(2)}, u32[]{:S(2)}) collective-permute-start(bf16[432,128]{1,0:T(8,128)(2,1)S(1)} %constant_dynamic-update-slice_fusion.3.sheet), channel_id=1, source_target_pairs={{64,0},{128,64},{192,128},{256,192},{320,256},{384,320},{448,384},... | collective-permute-start | bytes 331784 | tf_op jit(solution)/shard_map/ppermute | solution.py:561
  51.1 3.6 %collective-permute-start.4 = (bf16[432,128]{1,0:T(8,128)(2,1)S(1)}, bf16[432,128]{1,0:T(8,128)(2,1)S(1)}, u32[]{:S(2)}, u32[]{:S(2)}) collective-permute-start(bf16[432,128]{1,0:T(8,128)(2,1)S(1)} %constant_dynamic-update-slice_fusion.3.sheet), channel_id=1, source_target_pairs={{0,64},{64,128},{128,192},{192,256},{256,320},{320,384},{384,448},... | collective-permute-start | bytes 331784 | tf_op jit(solution)/shard_map/ppermute | solution.py:560
  54.7 5.0 %tables_kernel.1 = (bf16[24,576,256]{2,1,0:T(8,128)(2,1)}, bf16[3,256,24]{2,1,0:T(8,128)(2,1)S(1)}, f32[90,8,128]{2,1,0:T(8,128)S(1)}) custom-call(f32[3,192,32]{2,1,0:T(8,128)} %bitcast.10, f32[1,32]{1,0:T(1,128)} %bitcast.11, bf16[256,768]{1,0:T(8,128)(2,1)} %constant.16.clone.select_h, bf16[432,128]{1,0:T(8,128)(2,1)S(1)} %constant_dynamic-update-slice_fusion.3.sheet), custom_call_target="tpu_custom_call" | custom-call | flops 600000000 | bytes 8061056 | tf_op jit(solution)/shard_map/tables_kernel/pallas_call | solution.py:545
  59.7 0.0 collective-permute-done.5.right
  59.7 0.0 collective-permute-done.4.left
  59.7 0.0 all-to-all-done.1.planes
  59.7 8.3 %last_kernel.1 = (f32[8,512]{1,0:T(8,128)}, f32[1,512]{1,0:T(1,128)}) custom-call(s32[16,128]{1,0:T(8,128)S(1)} %get-tuple-element.8.numbers, bf16[432,128]{1,0:T(8,128)(2,1)S(1)} %collective-permute-done.4.left, f32[90,8,128]{2,1,0:T(8,128)S(1)} %get-tuple-element.10.centre, bf16[432,128]{1,0:T(8,128)(2,1)S(1)} %collective-permute-done.5.right, ...), custom_call_target="tpu_custom_call" | custom-call | flops 900000000 | bytes 8714240 | tf_op jit(solution)/shard_map/last_kernel/pallas_call | solution.py:545
  (8 shorter events, 0.1 us)
Async XLA Ops:
  5.6 23.7 %collective-permute-start = (bf16[48,128]{1,0:T(8,128)(2,1)S(1)}, bf16[48,128]{1,0:T(8,128)(2,1)S(1)}, u32[]{:S(2)}, u32[]{:S(2)}) collective-permute-start(bf16[48,128]{1,0:T(8,128)(2,1)S(1)} %get-tuple-element.9), channel_id=1, source_target_pairs={{0,1},{1,2},{2,3},{3,4},{4,5},{5,6},{6,7},{8,9},{9,10},{10,11},{11... | collective-permute-start | bytes 36872 | tf_op jit(solution)/shard_map/ppermute | solution.py:560
  9.7 19.7 %collective-permute-start.1 = (bf16[48,128]{1,0:T(8,128)(2,1)S(1)}, bf16[48,128]{1,0:T(8,128)(2,1)S(1)}, u32[]{:S(2)}, u32[]{:S(2)}) collective-permute-start(bf16[48,128]{1,0:T(8,128)(2,1)S(1)} %get-tuple-element.9), channel_id=1, source_target_pairs={{1,0},{2,1},{3,2},{4,3},{5,4},{6,5},{7,6},{9,8},{10,9},{11,10},{12... | collective-permute-start | bytes 36872 | tf_op jit(solution)/shard_map/ppermute | solution.py:561
  11.0 29.9 %all-to-all-start = ((bf16[64,8,128]{2,1,0:T(8,128)(2,1)}), bf16[64,8,128]{2,1,0:T(8,128)(2,1)S(1)}, u32[]{:S(2)}, u32[]{:S(2)}) async-start(bf16[64,8,128]{2,1,0:T(8,128)(2,1)} %get-tuple-element.11), calls=%async_computation | async-start | bytes 262144 | tf_op jit(solution)/shard_map/all_to_all | solution.py:610
  29.3 4.2 %collective-permute-start.2 = (bf16[144,128]{1,0:T(8,128)(2,1)S(1)}, bf16[144,128]{1,0:T(8,128)(2,1)S(1)}, u32[]{:S(2)}, u32[]{:S(2)}) collective-permute-start(bf16[144,128]{1,0:T(8,128)(2,1)S(1)} %constant_dynamic-update-slice_fusion), channel_id=1, source_target_pairs={{0,8},{8,16},{16,24},{24,32},{32,40},{40,48},{48,56},{1,9},{9,17},... | collective-permute-start | bytes 110600 | tf_op jit(solution)/shard_map/ppermute | solution.py:560
  32.3 16.8 %collective-permute-start.3 = (bf16[144,128]{1,0:T(8,128)(2,1)S(1)}, bf16[144,128]{1,0:T(8,128)(2,1)S(1)}, u32[]{:S(2)}, u32[]{:S(2)}) collective-permute-start(bf16[144,128]{1,0:T(8,128)(2,1)S(1)} %constant_dynamic-update-slice_fusion), channel_id=1, source_target_pairs={{8,0},{16,8},{24,16},{32,24},{40,32},{48,40},{56,48},{9,1},{17,9},... | collective-permute-start | bytes 110600 | tf_op jit(solution)/shard_map/ppermute | solution.py:561
  42.1 17.7 %all-to-all-start.1 = ((bf16[8,256,128]{2,1,0:T(8,128)(2,1)}), bf16[8,256,128]{2,1,0:T(8,128)(2,1)S(1)}, u32[]{:S(2)}, u32[]{:S(2)}) async-start(bf16[8,256,128]{2,1,0:T(8,128)(2,1)} %plane_kernel.1), calls=%async_computation.1 | async-start | bytes 1048576 | tf_op jit(solution)/shard_map/all_to_all | solution.py:620
  49.1 10.6 %collective-permute-start.5 = (bf16[432,128]{1,0:T(8,128)(2,1)S(1)}, bf16[432,128]{1,0:T(8,128)(2,1)S(1)}, u32[]{:S(2)}, u32[]{:S(2)}) collective-permute-start(bf16[432,128]{1,0:T(8,128)(2,1)S(1)} %constant_dynamic-update-slice_fusion.3.sheet), channel_id=1, source_target_pairs={{64,0},{128,64},{192,128},{256,192},{320,256},{384,320},{448,384},... | collective-permute-start | bytes 331784 | tf_op jit(solution)/shard_map/ppermute | solution.py:561
  51.1 8.7 %collective-permute-start.4 = (bf16[432,128]{1,0:T(8,128)(2,1)S(1)}, bf16[432,128]{1,0:T(8,128)(2,1)S(1)}, u32[]{:S(2)}, u32[]{:S(2)}) collective-permute-start(bf16[432,128]{1,0:T(8,128)(2,1)S(1)} %constant_dynamic-update-slice_fusion.3.sheet), channel_id=1, source_target_pairs={{0,64},{64,128},{128,192},{192,256},{256,320},{320,384},{384,448},... | collective-permute-start | bytes 331784 | tf_op jit(solution)/shard_map/ppermute | solution.py:560

commit v4 on v3

--- a/solution.py
+++ b/solution.py
@@ -267,9 +267,9 @@
 
 
 def first_kernel(
-    small_h, fine_h, mid_h, coarse_h, coef_h, leaf_h, filters_h, rows_h,
+    parent, refined, child_h, fine_h, mid_h, coarse_h, coef_h, leaf_h, filters_h, rows_h,
     halo, payload, numbers,
-    small, small_v, fine_nbr, mid_nbr, coarse_nbr, coef, leaf, filters, rows,
+    child, child_v, fine_nbr, mid_nbr, coarse_nbr, coef, leaf, filters, rows,
     source, detail, sems,
 ):
     copies = fetches(
@@ -277,9 +277,9 @@
         (coef_h, coef),
         (filters_h, filters),
         (rows_h, rows),
-        (small_h, small),
+        (child_h, child),
         (leaf_h, leaf),
-        (small_h, small_v),
+        (child_h, child_v),
         (fine_h, fine_nbr),
         (mid_h, mid_nbr),
         (coarse_h, coarse_nbr),
@@ -288,8 +288,8 @@
         copy.wait()
     comp = filters[0:256, :]
     prol = jnp.concatenate([filters[256 + 64 * k : 320 + 64 * k, :] for k in range(4)], axis=1)
-    slot = small[0, 8] >> 3
-    octant = small[0, 8] & 7
+    slot = parent[0] >> 3
+    octant = parent[0] & 7
     near = fine_nbr[...]
     own = near[:, 13:14] >> 3
     cell = local_cell(near >> 3, own) * 10 + (near & 7)
@@ -307,12 +307,14 @@
     )[0:1].astype(jnp.int32)
     numbers[9:10, 0:27] = jnp.where(near_coarse >= 0, near_coarse, 64)
     numbers[9:10, 27:28] = jnp.full((1, 1), 64, jnp.int32)
-    numbers[10:11, 0:10] = small_v[...]
+    numbers[10:11, 0:8] = child_v[...]
+    numbers[10:11, 8:9] = jnp.full((1, 1), parent[0], jnp.int32)
+    numbers[10:11, 9:10] = jnp.full((1, 1), refined[0], jnp.int32)
 
     values = coef[...].astype(F32)
     for a in range(8):
         source[:, a, :] = values[:, a * PLANE : (a + 1) * PLANE]
-    tiles = [source[small[0, o]] for o in range(8)]
+    tiles = [source[child[0, o]] for o in range(8)]
     lhs = jnp.concatenate(
         [jnp.concatenate(tiles[0:4], axis=1), jnp.concatenate(tiles[4:8], axis=1)], axis=0
     ).astype(BF16)
@@ -326,7 +328,7 @@
     leaf_tile = jnp.concatenate(
         [leaf_row[:, a * PLANE : (a + 1) * PLANE] for a in range(8)], axis=0
     )
-    middle = jnp.where(small[0, 9] > 0, compressed, leaf_tile).astype(BF16).astype(F32)
+    middle = jnp.where(refined[0] > 0, compressed, leaf_tile).astype(BF16).astype(F32)
 
     row_at = (octant >> 2) * 8
     inner = row_mix([rows[row_at + x, :, :PLANE] for x in range(8)], middle)
@@ -337,13 +339,13 @@
     tile = jnp.where(low8, jnp.concatenate([added, added], axis=1), tag).astype(BF16)
     payload[...] = jnp.broadcast_to(tile[None], payload.shape)
 
-    live = jnp.full((8, PLANE), small[0, 9], jnp.int32).astype(F32)
+    live = jnp.full((8, PLANE), refined[0], jnp.int32).astype(F32)
     upper = jnp.concatenate(two_row_mixes(rows.at[16:32], middle, PLANE), axis=0)
     spread = fine_dot(upper, prol)
     for o in range(8):
         i, jl = o // 4, o % 4
         part = spread[i * 8 : i * 8 + 8, jl * PLANE : (jl + 1) * PLANE]
-        detail[small[0, o]] = live * (tiles[o] - part)
+        detail[child[0, o]] = live * (tiles[o] - part)
     for group in range(2):
         base = group * 4
         halo[group * 16 : group * 16 + 16, :] = jnp.concatenate(
@@ -384,15 +386,12 @@
     return jnp.where(low_lanes((8, 128)), first, second)
 
 
-def last_kernel(
-    numbers, left, centre, right, planes, w_hbm, x_ref, rows_h, filters_h, mids_h,
-    fine_out, mid_out,
-    table, mixed, coarse, back, names_v, names_s, sem, rows_p, filters, mids, sems,
-    w_ref, w_sems,
+def fine_kernel(
+    numbers, left, centre, right, w_hbm, x_ref,
+    direct, mid_tiles, names_ref,
+    table, mixed, w_ref, sems,
 ):
-    levels = [pl.ds(level * QUADS, QUADS) for level in range(3)]
-    w_copies = fetches(w_sems, *((w_hbm.at[some], w_ref.at[some]) for some in levels))
-    copies = fetches(sems, (rows_h, rows_p), (filters_h, filters), (mids_h, mids))
+    copies = fetches(sems, (w_hbm.at[pl.ds(0, QUADS)], w_ref))
     lanes = lax.broadcasted_iota(jnp.int32, (1, 128), 1)
     low8 = low_lanes((8, 128))
     table[GONE] = jnp.zeros((8, 128), F32)
@@ -408,9 +407,9 @@
         other = turned(meta)
         name = jnp.where(low8[0:1], meta * 8.0 + other, other * 8.0 + meta).astype(jnp.int32)
         names = jnp.where(lanes == cell, name, names)
-    names_v[...] = names
-    fetch = pltpu.make_async_copy(names_v, names_s, sem)
-    fetch.start()
+    names_ref[...] = names
+    for cell in range(28):
+        mid_tiles[cell] = table[cell * 10 + 8]
 
     def source(t, ex, e):
         if e > 8:
@@ -438,12 +437,28 @@
             )
             row = term * PLANE + pair * 16
             mixed[quad, row : row + 16, :] = tile.astype(BF16)
-    w_copies[0].wait()
+    for copy in copies:
+        copy.wait()
     result = None
     for quad in range(QUADS):
         part = dot(mixed[quad, :, :576], w_ref[quad])
         result = part if result is None else result + part
-    direct = diagonal_sum(result, PLANE)
+    direct[...] = diagonal_sum(result, PLANE).reshape(8, 8, PLANE)
+
+
+def last_kernel(
+    numbers, names, planes, mid_tiles, direct, w_hbm, x_ref, rows_h, filters_h, mids_h,
+    fine_out, mid_out,
+    coarse, back, rows_p, filters, mids, sems, w_ref, w_sems,
+):
+    levels = [pl.ds((level + 1) * QUADS, QUADS) for level in range(2)]
+    homes = [pl.ds(level * QUADS, QUADS) for level in range(2)]
+    copies = fetches(sems, (rows_h, rows_p), (filters_h, filters), (mids_h, mids))
+    w_copies = fetches(
+        w_sems,
+        *((w_hbm.at[levels[level]], w_ref.at[homes[level]]) for level in range(2)),
+    )
+    low8 = low_lanes((8, 128))
 
     total = None
     for plane in range(8):
@@ -473,10 +488,9 @@
         ],
         axis=1,
     )
-    w_copies[2].wait()
-    coarse_result = apply_one(sources, x_ref[2], w_ref.at[16:24])
-
-    fetch.wait()
+    w_copies[1].wait()
+    coarse_result = apply_one(sources, x_ref[2], w_ref.at[8:16])
+
     for copy in copies:
         copy.wait()
     uppers, octants, owns = [], [], []
@@ -484,8 +498,8 @@
         for ex in range(3):
             first = numbers[8, ex * 9 + 2 * ep]
             second = numbers[8, ex * 9 + 2 * ep + 1 if ep < 4 else 27]
-            name_1, name_2 = names_s[0, first], names_s[0, second]
-            owns.append(pair_of(table[first * 10 + 8], table[second * 10 + 8]))
+            name_1, name_2 = names[0, first], names[0, second]
+            owns.append(pair_of(mid_tiles[first], mid_tiles[second]))
             both = pair_of(coarse[name_1 >> 3], coarse[name_2 >> 3])
             named = jnp.where(low8, name_1 & 7, name_2 & 7)
             octants.append(named)
@@ -508,8 +522,8 @@
                 )
             tiles.append(owns[at] - chosen)
         pieces.append(jnp.concatenate(tiles, axis=0).astype(BF16))
-    w_copies[1].wait()
-    mid_result = apply_one(jnp.concatenate(pieces, axis=1), x_ref[1], w_ref.at[8:16])
+    w_copies[0].wait()
+    mid_result = apply_one(jnp.concatenate(pieces, axis=1), x_ref[1], w_ref.at[0:8])
 
     row_at = (octant >> 2) * 8
     upper = row_mix([rows_p[row_at + p, :, :PLANE] for p in range(8)], coarse_result)
@@ -521,13 +535,11 @@
     upper = jnp.concatenate(two_row_mixes(rows_p, middle, PLANE), axis=0)
     prol = jnp.concatenate([filters[64 * k : 64 * k + 64, :] for k in range(4)], axis=1)
     spread = fine_dot(upper, prol)
-    for t in range(8):
-        back[t] = direct[t * 8 : t * 8 + 8, :]
     for o in range(8):
         i, jl = o // 4, o % 4
         slot = numbers[10, o]
         part = spread[i * 8 : i * 8 + 8, jl * PLANE : (jl + 1) * PLANE]
-        back[slot] = live * (back[slot] + part)
+        back[slot] = live * (direct[slot] + part)
     for a in range(8):
         fine_out[:, a * PLANE : (a + 1) * PLANE] = back[:, a, :]
 
@@ -582,16 +594,13 @@
     sds = jax.ShapeDtypeStruct
     vmem, smem = pltpu.VMEM, pltpu.SMEM
     i32 = jnp.int32
-    at = lax.broadcasted_iota(jnp.int32, (1, 10), 1)
-    named = jnp.where(at == 8, jnp.broadcast_to(mid_parent, (1, 10)), jnp.broadcast_to(mid_refined, (1, 10)))
-    small = jnp.where(at < 8, jnp.pad(mid_child, ((0, 0), (0, 2))), named)
     halo, payload, numbers = call(
         first_kernel,
-        "hhhhhhhh",
+        "sshhhhhhhh",
         [sds((48, 128), BF16), sds((64, 8, 128), BF16), sds((16, 128), i32)],
         [
-            smem((1, 10), i32),
-            vmem((1, 10), i32),
+            smem((1, 8), i32),
+            vmem((1, 8), i32),
             vmem((8, 27), i32),
             vmem((1, 27), i32),
             vmem((27, 64), i32),
@@ -604,7 +613,7 @@
             pltpu.SemaphoreType.DMA((9,)),
         ],
         2_000_000,
-        small, fine_nbr, mid_nbr, coarse_nbr.T, fine_coef, mid_leaf,
+        mid_parent, mid_refined, mid_child, fine_nbr, mid_nbr, coarse_nbr.T, fine_coef, mid_leaf,
         first_filters, rows_both,
     )
     arrived = lax.all_to_all(payload, ("gy", "gz"), 0, 0, tiled=True)
@@ -639,27 +648,36 @@
         600_000_000,
         factors, term_weight.reshape(1, TERMS), select, sheet,
     )
-    fine_out, mid_out = call(
-        last_kernel,
-        "svwvvhwhhh",
-        [sds((8, 512), F32), sds((1, 512), F32)],
+    direct, mid_tiles, names = call(
+        fine_kernel,
+        "svvvhw",
+        [sds((8, 8, PLANE), F32), sds((28, 8, 128), F32), sds((1, 128), i32)],
         [
             vmem((GONE + 9, 8, 128), F32),
             vmem((QUADS, 256, ROWS_W), BF16),
+            vmem((QUADS, 576, 256), BF16),
+            pltpu.SemaphoreType.DMA((1,)),
+        ],
+        100_000_000,
+        numbers, before, centre, after, w_tables, x_tables,
+    )
+    fine_out, mid_out = call(
+        last_kernel,
+        "ssvvvhwhhh",
+        [sds((8, 512), F32), sds((1, 512), F32)],
+        [
             vmem((65, 8, 128), F32),
             vmem((8, 8, PLANE), F32),
-            vmem((1, 128), i32),
-            smem((1, 128), i32),
-            pltpu.SemaphoreType.DMA,
             vmem((16, 8, 128), F32),
             vmem((512, 128), BF16),
             vmem((128, 1024), BF16),
             pltpu.SemaphoreType.DMA((3,)),
-            vmem((3 * QUADS, 576, 256), BF16),
-            pltpu.SemaphoreType.DMA((3,)),
+            vmem((2 * QUADS, 576, 256), BF16),
+            pltpu.SemaphoreType.DMA((2,)),
         ],
-        900_000_000,
-        numbers, before, centre, after, planes, w_tables, x_tables, rows_p, last_filters, mids,
+        200_000_000,
+        numbers, names, planes, mid_tiles, direct, w_tables, x_tables,
+        rows_p, last_filters, mids,
     )
     return fine_out, mid_out
 

time: 68.5 us -> 70.5 us (1.029)
  Pallas kernels: 17 us -> 20.3 us
  other arithmetic: 1.25 us -> 0 us
    pallas_call x4 -> x5, Pallas kernels: 17 us -> 20.3 us  [call(): pl.pallas_call(kernel, out_shape=outs, in_specs=[specs[kind] for kind in...]
    select_n x1 -> x0, other arithmetic: 1.25 us -> none  [shards(): small = jnp.where(at < 8, jnp.pad(mid_child, ((0, 0), (0, 2))), named)]
  transfers between devices with their start and end apart: 8 -> 8, of which waited for: 1 -> 1; matrix products, arithmetic and copies ran while one was open for 0% -> 0% of each run, Pallas kernels for 9% -> 16%
where the time goes in v4:
time: 70.5 us; the launch traced here: 70 us
  starting transfers between devices  40.3 us (57%)
  Pallas kernels  20.3 us (29%)
  waiting for transfers between devices  7.25 us (10%)
  between operations  2.09 us (3%)
    pallas_call x5, Pallas kernels, call(): pl.pallas_call(kernel, out_shape=outs, in_specs=[specs[kind] for kind in...  20.3 us
    all_to_all x1, starting transfers between devices, shards(): arrived = lax.all_to_all(payload, ('gy', 'gz'), 0, 0, tiled=True)  18.3 us
    ppermute x3, starting transfers between devices, both_ways(): before = lax.ppermute(x, axis, [(i, i + 1) for i in range(ends)])  10.5 us
    all_to_all x1, waiting for transfers between devices, shards(): arrived = lax.all_to_all(payload, ('gy', 'gz'), 0, 0, tiled=True)  7.24 us
    all_to_all x1, starting transfers between devices, shards(): planes = lax.all_to_all(copies, 'gx', 0, 0, tiled=True)  7.02 us
    ppermute x3, starting transfers between devices, both_ways(): after = lax.ppermute(x, axis, [(i + 1, i) for i in range(ends)])  4.5 us
  transfers between devices with their start and end apart: 8, of which 1 were waited for; matrix products, arithmetic and copies ran while one was open for 0% of the time, Pallas kernels for 16%

profile of v4, /device:TPU:1, one launch (start us, length us, event | category | flops | bytes accessed | tf_op | source)
XLA Modules:
  0.0 70.0 jit_solution(473186993288105481)
XLA Ops:
  1.9 2.5 %first_kernel.1 = (bf16[48,128]{1,0:T(8,128)(2,1)S(1)}, bf16[64,8,128]{2,1,0:T(8,128)(2,1)}, s32[16,128]{1,0:T(8,128)S(1)}) custom-call(s32[1]{0:T(128)S(6)} %copy.24.parent, s32[1]{0:T(128)S(6)} %copy.25.refined, s32[1,8]{1,0:T(1,128)} %child_h.1, s32[8,27]{1,0:T(8,128)} %fine_h.1, s32[1,27]{1,0:T(1,128)} %mid_h.1, s32[27,64]{1,0:T(8,128)} %bitcast.5, ...), custom_call_target="tpu_custom_call" | custom-call | flops 2000000 | bytes 496372 | tf_op jit(solution)/shard_map/first_kernel/pallas_call | solution.py:557
  4.4 4.0 %collective-permute-start = (bf16[48,128]{1,0:T(8,128)(2,1)S(1)}, bf16[48,128]{1,0:T(8,128)(2,1)S(1)}, u32[]{:S(2)}, u32[]{:S(2)}) collective-permute-start(bf16[48,128]{1,0:T(8,128)(2,1)S(1)} %get-tuple-element.12), channel_id=1, source_target_pairs={{0,1},{1,2},{2,3},{3,4},{4,5},{5,6},{6,7},{8,9},{9,10},{10,11},{11... | collective-permute-start | bytes 36872 | tf_op jit(solution)/shard_map/ppermute | solution.py:572
  8.4 1.3 %collective-permute-start.1 = (bf16[48,128]{1,0:T(8,128)(2,1)S(1)}, bf16[48,128]{1,0:T(8,128)(2,1)S(1)}, u32[]{:S(2)}, u32[]{:S(2)}) collective-permute-start(bf16[48,128]{1,0:T(8,128)(2,1)S(1)} %get-tuple-element.12), channel_id=1, source_target_pairs={{1,0},{2,1},{3,2},{4,3},{5,4},{6,5},{7,6},{9,8},{10,9},{11,10},{12... | collective-permute-start | bytes 36872 | tf_op jit(solution)/shard_map/ppermute | solution.py:573
  9.7 18.3 %all-to-all-start = ((bf16[64,8,128]{2,1,0:T(8,128)(2,1)}), bf16[64,8,128]{2,1,0:T(8,128)(2,1)S(1)}, u32[]{:S(2)}, u32[]{:S(2)}) async-start(bf16[64,8,128]{2,1,0:T(8,128)(2,1)} %get-tuple-element.17), calls=%async_computation | async-start | bytes 262144 | tf_op jit(solution)/shard_map/all_to_all | solution.py:619
  28.1 0.0 collective-permute-done
  28.1 0.0 collective-permute-done.1
  28.1 2.9 %collective-permute-start.2 = (bf16[144,128]{1,0:T(8,128)(2,1)S(1)}, bf16[144,128]{1,0:T(8,128)(2,1)S(1)}, u32[]{:S(2)}, u32[]{:S(2)}) collective-permute-start(bf16[144,128]{1,0:T(8,128)(2,1)S(1)} %constant_dynamic-update-slice_fusion), channel_id=1, source_target_pairs={{0,8},{8,16},{16,24},{24,32},{32,40},{40,48},{48,56},{1,9},{9,17},... | collective-permute-start | bytes 110600 | tf_op jit(solution)/shard_map/ppermute | solution.py:572
  31.0 1.3 %collective-permute-start.3 = (bf16[144,128]{1,0:T(8,128)(2,1)S(1)}, bf16[144,128]{1,0:T(8,128)(2,1)S(1)}, u32[]{:S(2)}, u32[]{:S(2)}) collective-permute-start(bf16[144,128]{1,0:T(8,128)(2,1)S(1)} %constant_dynamic-update-slice_fusion), channel_id=1, source_target_pairs={{8,0},{16,8},{24,16},{32,24},{40,32},{48,40},{56,48},{9,1},{17,9},... | collective-permute-start | bytes 110600 | tf_op jit(solution)/shard_map/ppermute | solution.py:573
  32.3 0.0 collective-permute-done.2
  32.4 7.2 %all-to-all-done.arrived = bf16[64,8,128]{2,1,0:T(8,128)(2,1)S(1)} async-done(((bf16[64,8,128]{2,1,0:T(8,128)(2,1)}), bf16[64,8,128]{2,1,0:T(8,128)(2,1)S(1)}, u32[]{:S(2)}, u32[]{:S(2)}) %all-to-all-start) | async-done | bytes 131104 | tf_op jit(solution)/shard_map/all_to_all | solution.py:619
  39.6 1.2 %plane_kernel.1 = bf16[8,256,128]{2,1,0:T(8,128)(2,1)} custom-call(bf16[64,8,128]{2,1,0:T(8,128)(2,1)S(1)} %all-to-all-done.arrived), custom_call_target="tpu_custom_call" | custom-call | flops 33000000 | bytes 655360 | tf_op jit(solution)/shard_map/plane_kernel/pallas_call | solution.py:557
  40.8 7.0 %all-to-all-start.1 = ((bf16[8,256,128]{2,1,0:T(8,128)(2,1)}), bf16[8,256,128]{2,1,0:T(8,128)(2,1)S(1)}, u32[]{:S(2)}, u32[]{:S(2)}) async-start(bf16[8,256,128]{2,1,0:T(8,128)(2,1)} %plane_kernel.1), calls=%async_computation.1 | async-start | bytes 1048576 | tf_op jit(solution)/shard_map/all_to_all | solution.py:629
  47.9 0.0 collective-permute-done.3
  47.9 3.5 %collective-permute-start.4 = (bf16[432,128]{1,0:T(8,128)(2,1)S(1)}, bf16[432,128]{1,0:T(8,128)(2,1)S(1)}, u32[]{:S(2)}, u32[]{:S(2)}) collective-permute-start(bf16[432,128]{1,0:T(8,128)(2,1)S(1)} %constant_dynamic-update-slice_fusion.3.sheet), channel_id=1, source_target_pairs={{0,64},{64,128},{128,192},{192,256},{256,320},{320,384},{384,448},... | collective-permute-start | bytes 331784 | tf_op jit(solution)/shard_map/ppermute | solution.py:572
  51.5 1.9 %collective-permute-start.5 = (bf16[432,128]{1,0:T(8,128)(2,1)S(1)}, bf16[432,128]{1,0:T(8,128)(2,1)S(1)}, u32[]{:S(2)}, u32[]{:S(2)}) collective-permute-start(bf16[432,128]{1,0:T(8,128)(2,1)S(1)} %constant_dynamic-update-slice_fusion.3.sheet), channel_id=1, source_target_pairs={{64,0},{128,64},{192,128},{256,192},{320,256},{384,320},{448,384},... | collective-permute-start | bytes 331784 | tf_op jit(solution)/shard_map/ppermute | solution.py:573
  53.4 5.0 %tables_kernel.1 = (bf16[24,576,256]{2,1,0:T(8,128)(2,1)}, bf16[3,256,24]{2,1,0:T(8,128)(2,1)S(1)}, f32[90,8,128]{2,1,0:T(8,128)S(1)}) custom-call(f32[3,192,32]{2,1,0:T(8,128)} %bitcast.6, f32[1,32]{1,0:T(1,128)} %bitcast.7, bf16[256,768]{1,0:T(8,128)(2,1)} %constant.12.clone.select_h, bf16[432,128]{1,0:T(8,128)(2,1)S(1)} %constant_dynamic-update-slice_fusion.3.sheet), custom_call_target="tpu_custom_call" | custom-call | flops 600000000 | bytes 8061056 | tf_op jit(solution)/shard_map/tables_kernel/pallas_call | solution.py:557
  58.4 0.0 collective-permute-done.4.left
  58.4 0.0 collective-permute-done.5.right
  58.4 5.2 %fine_kernel.1 = (f32[8,8,64]{2,1,0:T(8,128)S(1)}, f32[28,8,128]{2,1,0:T(8,128)S(1)}, s32[1,128]{1,0:T(1,128)S(1)}) custom-call(s32[16,128]{1,0:T(8,128)S(1)} %get-tuple-element.11.numbers, bf16[432,128]{1,0:T(8,128)(2,1)S(1)} %collective-permute-done.4.left, f32[90,8,128]{2,1,0:T(8,128)S(1)} %get-tuple-element.13.centre, ...), custom_call_target="tpu_custom_call" | custom-call | flops 100000000 | bytes 7844352 | tf_op jit(solution)/shard_map/fine_kernel/pallas_call | solution.py:557
  63.7 0.0 all-to-all-done.1.planes
  63.7 6.4 %last_kernel.1 = (f32[8,512]{1,0:T(8,128)}, f32[1,512]{1,0:T(1,128)}) custom-call(s32[16,128]{1,0:T(8,128)S(1)} %get-tuple-element.11.numbers, s32[1,128]{1,0:T(1,128)S(1)} %get-tuple-element.16.names, bf16[8,256,128]{2,1,0:T(8,128)(2,1)S(1)} %all-to-all-done.1.planes, f32[28,8,128]{2,1,0:T(8,128)S(1)} %get-tuple-element.18.mid_tiles, ...), custom_call_target="tpu_custom_call" | custom-call | flops 200000000 | bytes 8256000 | tf_op jit(solution)/shard_map/last_kernel/pallas_call | solution.py:557
  (8 shorter events, 0.1 us)
Async XLA Ops:
  4.4 23.7 %collective-permute-start = (bf16[48,128]{1,0:T(8,128)(2,1)S(1)}, bf16[48,128]{1,0:T(8,128)(2,1)S(1)}, u32[]{:S(2)}, u32[]{:S(2)}) collective-permute-start(bf16[48,128]{1,0:T(8,128)(2,1)S(1)} %get-tuple-element.12), channel_id=1, source_target_pairs={{0,1},{1,2},{2,3},{3,4},{4,5},{5,6},{6,7},{8,9},{9,10},{10,11},{11... | collective-permute-start | bytes 36872 | tf_op jit(solution)/shard_map/ppermute | solution.py:572
  8.4 19.7 %collective-permute-start.1 = (bf16[48,128]{1,0:T(8,128)(2,1)S(1)}, bf16[48,128]{1,0:T(8,128)(2,1)S(1)}, u32[]{:S(2)}, u32[]{:S(2)}) collective-permute-start(bf16[48,128]{1,0:T(8,128)(2,1)S(1)} %get-tuple-element.12), channel_id=1, source_target_pairs={{1,0},{2,1},{3,2},{4,3},{5,4},{6,5},{7,6},{9,8},{10,9},{11,10},{12... | collective-permute-start | bytes 36872 | tf_op jit(solution)/shard_map/ppermute | solution.py:573
  9.7 29.9 %all-to-all-start = ((bf16[64,8,128]{2,1,0:T(8,128)(2,1)}), bf16[64,8,128]{2,1,0:T(8,128)(2,1)S(1)}, u32[]{:S(2)}, u32[]{:S(2)}) async-start(bf16[64,8,128]{2,1,0:T(8,128)(2,1)} %get-tuple-element.17), calls=%async_computation | async-start | bytes 262144 | tf_op jit(solution)/shard_map/all_to_all | solution.py:619
  28.1 4.2 %collective-permute-start.2 = (bf16[144,128]{1,0:T(8,128)(2,1)S(1)}, bf16[144,128]{1,0:T(8,128)(2,1)S(1)}, u32[]{:S(2)}, u32[]{:S(2)}) collective-permute-start(bf16[144,128]{1,0:T(8,128)(2,1)S(1)} %constant_dynamic-update-slice_fusion), channel_id=1, source_target_pairs={{0,8},{8,16},{16,24},{24,32},{32,40},{40,48},{48,56},{1,9},{9,17},... | collective-permute-start | bytes 110600 | tf_op jit(solution)/shard_map/ppermute | solution.py:572
  31.0 16.8 %collective-permute-start.3 = (bf16[144,128]{1,0:T(8,128)(2,1)S(1)}, bf16[144,128]{1,0:T(8,128)(2,1)S(1)}, u32[]{:S(2)}, u32[]{:S(2)}) collective-permute-start(bf16[144,128]{1,0:T(8,128)(2,1)S(1)} %constant_dynamic-update-slice_fusion), channel_id=1, source_target_pairs={{8,0},{16,8},{24,16},{32,24},{40,32},{48,40},{56,48},{9,1},{17,9},... | collective-permute-start | bytes 110600 | tf_op jit(solution)/shard_map/ppermute | solution.py:573
  40.8 22.8 %all-to-all-start.1 = ((bf16[8,256,128]{2,1,0:T(8,128)(2,1)}), bf16[8,256,128]{2,1,0:T(8,128)(2,1)S(1)}, u32[]{:S(2)}, u32[]{:S(2)}) async-start(bf16[8,256,128]{2,1,0:T(8,128)(2,1)} %plane_kernel.1), calls=%async_computation.1 | async-start | bytes 1048576 | tf_op jit(solution)/shard_map/all_to_all | solution.py:629
  47.9 10.5 %collective-permute-start.4 = (bf16[432,128]{1,0:T(8,128)(2,1)S(1)}, bf16[432,128]{1,0:T(8,128)(2,1)S(1)}, u32[]{:S(2)}, u32[]{:S(2)}) collective-permute-start(bf16[432,128]{1,0:T(8,128)(2,1)S(1)} %constant_dynamic-update-slice_fusion.3.sheet), channel_id=1, source_target_pairs={{0,64},{64,128},{128,192},{192,256},{256,320},{320,384},{384,448},... | collective-permute-start | bytes 331784 | tf_op jit(solution)/shard_map/ppermute | solution.py:572
  51.5 6.9 %collective-permute-start.5 = (bf16[432,128]{1,0:T(8,128)(2,1)S(1)}, bf16[432,128]{1,0:T(8,128)(2,1)S(1)}, u32[]{:S(2)}, u32[]{:S(2)}) collective-permute-start(bf16[432,128]{1,0:T(8,128)(2,1)S(1)} %constant_dynamic-update-slice_fusion.3.sheet), channel_id=1, source_target_pairs={{64,0},{128,64},{192,128},{256,192},{320,256},{384,320},{448,384},... | collective-permute-start | bytes 331784 | tf_op jit(solution)/shard_map/ppermute | solution.py:573

commit v5 on v4

--- a/solution.py
+++ b/solution.py
@@ -172,8 +172,8 @@
 
 def tables_kernel(
     factors_h, weights_h, select_h, sheet,
-    w_hbm, x_ref, tiles,
-    ab_ref, factors, weights, select, sems, w_ref, w_sems,
+    ab_ref, x_ref, tiles,
+    factors, weights, select, sems,
 ):
     copies = fetches(sems, (factors_h, factors), (weights_h, weights), (select_h, select))
     for cell in range(9):
@@ -211,7 +211,10 @@
         )
         ab_ref[which] = (both[:576] + both[576:]).reshape(24, 24, 256)
 
-    def one_quad(at, carry):
+
+def build_w(ab_ref, level, w_ref):
+    def one_quad(quad, carry):
+        at = level * QUADS + quad
         inner = [ab_ref[1, at, ez * 8 : ez * 8 + 8, :] for ez in range(3)]
         for ey in range(3):
             for pair in range(4):
@@ -221,17 +224,10 @@
                 for ez in range(3):
                     tile = jnp.concatenate([first * inner[ez], second * inner[ez]], axis=0)
                     to = (ey * 3 + ez) * PLANE + pair * 16
-                    w_ref[at, to : to + 16, :] = tile.astype(BF16)
+                    w_ref[quad, to : to + 16, :] = tile.astype(BF16)
         return carry
 
-    copies = []
-    for level in range(3):
-        lax.fori_loop(level * QUADS, (level + 1) * QUADS, one_quad, 0)
-        some = pl.ds(level * QUADS, QUADS)
-        copies.append(pltpu.make_async_copy(w_ref.at[some], w_hbm.at[some], w_sems.at[level]))
-        copies[-1].start()
-    for copy in copies:
-        copy.wait()
+    lax.fori_loop(0, QUADS, one_quad, 0)
 
 
 def spread_cell(sheet, cell, tiles, to):
@@ -387,11 +383,11 @@
 
 
 def fine_kernel(
-    numbers, left, centre, right, w_hbm, x_ref,
+    numbers, left, centre, right, ab_ref, x_ref,
     direct, mid_tiles, names_ref,
-    table, mixed, w_ref, sems,
+    table, mixed, w_ref,
 ):
-    copies = fetches(sems, (w_hbm.at[pl.ds(0, QUADS)], w_ref))
+    build_w(ab_ref, 0, w_ref)
     lanes = lax.broadcasted_iota(jnp.int32, (1, 128), 1)
     low8 = low_lanes((8, 128))
     table[GONE] = jnp.zeros((8, 128), F32)
@@ -437,8 +433,6 @@
             )
             row = term * PLANE + pair * 16
             mixed[quad, row : row + 16, :] = tile.astype(BF16)
-    for copy in copies:
-        copy.wait()
     result = None
     for quad in range(QUADS):
         part = dot(mixed[quad, :, :576], w_ref[quad])
@@ -447,17 +441,13 @@
 
 
 def last_kernel(
-    numbers, names, planes, mid_tiles, direct, w_hbm, x_ref, rows_h, filters_h, mids_h,
+    numbers, names, planes, mid_tiles, direct, ab_ref, x_ref, rows_h, filters_h, mids_h,
     fine_out, mid_out,
-    coarse, back, rows_p, filters, mids, sems, w_ref, w_sems,
+    coarse, back, rows_p, filters, mids, sems, w_mid, w_coarse,
 ):
-    levels = [pl.ds((level + 1) * QUADS, QUADS) for level in range(2)]
-    homes = [pl.ds(level * QUADS, QUADS) for level in range(2)]
     copies = fetches(sems, (rows_h, rows_p), (filters_h, filters), (mids_h, mids))
-    w_copies = fetches(
-        w_sems,
-        *((w_hbm.at[levels[level]], w_ref.at[homes[level]]) for level in range(2)),
-    )
+    build_w(ab_ref, 1, w_mid)
+    build_w(ab_ref, 2, w_coarse)
     low8 = low_lanes((8, 128))
 
     total = None
@@ -488,8 +478,7 @@
         ],
         axis=1,
     )
-    w_copies[1].wait()
-    coarse_result = apply_one(sources, x_ref[2], w_ref.at[8:16])
+    coarse_result = apply_one(sources, x_ref[2], w_coarse)
 
     for copy in copies:
         copy.wait()
@@ -522,8 +511,7 @@
                 )
             tiles.append(owns[at] - chosen)
         pieces.append(jnp.concatenate(tiles, axis=0).astype(BF16))
-    w_copies[0].wait()
-    mid_result = apply_one(jnp.concatenate(pieces, axis=1), x_ref[1], w_ref.at[0:8])
+    mid_result = apply_one(jnp.concatenate(pieces, axis=1), x_ref[1], w_mid)
 
     row_at = (octant >> 2) * 8
     upper = row_mix([rows_p[row_at + p, :, :PLANE] for p in range(8)], coarse_result)
@@ -628,42 +616,38 @@
     )
     planes = lax.all_to_all(copies, "gx", 0, 0, tiled=True)
 
-    w_tables, x_tables, centre = call(
+    w_factors, x_tables, centre = call(
         tables_kernel,
         "hhhv",
         [
-            pltpu.HBM((3 * QUADS, 576, 256), BF16),
+            pltpu.VMEM((2, 3 * QUADS, 24, 256), F32),
             pltpu.VMEM((3, 256, 24), BF16),
             pltpu.VMEM((90, 8, 128), F32),
         ],
         [
-            vmem((2, 24, 24, 256), F32),
             vmem((3, 192, TERMS), F32),
             vmem((1, TERMS), F32),
             vmem((256, 768), BF16),
             pltpu.SemaphoreType.DMA((3,)),
-            vmem((3 * QUADS, 576, 256), BF16),
-            pltpu.SemaphoreType.DMA((3,)),
         ],
         600_000_000,
         factors, term_weight.reshape(1, TERMS), select, sheet,
     )
     direct, mid_tiles, names = call(
         fine_kernel,
-        "svvvhw",
+        "svvvww",
         [sds((8, 8, PLANE), F32), sds((28, 8, 128), F32), sds((1, 128), i32)],
         [
             vmem((GONE + 9, 8, 128), F32),
             vmem((QUADS, 256, ROWS_W), BF16),
             vmem((QUADS, 576, 256), BF16),
-            pltpu.SemaphoreType.DMA((1,)),
         ],
         100_000_000,
-        numbers, before, centre, after, w_tables, x_tables,
+        numbers, before, centre, after, w_factors, x_tables,
     )
     fine_out, mid_out = call(
         last_kernel,
-        "ssvvvhwhhh",
+        "ssvvvwwhhh",
         [sds((8, 512), F32), sds((1, 512), F32)],
         [
             vmem((65, 8, 128), F32),
@@ -672,11 +656,11 @@
             vmem((512, 128), BF16),
             vmem((128, 1024), BF16),
             pltpu.SemaphoreType.DMA((3,)),
-            vmem((2 * QUADS, 576, 256), BF16),
-            pltpu.SemaphoreType.DMA((2,)),
+            vmem((QUADS, 576, 256), BF16),
+            vmem((QUADS, 576, 256), BF16),
         ],
         200_000_000,
-        numbers, names, planes, mid_tiles, direct, w_tables, x_tables,
+        numbers, names, planes, mid_tiles, direct, w_factors, x_tables,
         rows_p, last_filters, mids,
     )
     return fine_out, mid_out

time: 70.5 us -> 66.9 us (0.949)
  Pallas kernels: 20.3 us -> 14.1 us
  waiting for transfers between devices: 7.25 us -> 9.89 us
    pallas_call x5, Pallas kernels: 20.3 us -> 14.1 us  [call(): pl.pallas_call(kernel, out_shape=outs, in_specs=[specs[kind] for kind in...]
    ppermute x3, waiting for transfers between devices: 0.01 us -> 2.4 us  [both_ways(): after = lax.ppermute(x, axis, [(i + 1, i) for i in range(ends)])]
  transfers between devices with their start and end apart: 8 -> 8, of which waited for: 1 -> 3; matrix products, arithmetic and copies ran while one was open for 0% -> 0% of each run, Pallas kernels for 16% -> 11%
where the time goes in v5:
time: 66.9 us; the launch traced here: 66.4 us
  starting transfers between devices  40.3 us (60%)
  Pallas kernels  14.1 us (21%)
  waiting for transfers between devices  9.89 us (15%)
  between operations  2.07 us (3%)
    all_to_all x1, starting transfers between devices, shards(): arrived = lax.all_to_all(payload, ('gy', 'gz'), 0, 0, tiled=True)  18.3 us
    pallas_call x5, Pallas kernels, call(): pl.pallas_call(kernel, out_shape=outs, in_specs=[specs[kind] for kind in...  14.1 us
    ppermute x3, starting transfers between devices, both_ways(): before = lax.ppermute(x, axis, [(i, i + 1) for i in range(ends)])  10.5 us
    all_to_all x1, waiting for transfers between devices, shards(): arrived = lax.all_to_all(payload, ('gy', 'gz'), 0, 0, tiled=True)  7.23 us
    all_to_all x1, starting transfers between devices, shards(): planes = lax.all_to_all(copies, 'gx', 0, 0, tiled=True)  7.02 us
    ppermute x3, starting transfers between devices, both_ways(): after = lax.ppermute(x, axis, [(i + 1, i) for i in range(ends)])  4.5 us
    ppermute x3, waiting for transfers between devices, both_ways(): after = lax.ppermute(x, axis, [(i + 1, i) for i in range(ends)])  2.4 us
  transfers between devices with their start and end apart: 8, of which 3 were waited for; matrix products, arithmetic and copies ran while one was open for 0% of the time, Pallas kernels for 11%

profile of v5, /device:TPU:1, one launch (start us, length us, event | category | flops | bytes accessed | tf_op | source)
XLA Modules:
  0.0 66.4 jit_solution(1416750840135211065)
XLA Ops:
  1.9 2.5 %first_kernel.1 = (bf16[48,128]{1,0:T(8,128)(2,1)S(1)}, bf16[64,8,128]{2,1,0:T(8,128)(2,1)}, s32[16,128]{1,0:T(8,128)S(1)}) custom-call(s32[1]{0:T(128)S(6)} %copy.24.parent, s32[1]{0:T(128)S(6)} %copy.25.refined, s32[1,8]{1,0:T(1,128)} %child_h.1, s32[8,27]{1,0:T(8,128)} %fine_h.1, s32[1,27]{1,0:T(1,128)} %mid_h.1, s32[27,64]{1,0:T(8,128)} %bitcast.5, ...), custom_call_target="tpu_custom_call" | custom-call | flops 2000000 | bytes 496372 | tf_op jit(solution)/shard_map/first_kernel/pallas_call | solution.py:545
  4.4 4.0 %collective-permute-start = (bf16[48,128]{1,0:T(8,128)(2,1)S(1)}, bf16[48,128]{1,0:T(8,128)(2,1)S(1)}, u32[]{:S(2)}, u32[]{:S(2)}) collective-permute-start(bf16[48,128]{1,0:T(8,128)(2,1)S(1)} %get-tuple-element.12), channel_id=1, source_target_pairs={{0,1},{1,2},{2,3},{3,4},{4,5},{5,6},{6,7},{8,9},{9,10},{10,11},{11... | collective-permute-start | bytes 36872 | tf_op jit(solution)/shard_map/ppermute | solution.py:560
  8.4 1.3 %collective-permute-start.1 = (bf16[48,128]{1,0:T(8,128)(2,1)S(1)}, bf16[48,128]{1,0:T(8,128)(2,1)S(1)}, u32[]{:S(2)}, u32[]{:S(2)}) collective-permute-start(bf16[48,128]{1,0:T(8,128)(2,1)S(1)} %get-tuple-element.12), channel_id=1, source_target_pairs={{1,0},{2,1},{3,2},{4,3},{5,4},{6,5},{7,6},{9,8},{10,9},{11,10},{12... | collective-permute-start | bytes 36872 | tf_op jit(solution)/shard_map/ppermute | solution.py:561
  9.7 18.3 %all-to-all-start = ((bf16[64,8,128]{2,1,0:T(8,128)(2,1)}), bf16[64,8,128]{2,1,0:T(8,128)(2,1)S(1)}, u32[]{:S(2)}, u32[]{:S(2)}) async-start(bf16[64,8,128]{2,1,0:T(8,128)(2,1)} %get-tuple-element.17), calls=%async_computation | async-start | bytes 262144 | tf_op jit(solution)/shard_map/all_to_all | solution.py:607
  28.1 0.0 collective-permute-done
  28.1 0.0 collective-permute-done.1
  28.1 2.9 %collective-permute-start.2 = (bf16[144,128]{1,0:T(8,128)(2,1)S(1)}, bf16[144,128]{1,0:T(8,128)(2,1)S(1)}, u32[]{:S(2)}, u32[]{:S(2)}) collective-permute-start(bf16[144,128]{1,0:T(8,128)(2,1)S(1)} %constant_dynamic-update-slice_fusion), channel_id=1, source_target_pairs={{0,8},{8,16},{16,24},{24,32},{32,40},{40,48},{48,56},{1,9},{9,17},... | collective-permute-start | bytes 110600 | tf_op jit(solution)/shard_map/ppermute | solution.py:560
  31.0 1.3 %collective-permute-start.3 = (bf16[144,128]{1,0:T(8,128)(2,1)S(1)}, bf16[144,128]{1,0:T(8,128)(2,1)S(1)}, u32[]{:S(2)}, u32[]{:S(2)}) collective-permute-start(bf16[144,128]{1,0:T(8,128)(2,1)S(1)} %constant_dynamic-update-slice_fusion), channel_id=1, source_target_pairs={{8,0},{16,8},{24,16},{32,24},{40,32},{48,40},{56,48},{9,1},{17,9},... | collective-permute-start | bytes 110600 | tf_op jit(solution)/shard_map/ppermute | solution.py:561
  32.3 0.0 collective-permute-done.2
  32.4 7.2 %all-to-all-done.arrived = bf16[64,8,128]{2,1,0:T(8,128)(2,1)S(1)} async-done(((bf16[64,8,128]{2,1,0:T(8,128)(2,1)}), bf16[64,8,128]{2,1,0:T(8,128)(2,1)S(1)}, u32[]{:S(2)}, u32[]{:S(2)}) %all-to-all-start) | async-done | bytes 131104 | tf_op jit(solution)/shard_map/all_to_all | solution.py:607
  39.6 1.2 %plane_kernel.1 = bf16[8,256,128]{2,1,0:T(8,128)(2,1)} custom-call(bf16[64,8,128]{2,1,0:T(8,128)(2,1)S(1)} %all-to-all-done.arrived), custom_call_target="tpu_custom_call" | custom-call | flops 33000000 | bytes 655360 | tf_op jit(solution)/shard_map/plane_kernel/pallas_call | solution.py:545
  40.8 7.0 %all-to-all-start.1 = ((bf16[8,256,128]{2,1,0:T(8,128)(2,1)}), bf16[8,256,128]{2,1,0:T(8,128)(2,1)S(1)}, u32[]{:S(2)}, u32[]{:S(2)}) async-start(bf16[8,256,128]{2,1,0:T(8,128)(2,1)} %plane_kernel.1), calls=%async_computation.1 | async-start | bytes 1048576 | tf_op jit(solution)/shard_map/all_to_all | solution.py:617
  47.9 0.0 collective-permute-done.3
  47.9 3.5 %collective-permute-start.4 = (bf16[432,128]{1,0:T(8,128)(2,1)S(1)}, bf16[432,128]{1,0:T(8,128)(2,1)S(1)}, u32[]{:S(2)}, u32[]{:S(2)}) collective-permute-start(bf16[432,128]{1,0:T(8,128)(2,1)S(1)} %constant_dynamic-update-slice_fusion.3.sheet), channel_id=1, source_target_pairs={{0,64},{64,128},{128,192},{192,256},{256,320},{320,384},{384,448},... | collective-permute-start | bytes 331784 | tf_op jit(solution)/shard_map/ppermute | solution.py:560
  51.5 1.9 %collective-permute-start.5 = (bf16[432,128]{1,0:T(8,128)(2,1)S(1)}, bf16[432,128]{1,0:T(8,128)(2,1)S(1)}, u32[]{:S(2)}, u32[]{:S(2)}) collective-permute-start(bf16[432,128]{1,0:T(8,128)(2,1)S(1)} %constant_dynamic-update-slice_fusion.3.sheet), channel_id=1, source_target_pairs={{64,0},{128,64},{192,128},{256,192},{320,256},{384,320},{448,384},... | collective-permute-start | bytes 331784 | tf_op jit(solution)/shard_map/ppermute | solution.py:561
  53.4 1.8 %tables_kernel.1 = (f32[2,24,24,256]{3,2,1,0:T(8,128)S(1)}, bf16[3,256,24]{2,1,0:T(8,128)(2,1)S(1)}, f32[90,8,128]{2,1,0:T(8,128)S(1)}) custom-call(f32[3,192,32]{2,1,0:T(8,128)} %bitcast.6, f32[1,32]{1,0:T(1,128)} %bitcast.7, bf16[256,768]{1,0:T(8,128)(2,1)} %constant.12.clone.select_h, bf16[432,128]{1,0:T(8,128)(2,1)S(1)} %constant_dynamic-update-slice_fusion.3.sheet), custom_call_target="tpu_custom_call" | custom-call | flops 600000000 | bytes 2162816 | tf_op jit(solution)/shard_map/tables_kernel/pallas_call | solution.py:545
  55.2 0.2 collective-permute-done.4.left
  55.4 2.4 %collective-permute-done.5.right = bf16[432,128]{1,0:T(8,128)(2,1)S(1)} collective-permute-done((bf16[432,128]{1,0:T(8,128)(2,1)S(1)}, bf16[432,128]{1,0:T(8,128)(2,1)S(1)}, u32[]{:S(2)}, u32[]{:S(2)}) %collective-permute-start.5) | collective-permute-done | bytes 110624 | tf_op jit(solution)/shard_map/ppermute | solution.py:561
  57.8 4.0 %fine_kernel.1 = (f32[8,8,64]{2,1,0:T(8,128)S(1)}, f32[28,8,128]{2,1,0:T(8,128)S(1)}, s32[1,128]{1,0:T(1,128)S(1)}) custom-call(s32[16,128]{1,0:T(8,128)S(1)} %get-tuple-element.11.numbers, bf16[432,128]{1,0:T(8,128)(2,1)S(1)} %collective-permute-done.4.left, f32[90,8,128]{2,1,0:T(8,128)S(1)} %get-tuple-element.13.centre, ...), custom_call_target="tpu_custom_call" | custom-call | flops 100000000 | bytes 1946112 | tf_op jit(solution)/shard_map/fine_kernel/pallas_call | solution.py:545
  61.8 0.0 all-to-all-done.1.planes
  61.8 4.6 %last_kernel.1 = (f32[8,512]{1,0:T(8,128)}, f32[1,512]{1,0:T(1,128)}) custom-call(s32[16,128]{1,0:T(8,128)S(1)} %get-tuple-element.11.numbers, s32[1,128]{1,0:T(1,128)S(1)} %get-tuple-element.16.names, bf16[8,256,128]{2,1,0:T(8,128)(2,1)S(1)} %all-to-all-done.1.planes, f32[28,8,128]{2,1,0:T(8,128)S(1)} %get-tuple-element.18.mid_tiles, ...), custom_call_target="tpu_custom_call" | custom-call | flops 200000000 | bytes 2357760 | tf_op jit(solution)/shard_map/last_kernel/pallas_call | solution.py:545
  (8 shorter events, 0.1 us)
Async XLA Ops:
  4.4 23.7 %collective-permute-start = (bf16[48,128]{1,0:T(8,128)(2,1)S(1)}, bf16[48,128]{1,0:T(8,128)(2,1)S(1)}, u32[]{:S(2)}, u32[]{:S(2)}) collective-permute-start(bf16[48,128]{1,0:T(8,128)(2,1)S(1)} %get-tuple-element.12), channel_id=1, source_target_pairs={{0,1},{1,2},{2,3},{3,4},{4,5},{5,6},{6,7},{8,9},{9,10},{10,11},{11... | collective-permute-start | bytes 36872 | tf_op jit(solution)/shard_map/ppermute | solution.py:560
  8.4 19.7 %collective-permute-start.1 = (bf16[48,128]{1,0:T(8,128)(2,1)S(1)}, bf16[48,128]{1,0:T(8,128)(2,1)S(1)}, u32[]{:S(2)}, u32[]{:S(2)}) collective-permute-start(bf16[48,128]{1,0:T(8,128)(2,1)S(1)} %get-tuple-element.12), channel_id=1, source_target_pairs={{1,0},{2,1},{3,2},{4,3},{5,4},{6,5},{7,6},{9,8},{10,9},{11,10},{12... | collective-permute-start | bytes 36872 | tf_op jit(solution)/shard_map/ppermute | solution.py:561
  9.7 29.9 %all-to-all-start = ((bf16[64,8,128]{2,1,0:T(8,128)(2,1)}), bf16[64,8,128]{2,1,0:T(8,128)(2,1)S(1)}, u32[]{:S(2)}, u32[]{:S(2)}) async-start(bf16[64,8,128]{2,1,0:T(8,128)(2,1)} %get-tuple-element.17), calls=%async_computation | async-start | bytes 262144 | tf_op jit(solution)/shard_map/all_to_all | solution.py:607
  28.1 4.2 %collective-permute-start.2 = (bf16[144,128]{1,0:T(8,128)(2,1)S(1)}, bf16[144,128]{1,0:T(8,128)(2,1)S(1)}, u32[]{:S(2)}, u32[]{:S(2)}) collective-permute-start(bf16[144,128]{1,0:T(8,128)(2,1)S(1)} %constant_dynamic-update-slice_fusion), channel_id=1, source_target_pairs={{0,8},{8,16},{16,24},{24,32},{32,40},{40,48},{48,56},{1,9},{9,17},... | collective-permute-start | bytes 110600 | tf_op jit(solution)/shard_map/ppermute | solution.py:560
  31.0 16.8 %collective-permute-start.3 = (bf16[144,128]{1,0:T(8,128)(2,1)S(1)}, bf16[144,128]{1,0:T(8,128)(2,1)S(1)}, u32[]{:S(2)}, u32[]{:S(2)}) collective-permute-start(bf16[144,128]{1,0:T(8,128)(2,1)S(1)} %constant_dynamic-update-slice_fusion), channel_id=1, source_target_pairs={{8,0},{16,8},{24,16},{32,24},{40,32},{48,40},{56,48},{9,1},{17,9},... | collective-permute-start | bytes 110600 | tf_op jit(solution)/shard_map/ppermute | solution.py:561
  40.8 21.0 %all-to-all-start.1 = ((bf16[8,256,128]{2,1,0:T(8,128)(2,1)}), bf16[8,256,128]{2,1,0:T(8,128)(2,1)S(1)}, u32[]{:S(2)}, u32[]{:S(2)}) async-start(bf16[8,256,128]{2,1,0:T(8,128)(2,1)} %plane_kernel.1), calls=%async_computation.1 | async-start | bytes 1048576 | tf_op jit(solution)/shard_map/all_to_all | solution.py:617
  47.9 7.5 %collective-permute-start.4 = (bf16[432,128]{1,0:T(8,128)(2,1)S(1)}, bf16[432,128]{1,0:T(8,128)(2,1)S(1)}, u32[]{:S(2)}, u32[]{:S(2)}) collective-permute-start(bf16[432,128]{1,0:T(8,128)(2,1)S(1)} %constant_dynamic-update-slice_fusion.3.sheet), channel_id=1, source_target_pairs={{0,64},{64,128},{128,192},{192,256},{256,320},{320,384},{384,448},... | collective-permute-start | bytes 331784 | tf_op jit(solution)/shard_map/ppermute | solution.py:560
  51.5 6.4 %collective-permute-start.5 = (bf16[432,128]{1,0:T(8,128)(2,1)S(1)}, bf16[432,128]{1,0:T(8,128)(2,1)S(1)}, u32[]{:S(2)}, u32[]{:S(2)}) collective-permute-start(bf16[432,128]{1,0:T(8,128)(2,1)S(1)} %constant_dynamic-update-slice_fusion.3.sheet), channel_id=1, source_target_pairs={{64,0},{128,64},{192,128},{256,192},{320,256},{384,320},{448,384},... | collective-permute-start | bytes 331784 | tf_op jit(solution)/shard_map/ppermute | solution.py:561

commit v6 on v5

--- a/solution.py
+++ b/solution.py
@@ -14,7 +14,7 @@
 PLANE = 64
 TERMS = 32
 QUADS = 8
-ROWS_W = 640
+ROWS_W = 4608
 GONE = 27 * 10
 BF16 = jnp.bfloat16
 F32 = jnp.float32
@@ -223,8 +223,10 @@
                 second = ab_ref[0, at, row + 1 : row + 2, :]
                 for ez in range(3):
                     tile = jnp.concatenate([first * inner[ez], second * inner[ez]], axis=0)
-                    to = (ey * 3 + ez) * PLANE + pair * 16
-                    w_ref[quad, to : to + 16, :] = tile.astype(BF16)
+                    e = ey * 3 + ez
+                    to = quad * 512 + e * PLANE if e < 8 else 4096 + quad * PLANE
+                    to = pl.multiple_of(to + pair * 16, 16)
+                    w_ref[pl.ds(to, 16), :] = tile.astype(BF16)
         return carry
 
     lax.fori_loop(0, QUADS, one_quad, 0)
@@ -254,11 +256,14 @@
 
 
 def apply_one(sources, x_table, w_ref):
-    mixed = dot(x_table, sources).astype(BF16)
-    result = None
-    for quad in range(QUADS):
-        part = dot(mixed[quad * 32 : quad * 32 + 32, :576], w_ref[quad])
-        result = part if result is None else result + part
+    product = dot(x_table, sources)
+    low = low_lanes((32, 128))
+    groups = [product[quad * 32 : quad * 32 + 32, :] for quad in range(QUADS)]
+    pieces = [group[:, :512].astype(BF16) for group in groups]
+    for quad in range(0, QUADS, 2):
+        both = jnp.where(low, groups[quad][:, 512:], groups[quad + 1][:, 512:])
+        pieces.append(both.astype(BF16))
+    result = dot(jnp.concatenate(pieces, axis=1), w_ref[...])
     return diagonal_sum(result, 8)
 
 
@@ -408,8 +413,6 @@
         mid_tiles[cell] = table[cell * 10 + 8]
 
     def source(t, ex, e):
-        if e > 8:
-            return table[GONE]
         return table[numbers[t, ex * 9 + e]]
 
     for pair in range(4):
@@ -419,25 +422,43 @@
                 pieces.append(
                     jnp.concatenate(
                         [
-                            pair_of(source(t, ex, 2 * ep), source(t, ex, 2 * ep + 1))
+                            pair_of(source(t, ex, 2 * ep), source(t, ex, min(2 * ep + 1, 8)))
                             for ex in range(3)
                         ],
                         axis=0,
                     ).astype(BF16)
                 )
         product = dot(x_ref[0], jnp.concatenate(pieces, axis=1))
-        for n in range(TERMS):
-            quad, term = n // 4, n % 4
-            tile = jnp.concatenate(
-                [product[n * 8 : n * 8 + 8, :640], product[n * 8 : n * 8 + 8, 640:]], axis=0
-            )
+        for term in range(4):
             row = term * PLANE + pair * 16
-            mixed[quad, row : row + 16, :] = tile.astype(BF16)
+            last = None
+            for quad in range(QUADS):
+                at = (quad * 4 + term) * 8
+                tile = jnp.concatenate(
+                    [product[at : at + 8, :512], product[at : at + 8, 640:1152]], axis=0
+                )
+                mixed[row : row + 16, quad * 512 : quad * 512 + 512] = tile.astype(BF16)
+                tile = jnp.concatenate(
+                    [product[at : at + 8, 512:640], product[at : at + 8, 1152:1280]], axis=0
+                )
+                if quad % 2 == 0:
+                    last = tile
+                else:
+                    to = 4096 + quad // 2 * 128
+                    tile = jnp.where(low_lanes((16, 128)), last, tile)
+                    mixed[row : row + 16, to : to + 128] = tile.astype(BF16)
     result = None
-    for quad in range(QUADS):
-        part = dot(mixed[quad, :, :576], w_ref[quad])
-        result = part if result is None else result + part
-    direct[...] = diagonal_sum(result, PLANE).reshape(8, 8, PLANE)
+    for half in range(2):
+        total = None
+        own = slice(half * 128, half * 128 + 128)
+        for part in range(9):
+            some = slice(part * 512, part * 512 + 512)
+            term = dot(mixed[own, some], w_ref[some, own])
+            total = term if total is None else total + term
+        for term in range(2):
+            rows = slice(term * PLANE, term * PLANE + PLANE)
+            result = total[rows, rows] if result is None else result + total[rows, rows]
+    direct[...] = result.reshape(8, 8, PLANE)
 
 
 def last_kernel(
@@ -463,13 +484,13 @@
     octant = numbers[10, 8] & 7
 
     def coarse_source(ex, e):
-        return coarse[numbers[9, ex * 9 + e if e < 9 else 27]]
+        return coarse[numbers[9, ex * 9 + e]]
 
     sources = jnp.concatenate(
         [
             jnp.concatenate(
                 [
-                    pair_of(coarse_source(ex, 2 * ep), coarse_source(ex, 2 * ep + 1))
+                    pair_of(coarse_source(ex, 2 * ep), coarse_source(ex, min(2 * ep + 1, 8)))
                     for ex in range(3)
                 ],
                 axis=0,
@@ -486,7 +507,7 @@
     for ep in range(5):
         for ex in range(3):
             first = numbers[8, ex * 9 + 2 * ep]
-            second = numbers[8, ex * 9 + 2 * ep + 1 if ep < 4 else 27]
+            second = numbers[8, ex * 9 + min(2 * ep + 1, 8)]
             name_1, name_2 = names[0, first], names[0, second]
             owns.append(pair_of(mid_tiles[first], mid_tiles[second]))
             both = pair_of(coarse[name_1 >> 3], coarse[name_2 >> 3])
@@ -639,8 +660,8 @@
         [sds((8, 8, PLANE), F32), sds((28, 8, 128), F32), sds((1, 128), i32)],
         [
             vmem((GONE + 9, 8, 128), F32),
-            vmem((QUADS, 256, ROWS_W), BF16),
-            vmem((QUADS, 576, 256), BF16),
+            vmem((256, ROWS_W), BF16),
+            vmem((ROWS_W, 256), BF16),
         ],
         100_000_000,
         numbers, before, centre, after, w_factors, x_tables,
@@ -656,8 +677,8 @@
             vmem((512, 128), BF16),
             vmem((128, 1024), BF16),
             pltpu.SemaphoreType.DMA((3,)),
-            vmem((QUADS, 576, 256), BF16),
-            vmem((QUADS, 576, 256), BF16),
+            vmem((ROWS_W, 256), BF16),
+            vmem((ROWS_W, 256), BF16),
         ],
         200_000_000,
         numbers, names, planes, mid_tiles, direct, w_factors, x_tables,

time: 66.9 us -> 65.8 us (0.984)
  Pallas kernels: 14.1 us -> 13 us
    pallas_call x5, Pallas kernels: 14.1 us -> 13 us  [call(): pl.pallas_call(kernel, out_shape=outs, in_specs=[specs[kind] for kind in...]
  transfers between devices with their start and end apart: 8 -> 8, of which waited for: 3 -> 3; matrix products, arithmetic and copies ran while one was open for 0% -> 0% of each run, Pallas kernels for 11% -> 9%
where the time goes in v6:
time: 65.8 us; the launch traced here: 65.4 us
  starting transfers between devices  40.3 us (61%)
  Pallas kernels  13 us (20%)
  waiting for transfers between devices  9.89 us (15%)
  between operations  2.07 us (3%)
    all_to_all x1, starting transfers between devices, shards(): arrived = lax.all_to_all(payload, ('gy', 'gz'), 0, 0, tiled=True)  18.3 us
    pallas_call x5, Pallas kernels, call(): pl.pallas_call(kernel, out_shape=outs, in_specs=[specs[kind] for kind in...  13 us
    ppermute x3, starting transfers between devices, both_ways(): before = lax.ppermute(x, axis, [(i, i + 1) for i in range(ends)])  10.5 us
    all_to_all x1, waiting for transfers between devices, shards(): arrived = lax.all_to_all(payload, ('gy', 'gz'), 0, 0, tiled=True)  7.23 us
    all_to_all x1, starting transfers between devices, shards(): planes = lax.all_to_all(copies, 'gx', 0, 0, tiled=True)  7.02 us
    ppermute x3, starting transfers between devices, both_ways(): after = lax.ppermute(x, axis, [(i + 1, i) for i in range(ends)])  4.5 us
    ppermute x3, waiting for transfers between devices, both_ways(): after = lax.ppermute(x, axis, [(i + 1, i) for i in range(ends)])  2.4 us
  transfers between devices with their start and end apart: 8, of which 3 were waited for; matrix products, arithmetic and copies ran while one was open for 0% of the time, Pallas kernels for 9%

profile of v6, /device:TPU:1, one launch (start us, length us, event | category | flops | bytes accessed | tf_op | source)
XLA Modules:
  0.0 65.4 jit_solution(96208447590509068)
XLA Ops:
  1.9 2.5 %first_kernel.1 = (bf16[48,128]{1,0:T(8,128)(2,1)S(1)}, bf16[64,8,128]{2,1,0:T(8,128)(2,1)}, s32[16,128]{1,0:T(8,128)S(1)}) custom-call(s32[1]{0:T(128)S(6)} %copy.24.parent, s32[1]{0:T(128)S(6)} %copy.25.refined, s32[1,8]{1,0:T(1,128)} %child_h.1, s32[8,27]{1,0:T(8,128)} %fine_h.1, s32[1,27]{1,0:T(1,128)} %mid_h.1, s32[27,64]{1,0:T(8,128)} %bitcast.5, ...), custom_call_target="tpu_custom_call" | custom-call | flops 2000000 | bytes 496372 | tf_op jit(solution)/shard_map/first_kernel/pallas_call | solution.py:566
  4.4 4.0 %collective-permute-start = (bf16[48,128]{1,0:T(8,128)(2,1)S(1)}, bf16[48,128]{1,0:T(8,128)(2,1)S(1)}, u32[]{:S(2)}, u32[]{:S(2)}) collective-permute-start(bf16[48,128]{1,0:T(8,128)(2,1)S(1)} %get-tuple-element.12), channel_id=1, source_target_pairs={{0,1},{1,2},{2,3},{3,4},{4,5},{5,6},{6,7},{8,9},{9,10},{10,11},{11... | collective-permute-start | bytes 36872 | tf_op jit(solution)/shard_map/ppermute | solution.py:581
  8.4 1.3 %collective-permute-start.1 = (bf16[48,128]{1,0:T(8,128)(2,1)S(1)}, bf16[48,128]{1,0:T(8,128)(2,1)S(1)}, u32[]{:S(2)}, u32[]{:S(2)}) collective-permute-start(bf16[48,128]{1,0:T(8,128)(2,1)S(1)} %get-tuple-element.12), channel_id=1, source_target_pairs={{1,0},{2,1},{3,2},{4,3},{5,4},{6,5},{7,6},{9,8},{10,9},{11,10},{12... | collective-permute-start | bytes 36872 | tf_op jit(solution)/shard_map/ppermute | solution.py:582
  9.7 18.3 %all-to-all-start = ((bf16[64,8,128]{2,1,0:T(8,128)(2,1)}), bf16[64,8,128]{2,1,0:T(8,128)(2,1)S(1)}, u32[]{:S(2)}, u32[]{:S(2)}) async-start(bf16[64,8,128]{2,1,0:T(8,128)(2,1)} %get-tuple-element.17), calls=%async_computation | async-start | bytes 262144 | tf_op jit(solution)/shard_map/all_to_all | solution.py:628
  28.1 0.0 collective-permute-done
  28.1 0.0 collective-permute-done.1
  28.1 2.9 %collective-permute-start.2 = (bf16[144,128]{1,0:T(8,128)(2,1)S(1)}, bf16[144,128]{1,0:T(8,128)(2,1)S(1)}, u32[]{:S(2)}, u32[]{:S(2)}) collective-permute-start(bf16[144,128]{1,0:T(8,128)(2,1)S(1)} %constant_dynamic-update-slice_fusion), channel_id=1, source_target_pairs={{0,8},{8,16},{16,24},{24,32},{32,40},{40,48},{48,56},{1,9},{9,17},... | collective-permute-start | bytes 110600 | tf_op jit(solution)/shard_map/ppermute | solution.py:581
  31.0 1.3 %collective-permute-start.3 = (bf16[144,128]{1,0:T(8,128)(2,1)S(1)}, bf16[144,128]{1,0:T(8,128)(2,1)S(1)}, u32[]{:S(2)}, u32[]{:S(2)}) collective-permute-start(bf16[144,128]{1,0:T(8,128)(2,1)S(1)} %constant_dynamic-update-slice_fusion), channel_id=1, source_target_pairs={{8,0},{16,8},{24,16},{32,24},{40,32},{48,40},{56,48},{9,1},{17,9},... | collective-permute-start | bytes 110600 | tf_op jit(solution)/shard_map/ppermute | solution.py:582
  32.3 0.0 collective-permute-done.2
  32.4 7.2 %all-to-all-done.arrived = bf16[64,8,128]{2,1,0:T(8,128)(2,1)S(1)} async-done(((bf16[64,8,128]{2,1,0:T(8,128)(2,1)}), bf16[64,8,128]{2,1,0:T(8,128)(2,1)S(1)}, u32[]{:S(2)}, u32[]{:S(2)}) %all-to-all-start) | async-done | bytes 131104 | tf_op jit(solution)/shard_map/all_to_all | solution.py:628
  39.6 1.2 %plane_kernel.1 = bf16[8,256,128]{2,1,0:T(8,128)(2,1)} custom-call(bf16[64,8,128]{2,1,0:T(8,128)(2,1)S(1)} %all-to-all-done.arrived), custom_call_target="tpu_custom_call" | custom-call | flops 33000000 | bytes 655360 | tf_op jit(solution)/shard_map/plane_kernel/pallas_call | solution.py:566
  40.8 7.0 %all-to-all-start.1 = ((bf16[8,256,128]{2,1,0:T(8,128)(2,1)}), bf16[8,256,128]{2,1,0:T(8,128)(2,1)S(1)}, u32[]{:S(2)}, u32[]{:S(2)}) async-start(bf16[8,256,128]{2,1,0:T(8,128)(2,1)} %plane_kernel.1), calls=%async_computation.1 | async-start | bytes 1048576 | tf_op jit(solution)/shard_map/all_to_all | solution.py:638
  47.9 0.0 collective-permute-done.3
  47.9 3.5 %collective-permute-start.4 = (bf16[432,128]{1,0:T(8,128)(2,1)S(1)}, bf16[432,128]{1,0:T(8,128)(2,1)S(1)}, u32[]{:S(2)}, u32[]{:S(2)}) collective-permute-start(bf16[432,128]{1,0:T(8,128)(2,1)S(1)} %constant_dynamic-update-slice_fusion.3.sheet), channel_id=1, source_target_pairs={{0,64},{64,128},{128,192},{192,256},{256,320},{320,384},{384,448},... | collective-permute-start | bytes 331784 | tf_op jit(solution)/shard_map/ppermute | solution.py:581
  51.5 1.9 %collective-permute-start.5 = (bf16[432,128]{1,0:T(8,128)(2,1)S(1)}, bf16[432,128]{1,0:T(8,128)(2,1)S(1)}, u32[]{:S(2)}, u32[]{:S(2)}) collective-permute-start(bf16[432,128]{1,0:T(8,128)(2,1)S(1)} %constant_dynamic-update-slice_fusion.3.sheet), channel_id=1, source_target_pairs={{64,0},{128,64},{192,128},{256,192},{320,256},{384,320},{448,384},... | collective-permute-start | bytes 331784 | tf_op jit(solution)/shard_map/ppermute | solution.py:582
  53.4 1.8 %tables_kernel.1 = (f32[2,24,24,256]{3,2,1,0:T(8,128)S(1)}, bf16[3,256,24]{2,1,0:T(8,128)(2,1)S(1)}, f32[90,8,128]{2,1,0:T(8,128)S(1)}) custom-call(f32[3,192,32]{2,1,0:T(8,128)} %bitcast.6, f32[1,32]{1,0:T(1,128)} %bitcast.7, bf16[256,768]{1,0:T(8,128)(2,1)} %constant.12.clone.select_h, bf16[432,128]{1,0:T(8,128)(2,1)S(1)} %constant_dynamic-update-slice_fusion.3.sheet), custom_call_target="tpu_custom_call" | custom-call | flops 600000000 | bytes 2162816 | tf_op jit(solution)/shard_map/tables_kernel/pallas_call | solution.py:566
  55.2 0.2 collective-permute-done.4.left
  55.4 2.4 %collective-permute-done.5.right = bf16[432,128]{1,0:T(8,128)(2,1)S(1)} collective-permute-done((bf16[432,128]{1,0:T(8,128)(2,1)S(1)}, bf16[432,128]{1,0:T(8,128)(2,1)S(1)}, u32[]{:S(2)}, u32[]{:S(2)}) %collective-permute-start.5) | collective-permute-done | bytes 110624 | tf_op jit(solution)/shard_map/ppermute | solution.py:582
  57.8 2.8 %fine_kernel.1 = (f32[8,8,64]{2,1,0:T(8,128)S(1)}, f32[28,8,128]{2,1,0:T(8,128)S(1)}, s32[1,128]{1,0:T(1,128)S(1)}) custom-call(s32[16,128]{1,0:T(8,128)S(1)} %get-tuple-element.11.numbers, bf16[432,128]{1,0:T(8,128)(2,1)S(1)} %collective-permute-done.4.left, f32[90,8,128]{2,1,0:T(8,128)S(1)} %get-tuple-element.13.centre, ...), custom_call_target="tpu_custom_call" | custom-call | flops 100000000 | bytes 1946112 | tf_op jit(solution)/shard_map/fine_kernel/pallas_call | solution.py:566
  60.6 0.0 all-to-all-done.1.planes
  60.6 4.8 %last_kernel.1 = (f32[8,512]{1,0:T(8,128)}, f32[1,512]{1,0:T(1,128)}) custom-call(s32[16,128]{1,0:T(8,128)S(1)} %get-tuple-element.11.numbers, s32[1,128]{1,0:T(1,128)S(1)} %get-tuple-element.16.names, bf16[8,256,128]{2,1,0:T(8,128)(2,1)S(1)} %all-to-all-done.1.planes, f32[28,8,128]{2,1,0:T(8,128)S(1)} %get-tuple-element.18.mid_tiles, ...), custom_call_target="tpu_custom_call" | custom-call | flops 200000000 | bytes 2357760 | tf_op jit(solution)/shard_map/last_kernel/pallas_call | solution.py:566
  (8 shorter events, 0.1 us)
Async XLA Ops:
  4.4 23.7 %collective-permute-start = (bf16[48,128]{1,0:T(8,128)(2,1)S(1)}, bf16[48,128]{1,0:T(8,128)(2,1)S(1)}, u32[]{:S(2)}, u32[]{:S(2)}) collective-permute-start(bf16[48,128]{1,0:T(8,128)(2,1)S(1)} %get-tuple-element.12), channel_id=1, source_target_pairs={{0,1},{1,2},{2,3},{3,4},{4,5},{5,6},{6,7},{8,9},{9,10},{10,11},{11... | collective-permute-start | bytes 36872 | tf_op jit(solution)/shard_map/ppermute | solution.py:581
  8.4 19.7 %collective-permute-start.1 = (bf16[48,128]{1,0:T(8,128)(2,1)S(1)}, bf16[48,128]{1,0:T(8,128)(2,1)S(1)}, u32[]{:S(2)}, u32[]{:S(2)}) collective-permute-start(bf16[48,128]{1,0:T(8,128)(2,1)S(1)} %get-tuple-element.12), channel_id=1, source_target_pairs={{1,0},{2,1},{3,2},{4,3},{5,4},{6,5},{7,6},{9,8},{10,9},{11,10},{12... | collective-permute-start | bytes 36872 | tf_op jit(solution)/shard_map/ppermute | solution.py:582
  9.7 29.9 %all-to-all-start = ((bf16[64,8,128]{2,1,0:T(8,128)(2,1)}), bf16[64,8,128]{2,1,0:T(8,128)(2,1)S(1)}, u32[]{:S(2)}, u32[]{:S(2)}) async-start(bf16[64,8,128]{2,1,0:T(8,128)(2,1)} %get-tuple-element.17), calls=%async_computation | async-start | bytes 262144 | tf_op jit(solution)/shard_map/all_to_all | solution.py:628
  28.1 4.2 %collective-permute-start.2 = (bf16[144,128]{1,0:T(8,128)(2,1)S(1)}, bf16[144,128]{1,0:T(8,128)(2,1)S(1)}, u32[]{:S(2)}, u32[]{:S(2)}) collective-permute-start(bf16[144,128]{1,0:T(8,128)(2,1)S(1)} %constant_dynamic-update-slice_fusion), channel_id=1, source_target_pairs={{0,8},{8,16},{16,24},{24,32},{32,40},{40,48},{48,56},{1,9},{9,17},... | collective-permute-start | bytes 110600 | tf_op jit(solution)/shard_map/ppermute | solution.py:581
  31.0 16.8 %collective-permute-start.3 = (bf16[144,128]{1,0:T(8,128)(2,1)S(1)}, bf16[144,128]{1,0:T(8,128)(2,1)S(1)}, u32[]{:S(2)}, u32[]{:S(2)}) collective-permute-start(bf16[144,128]{1,0:T(8,128)(2,1)S(1)} %constant_dynamic-update-slice_fusion), channel_id=1, source_target_pairs={{8,0},{16,8},{24,16},{32,24},{40,32},{48,40},{56,48},{9,1},{17,9},... | collective-permute-start | bytes 110600 | tf_op jit(solution)/shard_map/ppermute | solution.py:582
  40.8 19.8 %all-to-all-start.1 = ((bf16[8,256,128]{2,1,0:T(8,128)(2,1)}), bf16[8,256,128]{2,1,0:T(8,128)(2,1)S(1)}, u32[]{:S(2)}, u32[]{:S(2)}) async-start(bf16[8,256,128]{2,1,0:T(8,128)(2,1)} %plane_kernel.1), calls=%async_computation.1 | async-start | bytes 1048576 | tf_op jit(solution)/shard_map/all_to_all | solution.py:638
  47.9 7.5 %collective-permute-start.4 = (bf16[432,128]{1,0:T(8,128)(2,1)S(1)}, bf16[432,128]{1,0:T(8,128)(2,1)S(1)}, u32[]{:S(2)}, u32[]{:S(2)}) collective-permute-start(bf16[432,128]{1,0:T(8,128)(2,1)S(1)} %constant_dynamic-update-slice_fusion.3.sheet), channel_id=1, source_target_pairs={{0,64},{64,128},{128,192},{192,256},{256,320},{320,384},{384,448},... | collective-permute-start | bytes 331784 | tf_op jit(solution)/shard_map/ppermute | solution.py:581
  51.5 6.4 %collective-permute-start.5 = (bf16[432,128]{1,0:T(8,128)(2,1)S(1)}, bf16[432,128]{1,0:T(8,128)(2,1)S(1)}, u32[]{:S(2)}, u32[]{:S(2)}) collective-permute-start(bf16[432,128]{1,0:T(8,128)(2,1)S(1)} %constant_dynamic-update-slice_fusion.3.sheet), channel_id=1, source_target_pairs={{64,0},{128,64},{192,128},{256,192},{320,256},{384,320},{448,384},... | collective-permute-start | bytes 331784 | tf_op jit(solution)/shard_map/ppermute | solution.py:582

commit v7 on v6

--- a/solution.py
+++ b/solution.py
@@ -271,26 +271,80 @@
     parent, refined, child_h, fine_h, mid_h, coarse_h, coef_h, leaf_h, filters_h, rows_h,
     halo, payload, numbers,
     child, child_v, fine_nbr, mid_nbr, coarse_nbr, coef, leaf, filters, rows,
-    source, detail, sems,
+    source, detail, sems, payload_v, payload_sem,
 ):
     copies = fetches(
         sems,
+        (child_h, child),
         (coef_h, coef),
         (filters_h, filters),
         (rows_h, rows),
-        (child_h, child),
         (leaf_h, leaf),
         (child_h, child_v),
         (fine_h, fine_nbr),
         (mid_h, mid_nbr),
         (coarse_h, coarse_nbr),
     )
-    for copy in copies:
+    for copy in copies[:5]:
         copy.wait()
     comp = filters[0:256, :]
     prol = jnp.concatenate([filters[256 + 64 * k : 320 + 64 * k, :] for k in range(4)], axis=1)
     slot = parent[0] >> 3
     octant = parent[0] & 7
+
+    values = coef[...].astype(F32)
+    for a in range(8):
+        source[:, a, :] = values[:, a * PLANE : (a + 1) * PLANE]
+    tiles = [source[child[0, o]] for o in range(8)]
+    lhs = jnp.concatenate(
+        [jnp.concatenate(tiles[0:4], axis=1), jnp.concatenate(tiles[4:8], axis=1)], axis=0
+    ).astype(BF16)
+    both = dot(lhs, comp)
+    partial = both[:, :PLANE] + both[:, PLANE:]
+    compressed = None
+    for k in range(16):
+        term = rows[k, :, :PLANE] * partial[k : k + 1, :]
+        compressed = term if compressed is None else compressed + term
+    leaf_row = leaf[...].astype(F32)
+    leaf_tile = jnp.concatenate(
+        [leaf_row[:, a * PLANE : (a + 1) * PLANE] for a in range(8)], axis=0
+    )
+    middle = jnp.where(refined[0] > 0, compressed, leaf_tile).astype(BF16).astype(F32)
+
+    row_at = (octant >> 2) * 8
+    inner = row_mix([rows[row_at + x, :, :PLANE] for x in range(8)], middle)
+    table = filters[pl.ds(pl.multiple_of(512 + (octant & 3) * 64, 64), 64), :]
+    added = fine_dot(inner, table)
+    low8 = low_lanes((8, 128))
+    tag = jnp.full((8, 128), slot, jnp.int32).astype(F32)
+    tile = jnp.where(low8, jnp.concatenate([added, added], axis=1), tag).astype(BF16)
+    payload_v[...] = jnp.broadcast_to(tile[None], payload_v.shape)
+    send = pltpu.make_async_copy(payload_v, payload, payload_sem)
+    send.start()
+
+    live = jnp.full((8, PLANE), refined[0], jnp.int32).astype(F32)
+    upper = jnp.concatenate(two_row_mixes(rows.at[16:32], middle, PLANE), axis=0)
+    spread = fine_dot(upper, prol)
+    for o in range(8):
+        i, jl = o // 4, o % 4
+        part = spread[i * 8 : i * 8 + 8, jl * PLANE : (jl + 1) * PLANE]
+        detail[child[0, o]] = live * (tiles[o] - part)
+    for group in range(2):
+        base = group * 4
+        halo[group * 16 : group * 16 + 16, :] = jnp.concatenate(
+            [
+                jnp.concatenate([detail[base], detail[base + 1]], axis=1),
+                jnp.concatenate([detail[base + 2], detail[base + 3]], axis=1),
+            ],
+            axis=0,
+        ).astype(BF16)
+    meta = jnp.where(low8, tag, jnp.full((8, 128), octant, jnp.int32).astype(F32))
+    halo[32:48, :] = jnp.concatenate(
+        [jnp.concatenate([middle, middle], axis=1), meta], axis=0
+    ).astype(BF16)
+
+    for copy in copies[5:]:
+        copy.wait()
     near = fine_nbr[...]
     own = near[:, 13:14] >> 3
     cell = local_cell(near >> 3, own) * 10 + (near & 7)
@@ -311,58 +365,10 @@
     numbers[10:11, 0:8] = child_v[...]
     numbers[10:11, 8:9] = jnp.full((1, 1), parent[0], jnp.int32)
     numbers[10:11, 9:10] = jnp.full((1, 1), refined[0], jnp.int32)
-
-    values = coef[...].astype(F32)
-    for a in range(8):
-        source[:, a, :] = values[:, a * PLANE : (a + 1) * PLANE]
-    tiles = [source[child[0, o]] for o in range(8)]
-    lhs = jnp.concatenate(
-        [jnp.concatenate(tiles[0:4], axis=1), jnp.concatenate(tiles[4:8], axis=1)], axis=0
-    ).astype(BF16)
-    both = dot(lhs, comp)
-    partial = both[:, :PLANE] + both[:, PLANE:]
-    compressed = None
-    for k in range(16):
-        term = rows[k, :, :PLANE] * partial[k : k + 1, :]
-        compressed = term if compressed is None else compressed + term
-    leaf_row = leaf[...].astype(F32)
-    leaf_tile = jnp.concatenate(
-        [leaf_row[:, a * PLANE : (a + 1) * PLANE] for a in range(8)], axis=0
-    )
-    middle = jnp.where(refined[0] > 0, compressed, leaf_tile).astype(BF16).astype(F32)
-
-    row_at = (octant >> 2) * 8
-    inner = row_mix([rows[row_at + x, :, :PLANE] for x in range(8)], middle)
-    table = filters[pl.ds(pl.multiple_of(512 + (octant & 3) * 64, 64), 64), :]
-    added = fine_dot(inner, table)
-    low8 = low_lanes((8, 128))
-    tag = jnp.full((8, 128), slot, jnp.int32).astype(F32)
-    tile = jnp.where(low8, jnp.concatenate([added, added], axis=1), tag).astype(BF16)
-    payload[...] = jnp.broadcast_to(tile[None], payload.shape)
-
-    live = jnp.full((8, PLANE), refined[0], jnp.int32).astype(F32)
-    upper = jnp.concatenate(two_row_mixes(rows.at[16:32], middle, PLANE), axis=0)
-    spread = fine_dot(upper, prol)
-    for o in range(8):
-        i, jl = o // 4, o % 4
-        part = spread[i * 8 : i * 8 + 8, jl * PLANE : (jl + 1) * PLANE]
-        detail[child[0, o]] = live * (tiles[o] - part)
-    for group in range(2):
-        base = group * 4
-        halo[group * 16 : group * 16 + 16, :] = jnp.concatenate(
-            [
-                jnp.concatenate([detail[base], detail[base + 1]], axis=1),
-                jnp.concatenate([detail[base + 2], detail[base + 3]], axis=1),
-            ],
-            axis=0,
-        ).astype(BF16)
-    meta = jnp.where(low8, tag, jnp.full((8, 128), octant, jnp.int32).astype(F32))
-    halo[32:48, :] = jnp.concatenate(
-        [jnp.concatenate([middle, middle], axis=1), meta], axis=0
-    ).astype(BF16)
-
-
-def plane_kernel(arrived, copies):
+    send.wait()
+
+
+def plane_kernel(arrived, copies, partial, sems):
     rows = arrived[...].astype(F32).reshape(512, 128)
     other = turned(rows)
     low = low_lanes((512, 128))
@@ -379,8 +385,9 @@
     hot = jnp.concatenate(
         [jnp.where(key == c2, 1.0, 0.0) for c2 in range(32)], axis=0
     ).astype(BF16)
-    partial = dot(hot, rhs).astype(BF16)
-    copies[...] = jnp.broadcast_to(partial[None], copies.shape)
+    partial[...] = dot(hot, rhs).astype(BF16)
+    for copy in fetches(sems, *((partial, copies.at[at]) for at in range(8))):
+        copy.wait()
 
 
 def pair_of(first, second):
@@ -388,10 +395,11 @@
 
 
 def fine_kernel(
-    numbers, left, centre, right, ab_ref, x_ref,
+    numbers_h, left, centre, right, ab_ref, x_ref,
     direct, mid_tiles, names_ref,
-    table, mixed, w_ref,
+    table, mixed, w_ref, numbers, sems,
 ):
+    copies = fetches(sems, (numbers_h, numbers))
     build_w(ab_ref, 0, w_ref)
     lanes = lax.broadcasted_iota(jnp.int32, (1, 128), 1)
     low8 = low_lanes((8, 128))
@@ -411,6 +419,9 @@
     names_ref[...] = names
     for cell in range(28):
         mid_tiles[cell] = table[cell * 10 + 8]
+
+    for copy in copies:
+        copy.wait()
 
     def source(t, ex, e):
         return table[numbers[t, ex * 9 + e]]
@@ -462,11 +473,18 @@
 
 
 def last_kernel(
-    numbers, names, planes, mid_tiles, direct, ab_ref, x_ref, rows_h, filters_h, mids_h,
+    numbers_h, names_h, planes, mid_tiles, direct, ab_ref, x_ref, rows_h, filters_h, mids_h,
     fine_out, mid_out,
-    coarse, back, rows_p, filters, mids, sems, w_mid, w_coarse,
+    coarse, back, rows_p, filters, mids, sems, w_mid, w_coarse, numbers, names,
 ):
-    copies = fetches(sems, (rows_h, rows_p), (filters_h, filters), (mids_h, mids))
+    copies = fetches(
+        sems,
+        (numbers_h, numbers),
+        (names_h, names),
+        (rows_h, rows_p),
+        (filters_h, filters),
+        (mids_h, mids),
+    )
     build_w(ab_ref, 1, w_mid)
     build_w(ab_ref, 2, w_coarse)
     low8 = low_lanes((8, 128))
@@ -481,6 +499,8 @@
         coarse[2 * c2] = jnp.where(low8, tile, other)
         coarse[2 * c2 + 1] = jnp.where(low8, other, tile)
     coarse[64] = jnp.zeros((8, 128), F32)
+    for copy in copies:
+        copy.wait()
     octant = numbers[10, 8] & 7
 
     def coarse_source(ex, e):
@@ -501,8 +521,6 @@
     )
     coarse_result = apply_one(sources, x_ref[2], w_coarse)
 
-    for copy in copies:
-        copy.wait()
     uppers, octants, owns = [], [], []
     for ep in range(5):
         for ex in range(3):
@@ -556,7 +574,7 @@
 def call(kernel, kinds, outs, scratch, flops, *args):
     any_space = pl.BlockSpec(memory_space=pl.ANY)
     vmem = pl.BlockSpec(memory_space=pltpu.VMEM)
-    specs = dict(s=pl.BlockSpec(memory_space=pltpu.SMEM), v=vmem, w=vmem, h=any_space)
+    specs = dict(s=pl.BlockSpec(memory_space=pltpu.SMEM), v=vmem, w=vmem, h=any_space, a=any_space)
     moved = sum(math.prod(x.shape) * x.dtype.itemsize for x in (*args, *outs))
     spaces = dict(w=pltpu.VMEM, h=pltpu.HBM)
     args = [
@@ -606,7 +624,7 @@
     halo, payload, numbers = call(
         first_kernel,
         "sshhhhhhhh",
-        [sds((48, 128), BF16), sds((64, 8, 128), BF16), sds((16, 128), i32)],
+        [sds((48, 128), BF16), pltpu.HBM((64, 8, 128), BF16), sds((16, 128), i32)],
         [
             smem((1, 8), i32),
             vmem((1, 8), i32),
@@ -620,6 +638,8 @@
             vmem((8, 8, PLANE), F32),
             vmem((8, 8, PLANE), F32),
             pltpu.SemaphoreType.DMA((9,)),
+            vmem((64, 8, 128), BF16),
+            pltpu.SemaphoreType.DMA,
         ],
         2_000_000,
         mid_parent, mid_refined, mid_child, fine_nbr, mid_nbr, coarse_nbr.T, fine_coef, mid_leaf,
@@ -633,7 +653,8 @@
     before, after = both_ways(sheet, "gx")
 
     (copies,) = call(
-        plane_kernel, "v", [sds((8, 256, 128), BF16)], [], 33_000_000, arrived
+        plane_kernel, "v", [pltpu.HBM((8, 256, 128), BF16)],
+        [vmem((256, 128), BF16), pltpu.SemaphoreType.DMA((8,))], 33_000_000, arrived
     )
     planes = lax.all_to_all(copies, "gx", 0, 0, tiled=True)
 
@@ -656,19 +677,21 @@
     )
     direct, mid_tiles, names = call(
         fine_kernel,
-        "svvvww",
+        "avvvww",
         [sds((8, 8, PLANE), F32), sds((28, 8, 128), F32), sds((1, 128), i32)],
         [
             vmem((GONE + 9, 8, 128), F32),
             vmem((256, ROWS_W), BF16),
             vmem((ROWS_W, 256), BF16),
+            smem((16, 128), i32),
+            pltpu.SemaphoreType.DMA((1,)),
         ],
         100_000_000,
         numbers, before, centre, after, w_factors, x_tables,
     )
     fine_out, mid_out = call(
         last_kernel,
-        "ssvvvwwhhh",
+        "aavvvwwhhh",
         [sds((8, 512), F32), sds((1, 512), F32)],
         [
             vmem((65, 8, 128), F32),
@@ -676,9 +699,11 @@
             vmem((16, 8, 128), F32),
             vmem((512, 128), BF16),
             vmem((128, 1024), BF16),
-            pltpu.SemaphoreType.DMA((3,)),
+            pltpu.SemaphoreType.DMA((5,)),
             vmem((ROWS_W, 256), BF16),
             vmem((ROWS_W, 256), BF16),
+            smem((16, 128), i32),
+            smem((1, 128), i32),
         ],
         200_000_000,
         numbers, names, planes, mid_tiles, direct, w_factors, x_tables,

time: 65.8 us -> 64.3 us (0.977)
  Pallas kernels: 13 us -> 11.5 us
    pallas_call x5, Pallas kernels: 13 us -> 11.5 us  [call(): pl.pallas_call(kernel, out_shape=outs, in_specs=[specs[kind] for kind in...]
  transfers between devices with their start and end apart: 8 -> 8, of which waited for: 3 -> 3; matrix products, arithmetic and copies ran while one was open for 0% -> 0% of each run, Pallas kernels for 9% -> 8%
where the time goes in v7:
time: 64.3 us; the launch traced here: 63.9 us
  starting transfers between devices  40.3 us (63%)
  Pallas kernels  11.5 us (18%)
  waiting for transfers between devices  9.89 us (15%)
  between operations  2.08 us (3%)
    all_to_all x1, starting transfers between devices, shards(): arrived = lax.all_to_all(payload, ('gy', 'gz'), 0, 0, tiled=True)  18.3 us
    pallas_call x5, Pallas kernels, call(): pl.pallas_call(kernel, out_shape=outs, in_specs=[specs[kind] for kind in...  11.5 us
    ppermute x3, starting transfers between devices, both_ways(): before = lax.ppermute(x, axis, [(i, i + 1) for i in range(ends)])  10.5 us
    all_to_all x1, waiting for transfers between devices, shards(): arrived = lax.all_to_all(payload, ('gy', 'gz'), 0, 0, tiled=True)  7.23 us
    all_to_all x1, starting transfers between devices, shards(): planes = lax.all_to_all(copies, 'gx', 0, 0, tiled=True)  7.03 us
    ppermute x3, starting transfers between devices, both_ways(): after = lax.ppermute(x, axis, [(i + 1, i) for i in range(ends)])  4.5 us
    ppermute x3, waiting for transfers between devices, both_ways(): after = lax.ppermute(x, axis, [(i + 1, i) for i in range(ends)])  2.4 us
  transfers between devices with their start and end apart: 8, of which 3 were waited for; matrix products, arithmetic and copies ran while one was open for 0% of the time, Pallas kernels for 8%

profile of v7, /device:TPU:1, one launch (start us, length us, event | category | flops | bytes accessed | tf_op | source)
XLA Modules:
  0.0 63.9 jit_solution(13402013627799335320)
XLA Ops:
  1.9 2.5 %first_kernel.1 = (bf16[48,128]{1,0:T(8,128)(2,1)S(1)}, bf16[64,8,128]{2,1,0:T(8,128)(2,1)}, s32[16,128]{1,0:T(8,128)S(1)}) custom-call(s32[1]{0:T(128)S(6)} %copy.24.parent, s32[1]{0:T(128)S(6)} %copy.25.refined, s32[1,8]{1,0:T(1,128)} %child_h.1, s32[8,27]{1,0:T(8,128)} %fine_h.1, s32[1,27]{1,0:T(1,128)} %mid_h.1, s32[27,64]{1,0:T(8,128)} %bitcast.5, ...), custom_call_target="tpu_custom_call" | custom-call | flops 2000000 | bytes 496372 | tf_op jit(solution)/shard_map/first_kernel/pallas_call | solution.py:584
  4.4 4.0 %collective-permute-start = (bf16[48,128]{1,0:T(8,128)(2,1)S(1)}, bf16[48,128]{1,0:T(8,128)(2,1)S(1)}, u32[]{:S(2)}, u32[]{:S(2)}) collective-permute-start(bf16[48,128]{1,0:T(8,128)(2,1)S(1)} %get-tuple-element.12), channel_id=1, source_target_pairs={{0,1},{1,2},{2,3},{3,4},{4,5},{5,6},{6,7},{8,9},{9,10},{10,11},{11... | collective-permute-start | bytes 36872 | tf_op jit(solution)/shard_map/ppermute | solution.py:599
  8.4 1.3 %collective-permute-start.1 = (bf16[48,128]{1,0:T(8,128)(2,1)S(1)}, bf16[48,128]{1,0:T(8,128)(2,1)S(1)}, u32[]{:S(2)}, u32[]{:S(2)}) collective-permute-start(bf16[48,128]{1,0:T(8,128)(2,1)S(1)} %get-tuple-element.12), channel_id=1, source_target_pairs={{1,0},{2,1},{3,2},{4,3},{5,4},{6,5},{7,6},{9,8},{10,9},{11,10},{12... | collective-permute-start | bytes 36872 | tf_op jit(solution)/shard_map/ppermute | solution.py:600
  9.7 18.3 %all-to-all-start = ((bf16[64,8,128]{2,1,0:T(8,128)(2,1)}), bf16[64,8,128]{2,1,0:T(8,128)(2,1)S(1)}, u32[]{:S(2)}, u32[]{:S(2)}) async-start(bf16[64,8,128]{2,1,0:T(8,128)(2,1)} %get-tuple-element.17), calls=%async_computation | async-start | bytes 262144 | tf_op jit(solution)/shard_map/all_to_all | solution.py:648
  28.0 0.0 collective-permute-done
  28.1 0.0 collective-permute-done.1
  28.1 2.9 %collective-permute-start.2 = (bf16[144,128]{1,0:T(8,128)(2,1)S(1)}, bf16[144,128]{1,0:T(8,128)(2,1)S(1)}, u32[]{:S(2)}, u32[]{:S(2)}) collective-permute-start(bf16[144,128]{1,0:T(8,128)(2,1)S(1)} %constant_dynamic-update-slice_fusion), channel_id=1, source_target_pairs={{0,8},{8,16},{16,24},{24,32},{32,40},{40,48},{48,56},{1,9},{9,17},... | collective-permute-start | bytes 110600 | tf_op jit(solution)/shard_map/ppermute | solution.py:599
  31.0 1.3 %collective-permute-start.3 = (bf16[144,128]{1,0:T(8,128)(2,1)S(1)}, bf16[144,128]{1,0:T(8,128)(2,1)S(1)}, u32[]{:S(2)}, u32[]{:S(2)}) collective-permute-start(bf16[144,128]{1,0:T(8,128)(2,1)S(1)} %constant_dynamic-update-slice_fusion), channel_id=1, source_target_pairs={{8,0},{16,8},{24,16},{32,24},{40,32},{48,40},{56,48},{9,1},{17,9},... | collective-permute-start | bytes 110600 | tf_op jit(solution)/shard_map/ppermute | solution.py:600
  32.3 0.0 collective-permute-done.2
  32.4 7.2 %all-to-all-done.arrived = bf16[64,8,128]{2,1,0:T(8,128)(2,1)S(1)} async-done(((bf16[64,8,128]{2,1,0:T(8,128)(2,1)}), bf16[64,8,128]{2,1,0:T(8,128)(2,1)S(1)}, u32[]{:S(2)}, u32[]{:S(2)}) %all-to-all-start) | async-done | bytes 131104 | tf_op jit(solution)/shard_map/all_to_all | solution.py:648
  39.6 1.3 %plane_kernel.1 = bf16[8,256,128]{2,1,0:T(8,128)(2,1)} custom-call(bf16[64,8,128]{2,1,0:T(8,128)(2,1)S(1)} %all-to-all-done.arrived), custom_call_target="tpu_custom_call" | custom-call | flops 33000000 | bytes 655360 | tf_op jit(solution)/shard_map/plane_kernel/pallas_call | solution.py:584
  40.9 7.0 %all-to-all-start.1 = ((bf16[8,256,128]{2,1,0:T(8,128)(2,1)}), bf16[8,256,128]{2,1,0:T(8,128)(2,1)S(1)}, u32[]{:S(2)}, u32[]{:S(2)}) async-start(bf16[8,256,128]{2,1,0:T(8,128)(2,1)} %plane_kernel.1), calls=%async_computation.1 | async-start | bytes 1048576 | tf_op jit(solution)/shard_map/all_to_all | solution.py:659
  48.0 0.0 collective-permute-done.3
  48.0 3.5 %collective-permute-start.4 = (bf16[432,128]{1,0:T(8,128)(2,1)S(1)}, bf16[432,128]{1,0:T(8,128)(2,1)S(1)}, u32[]{:S(2)}, u32[]{:S(2)}) collective-permute-start(bf16[432,128]{1,0:T(8,128)(2,1)S(1)} %constant_dynamic-update-slice_fusion.3.sheet), channel_id=1, source_target_pairs={{0,64},{64,128},{128,192},{192,256},{256,320},{320,384},{384,448},... | collective-permute-start | bytes 331784 | tf_op jit(solution)/shard_map/ppermute | solution.py:599
  51.5 1.9 %collective-permute-start.5 = (bf16[432,128]{1,0:T(8,128)(2,1)S(1)}, bf16[432,128]{1,0:T(8,128)(2,1)S(1)}, u32[]{:S(2)}, u32[]{:S(2)}) collective-permute-start(bf16[432,128]{1,0:T(8,128)(2,1)S(1)} %constant_dynamic-update-slice_fusion.3.sheet), channel_id=1, source_target_pairs={{64,0},{128,64},{192,128},{256,192},{320,256},{384,320},{448,384},... | collective-permute-start | bytes 331784 | tf_op jit(solution)/shard_map/ppermute | solution.py:600
  53.5 1.8 %tables_kernel.1 = (f32[2,24,24,256]{3,2,1,0:T(8,128)S(1)}, bf16[3,256,24]{2,1,0:T(8,128)(2,1)S(1)}, f32[90,8,128]{2,1,0:T(8,128)S(1)}) custom-call(f32[3,192,32]{2,1,0:T(8,128)} %bitcast.6, f32[1,32]{1,0:T(1,128)} %bitcast.7, bf16[256,768]{1,0:T(8,128)(2,1)} %constant.12.clone.select_h, bf16[432,128]{1,0:T(8,128)(2,1)S(1)} %constant_dynamic-update-slice_fusion.3.sheet), custom_call_target="tpu_custom_call" | custom-call | flops 600000000 | bytes 2162816 | tf_op jit(solution)/shard_map/tables_kernel/pallas_call | solution.py:584
  55.3 0.2 collective-permute-done.4.left
  55.5 2.4 %collective-permute-done.5.right = bf16[432,128]{1,0:T(8,128)(2,1)S(1)} collective-permute-done((bf16[432,128]{1,0:T(8,128)(2,1)S(1)}, bf16[432,128]{1,0:T(8,128)(2,1)S(1)}, u32[]{:S(2)}, u32[]{:S(2)}) %collective-permute-start.5) | collective-permute-done | bytes 110624 | tf_op jit(solution)/shard_map/ppermute | solution.py:600
  57.9 2.3 %fine_kernel.1 = (f32[8,8,64]{2,1,0:T(8,128)S(1)}, f32[28,8,128]{2,1,0:T(8,128)S(1)}, s32[1,128]{1,0:T(1,128)S(1)}) custom-call(s32[16,128]{1,0:T(8,128)S(1)} %get-tuple-element.11.numbers_h, bf16[432,128]{1,0:T(8,128)(2,1)S(1)} %collective-permute-done.4.left, f32[90,8,128]{2,1,0:T(8,128)S(1)} %get-tuple-element.13.centre, ...), custom_call_target="tpu_custom_call" | custom-call | flops 100000000 | bytes 1946112 | tf_op jit(solution)/shard_map/fine_kernel/pallas_call | solution.py:584
  60.2 0.0 all-to-all-done.1.planes
  60.2 3.7 %last_kernel.1 = (f32[8,512]{1,0:T(8,128)}, f32[1,512]{1,0:T(1,128)}) custom-call(s32[16,128]{1,0:T(8,128)S(1)} %get-tuple-element.11.numbers_h, s32[1,128]{1,0:T(1,128)S(1)} %get-tuple-element.16.names_h, bf16[8,256,128]{2,1,0:T(8,128)(2,1)S(1)} %all-to-all-done.1.planes, f32[28,8,128]{2,1,0:T(8,128)S(1)} %get-tuple-element.18.mid_tiles, ...), custom_call_target="tpu_custom_call" | custom-call | flops 200000000 | bytes 2357760 | tf_op jit(solution)/shard_map/last_kernel/pallas_call | solution.py:584
  (8 shorter events, 0.1 us)
Async XLA Ops:
  4.4 23.7 %collective-permute-start = (bf16[48,128]{1,0:T(8,128)(2,1)S(1)}, bf16[48,128]{1,0:T(8,128)(2,1)S(1)}, u32[]{:S(2)}, u32[]{:S(2)}) collective-permute-start(bf16[48,128]{1,0:T(8,128)(2,1)S(1)} %get-tuple-element.12), channel_id=1, source_target_pairs={{0,1},{1,2},{2,3},{3,4},{4,5},{5,6},{6,7},{8,9},{9,10},{10,11},{11... | collective-permute-start | bytes 36872 | tf_op jit(solution)/shard_map/ppermute | solution.py:599
  8.4 19.7 %collective-permute-start.1 = (bf16[48,128]{1,0:T(8,128)(2,1)S(1)}, bf16[48,128]{1,0:T(8,128)(2,1)S(1)}, u32[]{:S(2)}, u32[]{:S(2)}) collective-permute-start(bf16[48,128]{1,0:T(8,128)(2,1)S(1)} %get-tuple-element.12), channel_id=1, source_target_pairs={{1,0},{2,1},{3,2},{4,3},{5,4},{6,5},{7,6},{9,8},{10,9},{11,10},{12... | collective-permute-start | bytes 36872 | tf_op jit(solution)/shard_map/ppermute | solution.py:600
  9.7 29.9 %all-to-all-start = ((bf16[64,8,128]{2,1,0:T(8,128)(2,1)}), bf16[64,8,128]{2,1,0:T(8,128)(2,1)S(1)}, u32[]{:S(2)}, u32[]{:S(2)}) async-start(bf16[64,8,128]{2,1,0:T(8,128)(2,1)} %get-tuple-element.17), calls=%async_computation | async-start | bytes 262144 | tf_op jit(solution)/shard_map/all_to_all | solution.py:648
  28.1 4.2 %collective-permute-start.2 = (bf16[144,128]{1,0:T(8,128)(2,1)S(1)}, bf16[144,128]{1,0:T(8,128)(2,1)S(1)}, u32[]{:S(2)}, u32[]{:S(2)}) collective-permute-start(bf16[144,128]{1,0:T(8,128)(2,1)S(1)} %constant_dynamic-update-slice_fusion), channel_id=1, source_target_pairs={{0,8},{8,16},{16,24},{24,32},{32,40},{40,48},{48,56},{1,9},{9,17},... | collective-permute-start | bytes 110600 | tf_op jit(solution)/shard_map/ppermute | solution.py:599
  31.0 16.9 %collective-permute-start.3 = (bf16[144,128]{1,0:T(8,128)(2,1)S(1)}, bf16[144,128]{1,0:T(8,128)(2,1)S(1)}, u32[]{:S(2)}, u32[]{:S(2)}) collective-permute-start(bf16[144,128]{1,0:T(8,128)(2,1)S(1)} %constant_dynamic-update-slice_fusion), channel_id=1, source_target_pairs={{8,0},{16,8},{24,16},{32,24},{40,32},{48,40},{56,48},{9,1},{17,9},... | collective-permute-start | bytes 110600 | tf_op jit(solution)/shard_map/ppermute | solution.py:600
  40.9 19.3 %all-to-all-start.1 = ((bf16[8,256,128]{2,1,0:T(8,128)(2,1)}), bf16[8,256,128]{2,1,0:T(8,128)(2,1)S(1)}, u32[]{:S(2)}, u32[]{:S(2)}) async-start(bf16[8,256,128]{2,1,0:T(8,128)(2,1)} %plane_kernel.1), calls=%async_computation.1 | async-start | bytes 1048576 | tf_op jit(solution)/shard_map/all_to_all | solution.py:659
  48.0 7.5 %collective-permute-start.4 = (bf16[432,128]{1,0:T(8,128)(2,1)S(1)}, bf16[432,128]{1,0:T(8,128)(2,1)S(1)}, u32[]{:S(2)}, u32[]{:S(2)}) collective-permute-start(bf16[432,128]{1,0:T(8,128)(2,1)S(1)} %constant_dynamic-update-slice_fusion.3.sheet), channel_id=1, source_target_pairs={{0,64},{64,128},{128,192},{192,256},{256,320},{320,384},{384,448},... | collective-permute-start | bytes 331784 | tf_op jit(solution)/shard_map/ppermute | solution.py:599
  51.5 6.4 %collective-permute-start.5 = (bf16[432,128]{1,0:T(8,128)(2,1)S(1)}, bf16[432,128]{1,0:T(8,128)(2,1)S(1)}, u32[]{:S(2)}, u32[]{:S(2)}) collective-permute-start(bf16[432,128]{1,0:T(8,128)(2,1)S(1)} %constant_dynamic-update-slice_fusion.3.sheet), channel_id=1, source_target_pairs={{64,0},{128,64},{192,128},{256,192},{320,256},{384,320},{448,384},... | collective-permute-start | bytes 331784 | tf_op jit(solution)/shard_map/ppermute | solution.py:600

commit v8 on v7

--- a/solution.py
+++ b/solution.py
@@ -15,6 +15,7 @@
 TERMS = 32
 QUADS = 8
 ROWS_W = 4608
+CELL = 40
 GONE = 27 * 10
 BF16 = jnp.bfloat16
 F32 = jnp.float32
@@ -176,8 +177,7 @@
     factors, weights, select, sems,
 ):
     copies = fetches(sems, (factors_h, factors), (weights_h, weights), (select_h, select))
-    for cell in range(9):
-        spread_cell(sheet, cell, tiles, cell)
+    spread_cells(sheet, tiles, 0)
     for copy in copies:
         copy.wait()
     lane = lax.broadcasted_iota(jnp.int32, (24, 256), 1)
@@ -232,19 +232,17 @@
     lax.fori_loop(0, QUADS, one_quad, 0)
 
 
-def spread_cell(sheet, cell, tiles, to):
+def spread_cells(sheet, tiles, at):
     low = low_lanes((8, 128))
-    base = cell * 48
-    for group in range(2):
-        both = sheet[base + group * 16 : base + group * 16 + 16, :].astype(F32)
-        for sub in range(2):
-            tile = both[sub * 8 : sub * 8 + 8, :]
+    values = sheet[...].astype(F32)
+    for cell in range(9):
+        to = (at + cell) * 10
+        for pair in range(5):
+            row = cell * CELL + pair * 8
+            tile = values[row : row + 8, :]
             other = turned(tile)
-            tiles[to * 10 + group * 4 + sub * 2] = jnp.where(low, tile, other)
-            tiles[to * 10 + group * 4 + sub * 2 + 1] = jnp.where(low, other, tile)
-    last = sheet[base + 32 : base + 48, :].astype(F32)
-    tiles[to * 10 + 8] = last[0:8, :]
-    tiles[to * 10 + 9] = last[8:16, :]
+            tiles[to + 2 * pair] = jnp.where(low, tile, other)
+            tiles[to + 2 * pair + 1] = tile if pair == 4 else jnp.where(low, other, tile)
 
 
 def diagonal_sum(result, rows):
@@ -329,19 +327,11 @@
         i, jl = o // 4, o % 4
         part = spread[i * 8 : i * 8 + 8, jl * PLANE : (jl + 1) * PLANE]
         detail[child[0, o]] = live * (tiles[o] - part)
-    for group in range(2):
-        base = group * 4
-        halo[group * 16 : group * 16 + 16, :] = jnp.concatenate(
-            [
-                jnp.concatenate([detail[base], detail[base + 1]], axis=1),
-                jnp.concatenate([detail[base + 2], detail[base + 3]], axis=1),
-            ],
-            axis=0,
-        ).astype(BF16)
-    meta = jnp.where(low8, tag, jnp.full((8, 128), octant, jnp.int32).astype(F32))
-    halo[32:48, :] = jnp.concatenate(
-        [jnp.concatenate([middle, middle], axis=1), meta], axis=0
-    ).astype(BF16)
+    lane = lax.broadcasted_iota(jnp.int32, (8, 128), 1)
+    name = jnp.where(lane < 96, tag, jnp.full((8, 128), octant, jnp.int32).astype(F32))
+    pairs = [jnp.concatenate([detail[2 * k], detail[2 * k + 1]], axis=1) for k in range(4)]
+    pairs.append(jnp.where(low8, jnp.concatenate([middle, middle], axis=1), name))
+    halo[...] = jnp.concatenate(pairs, axis=0).astype(BF16)
 
     for copy in copies[5:]:
         copy.wait()
@@ -405,17 +395,15 @@
     low8 = low_lanes((8, 128))
     table[GONE] = jnp.zeros((8, 128), F32)
     table[GONE + 8] = jnp.zeros((8, 128), F32)
-    for cell in range(9):
-        spread_cell(left, cell, table, cell)
-        spread_cell(right, cell, table, 18 + cell)
+    spread_cells(left, table, 0)
+    spread_cells(right, table, 18)
     for at in range(90):
         table[90 + at] = centre[at]
     names = jnp.full((1, 128), 512, jnp.int32)
     for cell in range(27):
         meta = table[cell * 10 + 9, 0:1, :]
-        other = turned(meta)
-        name = jnp.where(low8[0:1], meta * 8.0 + other, other * 8.0 + meta).astype(jnp.int32)
-        names = jnp.where(lanes == cell, name, names)
+        name = meta * 8.0 + pltpu.roll(meta, 96, 1)
+        names = jnp.where(lanes == PLANE + cell, name.astype(jnp.int32), names)
     names_ref[...] = names
     for cell in range(28):
         mid_tiles[cell] = table[cell * 10 + 8]
@@ -526,7 +514,7 @@
         for ex in range(3):
             first = numbers[8, ex * 9 + 2 * ep]
             second = numbers[8, ex * 9 + min(2 * ep + 1, 8)]
-            name_1, name_2 = names[0, first], names[0, second]
+            name_1, name_2 = names[0, PLANE + first], names[0, PLANE + second]
             owns.append(pair_of(mid_tiles[first], mid_tiles[second]))
             both = pair_of(coarse[name_1 >> 3], coarse[name_2 >> 3])
             named = jnp.where(low8, name_1 & 7, name_2 & 7)
@@ -624,7 +612,7 @@
     halo, payload, numbers = call(
         first_kernel,
         "sshhhhhhhh",
-        [sds((48, 128), BF16), pltpu.HBM((64, 8, 128), BF16), sds((16, 128), i32)],
+        [sds((CELL, 128), BF16), pltpu.HBM((64, 8, 128), BF16), sds((16, 128), i32)],
         [
             smem((1, 8), i32),
             vmem((1, 8), i32),

time: 64.3 us -> 64.1 us (level)
  transfers between devices with their start and end apart: 8 -> 8, of which waited for: 3 -> 2; matrix products, arithmetic and copies ran while one was open for 0% -> 0% of each run, Pallas kernels for 8% -> 8%
where the time goes in v8:
time: 64.1 us; the launch traced here: 63.7 us
  starting transfers between devices  40.3 us (63%)
  Pallas kernels  11.5 us (18%)
  waiting for transfers between devices  9.69 us (15%)
  between operations  2.08 us (3%)
    all_to_all x1, starting transfers between devices, shards(): arrived = lax.all_to_all(payload, ('gy', 'gz'), 0, 0, tiled=True)  18.3 us
    pallas_call x5, Pallas kernels, call(): pl.pallas_call(kernel, out_shape=outs, in_specs=[specs[kind] for kind in...  11.5 us
    ppermute x3, starting transfers between devices, both_ways(): before = lax.ppermute(x, axis, [(i, i + 1) for i in range(ends)])  10.5 us
    all_to_all x1, waiting for transfers between devices, shards(): arrived = lax.all_to_all(payload, ('gy', 'gz'), 0, 0, tiled=True)  7.23 us
    all_to_all x1, starting transfers between devices, shards(): planes = lax.all_to_all(copies, 'gx', 0, 0, tiled=True)  7.03 us
    ppermute x3, starting transfers between devices, both_ways(): after = lax.ppermute(x, axis, [(i + 1, i) for i in range(ends)])  4.5 us
    ppermute x3, waiting for transfers between devices, both_ways(): after = lax.ppermute(x, axis, [(i + 1, i) for i in range(ends)])  2.4 us
  transfers between devices with their start and end apart: 8, of which 2 were waited for; matrix products, arithmetic and copies ran while one was open for 0% of the time, Pallas kernels for 8%

profile of v8, /device:TPU:1, one launch (start us, length us, event | category | flops | bytes accessed | tf_op | source)
XLA Modules:
  0.0 63.7 jit_solution(16779698586166112000)
XLA Ops:
  1.9 2.4 %first_kernel.1 = (bf16[40,128]{1,0:T(8,128)(2,1)S(1)}, bf16[64,8,128]{2,1,0:T(8,128)(2,1)}, s32[16,128]{1,0:T(8,128)S(1)}) custom-call(s32[1]{0:T(128)S(6)} %copy.24.parent, s32[1]{0:T(128)S(6)} %copy.25.refined, s32[1,8]{1,0:T(1,128)} %child_h.1, s32[8,27]{1,0:T(8,128)} %fine_h.1, s32[1,27]{1,0:T(1,128)} %mid_h.1, s32[27,64]{1,0:T(8,128)} %bitcast.5, ...), custom_call_target="tpu_custom_call" | custom-call | flops 2000000 | bytes 494324 | tf_op jit(solution)/shard_map/first_kernel/pallas_call | solution.py:572
  4.4 4.0 %collective-permute-start = (bf16[40,128]{1,0:T(8,128)(2,1)S(1)}, bf16[40,128]{1,0:T(8,128)(2,1)S(1)}, u32[]{:S(2)}, u32[]{:S(2)}) collective-permute-start(bf16[40,128]{1,0:T(8,128)(2,1)S(1)} %get-tuple-element.12), channel_id=1, source_target_pairs={{0,1},{1,2},{2,3},{3,4},{4,5},{5,6},{6,7},{8,9},{9,10},{10,11},{11... | collective-permute-start | bytes 30728 | tf_op jit(solution)/shard_map/ppermute | solution.py:587
  8.4 1.3 %collective-permute-start.1 = (bf16[40,128]{1,0:T(8,128)(2,1)S(1)}, bf16[40,128]{1,0:T(8,128)(2,1)S(1)}, u32[]{:S(2)}, u32[]{:S(2)}) collective-permute-start(bf16[40,128]{1,0:T(8,128)(2,1)S(1)} %get-tuple-element.12), channel_id=1, source_target_pairs={{1,0},{2,1},{3,2},{4,3},{5,4},{6,5},{7,6},{9,8},{10,9},{11,10},{12... | collective-permute-start | bytes 30728 | tf_op jit(solution)/shard_map/ppermute | solution.py:588
  9.7 18.3 %all-to-all-start = ((bf16[64,8,128]{2,1,0:T(8,128)(2,1)}), bf16[64,8,128]{2,1,0:T(8,128)(2,1)S(1)}, u32[]{:S(2)}, u32[]{:S(2)}) async-start(bf16[64,8,128]{2,1,0:T(8,128)(2,1)} %get-tuple-element.17), calls=%async_computation | async-start | bytes 262144 | tf_op jit(solution)/shard_map/all_to_all | solution.py:636
  28.0 0.0 collective-permute-done
  28.1 0.0 collective-permute-done.1
  28.1 2.9 %collective-permute-start.2 = (bf16[120,128]{1,0:T(8,128)(2,1)S(1)}, bf16[120,128]{1,0:T(8,128)(2,1)S(1)}, u32[]{:S(2)}, u32[]{:S(2)}) collective-permute-start(bf16[120,128]{1,0:T(8,128)(2,1)S(1)} %constant_dynamic-update-slice_fusion), channel_id=1, source_target_pairs={{0,8},{8,16},{16,24},{24,32},{32,40},{40,48},{48,56},{1,9},{9,17},... | collective-permute-start | bytes 92168 | tf_op jit(solution)/shard_map/ppermute | solution.py:587
  31.0 1.3 %collective-permute-start.3 = (bf16[120,128]{1,0:T(8,128)(2,1)S(1)}, bf16[120,128]{1,0:T(8,128)(2,1)S(1)}, u32[]{:S(2)}, u32[]{:S(2)}) collective-permute-start(bf16[120,128]{1,0:T(8,128)(2,1)S(1)} %constant_dynamic-update-slice_fusion), channel_id=1, source_target_pairs={{8,0},{16,8},{24,16},{32,24},{40,32},{48,40},{56,48},{9,1},{17,9},... | collective-permute-start | bytes 92168 | tf_op jit(solution)/shard_map/ppermute | solution.py:588
  32.3 0.0 collective-permute-done.2
  32.4 7.2 %all-to-all-done.arrived = bf16[64,8,128]{2,1,0:T(8,128)(2,1)S(1)} async-done(((bf16[64,8,128]{2,1,0:T(8,128)(2,1)}), bf16[64,8,128]{2,1,0:T(8,128)(2,1)S(1)}, u32[]{:S(2)}, u32[]{:S(2)}) %all-to-all-start) | async-done | bytes 131104 | tf_op jit(solution)/shard_map/all_to_all | solution.py:636
  39.6 1.3 %plane_kernel.1 = bf16[8,256,128]{2,1,0:T(8,128)(2,1)} custom-call(bf16[64,8,128]{2,1,0:T(8,128)(2,1)S(1)} %all-to-all-done.arrived), custom_call_target="tpu_custom_call" | custom-call | flops 33000000 | bytes 655360 | tf_op jit(solution)/shard_map/plane_kernel/pallas_call | solution.py:572
  40.9 7.0 %all-to-all-start.1 = ((bf16[8,256,128]{2,1,0:T(8,128)(2,1)}), bf16[8,256,128]{2,1,0:T(8,128)(2,1)S(1)}, u32[]{:S(2)}, u32[]{:S(2)}) async-start(bf16[8,256,128]{2,1,0:T(8,128)(2,1)} %plane_kernel.1), calls=%async_computation.1 | async-start | bytes 1048576 | tf_op jit(solution)/shard_map/all_to_all | solution.py:647
  48.0 0.0 collective-permute-done.3
  48.0 3.5 %collective-permute-start.4 = (bf16[360,128]{1,0:T(8,128)(2,1)S(1)}, bf16[360,128]{1,0:T(8,128)(2,1)S(1)}, u32[]{:S(2)}, u32[]{:S(2)}) collective-permute-start(bf16[360,128]{1,0:T(8,128)(2,1)S(1)} %constant_dynamic-update-slice_fusion.3.sheet), channel_id=1, source_target_pairs={{0,64},{64,128},{128,192},{192,256},{256,320},{320,384},{384,448},... | collective-permute-start | bytes 276488 | tf_op jit(solution)/shard_map/ppermute | solution.py:587
  51.5 1.9 %collective-permute-start.5 = (bf16[360,128]{1,0:T(8,128)(2,1)S(1)}, bf16[360,128]{1,0:T(8,128)(2,1)S(1)}, u32[]{:S(2)}, u32[]{:S(2)}) collective-permute-start(bf16[360,128]{1,0:T(8,128)(2,1)S(1)} %constant_dynamic-update-slice_fusion.3.sheet), channel_id=1, source_target_pairs={{64,0},{128,64},{192,128},{256,192},{320,256},{384,320},{448,384},... | collective-permute-start | bytes 276488 | tf_op jit(solution)/shard_map/ppermute | solution.py:588
  53.5 1.8 %tables_kernel.1 = (f32[2,24,24,256]{3,2,1,0:T(8,128)S(1)}, bf16[3,256,24]{2,1,0:T(8,128)(2,1)S(1)}, f32[90,8,128]{2,1,0:T(8,128)S(1)}) custom-call(f32[3,192,32]{2,1,0:T(8,128)} %bitcast.6, f32[1,32]{1,0:T(1,128)} %bitcast.7, bf16[256,768]{1,0:T(8,128)(2,1)} %constant.12.clone.select_h, bf16[360,128]{1,0:T(8,128)(2,1)S(1)} %constant_dynamic-update-slice_fusion.3.sheet), custom_call_target="tpu_custom_call" | custom-call | flops 600000000 | bytes 2144384 | tf_op jit(solution)/shard_map/tables_kernel/pallas_call | solution.py:572
  55.3 0.0 collective-permute-done.4.left
  55.3 2.4 %collective-permute-done.5.right = bf16[360,128]{1,0:T(8,128)(2,1)S(1)} collective-permute-done((bf16[360,128]{1,0:T(8,128)(2,1)S(1)}, bf16[360,128]{1,0:T(8,128)(2,1)S(1)}, u32[]{:S(2)}, u32[]{:S(2)}) %collective-permute-start.5) | collective-permute-done | bytes 92192 | tf_op jit(solution)/shard_map/ppermute | solution.py:588
  57.7 2.3 %fine_kernel.1 = (f32[8,8,64]{2,1,0:T(8,128)S(1)}, f32[28,8,128]{2,1,0:T(8,128)S(1)}, s32[1,128]{1,0:T(1,128)S(1)}) custom-call(s32[16,128]{1,0:T(8,128)S(1)} %get-tuple-element.11.numbers_h, bf16[360,128]{1,0:T(8,128)(2,1)S(1)} %collective-permute-done.4.left, f32[90,8,128]{2,1,0:T(8,128)S(1)} %get-tuple-element.13.centre, ...), custom_call_target="tpu_custom_call" | custom-call | flops 100000000 | bytes 1909248 | tf_op jit(solution)/shard_map/fine_kernel/pallas_call | solution.py:572
  60.0 0.0 all-to-all-done.1.planes
  60.0 3.7 %last_kernel.1 = (f32[8,512]{1,0:T(8,128)}, f32[1,512]{1,0:T(1,128)}) custom-call(s32[16,128]{1,0:T(8,128)S(1)} %get-tuple-element.11.numbers_h, s32[1,128]{1,0:T(1,128)S(1)} %get-tuple-element.16.names_h, bf16[8,256,128]{2,1,0:T(8,128)(2,1)S(1)} %all-to-all-done.1.planes, f32[28,8,128]{2,1,0:T(8,128)S(1)} %get-tuple-element.18.mid_tiles, ...), custom_call_target="tpu_custom_call" | custom-call | flops 200000000 | bytes 2357760 | tf_op jit(solution)/shard_map/last_kernel/pallas_call | solution.py:572
  (8 shorter events, 0.1 us)
Async XLA Ops:
  4.4 23.7 %collective-permute-start = (bf16[40,128]{1,0:T(8,128)(2,1)S(1)}, bf16[40,128]{1,0:T(8,128)(2,1)S(1)}, u32[]{:S(2)}, u32[]{:S(2)}) collective-permute-start(bf16[40,128]{1,0:T(8,128)(2,1)S(1)} %get-tuple-element.12), channel_id=1, source_target_pairs={{0,1},{1,2},{2,3},{3,4},{4,5},{5,6},{6,7},{8,9},{9,10},{10,11},{11... | collective-permute-start | bytes 30728 | tf_op jit(solution)/shard_map/ppermute | solution.py:587
  8.4 19.7 %collective-permute-start.1 = (bf16[40,128]{1,0:T(8,128)(2,1)S(1)}, bf16[40,128]{1,0:T(8,128)(2,1)S(1)}, u32[]{:S(2)}, u32[]{:S(2)}) collective-permute-start(bf16[40,128]{1,0:T(8,128)(2,1)S(1)} %get-tuple-element.12), channel_id=1, source_target_pairs={{1,0},{2,1},{3,2},{4,3},{5,4},{6,5},{7,6},{9,8},{10,9},{11,10},{12... | collective-permute-start | bytes 30728 | tf_op jit(solution)/shard_map/ppermute | solution.py:588
  9.7 29.9 %all-to-all-start = ((bf16[64,8,128]{2,1,0:T(8,128)(2,1)}), bf16[64,8,128]{2,1,0:T(8,128)(2,1)S(1)}, u32[]{:S(2)}, u32[]{:S(2)}) async-start(bf16[64,8,128]{2,1,0:T(8,128)(2,1)} %get-tuple-element.17), calls=%async_computation | async-start | bytes 262144 | tf_op jit(solution)/shard_map/all_to_all | solution.py:636
  28.1 4.2 %collective-permute-start.2 = (bf16[120,128]{1,0:T(8,128)(2,1)S(1)}, bf16[120,128]{1,0:T(8,128)(2,1)S(1)}, u32[]{:S(2)}, u32[]{:S(2)}) collective-permute-start(bf16[120,128]{1,0:T(8,128)(2,1)S(1)} %constant_dynamic-update-slice_fusion), channel_id=1, source_target_pairs={{0,8},{8,16},{16,24},{24,32},{32,40},{40,48},{48,56},{1,9},{9,17},... | collective-permute-start | bytes 92168 | tf_op jit(solution)/shard_map/ppermute | solution.py:587
  31.0 16.9 %collective-permute-start.3 = (bf16[120,128]{1,0:T(8,128)(2,1)S(1)}, bf16[120,128]{1,0:T(8,128)(2,1)S(1)}, u32[]{:S(2)}, u32[]{:S(2)}) collective-permute-start(bf16[120,128]{1,0:T(8,128)(2,1)S(1)} %constant_dynamic-update-slice_fusion), channel_id=1, source_target_pairs={{8,0},{16,8},{24,16},{32,24},{40,32},{48,40},{56,48},{9,1},{17,9},... | collective-permute-start | bytes 92168 | tf_op jit(solution)/shard_map/ppermute | solution.py:588
  40.9 19.1 %all-to-all-start.1 = ((bf16[8,256,128]{2,1,0:T(8,128)(2,1)}), bf16[8,256,128]{2,1,0:T(8,128)(2,1)S(1)}, u32[]{:S(2)}, u32[]{:S(2)}) async-start(bf16[8,256,128]{2,1,0:T(8,128)(2,1)} %plane_kernel.1), calls=%async_computation.1 | async-start | bytes 1048576 | tf_op jit(solution)/shard_map/all_to_all | solution.py:647
  48.0 7.3 %collective-permute-start.4 = (bf16[360,128]{1,0:T(8,128)(2,1)S(1)}, bf16[360,128]{1,0:T(8,128)(2,1)S(1)}, u32[]{:S(2)}, u32[]{:S(2)}) collective-permute-start(bf16[360,128]{1,0:T(8,128)(2,1)S(1)} %constant_dynamic-update-slice_fusion.3.sheet), channel_id=1, source_target_pairs={{0,64},{64,128},{128,192},{192,256},{256,320},{320,384},{384,448},... | collective-permute-start | bytes 276488 | tf_op jit(solution)/shard_map/ppermute | solution.py:587
  51.5 6.2 %collective-permute-start.5 = (bf16[360,128]{1,0:T(8,128)(2,1)S(1)}, bf16[360,128]{1,0:T(8,128)(2,1)S(1)}, u32[]{:S(2)}, u32[]{:S(2)}) collective-permute-start(bf16[360,128]{1,0:T(8,128)(2,1)S(1)} %constant_dynamic-update-slice_fusion.3.sheet), channel_id=1, source_target_pairs={{64,0},{128,64},{192,128},{256,192},{320,256},{384,320},{448,384},... | collective-permute-start | bytes 276488 | tf_op jit(solution)/shard_map/ppermute | solution.py:588

commit v9 on v8

--- a/solution.py
+++ b/solution.py
@@ -172,13 +172,21 @@
 
 
 def tables_kernel(
-    factors_h, weights_h, select_h, sheet,
-    ab_ref, x_ref, tiles,
+    factors_h, weights_h, select_h, sheet, rows_h, filters_h, mids_h,
+    ab_ref, x_ref, tiles, rows_p, filters, mids,
     factors, weights, select, sems,
 ):
-    copies = fetches(sems, (factors_h, factors), (weights_h, weights), (select_h, select))
+    copies = fetches(
+        sems,
+        (factors_h, factors),
+        (weights_h, weights),
+        (select_h, select),
+        (mids_h, mids),
+        (filters_h, filters),
+        (rows_h, rows_p),
+    )
     spread_cells(sheet, tiles, 0)
-    for copy in copies:
+    for copy in copies[:3]:
         copy.wait()
     lane = lax.broadcasted_iota(jnp.int32, (24, 256), 1)
     quad_of = (lane & 31) >> 2
@@ -210,10 +218,12 @@
             select[:, which * 256 : which * 256 + 256],
         )
         ab_ref[which] = (both[:576] + both[576:]).reshape(24, 24, 256)
+    for copy in copies[3:]:
+        copy.wait()
 
 
 def build_w(ab_ref, level, w_ref):
-    def one_quad(quad, carry):
+    def one_quad(quad):
         at = level * QUADS + quad
         inner = [ab_ref[1, at, ez * 8 : ez * 8 + 8, :] for ez in range(3)]
         for ey in range(3):
@@ -225,11 +235,11 @@
                     tile = jnp.concatenate([first * inner[ez], second * inner[ez]], axis=0)
                     e = ey * 3 + ez
                     to = quad * 512 + e * PLANE if e < 8 else 4096 + quad * PLANE
-                    to = pl.multiple_of(to + pair * 16, 16)
-                    w_ref[pl.ds(to, 16), :] = tile.astype(BF16)
-        return carry
-
-    lax.fori_loop(0, QUADS, one_quad, 0)
+                    to += pair * 16
+                    w_ref[to : to + 16, :] = tile.astype(BF16)
+
+    for quad in range(QUADS):
+        one_quad(quad)
 
 
 def spread_cells(sheet, tiles, at):
@@ -461,18 +471,11 @@
 
 
 def last_kernel(
-    numbers_h, names_h, planes, mid_tiles, direct, ab_ref, x_ref, rows_h, filters_h, mids_h,
+    numbers_h, names_h, planes, mid_tiles, direct, ab_ref, x_ref, rows_p, filters, mids,
     fine_out, mid_out,
-    coarse, back, rows_p, filters, mids, sems, w_mid, w_coarse, numbers, names,
+    coarse, back, sems, w_mid, w_coarse, numbers, names,
 ):
-    copies = fetches(
-        sems,
-        (numbers_h, numbers),
-        (names_h, names),
-        (rows_h, rows_p),
-        (filters_h, filters),
-        (mids_h, mids),
-    )
+    copies = fetches(sems, (numbers_h, numbers), (names_h, names))
     build_w(ab_ref, 1, w_mid)
     build_w(ab_ref, 2, w_coarse)
     low8 = low_lanes((8, 128))
@@ -646,22 +649,25 @@
     )
     planes = lax.all_to_all(copies, "gx", 0, 0, tiled=True)
 
-    w_factors, x_tables, centre = call(
+    w_factors, x_tables, centre, rows_p, last_filters, mids = call(
         tables_kernel,
-        "hhhv",
+        "hhhvhhh",
         [
             pltpu.VMEM((2, 3 * QUADS, 24, 256), F32),
             pltpu.VMEM((3, 256, 24), BF16),
             pltpu.VMEM((90, 8, 128), F32),
+            pltpu.VMEM((16, 8, 128), F32),
+            pltpu.VMEM((512, 128), BF16),
+            pltpu.VMEM((128, 1024), BF16),
         ],
         [
             vmem((3, 192, TERMS), F32),
             vmem((1, TERMS), F32),
             vmem((256, 768), BF16),
-            pltpu.SemaphoreType.DMA((3,)),
+            pltpu.SemaphoreType.DMA((6,)),
         ],
         600_000_000,
-        factors, term_weight.reshape(1, TERMS), select, sheet,
+        factors, term_weight.reshape(1, TERMS), select, sheet, rows_p, last_filters, mids,
     )
     direct, mid_tiles, names = call(
         fine_kernel,
@@ -679,15 +685,12 @@
     )
     fine_out, mid_out = call(
         last_kernel,
-        "aavvvwwhhh",
+        "aavvvwwwww",
         [sds((8, 512), F32), sds((1, 512), F32)],
         [
             vmem((65, 8, 128), F32),
             vmem((8, 8, PLANE), F32),
-            vmem((16, 8, 128), F32),
-            vmem((512, 128), BF16),
-            vmem((128, 1024), BF16),
-            pltpu.SemaphoreType.DMA((5,)),
+            pltpu.SemaphoreType.DMA((2,)),
             vmem((ROWS_W, 256), BF16),
             vmem((ROWS_W, 256), BF16),
             smem((16, 128), i32),

time: 64.1 us -> 63.7 us (level)
  transfers between devices with their start and end apart: 8 -> 8, of which waited for: 2 -> 2; matrix products, arithmetic and copies ran while one was open for 0% -> 0% of each run, Pallas kernels for 8% -> 9%
where the time goes in v9:
time: 63.7 us; the launch traced here: 63.3 us
  starting transfers between devices  40.4 us (63%)
  Pallas kernels  11.2 us (18%)
  waiting for transfers between devices  9.66 us (15%)
  between operations  2.08 us (3%)
    all_to_all x1, starting transfers between devices, shards(): arrived = lax.all_to_all(payload, ('gy', 'gz'), 0, 0, tiled=True)  18.3 us
    pallas_call x5, Pallas kernels, call(): pl.pallas_call(kernel, out_shape=outs, in_specs=[specs[kind] for kind in...  11.2 us
    ppermute x3, starting transfers between devices, both_ways(): before = lax.ppermute(x, axis, [(i, i + 1) for i in range(ends)])  10.5 us
    all_to_all x1, waiting for transfers between devices, shards(): arrived = lax.all_to_all(payload, ('gy', 'gz'), 0, 0, tiled=True)  7.23 us
    all_to_all x1, starting transfers between devices, shards(): planes = lax.all_to_all(copies, 'gx', 0, 0, tiled=True)  7.04 us
    ppermute x3, starting transfers between devices, both_ways(): after = lax.ppermute(x, axis, [(i + 1, i) for i in range(ends)])  4.5 us
    ppermute x3, waiting for transfers between devices, both_ways(): after = lax.ppermute(x, axis, [(i + 1, i) for i in range(ends)])  2.4 us
  transfers between devices with their start and end apart: 8, of which 2 were waited for; matrix products, arithmetic and copies ran while one was open for 0% of the time, Pallas kernels for 9%

profile of v9, /device:TPU:1, one launch (start us, length us, event | category | flops | bytes accessed | tf_op | source)
XLA Modules:
  0.0 63.3 jit_solution(11880033131387405485)
XLA Ops:
  1.9 2.4 %first_kernel.1 = (bf16[40,128]{1,0:T(8,128)(2,1)S(1)}, bf16[64,8,128]{2,1,0:T(8,128)(2,1)}, s32[16,128]{1,0:T(8,128)S(1)}) custom-call(s32[1]{0:T(128)S(6)} %copy.24.parent, s32[1]{0:T(128)S(6)} %copy.25.refined, s32[1,8]{1,0:T(1,128)} %child_h.1, s32[8,27]{1,0:T(8,128)} %fine_h.1, s32[1,27]{1,0:T(1,128)} %mid_h.1, s32[27,64]{1,0:T(8,128)} %bitcast.5, ...), custom_call_target="tpu_custom_call" | custom-call | flops 2000000 | bytes 494324 | tf_op jit(solution)/shard_map/first_kernel/pallas_call | solution.py:575
  4.4 4.0 %collective-permute-start = (bf16[40,128]{1,0:T(8,128)(2,1)S(1)}, bf16[40,128]{1,0:T(8,128)(2,1)S(1)}, u32[]{:S(2)}, u32[]{:S(2)}) collective-permute-start(bf16[40,128]{1,0:T(8,128)(2,1)S(1)} %get-tuple-element.15), channel_id=1, source_target_pairs={{0,1},{1,2},{2,3},{3,4},{4,5},{5,6},{6,7},{8,9},{9,10},{10,11},{11... | collective-permute-start | bytes 30728 | tf_op jit(solution)/shard_map/ppermute | solution.py:590
  8.4 1.3 %collective-permute-start.1 = (bf16[40,128]{1,0:T(8,128)(2,1)S(1)}, bf16[40,128]{1,0:T(8,128)(2,1)S(1)}, u32[]{:S(2)}, u32[]{:S(2)}) collective-permute-start(bf16[40,128]{1,0:T(8,128)(2,1)S(1)} %get-tuple-element.15), channel_id=1, source_target_pairs={{1,0},{2,1},{3,2},{4,3},{5,4},{6,5},{7,6},{9,8},{10,9},{11,10},{12... | collective-permute-start | bytes 30728 | tf_op jit(solution)/shard_map/ppermute | solution.py:591
  9.7 18.3 %all-to-all-start = ((bf16[64,8,128]{2,1,0:T(8,128)(2,1)}), bf16[64,8,128]{2,1,0:T(8,128)(2,1)S(1)}, u32[]{:S(2)}, u32[]{:S(2)}) async-start(bf16[64,8,128]{2,1,0:T(8,128)(2,1)} %get-tuple-element.20), calls=%async_computation | async-start | bytes 262144 | tf_op jit(solution)/shard_map/all_to_all | solution.py:639
  28.0 0.0 collective-permute-done
  28.1 0.0 collective-permute-done.1
  28.1 2.9 %collective-permute-start.2 = (bf16[120,128]{1,0:T(8,128)(2,1)S(1)}, bf16[120,128]{1,0:T(8,128)(2,1)S(1)}, u32[]{:S(2)}, u32[]{:S(2)}) collective-permute-start(bf16[120,128]{1,0:T(8,128)(2,1)S(1)} %constant_dynamic-update-slice_fusion), channel_id=1, source_target_pairs={{0,8},{8,16},{16,24},{24,32},{32,40},{40,48},{48,56},{1,9},{9,17},... | collective-permute-start | bytes 92168 | tf_op jit(solution)/shard_map/ppermute | solution.py:590
  31.0 1.3 %collective-permute-start.3 = (bf16[120,128]{1,0:T(8,128)(2,1)S(1)}, bf16[120,128]{1,0:T(8,128)(2,1)S(1)}, u32[]{:S(2)}, u32[]{:S(2)}) collective-permute-start(bf16[120,128]{1,0:T(8,128)(2,1)S(1)} %constant_dynamic-update-slice_fusion), channel_id=1, source_target_pairs={{8,0},{16,8},{24,16},{32,24},{40,32},{48,40},{56,48},{9,1},{17,9},... | collective-permute-start | bytes 92168 | tf_op jit(solution)/shard_map/ppermute | solution.py:591
  32.3 0.0 collective-permute-done.2
  32.4 7.2 %all-to-all-done.arrived = bf16[64,8,128]{2,1,0:T(8,128)(2,1)S(1)} async-done(((bf16[64,8,128]{2,1,0:T(8,128)(2,1)}), bf16[64,8,128]{2,1,0:T(8,128)(2,1)S(1)}, u32[]{:S(2)}, u32[]{:S(2)}) %all-to-all-start) | async-done | bytes 131104 | tf_op jit(solution)/shard_map/all_to_all | solution.py:639
  39.6 1.3 %plane_kernel.1 = bf16[8,256,128]{2,1,0:T(8,128)(2,1)} custom-call(bf16[64,8,128]{2,1,0:T(8,128)(2,1)S(1)} %all-to-all-done.arrived), custom_call_target="tpu_custom_call" | custom-call | flops 33000000 | bytes 655360 | tf_op jit(solution)/shard_map/plane_kernel/pallas_call | solution.py:575
  40.9 7.0 %all-to-all-start.1 = ((bf16[8,256,128]{2,1,0:T(8,128)(2,1)}), bf16[8,256,128]{2,1,0:T(8,128)(2,1)S(1)}, u32[]{:S(2)}, u32[]{:S(2)}) async-start(bf16[8,256,128]{2,1,0:T(8,128)(2,1)} %plane_kernel.1), calls=%async_computation.1 | async-start | bytes 1048576 | tf_op jit(solution)/shard_map/all_to_all | solution.py:650
  48.0 0.0 collective-permute-done.3
  48.0 3.5 %collective-permute-start.4 = (bf16[360,128]{1,0:T(8,128)(2,1)S(1)}, bf16[360,128]{1,0:T(8,128)(2,1)S(1)}, u32[]{:S(2)}, u32[]{:S(2)}) collective-permute-start(bf16[360,128]{1,0:T(8,128)(2,1)S(1)} %constant_dynamic-update-slice_fusion.3.sheet), channel_id=1, source_target_pairs={{0,64},{64,128},{128,192},{192,256},{256,320},{320,384},{384,448},... | collective-permute-start | bytes 276488 | tf_op jit(solution)/shard_map/ppermute | solution.py:590
  51.5 1.9 %collective-permute-start.5 = (bf16[360,128]{1,0:T(8,128)(2,1)S(1)}, bf16[360,128]{1,0:T(8,128)(2,1)S(1)}, u32[]{:S(2)}, u32[]{:S(2)}) collective-permute-start(bf16[360,128]{1,0:T(8,128)(2,1)S(1)} %constant_dynamic-update-slice_fusion.3.sheet), channel_id=1, source_target_pairs={{64,0},{128,64},{192,128},{256,192},{320,256},{384,320},{448,384},... | collective-permute-start | bytes 276488 | tf_op jit(solution)/shard_map/ppermute | solution.py:591
  53.5 1.8 %tables_kernel.1 = (f32[2,24,24,256]{3,2,1,0:T(8,128)S(1)}, bf16[3,256,24]{2,1,0:T(8,128)(2,1)S(1)}, f32[90,8,128]{2,1,0:T(8,128)S(1)}, f32[16,8,128]{2,1,0:T(8,...) custom-call(f32[3,192,32]{2,1,0:T(8,128)} %bitcast.6, f32[1,32]{1,0:T(1,128)} %bitcast.7, ...), custom_call_target="tpu_custom_call" | custom-call | flops 600000000 | bytes 3061888 | tf_op jit(solution)/shard_map/tables_kernel/pallas_call | solution.py:575
  55.3 0.0 collective-permute-done.4.left
  55.3 2.4 %collective-permute-done.5.right = bf16[360,128]{1,0:T(8,128)(2,1)S(1)} collective-permute-done((bf16[360,128]{1,0:T(8,128)(2,1)S(1)}, bf16[360,128]{1,0:T(8,128)(2,1)S(1)}, u32[]{:S(2)}, u32[]{:S(2)}) %collective-permute-start.5) | collective-permute-done | bytes 92192 | tf_op jit(solution)/shard_map/ppermute | solution.py:591
  57.7 2.3 %fine_kernel.1 = (f32[8,8,64]{2,1,0:T(8,128)S(1)}, f32[28,8,128]{2,1,0:T(8,128)S(1)}, s32[1,128]{1,0:T(1,128)S(1)}) custom-call(s32[16,128]{1,0:T(8,128)S(1)} %get-tuple-element.14.numbers_h, bf16[360,128]{1,0:T(8,128)(2,1)S(1)} %collective-permute-done.4.left, f32[90,8,128]{2,1,0:T(8,128)S(1)} %get-tuple-element.16.centre, ...), custom_call_target="tpu_custom_call" | custom-call | flops 100000000 | bytes 1909248 | tf_op jit(solution)/shard_map/fine_kernel/pallas_call | solution.py:575
  60.0 0.0 all-to-all-done.1.planes
  60.0 3.3 %last_kernel.1 = (f32[8,512]{1,0:T(8,128)}, f32[1,512]{1,0:T(1,128)}) custom-call(s32[16,128]{1,0:T(8,128)S(1)} %get-tuple-element.14.numbers_h, s32[1,128]{1,0:T(1,128)S(1)} %get-tuple-element.19.names_h, bf16[8,256,128]{2,1,0:T(8,128)(2,1)S(1)} %all-to-all-done.1.planes, f32[28,8,128]{2,1,0:T(8,128)S(1)} %get-tuple-element.21.mid_tiles, ...), custom_call_target="tpu_custom_call" | custom-call | flops 200000000 | bytes 2357760 | tf_op jit(solution)/shard_map/last_kernel/pallas_call | solution.py:575
  (8 shorter events, 0.1 us)
Async XLA Ops:
  4.4 23.7 %collective-permute-start = (bf16[40,128]{1,0:T(8,128)(2,1)S(1)}, bf16[40,128]{1,0:T(8,128)(2,1)S(1)}, u32[]{:S(2)}, u32[]{:S(2)}) collective-permute-start(bf16[40,128]{1,0:T(8,128)(2,1)S(1)} %get-tuple-element.15), channel_id=1, source_target_pairs={{0,1},{1,2},{2,3},{3,4},{4,5},{5,6},{6,7},{8,9},{9,10},{10,11},{11... | collective-permute-start | bytes 30728 | tf_op jit(solution)/shard_map/ppermute | solution.py:590
  8.4 19.7 %collective-permute-start.1 = (bf16[40,128]{1,0:T(8,128)(2,1)S(1)}, bf16[40,128]{1,0:T(8,128)(2,1)S(1)}, u32[]{:S(2)}, u32[]{:S(2)}) collective-permute-start(bf16[40,128]{1,0:T(8,128)(2,1)S(1)} %get-tuple-element.15), channel_id=1, source_target_pairs={{1,0},{2,1},{3,2},{4,3},{5,4},{6,5},{7,6},{9,8},{10,9},{11,10},{12... | collective-permute-start | bytes 30728 | tf_op jit(solution)/shard_map/ppermute | solution.py:591
  9.7 29.9 %all-to-all-start = ((bf16[64,8,128]{2,1,0:T(8,128)(2,1)}), bf16[64,8,128]{2,1,0:T(8,128)(2,1)S(1)}, u32[]{:S(2)}, u32[]{:S(2)}) async-start(bf16[64,8,128]{2,1,0:T(8,128)(2,1)} %get-tuple-element.20), calls=%async_computation | async-start | bytes 262144 | tf_op jit(solution)/shard_map/all_to_all | solution.py:639
  28.1 4.2 %collective-permute-start.2 = (bf16[120,128]{1,0:T(8,128)(2,1)S(1)}, bf16[120,128]{1,0:T(8,128)(2,1)S(1)}, u32[]{:S(2)}, u32[]{:S(2)}) collective-permute-start(bf16[120,128]{1,0:T(8,128)(2,1)S(1)} %constant_dynamic-update-slice_fusion), channel_id=1, source_target_pairs={{0,8},{8,16},{16,24},{24,32},{32,40},{40,48},{48,56},{1,9},{9,17},... | collective-permute-start | bytes 92168 | tf_op jit(solution)/shard_map/ppermute | solution.py:590
  31.0 16.9 %collective-permute-start.3 = (bf16[120,128]{1,0:T(8,128)(2,1)S(1)}, bf16[120,128]{1,0:T(8,128)(2,1)S(1)}, u32[]{:S(2)}, u32[]{:S(2)}) collective-permute-start(bf16[120,128]{1,0:T(8,128)(2,1)S(1)} %constant_dynamic-update-slice_fusion), channel_id=1, source_target_pairs={{8,0},{16,8},{24,16},{32,24},{40,32},{48,40},{56,48},{9,1},{17,9},... | collective-permute-start | bytes 92168 | tf_op jit(solution)/shard_map/ppermute | solution.py:591
  40.9 19.1 %all-to-all-start.1 = ((bf16[8,256,128]{2,1,0:T(8,128)(2,1)}), bf16[8,256,128]{2,1,0:T(8,128)(2,1)S(1)}, u32[]{:S(2)}, u32[]{:S(2)}) async-start(bf16[8,256,128]{2,1,0:T(8,128)(2,1)} %plane_kernel.1), calls=%async_computation.1 | async-start | bytes 1048576 | tf_op jit(solution)/shard_map/all_to_all | solution.py:650
  48.0 7.3 %collective-permute-start.4 = (bf16[360,128]{1,0:T(8,128)(2,1)S(1)}, bf16[360,128]{1,0:T(8,128)(2,1)S(1)}, u32[]{:S(2)}, u32[]{:S(2)}) collective-permute-start(bf16[360,128]{1,0:T(8,128)(2,1)S(1)} %constant_dynamic-update-slice_fusion.3.sheet), channel_id=1, source_target_pairs={{0,64},{64,128},{128,192},{192,256},{256,320},{320,384},{384,448},... | collective-permute-start | bytes 276488 | tf_op jit(solution)/shard_map/ppermute | solution.py:590
  51.5 6.2 %collective-permute-start.5 = (bf16[360,128]{1,0:T(8,128)(2,1)S(1)}, bf16[360,128]{1,0:T(8,128)(2,1)S(1)}, u32[]{:S(2)}, u32[]{:S(2)}) collective-permute-start(bf16[360,128]{1,0:T(8,128)(2,1)S(1)} %constant_dynamic-update-slice_fusion.3.sheet), channel_id=1, source_target_pairs={{64,0},{128,64},{192,128},{256,192},{320,256},{384,320},{448,384},... | collective-permute-start | bytes 276488 | tf_op jit(solution)/shard_map/ppermute | solution.py:591

commit v10 on v9

--- a/solution.py
+++ b/solution.py
@@ -271,7 +271,13 @@
     for quad in range(0, QUADS, 2):
         both = jnp.where(low, groups[quad][:, 512:], groups[quad + 1][:, 512:])
         pieces.append(both.astype(BF16))
-    result = dot(jnp.concatenate(pieces, axis=1), w_ref[...])
+    result = None
+    for quad in range(QUADS):
+        part = dot(pieces[quad], w_ref[quad * 512 : quad * 512 + 512, :])
+        result = part if result is None else result + part
+    for pair in range(4):
+        at = 4096 + pair * 128
+        result += dot(pieces[QUADS + pair], w_ref[at : at + 128, :])
     return diagonal_sum(result, 8)
 
 
@@ -279,15 +285,21 @@
     parent, refined, child_h, fine_h, mid_h, coarse_h, coef_h, leaf_h, filters_h, rows_h,
     halo, payload, numbers,
     child, child_v, fine_nbr, mid_nbr, coarse_nbr, coef, leaf, filters, rows,
-    source, detail, sems, payload_v, payload_sem,
+    source, detail, sems, payload_v, payload_sem, contrib,
 ):
+    slot = parent[0] >> 3
+    octant = parent[0] & 7
+    contrib_at = pl.multiple_of(512 + (octant & 3) * 64, 64)
     copies = fetches(
         sems,
         (child_h, child),
         (coef_h, coef),
-        (filters_h, filters),
-        (rows_h, rows),
+        (filters_h.at[pl.ds(0, 256)], filters.at[pl.ds(0, 256)]),
+        (rows_h.at[pl.ds(0, 16)], rows.at[pl.ds(0, 16)]),
         (leaf_h, leaf),
+        (filters_h.at[pl.ds(contrib_at, 64)], contrib),
+        (filters_h.at[pl.ds(256, 256)], filters.at[pl.ds(256, 256)]),
+        (rows_h.at[pl.ds(16, 16)], rows.at[pl.ds(16, 16)]),
         (child_h, child_v),
         (fine_h, fine_nbr),
         (mid_h, mid_nbr),
@@ -296,9 +308,6 @@
     for copy in copies[:5]:
         copy.wait()
     comp = filters[0:256, :]
-    prol = jnp.concatenate([filters[256 + 64 * k : 320 + 64 * k, :] for k in range(4)], axis=1)
-    slot = parent[0] >> 3
-    octant = parent[0] & 7
 
     values = coef[...].astype(F32)
     for a in range(8):
@@ -321,8 +330,8 @@
 
     row_at = (octant >> 2) * 8
     inner = row_mix([rows[row_at + x, :, :PLANE] for x in range(8)], middle)
-    table = filters[pl.ds(pl.multiple_of(512 + (octant & 3) * 64, 64), 64), :]
-    added = fine_dot(inner, table)
+    copies[5].wait()
+    added = fine_dot(inner, contrib[...])
     low8 = low_lanes((8, 128))
     tag = jnp.full((8, 128), slot, jnp.int32).astype(F32)
     tile = jnp.where(low8, jnp.concatenate([added, added], axis=1), tag).astype(BF16)
@@ -330,6 +339,9 @@
     send = pltpu.make_async_copy(payload_v, payload, payload_sem)
     send.start()
 
+    for copy in copies[6:8]:
+        copy.wait()
+    prol = jnp.concatenate([filters[256 + 64 * k : 320 + 64 * k, :] for k in range(4)], axis=1)
     live = jnp.full((8, PLANE), refined[0], jnp.int32).astype(F32)
     upper = jnp.concatenate(two_row_mixes(rows.at[16:32], middle, PLANE), axis=0)
     spread = fine_dot(upper, prol)
@@ -343,7 +355,7 @@
     pairs.append(jnp.where(low8, jnp.concatenate([middle, middle], axis=1), name))
     halo[...] = jnp.concatenate(pairs, axis=0).astype(BF16)
 
-    for copy in copies[5:]:
+    for copy in copies[8:]:
         copy.wait()
     near = fine_nbr[...]
     own = near[:, 13:14] >> 3
@@ -494,24 +506,6 @@
         copy.wait()
     octant = numbers[10, 8] & 7
 
-    def coarse_source(ex, e):
-        return coarse[numbers[9, ex * 9 + e]]
-
-    sources = jnp.concatenate(
-        [
-            jnp.concatenate(
-                [
-                    pair_of(coarse_source(ex, 2 * ep), coarse_source(ex, min(2 * ep + 1, 8)))
-                    for ex in range(3)
-                ],
-                axis=0,
-            ).astype(BF16)
-            for ep in range(5)
-        ],
-        axis=1,
-    )
-    coarse_result = apply_one(sources, x_ref[2], w_coarse)
-
     uppers, octants, owns = [], [], []
     for ep in range(5):
         for ex in range(3):
@@ -543,6 +537,24 @@
         pieces.append(jnp.concatenate(tiles, axis=0).astype(BF16))
     mid_result = apply_one(jnp.concatenate(pieces, axis=1), x_ref[1], w_mid)
 
+    def coarse_source(ex, e):
+        return coarse[numbers[9, ex * 9 + e]]
+
+    sources = jnp.concatenate(
+        [
+            jnp.concatenate(
+                [
+                    pair_of(coarse_source(ex, 2 * ep), coarse_source(ex, min(2 * ep + 1, 8)))
+                    for ex in range(3)
+                ],
+                axis=0,
+            ).astype(BF16)
+            for ep in range(5)
+        ],
+        axis=1,
+    )
+    coarse_result = apply_one(sources, x_ref[2], w_coarse)
+
     row_at = (octant >> 2) * 8
     upper = row_mix([rows_p[row_at + p, :, :PLANE] for p in range(8)], coarse_result)
     single = filters[pl.ds(pl.multiple_of(256 + (octant & 3) * 64, 64), 64), :]
@@ -624,13 +636,14 @@
             vmem((27, 64), i32),
             vmem((8, 512), BF16),
             vmem((1, 512), BF16),
-            vmem((768, 128), BF16),
+            vmem((512, 128), BF16),
             vmem((32, 8, 128), F32),
             vmem((8, 8, PLANE), F32),
             vmem((8, 8, PLANE), F32),
-            pltpu.SemaphoreType.DMA((9,)),
+            pltpu.SemaphoreType.DMA((12,)),
             vmem((64, 8, 128), BF16),
             pltpu.SemaphoreType.DMA,
+            vmem((64, 128), BF16),
         ],
         2_000_000,
         mid_parent, mid_refined, mid_child, fine_nbr, mid_nbr, coarse_nbr.T, fine_coef, mid_leaf,

time: 63.7 us -> 63.6 us (level)
  no operation moved by 1% of the time
where the time goes in v10:
time: 63.6 us; the launch traced here: 63.1 us
  starting transfers between devices  40.3 us (63%)
  Pallas kernels  11 us (17%)
  waiting for transfers between devices  9.66 us (15%)
  between operations  2.08 us (3%)
    all_to_all x1, starting transfers between devices, shards(): arrived = lax.all_to_all(payload, ('gy', 'gz'), 0, 0, tiled=True)  18.3 us
    pallas_call x5, Pallas kernels, call(): pl.pallas_call(kernel, out_shape=outs, in_specs=[specs[kind] for kind in...  11 us
    ppermute x3, starting transfers between devices, both_ways(): before = lax.ppermute(x, axis, [(i, i + 1) for i in range(ends)])  10.5 us
    all_to_all x1, waiting for transfers between devices, shards(): arrived = lax.all_to_all(payload, ('gy', 'gz'), 0, 0, tiled=True)  7.23 us
    all_to_all x1, starting transfers between devices, shards(): planes = lax.all_to_all(copies, 'gx', 0, 0, tiled=True)  7.04 us
    ppermute x3, starting transfers between devices, both_ways(): after = lax.ppermute(x, axis, [(i + 1, i) for i in range(ends)])  4.5 us
    ppermute x3, waiting for transfers between devices, both_ways(): after = lax.ppermute(x, axis, [(i + 1, i) for i in range(ends)])  2.4 us
  transfers between devices with their start and end apart: 8, of which 2 were waited for; matrix products, arithmetic and copies ran while one was open for 0% of the time, Pallas kernels for 9%

profile of v10, /device:TPU:1, one launch (start us, length us, event | category | flops | bytes accessed | tf_op | source)
XLA Modules:
  0.0 63.1 jit_solution(5713479797620211189)
XLA Ops:
  1.9 2.3 %first_kernel.1 = (bf16[40,128]{1,0:T(8,128)(2,1)S(1)}, bf16[64,8,128]{2,1,0:T(8,128)(2,1)}, s32[16,128]{1,0:T(8,128)S(1)}) custom-call(s32[1]{0:T(128)S(6)} %copy.24.parent, s32[1]{0:T(128)S(6)} %copy.25.refined, s32[1,8]{1,0:T(1,128)} %child_h.1, s32[8,27]{1,0:T(8,128)} %fine_h.1, s32[1,27]{1,0:T(1,128)} %mid_h.1, s32[27,64]{1,0:T(8,128)} %bitcast.5, ...), custom_call_target="tpu_custom_call" | custom-call | flops 2000000 | bytes 494324 | tf_op jit(solution)/shard_map/first_kernel/pallas_call | solution.py:587
  4.3 4.0 %collective-permute-start = (bf16[40,128]{1,0:T(8,128)(2,1)S(1)}, bf16[40,128]{1,0:T(8,128)(2,1)S(1)}, u32[]{:S(2)}, u32[]{:S(2)}) collective-permute-start(bf16[40,128]{1,0:T(8,128)(2,1)S(1)} %get-tuple-element.15), channel_id=1, source_target_pairs={{0,1},{1,2},{2,3},{3,4},{4,5},{5,6},{6,7},{8,9},{9,10},{10,11},{11... | collective-permute-start | bytes 30728 | tf_op jit(solution)/shard_map/ppermute | solution.py:602
  8.3 1.3 %collective-permute-start.1 = (bf16[40,128]{1,0:T(8,128)(2,1)S(1)}, bf16[40,128]{1,0:T(8,128)(2,1)S(1)}, u32[]{:S(2)}, u32[]{:S(2)}) collective-permute-start(bf16[40,128]{1,0:T(8,128)(2,1)S(1)} %get-tuple-element.15), channel_id=1, source_target_pairs={{1,0},{2,1},{3,2},{4,3},{5,4},{6,5},{7,6},{9,8},{10,9},{11,10},{12... | collective-permute-start | bytes 30728 | tf_op jit(solution)/shard_map/ppermute | solution.py:603
  9.6 18.3 %all-to-all-start = ((bf16[64,8,128]{2,1,0:T(8,128)(2,1)}), bf16[64,8,128]{2,1,0:T(8,128)(2,1)S(1)}, u32[]{:S(2)}, u32[]{:S(2)}) async-start(bf16[64,8,128]{2,1,0:T(8,128)(2,1)} %get-tuple-element.20), calls=%async_computation | async-start | bytes 262144 | tf_op jit(solution)/shard_map/all_to_all | solution.py:652
  27.9 0.0 collective-permute-done
  28.0 0.0 collective-permute-done.1
  28.0 2.9 %collective-permute-start.2 = (bf16[120,128]{1,0:T(8,128)(2,1)S(1)}, bf16[120,128]{1,0:T(8,128)(2,1)S(1)}, u32[]{:S(2)}, u32[]{:S(2)}) collective-permute-start(bf16[120,128]{1,0:T(8,128)(2,1)S(1)} %constant_dynamic-update-slice_fusion), channel_id=1, source_target_pairs={{0,8},{8,16},{16,24},{24,32},{32,40},{40,48},{48,56},{1,9},{9,17},... | collective-permute-start | bytes 92168 | tf_op jit(solution)/shard_map/ppermute | solution.py:602
  30.9 1.3 %collective-permute-start.3 = (bf16[120,128]{1,0:T(8,128)(2,1)S(1)}, bf16[120,128]{1,0:T(8,128)(2,1)S(1)}, u32[]{:S(2)}, u32[]{:S(2)}) collective-permute-start(bf16[120,128]{1,0:T(8,128)(2,1)S(1)} %constant_dynamic-update-slice_fusion), channel_id=1, source_target_pairs={{8,0},{16,8},{24,16},{32,24},{40,32},{48,40},{56,48},{9,1},{17,9},... | collective-permute-start | bytes 92168 | tf_op jit(solution)/shard_map/ppermute | solution.py:603
  32.2 0.0 collective-permute-done.2
  32.2 7.2 %all-to-all-done.arrived = bf16[64,8,128]{2,1,0:T(8,128)(2,1)S(1)} async-done(((bf16[64,8,128]{2,1,0:T(8,128)(2,1)}), bf16[64,8,128]{2,1,0:T(8,128)(2,1)S(1)}, u32[]{:S(2)}, u32[]{:S(2)}) %all-to-all-start) | async-done | bytes 131104 | tf_op jit(solution)/shard_map/all_to_all | solution.py:652
  39.5 1.3 %plane_kernel.1 = bf16[8,256,128]{2,1,0:T(8,128)(2,1)} custom-call(bf16[64,8,128]{2,1,0:T(8,128)(2,1)S(1)} %all-to-all-done.arrived), custom_call_target="tpu_custom_call" | custom-call | flops 33000000 | bytes 655360 | tf_op jit(solution)/shard_map/plane_kernel/pallas_call | solution.py:587
  40.8 7.0 %all-to-all-start.1 = ((bf16[8,256,128]{2,1,0:T(8,128)(2,1)}), bf16[8,256,128]{2,1,0:T(8,128)(2,1)S(1)}, u32[]{:S(2)}, u32[]{:S(2)}) async-start(bf16[8,256,128]{2,1,0:T(8,128)(2,1)} %plane_kernel.1), calls=%async_computation.1 | async-start | bytes 1048576 | tf_op jit(solution)/shard_map/all_to_all | solution.py:663
  47.8 0.0 collective-permute-done.3
  47.9 3.5 %collective-permute-start.4 = (bf16[360,128]{1,0:T(8,128)(2,1)S(1)}, bf16[360,128]{1,0:T(8,128)(2,1)S(1)}, u32[]{:S(2)}, u32[]{:S(2)}) collective-permute-start(bf16[360,128]{1,0:T(8,128)(2,1)S(1)} %constant_dynamic-update-slice_fusion.3.sheet), channel_id=1, source_target_pairs={{0,64},{64,128},{128,192},{192,256},{256,320},{320,384},{384,448},... | collective-permute-start | bytes 276488 | tf_op jit(solution)/shard_map/ppermute | solution.py:602
  51.4 1.9 %collective-permute-start.5 = (bf16[360,128]{1,0:T(8,128)(2,1)S(1)}, bf16[360,128]{1,0:T(8,128)(2,1)S(1)}, u32[]{:S(2)}, u32[]{:S(2)}) collective-permute-start(bf16[360,128]{1,0:T(8,128)(2,1)S(1)} %constant_dynamic-update-slice_fusion.3.sheet), channel_id=1, source_target_pairs={{64,0},{128,64},{192,128},{256,192},{320,256},{384,320},{448,384},... | collective-permute-start | bytes 276488 | tf_op jit(solution)/shard_map/ppermute | solution.py:603
  53.3 1.8 %tables_kernel.1 = (f32[2,24,24,256]{3,2,1,0:T(8,128)S(1)}, bf16[3,256,24]{2,1,0:T(8,128)(2,1)S(1)}, f32[90,8,128]{2,1,0:T(8,128)S(1)}, f32[16,8,128]{2,1,0:T(8,...) custom-call(f32[3,192,32]{2,1,0:T(8,128)} %bitcast.6, f32[1,32]{1,0:T(1,128)} %bitcast.7, ...), custom_call_target="tpu_custom_call" | custom-call | flops 600000000 | bytes 3061888 | tf_op jit(solution)/shard_map/tables_kernel/pallas_call | solution.py:587
  55.2 0.0 collective-permute-done.4.left
  55.2 2.4 %collective-permute-done.5.right = bf16[360,128]{1,0:T(8,128)(2,1)S(1)} collective-permute-done((bf16[360,128]{1,0:T(8,128)(2,1)S(1)}, bf16[360,128]{1,0:T(8,128)(2,1)S(1)}, u32[]{:S(2)}, u32[]{:S(2)}) %collective-permute-start.5) | collective-permute-done | bytes 92192 | tf_op jit(solution)/shard_map/ppermute | solution.py:603
  57.6 2.3 %fine_kernel.1 = (f32[8,8,64]{2,1,0:T(8,128)S(1)}, f32[28,8,128]{2,1,0:T(8,128)S(1)}, s32[1,128]{1,0:T(1,128)S(1)}) custom-call(s32[16,128]{1,0:T(8,128)S(1)} %get-tuple-element.14.numbers_h, bf16[360,128]{1,0:T(8,128)(2,1)S(1)} %collective-permute-done.4.left, f32[90,8,128]{2,1,0:T(8,128)S(1)} %get-tuple-element.16.centre, ...), custom_call_target="tpu_custom_call" | custom-call | flops 100000000 | bytes 1909248 | tf_op jit(solution)/shard_map/fine_kernel/pallas_call | solution.py:587
  59.9 0.0 all-to-all-done.1.planes
  59.9 3.2 %last_kernel.1 = (f32[8,512]{1,0:T(8,128)}, f32[1,512]{1,0:T(1,128)}) custom-call(s32[16,128]{1,0:T(8,128)S(1)} %get-tuple-element.14.numbers_h, s32[1,128]{1,0:T(1,128)S(1)} %get-tuple-element.19.names_h, bf16[8,256,128]{2,1,0:T(8,128)(2,1)S(1)} %all-to-all-done.1.planes, f32[28,8,128]{2,1,0:T(8,128)S(1)} %get-tuple-element.21.mid_tiles, ...), custom_call_target="tpu_custom_call" | custom-call | flops 200000000 | bytes 2357760 | tf_op jit(solution)/shard_map/last_kernel/pallas_call | solution.py:587
  (8 shorter events, 0.1 us)
Async XLA Ops:
  4.3 23.7 %collective-permute-start = (bf16[40,128]{1,0:T(8,128)(2,1)S(1)}, bf16[40,128]{1,0:T(8,128)(2,1)S(1)}, u32[]{:S(2)}, u32[]{:S(2)}) collective-permute-start(bf16[40,128]{1,0:T(8,128)(2,1)S(1)} %get-tuple-element.15), channel_id=1, source_target_pairs={{0,1},{1,2},{2,3},{3,4},{4,5},{5,6},{6,7},{8,9},{9,10},{10,11},{11... | collective-permute-start | bytes 30728 | tf_op jit(solution)/shard_map/ppermute | solution.py:602
  8.3 19.7 %collective-permute-start.1 = (bf16[40,128]{1,0:T(8,128)(2,1)S(1)}, bf16[40,128]{1,0:T(8,128)(2,1)S(1)}, u32[]{:S(2)}, u32[]{:S(2)}) collective-permute-start(bf16[40,128]{1,0:T(8,128)(2,1)S(1)} %get-tuple-element.15), channel_id=1, source_target_pairs={{1,0},{2,1},{3,2},{4,3},{5,4},{6,5},{7,6},{9,8},{10,9},{11,10},{12... | collective-permute-start | bytes 30728 | tf_op jit(solution)/shard_map/ppermute | solution.py:603
  9.6 29.9 %all-to-all-start = ((bf16[64,8,128]{2,1,0:T(8,128)(2,1)}), bf16[64,8,128]{2,1,0:T(8,128)(2,1)S(1)}, u32[]{:S(2)}, u32[]{:S(2)}) async-start(bf16[64,8,128]{2,1,0:T(8,128)(2,1)} %get-tuple-element.20), calls=%async_computation | async-start | bytes 262144 | tf_op jit(solution)/shard_map/all_to_all | solution.py:652
  28.0 4.2 %collective-permute-start.2 = (bf16[120,128]{1,0:T(8,128)(2,1)S(1)}, bf16[120,128]{1,0:T(8,128)(2,1)S(1)}, u32[]{:S(2)}, u32[]{:S(2)}) collective-permute-start(bf16[120,128]{1,0:T(8,128)(2,1)S(1)} %constant_dynamic-update-slice_fusion), channel_id=1, source_target_pairs={{0,8},{8,16},{16,24},{24,32},{32,40},{40,48},{48,56},{1,9},{9,17},... | collective-permute-start | bytes 92168 | tf_op jit(solution)/shard_map/ppermute | solution.py:602
  30.9 16.9 %collective-permute-start.3 = (bf16[120,128]{1,0:T(8,128)(2,1)S(1)}, bf16[120,128]{1,0:T(8,128)(2,1)S(1)}, u32[]{:S(2)}, u32[]{:S(2)}) collective-permute-start(bf16[120,128]{1,0:T(8,128)(2,1)S(1)} %constant_dynamic-update-slice_fusion), channel_id=1, source_target_pairs={{8,0},{16,8},{24,16},{32,24},{40,32},{48,40},{56,48},{9,1},{17,9},... | collective-permute-start | bytes 92168 | tf_op jit(solution)/shard_map/ppermute | solution.py:603
  40.8 19.1 %all-to-all-start.1 = ((bf16[8,256,128]{2,1,0:T(8,128)(2,1)}), bf16[8,256,128]{2,1,0:T(8,128)(2,1)S(1)}, u32[]{:S(2)}, u32[]{:S(2)}) async-start(bf16[8,256,128]{2,1,0:T(8,128)(2,1)} %plane_kernel.1), calls=%async_computation.1 | async-start | bytes 1048576 | tf_op jit(solution)/shard_map/all_to_all | solution.py:663
  47.9 7.3 %collective-permute-start.4 = (bf16[360,128]{1,0:T(8,128)(2,1)S(1)}, bf16[360,128]{1,0:T(8,128)(2,1)S(1)}, u32[]{:S(2)}, u32[]{:S(2)}) collective-permute-start(bf16[360,128]{1,0:T(8,128)(2,1)S(1)} %constant_dynamic-update-slice_fusion.3.sheet), channel_id=1, source_target_pairs={{0,64},{64,128},{128,192},{192,256},{256,320},{320,384},{384,448},... | collective-permute-start | bytes 276488 | tf_op jit(solution)/shard_map/ppermute | solution.py:602
  51.4 6.2 %collective-permute-start.5 = (bf16[360,128]{1,0:T(8,128)(2,1)S(1)}, bf16[360,128]{1,0:T(8,128)(2,1)S(1)}, u32[]{:S(2)}, u32[]{:S(2)}) collective-permute-start(bf16[360,128]{1,0:T(8,128)(2,1)S(1)} %constant_dynamic-update-slice_fusion.3.sheet), channel_id=1, source_target_pairs={{64,0},{128,64},{192,128},{256,192},{320,256},{384,320},{448,384},... | collective-permute-start | bytes 276488 | tf_op jit(solution)/shard_map/ppermute | solution.py:603

commit v11 on v10

--- a/solution.py
+++ b/solution.py
@@ -168,7 +168,7 @@
     step_x = (device >> 6) - (own >> 6) + 1
     step_y = ((device >> 3) & 7) - ((own >> 3) & 7) + 1
     step_z = (device & 7) - (own & 7) + 1
-    return step_x * 9 + step_y * 3 + step_z
+    return step_y * 9 + step_z * 3 + step_x
 
 
 def tables_kernel(
@@ -650,11 +650,11 @@
         first_filters, rows_both,
     )
     arrived = lax.all_to_all(payload, ("gy", "gz"), 0, 0, tiled=True)
-    before, after = both_ways(halo, "gz")
+    before, after = both_ways(halo, "gx")
     line = jnp.concatenate([before, halo, after], axis=0)
-    before, after = both_ways(line, "gy")
+    before, after = both_ways(line, "gz")
     sheet = jnp.concatenate([before, line, after], axis=0)
-    before, after = both_ways(sheet, "gx")
+    before, after = both_ways(sheet, "gy")
 
     (copies,) = call(
         plane_kernel, "v", [pltpu.HBM((8, 256, 128), BF16)],

time: 63.6 us -> 60.8 us (0.956)
  starting transfers between devices: 40.3 us -> 37.1 us
    all_to_all x1, starting transfers between devices: 18.3 us -> 12.7 us  [shards(): arrived = lax.all_to_all(payload, ('gy', 'gz'), 0, 0, tiled=True)]
    ppermute x3, starting transfers between devices: 4.5 us -> 8.15 us  [both_ways(): after = lax.ppermute(x, axis, [(i + 1, i) for i in range(ends)])]
    ppermute x3, starting transfers between devices: 10.5 us -> 9.68 us  [both_ways(): before = lax.ppermute(x, axis, [(i, i + 1) for i in range(ends)])]
where the time goes in v11:
time: 60.8 us; the launch traced here: 60.3 us
  starting transfers between devices  37.1 us (61%)
  Pallas kernels  11 us (18%)
  waiting for transfers between devices  10.1 us (17%)
  between operations  2.09 us (3%)
    all_to_all x1, starting transfers between devices, shards(): arrived = lax.all_to_all(payload, ('gy', 'gz'), 0, 0, tiled=True)  12.7 us
    pallas_call x5, Pallas kernels, call(): pl.pallas_call(kernel, out_shape=outs, in_specs=[specs[kind] for kind in...  11 us
    ppermute x3, starting transfers between devices, both_ways(): before = lax.ppermute(x, axis, [(i, i + 1) for i in range(ends)])  9.68 us
    ppermute x3, starting transfers between devices, both_ways(): after = lax.ppermute(x, axis, [(i + 1, i) for i in range(ends)])  8.15 us
    all_to_all x1, waiting for transfers between devices, shards(): arrived = lax.all_to_all(payload, ('gy', 'gz'), 0, 0, tiled=True)  7.36 us
    all_to_all x1, starting transfers between devices, shards(): planes = lax.all_to_all(copies, 'gx', 0, 0, tiled=True)  6.59 us
    ppermute x3, waiting for transfers between devices, both_ways(): after = lax.ppermute(x, axis, [(i + 1, i) for i in range(ends)])  2.73 us
  transfers between devices with their start and end apart: 8, of which 2 were waited for; matrix products, arithmetic and copies ran while one was open for 0% of the time, Pallas kernels for 9%

profile of v11, /device:TPU:1, one launch (start us, length us, event | category | flops | bytes accessed | tf_op | source)
XLA Modules:
  0.0 60.3 jit_solution(13817082565512504938)
XLA Ops:
  1.9 2.3 %first_kernel.1 = (bf16[40,128]{1,0:T(8,128)(2,1)S(1)}, bf16[64,8,128]{2,1,0:T(8,128)(2,1)}, s32[16,128]{1,0:T(8,128)S(1)}) custom-call(s32[1]{0:T(128)S(6)} %copy.24.parent, s32[1]{0:T(128)S(6)} %copy.25.refined, s32[1,8]{1,0:T(1,128)} %child_h.1, s32[8,27]{1,0:T(8,128)} %fine_h.1, s32[1,27]{1,0:T(1,128)} %mid_h.1, s32[27,64]{1,0:T(8,128)} %bitcast.5, ...), custom_call_target="tpu_custom_call" | custom-call | flops 2000000 | bytes 494324 | tf_op jit(solution)/shard_map/first_kernel/pallas_call | solution.py:587
  4.3 4.5 %collective-permute-start = (bf16[40,128]{1,0:T(8,128)(2,1)S(1)}, bf16[40,128]{1,0:T(8,128)(2,1)S(1)}, u32[]{:S(2)}, u32[]{:S(2)}) collective-permute-start(bf16[40,128]{1,0:T(8,128)(2,1)S(1)} %get-tuple-element.15), channel_id=1, source_target_pairs={{0,64},{64,128},{128,192},{192,256},{256,320},{320,384},{384,448},... | collective-permute-start | bytes 30728 | tf_op jit(solution)/shard_map/ppermute | solution.py:602
  8.8 5.6 %collective-permute-start.1 = (bf16[40,128]{1,0:T(8,128)(2,1)S(1)}, bf16[40,128]{1,0:T(8,128)(2,1)S(1)}, u32[]{:S(2)}, u32[]{:S(2)}) collective-permute-start(bf16[40,128]{1,0:T(8,128)(2,1)S(1)} %get-tuple-element.15), channel_id=1, source_target_pairs={{64,0},{128,64},{192,128},{256,192},{320,256},{384,320},{448,384},... | collective-permute-start | bytes 30728 | tf_op jit(solution)/shard_map/ppermute | solution.py:603
  14.3 12.7 %all-to-all-start = ((bf16[64,8,128]{2,1,0:T(8,128)(2,1)}), bf16[64,8,128]{2,1,0:T(8,128)(2,1)S(1)}, u32[]{:S(2)}, u32[]{:S(2)}) async-start(bf16[64,8,128]{2,1,0:T(8,128)(2,1)} %get-tuple-element.20), calls=%async_computation | async-start | bytes 262144 | tf_op jit(solution)/shard_map/all_to_all | solution.py:652
  27.0 0.0 collective-permute-done
  27.1 0.0 collective-permute-done.1
  27.1 2.9 %collective-permute-start.2 = (bf16[120,128]{1,0:T(8,128)(2,1)S(1)}, bf16[120,128]{1,0:T(8,128)(2,1)S(1)}, u32[]{:S(2)}, u32[]{:S(2)}) collective-permute-start(bf16[120,128]{1,0:T(8,128)(2,1)S(1)} %constant_dynamic-update-slice_fusion), channel_id=1, source_target_pairs={{0,1},{1,2},{2,3},{3,4},{4,5},{5,6},{6,7},{8,9},{9,10},{10,11},{11... | collective-permute-start | bytes 92168 | tf_op jit(solution)/shard_map/ppermute | solution.py:602
  30.0 1.3 %collective-permute-start.3 = (bf16[120,128]{1,0:T(8,128)(2,1)S(1)}, bf16[120,128]{1,0:T(8,128)(2,1)S(1)}, u32[]{:S(2)}, u32[]{:S(2)}) collective-permute-start(bf16[120,128]{1,0:T(8,128)(2,1)S(1)} %constant_dynamic-update-slice_fusion), channel_id=1, source_target_pairs={{1,0},{2,1},{3,2},{4,3},{5,4},{6,5},{7,6},{9,8},{10,9},{11,10},{12... | collective-permute-start | bytes 92168 | tf_op jit(solution)/shard_map/ppermute | solution.py:603
  31.3 0.0 collective-permute-done.2
  31.3 7.4 %all-to-all-done.arrived = bf16[64,8,128]{2,1,0:T(8,128)(2,1)S(1)} async-done(((bf16[64,8,128]{2,1,0:T(8,128)(2,1)}), bf16[64,8,128]{2,1,0:T(8,128)(2,1)S(1)}, u32[]{:S(2)}, u32[]{:S(2)}) %all-to-all-start) | async-done | bytes 131104 | tf_op jit(solution)/shard_map/all_to_all | solution.py:652
  38.7 1.3 %plane_kernel.1 = bf16[8,256,128]{2,1,0:T(8,128)(2,1)} custom-call(bf16[64,8,128]{2,1,0:T(8,128)(2,1)S(1)} %all-to-all-done.arrived), custom_call_target="tpu_custom_call" | custom-call | flops 33000000 | bytes 655360 | tf_op jit(solution)/shard_map/plane_kernel/pallas_call | solution.py:587
  40.0 6.6 %all-to-all-start.1 = ((bf16[8,256,128]{2,1,0:T(8,128)(2,1)}), bf16[8,256,128]{2,1,0:T(8,128)(2,1)S(1)}, u32[]{:S(2)}, u32[]{:S(2)}) async-start(bf16[8,256,128]{2,1,0:T(8,128)(2,1)} %plane_kernel.1), calls=%async_computation.1 | async-start | bytes 1048576 | tf_op jit(solution)/shard_map/all_to_all | solution.py:663
  46.6 0.0 collective-permute-done.3
  46.6 2.2 %collective-permute-start.4 = (bf16[360,128]{1,0:T(8,128)(2,1)S(1)}, bf16[360,128]{1,0:T(8,128)(2,1)S(1)}, u32[]{:S(2)}, u32[]{:S(2)}) collective-permute-start(bf16[360,128]{1,0:T(8,128)(2,1)S(1)} %constant_dynamic-update-slice_fusion.3.sheet), channel_id=1, source_target_pairs={{0,8},{8,16},{16,24},{24,32},{32,40},{40,48},{48,56},{1,9},{9,17},... | collective-permute-start | bytes 276488 | tf_op jit(solution)/shard_map/ppermute | solution.py:602
  48.9 1.3 %collective-permute-start.5 = (bf16[360,128]{1,0:T(8,128)(2,1)S(1)}, bf16[360,128]{1,0:T(8,128)(2,1)S(1)}, u32[]{:S(2)}, u32[]{:S(2)}) collective-permute-start(bf16[360,128]{1,0:T(8,128)(2,1)S(1)} %constant_dynamic-update-slice_fusion.3.sheet), channel_id=1, source_target_pairs={{8,0},{16,8},{24,16},{32,24},{40,32},{48,40},{56,48},{9,1},{17,9},... | collective-permute-start | bytes 276488 | tf_op jit(solution)/shard_map/ppermute | solution.py:603
  50.2 1.8 %tables_kernel.1 = (f32[2,24,24,256]{3,2,1,0:T(8,128)S(1)}, bf16[3,256,24]{2,1,0:T(8,128)(2,1)S(1)}, f32[90,8,128]{2,1,0:T(8,128)S(1)}, f32[16,8,128]{2,1,0:T(8,...) custom-call(f32[3,192,32]{2,1,0:T(8,128)} %bitcast.6, f32[1,32]{1,0:T(1,128)} %bitcast.7, ...), custom_call_target="tpu_custom_call" | custom-call | flops 600000000 | bytes 3061888 | tf_op jit(solution)/shard_map/tables_kernel/pallas_call | solution.py:587
  52.0 0.0 collective-permute-done.4.left
  52.0 2.7 %collective-permute-done.5.right = bf16[360,128]{1,0:T(8,128)(2,1)S(1)} collective-permute-done((bf16[360,128]{1,0:T(8,128)(2,1)S(1)}, bf16[360,128]{1,0:T(8,128)(2,1)S(1)}, u32[]{:S(2)}, u32[]{:S(2)}) %collective-permute-start.5) | collective-permute-done | bytes 92192 | tf_op jit(solution)/shard_map/ppermute | solution.py:603
  54.8 2.3 %fine_kernel.1 = (f32[8,8,64]{2,1,0:T(8,128)S(1)}, f32[28,8,128]{2,1,0:T(8,128)S(1)}, s32[1,128]{1,0:T(1,128)S(1)}) custom-call(s32[16,128]{1,0:T(8,128)S(1)} %get-tuple-element.14.numbers_h, bf16[360,128]{1,0:T(8,128)(2,1)S(1)} %collective-permute-done.4.left, f32[90,8,128]{2,1,0:T(8,128)S(1)} %get-tuple-element.16.centre, ...), custom_call_target="tpu_custom_call" | custom-call | flops 100000000 | bytes 1909248 | tf_op jit(solution)/shard_map/fine_kernel/pallas_call | solution.py:587
  57.0 0.0 all-to-all-done.1.planes
  57.1 3.2 %last_kernel.1 = (f32[8,512]{1,0:T(8,128)}, f32[1,512]{1,0:T(1,128)}) custom-call(s32[16,128]{1,0:T(8,128)S(1)} %get-tuple-element.14.numbers_h, s32[1,128]{1,0:T(1,128)S(1)} %get-tuple-element.19.names_h, bf16[8,256,128]{2,1,0:T(8,128)(2,1)S(1)} %all-to-all-done.1.planes, f32[28,8,128]{2,1,0:T(8,128)S(1)} %get-tuple-element.21.mid_tiles, ...), custom_call_target="tpu_custom_call" | custom-call | flops 200000000 | bytes 2357760 | tf_op jit(solution)/shard_map/last_kernel/pallas_call | solution.py:587
  (8 shorter events, 0.1 us)
Async XLA Ops:
  4.3 22.8 %collective-permute-start = (bf16[40,128]{1,0:T(8,128)(2,1)S(1)}, bf16[40,128]{1,0:T(8,128)(2,1)S(1)}, u32[]{:S(2)}, u32[]{:S(2)}) collective-permute-start(bf16[40,128]{1,0:T(8,128)(2,1)S(1)} %get-tuple-element.15), channel_id=1, source_target_pairs={{0,64},{64,128},{128,192},{192,256},{256,320},{320,384},{384,448},... | collective-permute-start | bytes 30728 | tf_op jit(solution)/shard_map/ppermute | solution.py:602
  8.8 18.3 %collective-permute-start.1 = (bf16[40,128]{1,0:T(8,128)(2,1)S(1)}, bf16[40,128]{1,0:T(8,128)(2,1)S(1)}, u32[]{:S(2)}, u32[]{:S(2)}) collective-permute-start(bf16[40,128]{1,0:T(8,128)(2,1)S(1)} %get-tuple-element.15), channel_id=1, source_target_pairs={{64,0},{128,64},{192,128},{256,192},{320,256},{384,320},{448,384},... | collective-permute-start | bytes 30728 | tf_op jit(solution)/shard_map/ppermute | solution.py:603
  14.3 24.3 %all-to-all-start = ((bf16[64,8,128]{2,1,0:T(8,128)(2,1)}), bf16[64,8,128]{2,1,0:T(8,128)(2,1)S(1)}, u32[]{:S(2)}, u32[]{:S(2)}) async-start(bf16[64,8,128]{2,1,0:T(8,128)(2,1)} %get-tuple-element.20), calls=%async_computation | async-start | bytes 262144 | tf_op jit(solution)/shard_map/all_to_all | solution.py:652
  27.1 4.2 %collective-permute-start.2 = (bf16[120,128]{1,0:T(8,128)(2,1)S(1)}, bf16[120,128]{1,0:T(8,128)(2,1)S(1)}, u32[]{:S(2)}, u32[]{:S(2)}) collective-permute-start(bf16[120,128]{1,0:T(8,128)(2,1)S(1)} %constant_dynamic-update-slice_fusion), channel_id=1, source_target_pairs={{0,1},{1,2},{2,3},{3,4},{4,5},{5,6},{6,7},{8,9},{9,10},{10,11},{11... | collective-permute-start | bytes 92168 | tf_op jit(solution)/shard_map/ppermute | solution.py:602
  30.0 16.6 %collective-permute-start.3 = (bf16[120,128]{1,0:T(8,128)(2,1)S(1)}, bf16[120,128]{1,0:T(8,128)(2,1)S(1)}, u32[]{:S(2)}, u32[]{:S(2)}) collective-permute-start(bf16[120,128]{1,0:T(8,128)(2,1)S(1)} %constant_dynamic-update-slice_fusion), channel_id=1, source_target_pairs={{1,0},{2,1},{3,2},{4,3},{5,4},{6,5},{7,6},{9,8},{10,9},{11,10},{12... | collective-permute-start | bytes 92168 | tf_op jit(solution)/shard_map/ppermute | solution.py:603
  40.0 17.0 %all-to-all-start.1 = ((bf16[8,256,128]{2,1,0:T(8,128)(2,1)}), bf16[8,256,128]{2,1,0:T(8,128)(2,1)S(1)}, u32[]{:S(2)}, u32[]{:S(2)}) async-start(bf16[8,256,128]{2,1,0:T(8,128)(2,1)} %plane_kernel.1), calls=%async_computation.1 | async-start | bytes 1048576 | tf_op jit(solution)/shard_map/all_to_all | solution.py:663
  46.6 5.4 %collective-permute-start.4 = (bf16[360,128]{1,0:T(8,128)(2,1)S(1)}, bf16[360,128]{1,0:T(8,128)(2,1)S(1)}, u32[]{:S(2)}, u32[]{:S(2)}) collective-permute-start(bf16[360,128]{1,0:T(8,128)(2,1)S(1)} %constant_dynamic-update-slice_fusion.3.sheet), channel_id=1, source_target_pairs={{0,8},{8,16},{16,24},{24,32},{32,40},{40,48},{48,56},{1,9},{9,17},... | collective-permute-start | bytes 276488 | tf_op jit(solution)/shard_map/ppermute | solution.py:602
  48.9 5.9 %collective-permute-start.5 = (bf16[360,128]{1,0:T(8,128)(2,1)S(1)}, bf16[360,128]{1,0:T(8,128)(2,1)S(1)}, u32[]{:S(2)}, u32[]{:S(2)}) collective-permute-start(bf16[360,128]{1,0:T(8,128)(2,1)S(1)} %constant_dynamic-update-slice_fusion.3.sheet), channel_id=1, source_target_pairs={{8,0},{16,8},{24,16},{32,24},{40,32},{48,40},{56,48},{9,1},{17,9},... | collective-permute-start | bytes 276488 | tf_op jit(solution)/shard_map/ppermute | solution.py:603

commit v12 on v11

--- a/solution.py
+++ b/solution.py
@@ -168,7 +168,7 @@
     step_x = (device >> 6) - (own >> 6) + 1
     step_y = ((device >> 3) & 7) - ((own >> 3) & 7) + 1
     step_z = (device & 7) - (own & 7) + 1
-    return step_y * 9 + step_z * 3 + step_x
+    return step_z * 9 + step_y * 3 + step_x
 
 
 def tables_kernel(
@@ -652,9 +652,9 @@
     arrived = lax.all_to_all(payload, ("gy", "gz"), 0, 0, tiled=True)
     before, after = both_ways(halo, "gx")
     line = jnp.concatenate([before, halo, after], axis=0)
-    before, after = both_ways(line, "gz")
+    before, after = both_ways(line, "gy")
     sheet = jnp.concatenate([before, line, after], axis=0)
-    before, after = both_ways(sheet, "gy")
+    before, after = both_ways(sheet, "gz")
 
     (copies,) = call(
         plane_kernel, "v", [pltpu.HBM((8, 256, 128), BF16)],

time: 60.8 us -> 60.6 us (level)
  no operation moved by 1% of the time
where the time goes in v12:
time: 60.6 us; the launch traced here: 60.1 us
  starting transfers between devices  36.9 us (61%)
  Pallas kernels  11 us (18%)
  waiting for transfers between devices  10.1 us (17%)
  between operations  2.09 us (3%)
    all_to_all x1, starting transfers between devices, shards(): arrived = lax.all_to_all(payload, ('gy', 'gz'), 0, 0, tiled=True)  12.7 us
    pallas_call x5, Pallas kernels, call(): pl.pallas_call(kernel, out_shape=outs, in_specs=[specs[kind] for kind in...  11 us
    ppermute x3, starting transfers between devices, both_ways(): before = lax.ppermute(x, axis, [(i, i + 1) for i in range(ends)])  9.79 us
    ppermute x3, starting transfers between devices, both_ways(): after = lax.ppermute(x, axis, [(i + 1, i) for i in range(ends)])  8.15 us
    all_to_all x1, waiting for transfers between devices, shards(): arrived = lax.all_to_all(payload, ('gy', 'gz'), 0, 0, tiled=True)  7.36 us
    all_to_all x1, starting transfers between devices, shards(): planes = lax.all_to_all(copies, 'gx', 0, 0, tiled=True)  6.31 us
    ppermute x3, waiting for transfers between devices, both_ways(): after = lax.ppermute(x, axis, [(i + 1, i) for i in range(ends)])  2.73 us
  transfers between devices with their start and end apart: 8, of which 2 were waited for; matrix products, arithmetic and copies ran while one was open for 0% of the time, Pallas kernels for 9%

profile of v12, /device:TPU:1, one launch (start us, length us, event | category | flops | bytes accessed | tf_op | source)
XLA Modules:
  0.0 60.1 jit_solution(5220764830634338484)
XLA Ops:
  1.9 2.3 %first_kernel.1 = (bf16[40,128]{1,0:T(8,128)(2,1)S(1)}, bf16[64,8,128]{2,1,0:T(8,128)(2,1)}, s32[16,128]{1,0:T(8,128)S(1)}) custom-call(s32[1]{0:T(128)S(6)} %copy.24.parent, s32[1]{0:T(128)S(6)} %copy.25.refined, s32[1,8]{1,0:T(1,128)} %child_h.1, s32[8,27]{1,0:T(8,128)} %fine_h.1, s32[1,27]{1,0:T(1,128)} %mid_h.1, s32[27,64]{1,0:T(8,128)} %bitcast.5, ...), custom_call_target="tpu_custom_call" | custom-call | flops 2000000 | bytes 494324 | tf_op jit(solution)/shard_map/first_kernel/pallas_call | solution.py:587
  4.3 4.5 %collective-permute-start = (bf16[40,128]{1,0:T(8,128)(2,1)S(1)}, bf16[40,128]{1,0:T(8,128)(2,1)S(1)}, u32[]{:S(2)}, u32[]{:S(2)}) collective-permute-start(bf16[40,128]{1,0:T(8,128)(2,1)S(1)} %get-tuple-element.15), channel_id=1, source_target_pairs={{0,64},{64,128},{128,192},{192,256},{256,320},{320,384},{384,448},... | collective-permute-start | bytes 30728 | tf_op jit(solution)/shard_map/ppermute | solution.py:602
  8.8 5.6 %collective-permute-start.1 = (bf16[40,128]{1,0:T(8,128)(2,1)S(1)}, bf16[40,128]{1,0:T(8,128)(2,1)S(1)}, u32[]{:S(2)}, u32[]{:S(2)}) collective-permute-start(bf16[40,128]{1,0:T(8,128)(2,1)S(1)} %get-tuple-element.15), channel_id=1, source_target_pairs={{64,0},{128,64},{192,128},{256,192},{320,256},{384,320},{448,384},... | collective-permute-start | bytes 30728 | tf_op jit(solution)/shard_map/ppermute | solution.py:603
  14.3 12.7 %all-to-all-start = ((bf16[64,8,128]{2,1,0:T(8,128)(2,1)}), bf16[64,8,128]{2,1,0:T(8,128)(2,1)S(1)}, u32[]{:S(2)}, u32[]{:S(2)}) async-start(bf16[64,8,128]{2,1,0:T(8,128)(2,1)} %get-tuple-element.20), calls=%async_computation | async-start | bytes 262144 | tf_op jit(solution)/shard_map/all_to_all | solution.py:652
  27.0 0.0 collective-permute-done
  27.1 0.0 collective-permute-done.1
  27.1 2.9 %collective-permute-start.2 = (bf16[120,128]{1,0:T(8,128)(2,1)S(1)}, bf16[120,128]{1,0:T(8,128)(2,1)S(1)}, u32[]{:S(2)}, u32[]{:S(2)}) collective-permute-start(bf16[120,128]{1,0:T(8,128)(2,1)S(1)} %constant_dynamic-update-slice_fusion), channel_id=1, source_target_pairs={{0,8},{8,16},{16,24},{24,32},{32,40},{40,48},{48,56},{1,9},{9,17},... | collective-permute-start | bytes 92168 | tf_op jit(solution)/shard_map/ppermute | solution.py:602
  30.0 1.3 %collective-permute-start.3 = (bf16[120,128]{1,0:T(8,128)(2,1)S(1)}, bf16[120,128]{1,0:T(8,128)(2,1)S(1)}, u32[]{:S(2)}, u32[]{:S(2)}) collective-permute-start(bf16[120,128]{1,0:T(8,128)(2,1)S(1)} %constant_dynamic-update-slice_fusion), channel_id=1, source_target_pairs={{8,0},{16,8},{24,16},{32,24},{40,32},{48,40},{56,48},{9,1},{17,9},... | collective-permute-start | bytes 92168 | tf_op jit(solution)/shard_map/ppermute | solution.py:603
  31.3 0.0 collective-permute-done.2
  31.3 7.4 %all-to-all-done.arrived = bf16[64,8,128]{2,1,0:T(8,128)(2,1)S(1)} async-done(((bf16[64,8,128]{2,1,0:T(8,128)(2,1)}), bf16[64,8,128]{2,1,0:T(8,128)(2,1)S(1)}, u32[]{:S(2)}, u32[]{:S(2)}) %all-to-all-start) | async-done | bytes 131104 | tf_op jit(solution)/shard_map/all_to_all | solution.py:652
  38.7 1.3 %plane_kernel.1 = bf16[8,256,128]{2,1,0:T(8,128)(2,1)} custom-call(bf16[64,8,128]{2,1,0:T(8,128)(2,1)S(1)} %all-to-all-done.arrived), custom_call_target="tpu_custom_call" | custom-call | flops 33000000 | bytes 655360 | tf_op jit(solution)/shard_map/plane_kernel/pallas_call | solution.py:587
  40.0 6.3 %all-to-all-start.1 = ((bf16[8,256,128]{2,1,0:T(8,128)(2,1)}), bf16[8,256,128]{2,1,0:T(8,128)(2,1)S(1)}, u32[]{:S(2)}, u32[]{:S(2)}) async-start(bf16[8,256,128]{2,1,0:T(8,128)(2,1)} %plane_kernel.1), calls=%async_computation.1 | async-start | bytes 1048576 | tf_op jit(solution)/shard_map/all_to_all | solution.py:663
  46.4 0.0 collective-permute-done.3
  46.4 2.4 %collective-permute-start.4 = (bf16[360,128]{1,0:T(8,128)(2,1)S(1)}, bf16[360,128]{1,0:T(8,128)(2,1)S(1)}, u32[]{:S(2)}, u32[]{:S(2)}) collective-permute-start(bf16[360,128]{1,0:T(8,128)(2,1)S(1)} %constant_dynamic-update-slice_fusion.3.sheet), channel_id=1, source_target_pairs={{0,1},{1,2},{2,3},{3,4},{4,5},{5,6},{6,7},{8,9},{9,10},{10,11},{11... | collective-permute-start | bytes 276488 | tf_op jit(solution)/shard_map/ppermute | solution.py:602
  48.7 1.3 %collective-permute-start.5 = (bf16[360,128]{1,0:T(8,128)(2,1)S(1)}, bf16[360,128]{1,0:T(8,128)(2,1)S(1)}, u32[]{:S(2)}, u32[]{:S(2)}) collective-permute-start(bf16[360,128]{1,0:T(8,128)(2,1)S(1)} %constant_dynamic-update-slice_fusion.3.sheet), channel_id=1, source_target_pairs={{1,0},{2,1},{3,2},{4,3},{5,4},{6,5},{7,6},{9,8},{10,9},{11,10},{12... | collective-permute-start | bytes 276488 | tf_op jit(solution)/shard_map/ppermute | solution.py:603
  50.0 1.8 %tables_kernel.1 = (f32[2,24,24,256]{3,2,1,0:T(8,128)S(1)}, bf16[3,256,24]{2,1,0:T(8,128)(2,1)S(1)}, f32[90,8,128]{2,1,0:T(8,128)S(1)}, f32[16,8,128]{2,1,0:T(8,...) custom-call(f32[3,192,32]{2,1,0:T(8,128)} %bitcast.6, f32[1,32]{1,0:T(1,128)} %bitcast.7, ...), custom_call_target="tpu_custom_call" | custom-call | flops 600000000 | bytes 3061888 | tf_op jit(solution)/shard_map/tables_kernel/pallas_call | solution.py:587
  51.9 0.0 collective-permute-done.4.left
  51.9 2.7 %collective-permute-done.5.right = bf16[360,128]{1,0:T(8,128)(2,1)S(1)} collective-permute-done((bf16[360,128]{1,0:T(8,128)(2,1)S(1)}, bf16[360,128]{1,0:T(8,128)(2,1)S(1)}, u32[]{:S(2)}, u32[]{:S(2)}) %collective-permute-start.5) | collective-permute-done | bytes 92192 | tf_op jit(solution)/shard_map/ppermute | solution.py:603
  54.6 2.3 %fine_kernel.1 = (f32[8,8,64]{2,1,0:T(8,128)S(1)}, f32[28,8,128]{2,1,0:T(8,128)S(1)}, s32[1,128]{1,0:T(1,128)S(1)}) custom-call(s32[16,128]{1,0:T(8,128)S(1)} %get-tuple-element.14.numbers_h, bf16[360,128]{1,0:T(8,128)(2,1)S(1)} %collective-permute-done.4.left, f32[90,8,128]{2,1,0:T(8,128)S(1)} %get-tuple-element.16.centre, ...), custom_call_target="tpu_custom_call" | custom-call | flops 100000000 | bytes 1909248 | tf_op jit(solution)/shard_map/fine_kernel/pallas_call | solution.py:587
  56.9 0.0 all-to-all-done.1.planes
  56.9 3.2 %last_kernel.1 = (f32[8,512]{1,0:T(8,128)}, f32[1,512]{1,0:T(1,128)}) custom-call(s32[16,128]{1,0:T(8,128)S(1)} %get-tuple-element.14.numbers_h, s32[1,128]{1,0:T(1,128)S(1)} %get-tuple-element.19.names_h, bf16[8,256,128]{2,1,0:T(8,128)(2,1)S(1)} %all-to-all-done.1.planes, f32[28,8,128]{2,1,0:T(8,128)S(1)} %get-tuple-element.21.mid_tiles, ...), custom_call_target="tpu_custom_call" | custom-call | flops 200000000 | bytes 2357760 | tf_op jit(solution)/shard_map/last_kernel/pallas_call | solution.py:587
  (8 shorter events, 0.1 us)
Async XLA Ops:
  4.3 22.8 %collective-permute-start = (bf16[40,128]{1,0:T(8,128)(2,1)S(1)}, bf16[40,128]{1,0:T(8,128)(2,1)S(1)}, u32[]{:S(2)}, u32[]{:S(2)}) collective-permute-start(bf16[40,128]{1,0:T(8,128)(2,1)S(1)} %get-tuple-element.15), channel_id=1, source_target_pairs={{0,64},{64,128},{128,192},{192,256},{256,320},{320,384},{384,448},... | collective-permute-start | bytes 30728 | tf_op jit(solution)/shard_map/ppermute | solution.py:602
  8.8 18.3 %collective-permute-start.1 = (bf16[40,128]{1,0:T(8,128)(2,1)S(1)}, bf16[40,128]{1,0:T(8,128)(2,1)S(1)}, u32[]{:S(2)}, u32[]{:S(2)}) collective-permute-start(bf16[40,128]{1,0:T(8,128)(2,1)S(1)} %get-tuple-element.15), channel_id=1, source_target_pairs={{64,0},{128,64},{192,128},{256,192},{320,256},{384,320},{448,384},... | collective-permute-start | bytes 30728 | tf_op jit(solution)/shard_map/ppermute | solution.py:603
  14.3 24.3 %all-to-all-start = ((bf16[64,8,128]{2,1,0:T(8,128)(2,1)}), bf16[64,8,128]{2,1,0:T(8,128)(2,1)S(1)}, u32[]{:S(2)}, u32[]{:S(2)}) async-start(bf16[64,8,128]{2,1,0:T(8,128)(2,1)} %get-tuple-element.20), calls=%async_computation | async-start | bytes 262144 | tf_op jit(solution)/shard_map/all_to_all | solution.py:652
  27.1 4.2 %collective-permute-start.2 = (bf16[120,128]{1,0:T(8,128)(2,1)S(1)}, bf16[120,128]{1,0:T(8,128)(2,1)S(1)}, u32[]{:S(2)}, u32[]{:S(2)}) collective-permute-start(bf16[120,128]{1,0:T(8,128)(2,1)S(1)} %constant_dynamic-update-slice_fusion), channel_id=1, source_target_pairs={{0,8},{8,16},{16,24},{24,32},{32,40},{40,48},{48,56},{1,9},{9,17},... | collective-permute-start | bytes 92168 | tf_op jit(solution)/shard_map/ppermute | solution.py:602
  30.0 16.3 %collective-permute-start.3 = (bf16[120,128]{1,0:T(8,128)(2,1)S(1)}, bf16[120,128]{1,0:T(8,128)(2,1)S(1)}, u32[]{:S(2)}, u32[]{:S(2)}) collective-permute-start(bf16[120,128]{1,0:T(8,128)(2,1)S(1)} %constant_dynamic-update-slice_fusion), channel_id=1, source_target_pairs={{8,0},{16,8},{24,16},{32,24},{40,32},{48,40},{56,48},{9,1},{17,9},... | collective-permute-start | bytes 92168 | tf_op jit(solution)/shard_map/ppermute | solution.py:603
  40.0 16.9 %all-to-all-start.1 = ((bf16[8,256,128]{2,1,0:T(8,128)(2,1)}), bf16[8,256,128]{2,1,0:T(8,128)(2,1)S(1)}, u32[]{:S(2)}, u32[]{:S(2)}) async-start(bf16[8,256,128]{2,1,0:T(8,128)(2,1)} %plane_kernel.1), calls=%async_computation.1 | async-start | bytes 1048576 | tf_op jit(solution)/shard_map/all_to_all | solution.py:663
  46.4 5.5 %collective-permute-start.4 = (bf16[360,128]{1,0:T(8,128)(2,1)S(1)}, bf16[360,128]{1,0:T(8,128)(2,1)S(1)}, u32[]{:S(2)}, u32[]{:S(2)}) collective-permute-start(bf16[360,128]{1,0:T(8,128)(2,1)S(1)} %constant_dynamic-update-slice_fusion.3.sheet), channel_id=1, source_target_pairs={{0,1},{1,2},{2,3},{3,4},{4,5},{5,6},{6,7},{8,9},{9,10},{10,11},{11... | collective-permute-start | bytes 276488 | tf_op jit(solution)/shard_map/ppermute | solution.py:602
  48.7 5.9 %collective-permute-start.5 = (bf16[360,128]{1,0:T(8,128)(2,1)S(1)}, bf16[360,128]{1,0:T(8,128)(2,1)S(1)}, u32[]{:S(2)}, u32[]{:S(2)}) collective-permute-start(bf16[360,128]{1,0:T(8,128)(2,1)S(1)} %constant_dynamic-update-slice_fusion.3.sheet), channel_id=1, source_target_pairs={{1,0},{2,1},{3,2},{4,3},{5,4},{6,5},{7,6},{9,8},{10,9},{11,10},{12... | collective-permute-start | bytes 276488 | tf_op jit(solution)/shard_map/ppermute | solution.py:603

commit v13 on v12

--- a/solution.py
+++ b/solution.py
@@ -482,13 +482,8 @@
     direct[...] = result.reshape(8, 8, PLANE)
 
 
-def last_kernel(
-    numbers_h, names_h, planes, mid_tiles, direct, ab_ref, x_ref, rows_p, filters, mids,
-    fine_out, mid_out,
-    coarse, back, sems, w_mid, w_coarse, numbers, names,
-):
-    copies = fetches(sems, (numbers_h, numbers), (names_h, names))
-    build_w(ab_ref, 1, w_mid)
+def coarse_kernel(numbers_h, planes, ab_ref, x_ref, coarse, result, w_coarse, numbers, sems):
+    copies = fetches(sems, (numbers_h, numbers))
     build_w(ab_ref, 2, w_coarse)
     low8 = low_lanes((8, 128))
 
@@ -504,7 +499,39 @@
     coarse[64] = jnp.zeros((8, 128), F32)
     for copy in copies:
         copy.wait()
+
+    def coarse_source(ex, e):
+        return coarse[numbers[9, ex * 9 + e]]
+
+    sources = jnp.concatenate(
+        [
+            jnp.concatenate(
+                [
+                    pair_of(coarse_source(ex, 2 * ep), coarse_source(ex, min(2 * ep + 1, 8)))
+                    for ex in range(3)
+                ],
+                axis=0,
+            ).astype(BF16)
+            for ep in range(5)
+        ],
+        axis=1,
+    )
+    result[...] = apply_one(sources, x_ref[2], w_coarse)
+
+
+def last_kernel(
+    numbers_h, names_h, coarse, coarse_ref, mid_tiles, direct, ab_ref, x_ref, rows_p, filters, mids,
+    fine_out, mid_out,
+    back, sems, w_mid, numbers, names,
+):
+    copies = fetches(sems, (numbers_h, numbers), (names_h, names))
+    build_w(ab_ref, 1, w_mid)
+    low8 = low_lanes((8, 128))
+
+    for copy in copies:
+        copy.wait()
     octant = numbers[10, 8] & 7
+    coarse_result = coarse_ref[...]
 
     uppers, octants, owns = [], [], []
     for ep in range(5):
@@ -537,24 +564,6 @@
         pieces.append(jnp.concatenate(tiles, axis=0).astype(BF16))
     mid_result = apply_one(jnp.concatenate(pieces, axis=1), x_ref[1], w_mid)
 
-    def coarse_source(ex, e):
-        return coarse[numbers[9, ex * 9 + e]]
-
-    sources = jnp.concatenate(
-        [
-            jnp.concatenate(
-                [
-                    pair_of(coarse_source(ex, 2 * ep), coarse_source(ex, min(2 * ep + 1, 8)))
-                    for ex in range(3)
-                ],
-                axis=0,
-            ).astype(BF16)
-            for ep in range(5)
-        ],
-        axis=1,
-    )
-    coarse_result = apply_one(sources, x_ref[2], w_coarse)
-
     row_at = (octant >> 2) * 8
     upper = row_mix([rows_p[row_at + p, :, :PLANE] for p in range(8)], coarse_result)
     single = filters[pl.ds(pl.multiple_of(256 + (octant & 3) * 64, 64), 64), :]
@@ -682,6 +691,15 @@
         600_000_000,
         factors, term_weight.reshape(1, TERMS), select, sheet, rows_p, last_filters, mids,
     )
+    coarse, coarse_result = call(
+        coarse_kernel,
+        "avww",
+        [sds((65, 8, 128), F32), sds((8, PLANE), F32)],
+        [vmem((ROWS_W, 256), BF16), smem((16, 128), i32), pltpu.SemaphoreType.DMA((1,))],
+        20_000_000,
+        numbers, planes, w_factors, x_tables,
+    )
+    centre, coarse_result = lax.optimization_barrier((centre, coarse_result))
     direct, mid_tiles, names = call(
         fine_kernel,
         "avvvww",
@@ -698,19 +716,17 @@
     )
     fine_out, mid_out = call(
         last_kernel,
-        "aavvvwwwww",
+        "aavvvvwwwww",
         [sds((8, 512), F32), sds((1, 512), F32)],
         [
-            vmem((65, 8, 128), F32),
             vmem((8, 8, PLANE), F32),
             pltpu.SemaphoreType.DMA((2,)),
-            vmem((ROWS_W, 256), BF16),
             vmem((ROWS_W, 256), BF16),
             smem((16, 128), i32),
             smem((1, 128), i32),
         ],
         200_000_000,
-        numbers, names, planes, mid_tiles, direct, w_factors, x_tables,
+        numbers, names, coarse, coarse_result, mid_tiles, direct, w_factors, x_tables,
         rows_p, last_filters, mids,
     )
     return fine_out, mid_out

time: 60.6 us -> 62.9 us (1.038)
  starting transfers between devices: 36.9 us -> 38.6 us
  Pallas kernels: 11 us -> 12 us
    ppermute x3, waiting for transfers between devices: 2.73 us -> 0.01 us  [both_ways(): after = lax.ppermute(x, axis, [(i + 1, i) for i in range(ends)])]
    all_to_all x1, waiting for transfers between devices: 0.01 us -> 2.31 us  [shards(): planes = lax.all_to_all(copies, 'gx', 0, 0, tiled=True)]
    ppermute x3, starting transfers between devices: 9.79 us -> 11.4 us  [both_ways(): before = lax.ppermute(x, axis, [(i, i + 1) for i in range(ends)])]
    pallas_call x5 -> x6, Pallas kernels: 11 us -> 12 us  [call(): pl.pallas_call(kernel, out_shape=outs, in_specs=[specs[kind] for kind in...]
  transfers between devices with their start and end apart: 8 -> 8, of which waited for: 2 -> 2; matrix products, arithmetic and copies ran while one was open for 0% -> 0% of each run, Pallas kernels for 9% -> 7%
where the time goes in v13:
time: 62.9 us; the launch traced here: 62.4 us
  starting transfers between devices  38.6 us (61%)
  Pallas kernels  12 us (19%)
  waiting for transfers between devices  9.68 us (15%)
  between operations  2.09 us (3%)
    all_to_all x1, starting transfers between devices, shards(): arrived = lax.all_to_all(payload, ('gy', 'gz'), 0, 0, tiled=True)  12.7 us
    pallas_call x6, Pallas kernels, call(): pl.pallas_call(kernel, out_shape=outs, in_specs=[specs[kind] for kind in...  12 us
    ppermute x3, starting transfers between devices, both_ways(): before = lax.ppermute(x, axis, [(i, i + 1) for i in range(ends)])  11.4 us
    ppermute x3, starting transfers between devices, both_ways(): after = lax.ppermute(x, axis, [(i + 1, i) for i in range(ends)])  8.15 us
    all_to_all x1, waiting for transfers between devices, shards(): arrived = lax.all_to_all(payload, ('gy', 'gz'), 0, 0, tiled=True)  7.36 us
    all_to_all x1, starting transfers between devices, shards(): planes = lax.all_to_all(copies, 'gx', 0, 0, tiled=True)  6.31 us
    all_to_all x1, waiting for transfers between devices, shards(): planes = lax.all_to_all(copies, 'gx', 0, 0, tiled=True)  2.31 us
  transfers between devices with their start and end apart: 8, of which 2 were waited for; matrix products, arithmetic and copies ran while one was open for 0% of the time, Pallas kernels for 7%

profile of v13, /device:TPU:1, one launch (start us, length us, event | category | flops | bytes accessed | tf_op | source)
XLA Modules:
  0.0 62.4 jit_solution(18373830744580914164)
XLA Ops:
  1.9 2.3 %first_kernel.1 = (bf16[40,128]{1,0:T(8,128)(2,1)S(1)}, bf16[64,8,128]{2,1,0:T(8,128)(2,1)}, s32[16,128]{1,0:T(8,128)S(1)}) custom-call(s32[1]{0:T(128)S(6)} %copy.24.parent, s32[1]{0:T(128)S(6)} %copy.25.refined, s32[1,8]{1,0:T(1,128)} %child_h.1, s32[8,27]{1,0:T(8,128)} %fine_h.1, s32[1,27]{1,0:T(1,128)} %mid_h.1, s32[27,64]{1,0:T(8,128)} %bitcast.5, ...), custom_call_target="tpu_custom_call" | custom-call | flops 2000000 | bytes 494324 | tf_op jit(solution)/shard_map/first_kernel/pallas_call | solution.py:596
  4.3 4.5 %collective-permute-start = (bf16[40,128]{1,0:T(8,128)(2,1)S(1)}, bf16[40,128]{1,0:T(8,128)(2,1)S(1)}, u32[]{:S(2)}, u32[]{:S(2)}) collective-permute-start(bf16[40,128]{1,0:T(8,128)(2,1)S(1)} %get-tuple-element.19), channel_id=1, source_target_pairs={{0,64},{64,128},{128,192},{192,256},{256,320},{320,384},{384,448},... | collective-permute-start | bytes 30728 | tf_op jit(solution)/shard_map/ppermute | solution.py:611
  8.8 5.6 %collective-permute-start.1 = (bf16[40,128]{1,0:T(8,128)(2,1)S(1)}, bf16[40,128]{1,0:T(8,128)(2,1)S(1)}, u32[]{:S(2)}, u32[]{:S(2)}) collective-permute-start(bf16[40,128]{1,0:T(8,128)(2,1)S(1)} %get-tuple-element.19), channel_id=1, source_target_pairs={{64,0},{128,64},{192,128},{256,192},{320,256},{384,320},{448,384},... | collective-permute-start | bytes 30728 | tf_op jit(solution)/shard_map/ppermute | solution.py:612
  14.3 12.7 %all-to-all-start = ((bf16[64,8,128]{2,1,0:T(8,128)(2,1)}), bf16[64,8,128]{2,1,0:T(8,128)(2,1)S(1)}, u32[]{:S(2)}, u32[]{:S(2)}) async-start(bf16[64,8,128]{2,1,0:T(8,128)(2,1)} %get-tuple-element.21), calls=%async_computation | async-start | bytes 262144 | tf_op jit(solution)/shard_map/all_to_all | solution.py:661
  27.0 0.0 collective-permute-done
  27.1 0.0 collective-permute-done.1
  27.1 2.9 %collective-permute-start.2 = (bf16[120,128]{1,0:T(8,128)(2,1)S(1)}, bf16[120,128]{1,0:T(8,128)(2,1)S(1)}, u32[]{:S(2)}, u32[]{:S(2)}) collective-permute-start(bf16[120,128]{1,0:T(8,128)(2,1)S(1)} %constant_dynamic-update-slice_fusion), channel_id=1, source_target_pairs={{0,8},{8,16},{16,24},{24,32},{32,40},{40,48},{48,56},{1,9},{9,17},... | collective-permute-start | bytes 92168 | tf_op jit(solution)/shard_map/ppermute | solution.py:611
  30.0 1.3 %collective-permute-start.3 = (bf16[120,128]{1,0:T(8,128)(2,1)S(1)}, bf16[120,128]{1,0:T(8,128)(2,1)S(1)}, u32[]{:S(2)}, u32[]{:S(2)}) collective-permute-start(bf16[120,128]{1,0:T(8,128)(2,1)S(1)} %constant_dynamic-update-slice_fusion), channel_id=1, source_target_pairs={{8,0},{16,8},{24,16},{32,24},{40,32},{48,40},{56,48},{9,1},{17,9},... | collective-permute-start | bytes 92168 | tf_op jit(solution)/shard_map/ppermute | solution.py:612
  31.3 0.0 collective-permute-done.2
  31.3 7.4 %all-to-all-done.arrived = bf16[64,8,128]{2,1,0:T(8,128)(2,1)S(1)} async-done(((bf16[64,8,128]{2,1,0:T(8,128)(2,1)}), bf16[64,8,128]{2,1,0:T(8,128)(2,1)S(1)}, u32[]{:S(2)}, u32[]{:S(2)}) %all-to-all-start) | async-done | bytes 131104 | tf_op jit(solution)/shard_map/all_to_all | solution.py:661
  38.7 1.3 %plane_kernel.1 = bf16[8,256,128]{2,1,0:T(8,128)(2,1)} custom-call(bf16[64,8,128]{2,1,0:T(8,128)(2,1)S(1)} %all-to-all-done.arrived), custom_call_target="tpu_custom_call" | custom-call | flops 33000000 | bytes 655360 | tf_op jit(solution)/shard_map/plane_kernel/pallas_call | solution.py:596
  40.0 6.3 %all-to-all-start.1 = ((bf16[8,256,128]{2,1,0:T(8,128)(2,1)}), bf16[8,256,128]{2,1,0:T(8,128)(2,1)S(1)}, u32[]{:S(2)}, u32[]{:S(2)}) async-start(bf16[8,256,128]{2,1,0:T(8,128)(2,1)} %plane_kernel.1), calls=%async_computation.1 | async-start | bytes 1048576 | tf_op jit(solution)/shard_map/all_to_all | solution.py:672
  46.3 0.0 collective-permute-done.3
  46.4 1.3 %collective-permute-start.5 = (bf16[360,128]{1,0:T(8,128)(2,1)S(1)}, bf16[360,128]{1,0:T(8,128)(2,1)S(1)}, u32[]{:S(2)}, u32[]{:S(2)}) collective-permute-start(bf16[360,128]{1,0:T(8,128)(2,1)S(1)} %constant_dynamic-update-slice_fusion.3.sheet), channel_id=1, source_target_pairs={{1,0},{2,1},{3,2},{4,3},{5,4},{6,5},{7,6},{9,8},{10,9},{11,10},{12... | collective-permute-start | bytes 276488 | tf_op jit(solution)/shard_map/ppermute | solution.py:612
  47.7 4.0 %collective-permute-start.4 = (bf16[360,128]{1,0:T(8,128)(2,1)S(1)}, bf16[360,128]{1,0:T(8,128)(2,1)S(1)}, u32[]{:S(2)}, u32[]{:S(2)}) collective-permute-start(bf16[360,128]{1,0:T(8,128)(2,1)S(1)} %constant_dynamic-update-slice_fusion.3.sheet), channel_id=1, source_target_pairs={{0,1},{1,2},{2,3},{3,4},{4,5},{5,6},{6,7},{8,9},{9,10},{10,11},{11... | collective-permute-start | bytes 276488 | tf_op jit(solution)/shard_map/ppermute | solution.py:611
  51.7 1.8 %tables_kernel.1 = (f32[2,24,24,256]{3,2,1,0:T(8,128)S(1)}, bf16[3,256,24]{2,1,0:T(8,128)(2,1)S(1)}, f32[90,8,128]{2,1,0:T(8,128)S(1)}, f32[16,8,128]{2,1,0:T(8,...) custom-call(f32[3,192,32]{2,1,0:T(8,128)} %bitcast.6, f32[1,32]{1,0:T(1,128)} %bitcast.7, ...), custom_call_target="tpu_custom_call" | custom-call | flops 600000000 | bytes 3061888 | tf_op jit(solution)/shard_map/tables_kernel/pallas_call | solution.py:596
  53.5 2.3 %all-to-all-done.1.planes = bf16[8,256,128]{2,1,0:T(8,128)(2,1)S(1)} async-done(((bf16[8,256,128]{2,1,0:T(8,128)(2,1)}), bf16[8,256,128]{2,1,0:T(8,128)(2,1)S(1)}, u32[]{:S(2)}, u32[]{:S(2)}) %all-to-all-start.1) | async-done | bytes 524320 | tf_op jit(solution)/shard_map/all_to_all | solution.py:672
  55.8 1.5 %coarse_kernel.1 = (f32[65,8,128]{2,1,0:T(8,128)S(1)}, f32[8,64]{1,0:T(8,128)S(1)}) custom-call(s32[16,128]{1,0:T(8,128)S(1)} %get-tuple-element.18.numbers_h, bf16[8,256,128]{2,1,0:T(8,128)(2,1)S(1)} %all-to-all-done.1.planes, f32[2,24,24,256]{3,2,1,0:T(8,128)S(1)} %get-tuple-element.22.ab_ref, bf16[3,256,24]{2,1,0:T(8,128)(2,1)S(1)} %get-tuple-element.23.x_ref), custom_call_target="tpu_custom_call" | custom-call | flops 20000000 | bytes 2017280 | tf_op jit(solution)/shard_map/coarse_kernel/pallas_call | solution.py:596
  57.3 0.0 collective-permute-done.5.right
  57.3 0.0 collective-permute-done.4.left
  57.3 2.3 %fine_kernel.1 = (f32[8,8,64]{2,1,0:T(8,128)S(1)}, f32[28,8,128]{2,1,0:T(8,128)S(1)}, s32[1,128]{1,0:T(1,128)S(1)}) custom-call(s32[16,128]{1,0:T(8,128)S(1)} %get-tuple-element.18.numbers_h, bf16[360,128]{1,0:T(8,128)(2,1)S(1)} %collective-permute-done.4.left, f32[90,8,128]{2,1,0:T(8,128)S(1)} %get-tuple-element.25.centre, ...), custom_call_target="tpu_custom_call" | custom-call | flops 100000000 | bytes 1909248 | tf_op jit(solution)/shard_map/fine_kernel/pallas_call | solution.py:596
  59.6 2.8 %last_kernel.1 = (f32[8,512]{1,0:T(8,128)}, f32[1,512]{1,0:T(1,128)}) custom-call(s32[16,128]{1,0:T(8,128)S(1)} %get-tuple-element.18.numbers_h, s32[1,128]{1,0:T(1,128)S(1)} %get-tuple-element.26.names_h, f32[65,8,128]{2,1,0:T(8,128)S(1)} %get-tuple-element.27.coarse, f32[8,64]{1,0:T(8,128)S(1)} %get-tuple-element.28.coarse_ref, ...), custom_call_target="tpu_custom_call" | custom-call | flops 200000000 | bytes 2101760 | tf_op jit(solution)/shard_map/last_kernel/pallas_call | solution.py:596
  (8 shorter events, 0.1 us)
Async XLA Ops:
  4.3 22.8 %collective-permute-start = (bf16[40,128]{1,0:T(8,128)(2,1)S(1)}, bf16[40,128]{1,0:T(8,128)(2,1)S(1)}, u32[]{:S(2)}, u32[]{:S(2)}) collective-permute-start(bf16[40,128]{1,0:T(8,128)(2,1)S(1)} %get-tuple-element.19), channel_id=1, source_target_pairs={{0,64},{64,128},{128,192},{192,256},{256,320},{320,384},{384,448},... | collective-permute-start | bytes 30728 | tf_op jit(solution)/shard_map/ppermute | solution.py:611
  8.8 18.3 %collective-permute-start.1 = (bf16[40,128]{1,0:T(8,128)(2,1)S(1)}, bf16[40,128]{1,0:T(8,128)(2,1)S(1)}, u32[]{:S(2)}, u32[]{:S(2)}) collective-permute-start(bf16[40,128]{1,0:T(8,128)(2,1)S(1)} %get-tuple-element.19), channel_id=1, source_target_pairs={{64,0},{128,64},{192,128},{256,192},{320,256},{384,320},{448,384},... | collective-permute-start | bytes 30728 | tf_op jit(solution)/shard_map/ppermute | solution.py:612
  14.3 24.3 %all-to-all-start = ((bf16[64,8,128]{2,1,0:T(8,128)(2,1)}), bf16[64,8,128]{2,1,0:T(8,128)(2,1)S(1)}, u32[]{:S(2)}, u32[]{:S(2)}) async-start(bf16[64,8,128]{2,1,0:T(8,128)(2,1)} %get-tuple-element.21), calls=%async_computation | async-start | bytes 262144 | tf_op jit(solution)/shard_map/all_to_all | solution.py:661
  27.1 4.2 %collective-permute-start.2 = (bf16[120,128]{1,0:T(8,128)(2,1)S(1)}, bf16[120,128]{1,0:T(8,128)(2,1)S(1)}, u32[]{:S(2)}, u32[]{:S(2)}) collective-permute-start(bf16[120,128]{1,0:T(8,128)(2,1)S(1)} %constant_dynamic-update-slice_fusion), channel_id=1, source_target_pairs={{0,8},{8,16},{16,24},{24,32},{32,40},{40,48},{48,56},{1,9},{9,17},... | collective-permute-start | bytes 92168 | tf_op jit(solution)/shard_map/ppermute | solution.py:611
  30.0 16.3 %collective-permute-start.3 = (bf16[120,128]{1,0:T(8,128)(2,1)S(1)}, bf16[120,128]{1,0:T(8,128)(2,1)S(1)}, u32[]{:S(2)}, u32[]{:S(2)}) collective-permute-start(bf16[120,128]{1,0:T(8,128)(2,1)S(1)} %constant_dynamic-update-slice_fusion), channel_id=1, source_target_pairs={{8,0},{16,8},{24,16},{32,24},{40,32},{48,40},{56,48},{9,1},{17,9},... | collective-permute-start | bytes 92168 | tf_op jit(solution)/shard_map/ppermute | solution.py:612
  40.0 15.8 %all-to-all-start.1 = ((bf16[8,256,128]{2,1,0:T(8,128)(2,1)}), bf16[8,256,128]{2,1,0:T(8,128)(2,1)S(1)}, u32[]{:S(2)}, u32[]{:S(2)}) async-start(bf16[8,256,128]{2,1,0:T(8,128)(2,1)} %plane_kernel.1), calls=%async_computation.1 | async-start | bytes 1048576 | tf_op jit(solution)/shard_map/all_to_all | solution.py:672
  46.4 10.9 %collective-permute-start.5 = (bf16[360,128]{1,0:T(8,128)(2,1)S(1)}, bf16[360,128]{1,0:T(8,128)(2,1)S(1)}, u32[]{:S(2)}, u32[]{:S(2)}) collective-permute-start(bf16[360,128]{1,0:T(8,128)(2,1)S(1)} %constant_dynamic-update-slice_fusion.3.sheet), channel_id=1, source_target_pairs={{1,0},{2,1},{3,2},{4,3},{5,4},{6,5},{7,6},{9,8},{10,9},{11,10},{12... | collective-permute-start | bytes 276488 | tf_op jit(solution)/shard_map/ppermute | solution.py:612
  47.7 9.6 %collective-permute-start.4 = (bf16[360,128]{1,0:T(8,128)(2,1)S(1)}, bf16[360,128]{1,0:T(8,128)(2,1)S(1)}, u32[]{:S(2)}, u32[]{:S(2)}) collective-permute-start(bf16[360,128]{1,0:T(8,128)(2,1)S(1)} %constant_dynamic-update-slice_fusion.3.sheet), channel_id=1, source_target_pairs={{0,1},{1,2},{2,3},{3,4},{4,5},{5,6},{6,7},{8,9},{9,10},{10,11},{11... | collective-permute-start | bytes 276488 | tf_op jit(solution)/shard_map/ppermute | solution.py:611
